TPU v7x, 128 devices: a whole 4x4x4 slice. The times are simulated.
128 devices in a mesh: dp: 8 (over x, core), shard: 16 (over z, y).
Axes of the slice: x: 4, y: 4, z: 4, core: 2. Of those that a mesh axis runs over, the one named last changes fastest.
Arguments:
- partials: bfloat16 [8, 16, 1024, 3968], P('dp', 'shard'), may hold values from -6 to 6
- error: float32 [8, 1024, 3968], P('dp', 'shard'), may hold values from -4 to 4
- basis: float32 [3968, 32], replicated, may hold values from -6 to 6
Outputs:
- approx_grad: bfloat16 [1024, 3968], P('shard')
- error_next: float32 [8, 1024, 3968], P('dp', 'shard')
- basis_next: float32 [3968, 32], replicated
All inputs are finite; a program needn't handle non-finite values.
Results may differ from a plain program's by a relative error of at most 0.0012.
Values sent between devices are 32-bit elements; how exact they have to be, the bound alone decides.
No kernel may reach another device: no remote copies, remote signals or barrier semaphores. Data moves between devices by JAX's collectives and lax.ppermute only.
A program may use at most 128 MiB of HBM per device.

v0:
```python
import jax
import jax.numpy as jnp
from jax import lax
from jax.sharding import PartitionSpec as P


def orthonormal(pmat, summed):
    count = pmat.shape[1]
    order = jnp.arange(count)

    def sweep(index, mat):
        column = lax.dynamic_slice_in_dim(mat, index, 1, 1)[:, 0]
        products = summed(jnp.dot(column, mat, precision=lax.Precision.HIGHEST))
        own_norm = lax.dynamic_slice_in_dim(products, index, 1, 0)[0]
        weights = jnp.where(order > index, products / own_norm, jnp.zeros_like(products))
        mat = mat - column[:, None] * weights[None, :]
        scaled = column / jnp.sqrt(own_norm)
        return lax.dynamic_update_slice_in_dim(mat, scaled[:, None], index, 1)

    return lax.fori_loop(0, count, sweep, pmat)


def across_shard(values):
    return lax.psum(values, "shard")


def shards(partials, error, basis):
    replicas = lax.axis_size("dp")
    owned_sum = lax.psum_scatter(
        partials[0, 0].astype(jnp.float32), "shard", scatter_dimension=0, tiled=True
    )
    merged = error[0] + owned_sum
    local_terms = jnp.dot(merged, basis, precision=lax.Precision.HIGHEST)
    pmat = lax.psum(local_terms, "dp")
    phat = orthonormal(pmat, across_shard)
    q_terms = lax.dot_general(
        merged, phat, (((0,), (0,)), ((), ())), precision=lax.Precision.HIGHEST
    )
    qsum = lax.psum(q_terms, ("dp", "shard"))
    approx = jnp.dot(phat, qsum.T, precision=lax.Precision.HIGHEST) / replicas
    return (approx.astype(jnp.bfloat16), (merged - approx)[None], qsum / replicas)


def solution(mesh):
    return jax.shard_map(
        shards,
        mesh=mesh,
        in_specs=(P("dp", "shard", None, None), P("dp", "shard", None), P()),
        out_specs=(P("shard", None), P("dp", "shard", None), P()),
        check_vma=False,
    )
```

profile of v0, /device:TPU:1, one launch (start us, length us, event | category | flops | bytes accessed | tf_op | source)
XLA Modules:
  0.0 1549.8 jit_solution(6619185661377790086)
XLA Ops:
  7.2 10.1 bitcast_convert_fusion
  17.4 111.4 %reduce-scatter.2.cloned.1.call-done = f32[64,3968]{1,0:T(8,128)} async-done(((f32[1024,3968]{1,0:T(8,128)}), f32[64,3968]{1,0:T(8,128)}) %reduce-scatter.2.cloned.1.call-update) | async-done | bytes 1015824 | tf_op jit(solution)/shard_map/reduce_scatter | solution.py:29
  128.8 2.2 fusion.4
  131.0 22.5 %psum.25 = f32[64,32]{0,1:T(8,128)S(1)} all-reduce(f32[64,32]{0,1:T(8,128)S(1)} %fusion.4), channel_id=1, replica_groups=mesh['dp'=8,'shard'=16] {'dp'}, use_global_device_ids=true, to_apply=%region_1.0 | all-reduce | flops 2048 | bytes 16384 | tf_op jit(solution)/shard_map/psum | solution.py:34
  153.6 1011.9 %while.14 = (s32[]{:T(128)}, f32[64,32]{0,1:T(8,128)S(1)}, s32[]{:T(128)}, s32[]{:T(128)}) while((s32[]{:T(128)}, f32[64,32]{0,1:T(8,128)S(1)}, s32[]{:T(128)}, s32[]{:T(128)}) %tuple.39), condition=%wide.region_4.5_spmd.clone, body=%wide.region_2.4_spmd.clone.sunk | while | flops 28866 | bytes 35681 | solution.py:20
  153.7 31.3 %psum.29 = f32[32]{0:T(128)S(1)} all-reduce(f32[32]{0:T(128)S(1)} %convolution_bitcast_fusion.2), channel_id=1, replica_groups=mesh['dp'=8,'shard'=16] {'shard'}, use_global_device_ids=true, to_apply=%region_3.0 | all-reduce | flops 32 | bytes 256 | tf_op jit(solution)/shard_map/while/body/eval_jaxpr/psum | solution.py:24
  186.3 0.7 compare_select_fusion.2
  187.2 28.7 %psum.29 = f32[32]{0:T(128)S(1)} all-reduce(f32[32]{0:T(128)S(1)} %convolution_bitcast_fusion.2), channel_id=1, replica_groups=mesh['dp'=8,'shard'=16] {'shard'}, use_global_device_ids=true, to_apply=%region_3.0 | all-reduce | flops 32 | bytes 256 | tf_op jit(solution)/shard_map/while/body/eval_jaxpr/psum | solution.py:24
  217.2 0.7 compare_select_fusion.2
  218.1 30.2 %psum.29 = f32[32]{0:T(128)S(1)} all-reduce(f32[32]{0:T(128)S(1)} %convolution_bitcast_fusion.2), channel_id=1, replica_groups=mesh['dp'=8,'shard'=16] {'shard'}, use_global_device_ids=true, to_apply=%region_3.0 | all-reduce | flops 32 | bytes 256 | tf_op jit(solution)/shard_map/while/body/eval_jaxpr/psum | solution.py:24
  249.6 0.7 compare_select_fusion.2
  250.5 28.8 %psum.29 = f32[32]{0:T(128)S(1)} all-reduce(f32[32]{0:T(128)S(1)} %convolution_bitcast_fusion.2), channel_id=1, replica_groups=mesh['dp'=8,'shard'=16] {'shard'}, use_global_device_ids=true, to_apply=%region_3.0 | all-reduce | flops 32 | bytes 256 | tf_op jit(solution)/shard_map/while/body/eval_jaxpr/psum | solution.py:24
  280.7 0.7 compare_select_fusion.2
  281.6 29.6 %psum.29 = f32[32]{0:T(128)S(1)} all-reduce(f32[32]{0:T(128)S(1)} %convolution_bitcast_fusion.2), channel_id=1, replica_groups=mesh['dp'=8,'shard'=16] {'shard'}, use_global_device_ids=true, to_apply=%region_3.0 | all-reduce | flops 32 | bytes 256 | tf_op jit(solution)/shard_map/while/body/eval_jaxpr/psum | solution.py:24
  312.5 0.7 compare_select_fusion.2
  313.4 28.8 %psum.29 = f32[32]{0:T(128)S(1)} all-reduce(f32[32]{0:T(128)S(1)} %convolution_bitcast_fusion.2), channel_id=1, replica_groups=mesh['dp'=8,'shard'=16] {'shard'}, use_global_device_ids=true, to_apply=%region_3.0 | all-reduce | flops 32 | bytes 256 | tf_op jit(solution)/shard_map/while/body/eval_jaxpr/psum | solution.py:24
  343.5 0.7 compare_select_fusion.2
  344.4 30.5 %psum.29 = f32[32]{0:T(128)S(1)} all-reduce(f32[32]{0:T(128)S(1)} %convolution_bitcast_fusion.2), channel_id=1, replica_groups=mesh['dp'=8,'shard'=16] {'shard'}, use_global_device_ids=true, to_apply=%region_3.0 | all-reduce | flops 32 | bytes 256 | tf_op jit(solution)/shard_map/while/body/eval_jaxpr/psum | solution.py:24
  376.2 0.7 compare_select_fusion.2
  377.1 28.7 %psum.29 = f32[32]{0:T(128)S(1)} all-reduce(f32[32]{0:T(128)S(1)} %convolution_bitcast_fusion.2), channel_id=1, replica_groups=mesh['dp'=8,'shard'=16] {'shard'}, use_global_device_ids=true, to_apply=%region_3.0 | all-reduce | flops 32 | bytes 256 | tf_op jit(solution)/shard_map/while/body/eval_jaxpr/psum | solution.py:24
  407.1 0.7 compare_select_fusion.2
  408.0 30.6 %psum.29 = f32[32]{0:T(128)S(1)} all-reduce(f32[32]{0:T(128)S(1)} %convolution_bitcast_fusion.2), channel_id=1, replica_groups=mesh['dp'=8,'shard'=16] {'shard'}, use_global_device_ids=true, to_apply=%region_3.0 | all-reduce | flops 32 | bytes 256 | tf_op jit(solution)/shard_map/while/body/eval_jaxpr/psum | solution.py:24
  439.9 0.7 compare_select_fusion.2
  440.8 28.5 %psum.29 = f32[32]{0:T(128)S(1)} all-reduce(f32[32]{0:T(128)S(1)} %convolution_bitcast_fusion.2), channel_id=1, replica_groups=mesh['dp'=8,'shard'=16] {'shard'}, use_global_device_ids=true, to_apply=%region_3.0 | all-reduce | flops 32 | bytes 256 | tf_op jit(solution)/shard_map/while/body/eval_jaxpr/psum | solution.py:24
  470.6 0.7 compare_select_fusion.2
  471.5 30.1 %psum.29 = f32[32]{0:T(128)S(1)} all-reduce(f32[32]{0:T(128)S(1)} %convolution_bitcast_fusion.2), channel_id=1, replica_groups=mesh['dp'=8,'shard'=16] {'shard'}, use_global_device_ids=true, to_apply=%region_3.0 | all-reduce | flops 32 | bytes 256 | tf_op jit(solution)/shard_map/while/body/eval_jaxpr/psum | solution.py:24
  503.7 29.2 %psum.29 = f32[32]{0:T(128)S(1)} all-reduce(f32[32]{0:T(128)S(1)} %convolution_bitcast_fusion.2), channel_id=1, replica_groups=mesh['dp'=8,'shard'=16] {'shard'}, use_global_device_ids=true, to_apply=%region_3.0 | all-reduce | flops 32 | bytes 256 | tf_op jit(solution)/shard_map/while/body/eval_jaxpr/psum | solution.py:24
  534.2 0.7 compare_select_fusion.2
  535.1 29.4 %psum.29 = f32[32]{0:T(128)S(1)} all-reduce(f32[32]{0:T(128)S(1)} %convolution_bitcast_fusion.2), channel_id=1, replica_groups=mesh['dp'=8,'shard'=16] {'shard'}, use_global_device_ids=true, to_apply=%region_3.0 | all-reduce | flops 32 | bytes 256 | tf_op jit(solution)/shard_map/while/body/eval_jaxpr/psum | solution.py:24
  565.8 0.7 compare_select_fusion.2
  566.7 29.1 %psum.29 = f32[32]{0:T(128)S(1)} all-reduce(f32[32]{0:T(128)S(1)} %convolution_bitcast_fusion.2), channel_id=1, replica_groups=mesh['dp'=8,'shard'=16] {'shard'}, use_global_device_ids=true, to_apply=%region_3.0 | all-reduce | flops 32 | bytes 256 | tf_op jit(solution)/shard_map/while/body/eval_jaxpr/psum | solution.py:24
  597.1 0.7 compare_select_fusion.2
  598.0 29.4 %psum.29 = f32[32]{0:T(128)S(1)} all-reduce(f32[32]{0:T(128)S(1)} %convolution_bitcast_fusion.2), channel_id=1, replica_groups=mesh['dp'=8,'shard'=16] {'shard'}, use_global_device_ids=true, to_apply=%region_3.0 | all-reduce | flops 32 | bytes 256 | tf_op jit(solution)/shard_map/while/body/eval_jaxpr/psum | solution.py:24
  628.6 0.7 compare_select_fusion.2
  629.5 29.7 %psum.29 = f32[32]{0:T(128)S(1)} all-reduce(f32[32]{0:T(128)S(1)} %convolution_bitcast_fusion.2), channel_id=1, replica_groups=mesh['dp'=8,'shard'=16] {'shard'}, use_global_device_ids=true, to_apply=%region_3.0 | all-reduce | flops 32 | bytes 256 | tf_op jit(solution)/shard_map/while/body/eval_jaxpr/psum | solution.py:24
  660.5 0.7 compare_select_fusion.2
  661.4 28.7 %psum.29 = f32[32]{0:T(128)S(1)} all-reduce(f32[32]{0:T(128)S(1)} %convolution_bitcast_fusion.2), channel_id=1, replica_groups=mesh['dp'=8,'shard'=16] {'shard'}, use_global_device_ids=true, to_apply=%region_3.0 | all-reduce | flops 32 | bytes 256 | tf_op jit(solution)/shard_map/while/body/eval_jaxpr/psum | solution.py:24
  691.5 0.7 compare_select_fusion.2
  692.4 29.7 %psum.29 = f32[32]{0:T(128)S(1)} all-reduce(f32[32]{0:T(128)S(1)} %convolution_bitcast_fusion.2), channel_id=1, replica_groups=mesh['dp'=8,'shard'=16] {'shard'}, use_global_device_ids=true, to_apply=%region_3.0 | all-reduce | flops 32 | bytes 256 | tf_op jit(solution)/shard_map/while/body/eval_jaxpr/psum | solution.py:24
  723.4 0.7 compare_select_fusion.2
  724.3 29.1 %psum.29 = f32[32]{0:T(128)S(1)} all-reduce(f32[32]{0:T(128)S(1)} %convolution_bitcast_fusion.2), channel_id=1, replica_groups=mesh['dp'=8,'shard'=16] {'shard'}, use_global_device_ids=true, to_apply=%region_3.0 | all-reduce | flops 32 | bytes 256 | tf_op jit(solution)/shard_map/while/body/eval_jaxpr/psum | solution.py:24
  754.7 0.7 compare_select_fusion.2
  755.5 29.8 %psum.29 = f32[32]{0:T(128)S(1)} all-reduce(f32[32]{0:T(128)S(1)} %convolution_bitcast_fusion.2), channel_id=1, replica_groups=mesh['dp'=8,'shard'=16] {'shard'}, use_global_device_ids=true, to_apply=%region_3.0 | all-reduce | flops 32 | bytes 256 | tf_op jit(solution)/shard_map/while/body/eval_jaxpr/psum | solution.py:24
  786.6 0.7 compare_select_fusion.2
  787.5 29.0 %psum.29 = f32[32]{0:T(128)S(1)} all-reduce(f32[32]{0:T(128)S(1)} %convolution_bitcast_fusion.2), channel_id=1, replica_groups=mesh['dp'=8,'shard'=16] {'shard'}, use_global_device_ids=true, to_apply=%region_3.0 | all-reduce | flops 32 | bytes 256 | tf_op jit(solution)/shard_map/while/body/eval_jaxpr/psum | solution.py:24
  817.8 0.7 compare_select_fusion.2
  818.7 29.5 %psum.29 = f32[32]{0:T(128)S(1)} all-reduce(f32[32]{0:T(128)S(1)} %convolution_bitcast_fusion.2), channel_id=1, replica_groups=mesh['dp'=8,'shard'=16] {'shard'}, use_global_device_ids=true, to_apply=%region_3.0 | all-reduce | flops 32 | bytes 256 | tf_op jit(solution)/shard_map/while/body/eval_jaxpr/psum | solution.py:24
  849.5 0.7 compare_select_fusion.2
  850.4 29.7 %psum.29 = f32[32]{0:T(128)S(1)} all-reduce(f32[32]{0:T(128)S(1)} %convolution_bitcast_fusion.2), channel_id=1, replica_groups=mesh['dp'=8,'shard'=16] {'shard'}, use_global_device_ids=true, to_apply=%region_3.0 | all-reduce | flops 32 | bytes 256 | tf_op jit(solution)/shard_map/while/body/eval_jaxpr/psum | solution.py:24
  881.4 0.7 compare_select_fusion.2
  882.3 29.2 %psum.29 = f32[32]{0:T(128)S(1)} all-reduce(f32[32]{0:T(128)S(1)} %convolution_bitcast_fusion.2), channel_id=1, replica_groups=mesh['dp'=8,'shard'=16] {'shard'}, use_global_device_ids=true, to_apply=%region_3.0 | all-reduce | flops 32 | bytes 256 | tf_op jit(solution)/shard_map/while/body/eval_jaxpr/psum | solution.py:24
  912.8 0.7 compare_select_fusion.2
  913.7 29.3 %psum.29 = f32[32]{0:T(128)S(1)} all-reduce(f32[32]{0:T(128)S(1)} %convolution_bitcast_fusion.2), channel_id=1, replica_groups=mesh['dp'=8,'shard'=16] {'shard'}, use_global_device_ids=true, to_apply=%region_3.0 | all-reduce | flops 32 | bytes 256 | tf_op jit(solution)/shard_map/while/body/eval_jaxpr/psum | solution.py:24
  945.2 29.2 %psum.29 = f32[32]{0:T(128)S(1)} all-reduce(f32[32]{0:T(128)S(1)} %convolution_bitcast_fusion.2), channel_id=1, replica_groups=mesh['dp'=8,'shard'=16] {'shard'}, use_global_device_ids=true, to_apply=%region_3.0 | all-reduce | flops 32 | bytes 256 | tf_op jit(solution)/shard_map/while/body/eval_jaxpr/psum | solution.py:24
  976.6 29.2 %psum.29 = f32[32]{0:T(128)S(1)} all-reduce(f32[32]{0:T(128)S(1)} %convolution_bitcast_fusion.2), channel_id=1, replica_groups=mesh['dp'=8,'shard'=16] {'shard'}, use_global_device_ids=true, to_apply=%region_3.0 | all-reduce | flops 32 | bytes 256 | tf_op jit(solution)/shard_map/while/body/eval_jaxpr/psum | solution.py:24
  1008.0 29.3 %psum.29 = f32[32]{0:T(128)S(1)} all-reduce(f32[32]{0:T(128)S(1)} %convolution_bitcast_fusion.2), channel_id=1, replica_groups=mesh['dp'=8,'shard'=16] {'shard'}, use_global_device_ids=true, to_apply=%region_3.0 | all-reduce | flops 32 | bytes 256 | tf_op jit(solution)/shard_map/while/body/eval_jaxpr/psum | solution.py:24
  1039.5 29.2 %psum.29 = f32[32]{0:T(128)S(1)} all-reduce(f32[32]{0:T(128)S(1)} %convolution_bitcast_fusion.2), channel_id=1, replica_groups=mesh['dp'=8,'shard'=16] {'shard'}, use_global_device_ids=true, to_apply=%region_3.0 | all-reduce | flops 32 | bytes 256 | tf_op jit(solution)/shard_map/while/body/eval_jaxpr/psum | solution.py:24
  1070.9 29.2 %psum.29 = f32[32]{0:T(128)S(1)} all-reduce(f32[32]{0:T(128)S(1)} %convolution_bitcast_fusion.2), channel_id=1, replica_groups=mesh['dp'=8,'shard'=16] {'shard'}, use_global_device_ids=true, to_apply=%region_3.0 | all-reduce | flops 32 | bytes 256 | tf_op jit(solution)/shard_map/while/body/eval_jaxpr/psum | solution.py:24
  1102.4 29.3 %psum.29 = f32[32]{0:T(128)S(1)} all-reduce(f32[32]{0:T(128)S(1)} %convolution_bitcast_fusion.2), channel_id=1, replica_groups=mesh['dp'=8,'shard'=16] {'shard'}, use_global_device_ids=true, to_apply=%region_3.0 | all-reduce | flops 32 | bytes 256 | tf_op jit(solution)/shard_map/while/body/eval_jaxpr/psum | solution.py:24
  1133.9 29.5 %psum.29 = f32[32]{0:T(128)S(1)} all-reduce(f32[32]{0:T(128)S(1)} %convolution_bitcast_fusion.2), channel_id=1, replica_groups=mesh['dp'=8,'shard'=16] {'shard'}, use_global_device_ids=true, to_apply=%region_3.0 | all-reduce | flops 32 | bytes 256 | tf_op jit(solution)/shard_map/while/body/eval_jaxpr/psum | solution.py:24
  1165.4 2.7 fusion.3
  1168.2 369.3 %all-reduce.2.cloned.1.call-done = f32[3968,32]{0,1:T(8,128)} async-done(((f32[3968,32]{0,1:T(8,128)}), f32[3968,32]{0,1:T(8,128)}) %all-reduce.2.cloned.1.call-update) | async-done | bytes 507920 | tf_op jit(solution)/shard_map/psum | solution.py:39
  1537.5 3.6 subtract_bitcast_fusion
  1541.1 1.9 broadcast_multiply_fusion
  (177 shorter events, 32.6 us)
Async XLA Ops:
  7.2 121.6 %copy-start = (f32[3968,32]{0,1:T(8,128)S(1)}, f32[3968,32]{0,1:T(8,128)}, u32[]{:S(2)}) copy-start(f32[3968,32]{0,1:T(8,128)} %param.7) | copy-start | bytes 1523716
  7.2 121.6 %copy-start.1 = (f32[1,64,3968]{2,1,0:T(8,128)S(1)}, f32[1,64,3968]{2,1,0:T(8,128)}, u32[]{:S(2)}) copy-start(f32[1,64,3968]{2,1,0:T(8,128)} %param.6) | copy-start | bytes 3047428
  7.2 121.6 %reduce-scatter.2.cloned.1.call-start = ((), (), s32[]{:S(2)}) async-start(), calls=%async_computation.1 | async-start | bytes 17268736 | tf_op jit(solution)/shard_map/reduce_scatter | solution.py:29
  17.3 1520.2 %all-reduce.2.cloned.1.call-start = ((), (), s32[]{:S(2)}) async-start(), calls=%async_computation.2 | async-start | bytes 1015808 | tf_op jit(solution)/shard_map/psum | solution.py:39
Sparse Core Ops, SparseCore 0:
  17.5 111.2 reduce-scatter.1
  1168.3 369.1 all-reduce.1
where the time goes:
time: 1550 us
  blocking collectives  964 us (62%)
  waiting for transfers between devices  481 us (31%)
  other arithmetic  35.6 us (2%)
  loops' own time  22.8 us (1%)
  local copies, waits for them, and re-layouts  19.7 us (1%)
    psum x32, blocking collectives, across_shard(): return lax.psum(values, 'shard')  942 us
    psum x1, waiting for transfers between devices, shards(): qsum = lax.psum(q_terms, ('dp', 'shard'))  369 us
    reduce_scatter x1, waiting for transfers between devices, shards(): lax.psum_scatter(partials[0, 0].astype(jnp.float32), 'shard', scatter_dim...  111 us
  transfers between devices with their start and end apart: 2, of which 2 were waited for; matrix products, arithmetic and copies ran while one was open for 0% of the time, Pallas kernels for 0%

commit v1 on v0

v1 whole, which is shorter than its diff:
```python
import jax
import jax.numpy as jnp
from jax import lax
from jax.experimental import pallas as pl
from jax.experimental.pallas import tpu as pltpu
from jax.sharding import PartitionSpec as P

BOTH = ("dp", "shard")
SIDE = 4


def place(x, c, z, y):
    return ((x % SIDE) * 2 + c % 2) * SIDE * SIDE + (z % SIDE) * SIDE + y % SIDE


def moved(values, dx=0, dc=0, dz=0, dy=0):
    pairs = [
        (place(x, c, z, y), place(x + dx, c + dc, z + dz, y + dy))
        for x in range(SIDE)
        for c in range(2)
        for z in range(SIDE)
        for y in range(SIDE)
    ]
    return lax.ppermute(values, BOTH, pairs)


def split3(values):
    high = lax.reduce_precision(values, 8, 7)
    rest = values - high
    middle = lax.reduce_precision(rest, 8, 7)
    low = rest - middle
    return [piece.astype(jnp.bfloat16) for piece in (high, middle, low)]


def sum_axis(values, axis):
    ahead = moved(values, **{axis: 1})
    behind = moved(values, **{axis: -1})
    across = moved(values, **{axis: 2})
    return (values + across) + (ahead + behind)


def pick(values, index, size, dim):
    return lax.dynamic_slice_in_dim(values, index * size, size, dim)


def core_scatter(values, core):
    half = values.shape[0] // 2
    other = moved(pick(values, 1 - core, half, 0), dc=1)
    return pick(values, core, half, 0) + other


def core_gather(values, core):
    other = moved(values, dc=1)
    first = jnp.where(core == 0, values, other)
    second = jnp.where(core == 0, other, values)
    return jnp.concatenate([first, second], axis=0)


def sum_left(terms, core):
    half = core_scatter(terms, core)
    for axis in ("dx", "dy", "dz"):
        half = sum_axis(half, axis)
    return core_gather(half, core)


def sum_right(terms, core, x):
    half = core_scatter(terms, core)
    size = half.shape[1] // SIDE
    part = lambda k: pick(half, (x + k) % SIDE, size, 1)
    quarter = (part(0) + moved(part(2), dx=2)) + (
        moved(part(1), dx=1) + moved(part(3), dx=-1)
    )
    for axis in ("dy", "dz"):
        quarter = sum_axis(quarter, axis)
    ring = [quarter, moved(quarter, dx=-1), moved(quarter, dx=2), moved(quarter, dx=1)]
    ring = jnp.stack(ring)
    order = (jnp.arange(SIDE) - x) % SIDE
    whole = jnp.concatenate([lax.dynamic_index_in_dim(ring, order[k], 0, False) for k in range(SIDE)], axis=1)
    return core_gather(whole, core)


def orthonormal_kernel(mat_ref, out_ref, pieces_ref):
    count, rows = mat_ref.shape
    mat = mat_ref[...]
    order = lax.broadcasted_iota(jnp.int32, (count, 1), 0)
    for index in range(count):
        column = mat[index : index + 1, :]
        products = jnp.sum(mat * column, axis=1, keepdims=True)
        own_norm = products[index : index + 1, :]
        weights = jnp.where(order > index, products / own_norm, 0.0)
        scaled = column / jnp.sqrt(own_norm)
        mat = jnp.where(order == index, scaled, mat - weights * column)
    out_ref[...] = mat
    high = mat.astype(jnp.bfloat16)
    rest = mat - high.astype(jnp.float32)
    middle = rest.astype(jnp.bfloat16)
    low = (rest - middle.astype(jnp.float32)).astype(jnp.bfloat16)
    pieces_ref[0:count, :] = high
    pieces_ref[count : 2 * count, :] = middle
    pieces_ref[2 * count : 3 * count, :] = low


def orthonormal(mat):
    count, rows = mat.shape
    return pl.pallas_call(
        orthonormal_kernel,
        out_shape=(
            jax.ShapeDtypeStruct((count, rows), jnp.float32),
            jax.ShapeDtypeStruct((3 * count, rows), jnp.bfloat16),
        ),
        name="orthonormal",
    )(mat)


def shards(partials, error, basis):
    replicas = lax.axis_size("dp")
    dp, shard = lax.axis_index("dp"), lax.axis_index("shard")
    x, core = dp // 2, dp % 2
    partial = partials[0, 0]
    rows, width = partial.shape
    rank = basis.shape[1]
    own = error.shape[1]

    owned_sum = lax.psum_scatter(
        partial.astype(jnp.float32), "shard", scatter_dimension=0, tiled=True
    )

    pieces = jnp.concatenate(split3(basis), axis=1)
    three = jnp.dot(partial, pieces, preferred_element_type=jnp.float32)
    terms = three[:, :rank] + (three[:, rank : 2 * rank] + three[:, 2 * rank :])
    kept = jnp.dot(error[0], basis, precision=lax.Precision.HIGHEST)
    terms = lax.dynamic_update_slice_in_dim(
        terms, pick(terms, shard, own, 0) + kept, shard * own, 0
    )
    pmat = sum_left(terms.T, core)

    phat, phat_pieces = orthonormal(pmat)

    three = jnp.dot(phat_pieces, partial, preferred_element_type=jnp.float32)
    own_phat = pick(phat, shard, own, 1)
    kept = jnp.dot(own_phat, error[0], precision=lax.Precision.HIGHEST)
    terms = kept + (three[:rank] + (three[rank : 2 * rank] + three[2 * rank :]))
    padded = -(-width // (128 * SIDE)) * 128 * SIDE
    terms = jnp.pad(terms, ((0, 0), (0, padded - width)))
    qsum = sum_right(terms, core, x)[:, :width]

    approx = lax.dot_general(
        own_phat, qsum, (((0,), (0,)), ((), ())), precision=lax.Precision.HIGHEST
    ) / replicas
    merged = error[0] + owned_sum
    return (approx.astype(jnp.bfloat16), (merged - approx)[None], qsum.T / replicas)


def solution(mesh):
    return jax.shard_map(
        shards,
        mesh=mesh,
        in_specs=(P("dp", "shard", None, None), P("dp", "shard", None), P()),
        out_specs=(P("shard", None), P("dp", "shard", None), P()),
        check_vma=False,
    )
```

time: 1550 us -> 147 us (0.09)
  blocking collectives: 964 us -> 0 us
  waiting for transfers between devices: 481 us -> 50.1 us
  starting transfers between devices: 0.08 us -> 38.1 us
  other arithmetic: 35.6 us -> 11.8 us
  loops' own time: 22.8 us -> 0 us
  local copies, waits for them, and re-layouts: 19.7 us -> 2.02 us
    psum x33 -> x0, blocking collectives: 964 us -> none  [the longest x32 942 us: across_shard(): return lax.psum(values, 'shard')]
    psum x1 -> x0, waiting for transfers between devices: 369 us -> none  [shards(): qsum = lax.psum(q_terms, ('dp', 'shard'))]
    reduce_scatter x1, waiting for transfers between devices: 111 us -> 16.4 us  [shards(): lax.psum_scatter(partial.astype(jnp.float32), 'shard', scatter_dimension=...]
    ppermute x0 -> x25, starting transfers between devices: none -> 38.1 us  [moved(): return lax.ppermute(values, BOTH, pairs)]
    ppermute x0 -> x25, waiting for transfers between devices: none -> 33.7 us  [moved(): return lax.ppermute(values, BOTH, pairs)]
    another operation x1 -> x0, loops' own time: 22.8 us -> none  [orthonormal(): return lax.fori_loop(0, count, sweep, pmat)]
    select_n x32 -> x3, other arithmetic: 20.9 us -> 0.06 us  [the longest x2 0.05 us: core_gather(): first = jnp.where(core == 0, values, other)]
    dynamic_slice x32 -> x3, local copies, waits for them, and re-layouts: 18.7 us -> 0.06 us  [pick(): return lax.dynamic_slice_in_dim(values, index * size, size, dim)]
  transfers between devices with their start and end apart: 2 -> 26, of which waited for: 2 -> 20; matrix products, arithmetic and copies ran while one was open for 0% -> 11% of each run, Pallas kernels for 0% -> 3%
where the time goes in v1:
time: 147 us; the launch traced here: 146 us
  waiting for transfers between devices  50.1 us (34%)
  starting transfers between devices  38.1 us (26%)
  between operations  21.9 us (15%)
  matrix products  17.2 us (12%)
  other arithmetic  11.8 us (8%)
  Pallas kernels  4.99 us (3%)
  local copies, waits for them, and re-layouts  2.02 us (1%)
    ppermute x25, starting transfers between devices, moved(): return lax.ppermute(values, BOTH, pairs)  38.1 us
    ppermute x25, waiting for transfers between devices, moved(): return lax.ppermute(values, BOTH, pairs)  33.7 us
    reduce_scatter x1, waiting for transfers between devices, shards(): lax.psum_scatter(partial.astype(jnp.float32), 'shard', scatter_dimension=...  16.4 us
    convert_element_type x1, other arithmetic, shards(): partial.astype(jnp.float32)  9.92 us
    dot_general x1, matrix products, shards(): three = jnp.dot(partial, pieces, preferred_element_type=jnp.float32)  5.88 us
    dot_general x1, matrix products, shards(): three = jnp.dot(phat_pieces, partial, preferred_element_type=jnp.float32)  5.39 us
    pallas_call x1, Pallas kernels, orthonormal(): pl.pallas_call(orthonormal_kernel, out_shape=(jax.ShapeDtypeStruct((count...  4.99 us
    dot_general x1, matrix products, shards(): lax.dot_general(own_phat, qsum, (((0,), (0,)), ((), ())), precision=lax.P...  3.49 us
  transfers between devices with their start and end apart: 26, of which 20 were waited for; matrix products, arithmetic and copies ran while one was open for 11% of the time, Pallas kernels for 3%

profile of v1, /device:TPU:1, one launch (start us, length us, event | category | flops | bytes accessed | tf_op | source)
XLA Modules:
  0.0 146.1 jit_solution(1194331821137618917)
XLA Ops:
  7.2 0.0 reduce-scatter.2.cloned.1.call-start
  7.2 9.9 %bitcast_convert_fusion = f32[1024,3968]{1,0:T(8,128)} fusion(bf16[1,1,1024,3968]{3,2,1,0:T(8,128)(2,1)} %param.3), kind=kLoop, calls=%fused_computation | loop fusion | flops 4063232 | bytes 24379392 | tf_op jit(solution)/shard_map/convert_element_type | solution.py:125
  17.1 0.0 reduce-scatter.2.cloned.1.call-update
  17.2 0.0 copy-start
  17.2 1.0 copy-done.1
  18.2 0.1 reduce-precision_convert_fusion.1
  18.3 5.9 %fusion.4 = f32[1024,96]{0,1:T(8,128)S(1)} fusion(bf16[1,1,1024,3968]{3,2,1,0:T(8,128)(2,1)} %param.3, bf16[3968,32]{0,1:T(8,128)(2,1)S(1)} %get-tuple-element.12, bf16[3968,32]{0,1:T(8,128)(2,1)S(1)} %get-tuple-element.13, bf16[3968,32]{0,1:T(8,128)(2,1)S(1)} %get-tuple-element.11), kind=kOutput, calls=%fused_computation.7 | convolution fusion | flops 782426112 | bytes 9281536 | tf_op jit(solution)/shard_map/dot_general | solution.py:129
  24.2 1.0 convolution_add_fusion.1
  25.2 0.3 dynamic_update_slice.3
  25.6 1.5 %collective-permute-start = (f32[16,1024]{1,0:T(8,128)S(1)}, f32[16,1024]{1,0:T(8,128)S(1)}, u32[]{:S(2)}, u32[]{:S(2)}) collective-permute-start(f32[16,1024]{1,0:T(8,128)S(1)} %dynamic-slice_bitcast_fusion.4), channel_id=1, source_target_pairs={{0,16},{1,17},{2,18},{3,19},{4,20},{5,21},{6,22},{7,23},{8,24},{9,... | collective-permute-start | bytes 196616 | tf_op jit(solution)/shard_map/ppermute | solution.py:24
  27.1 0.9 collective-permute-done
  28.0 1.4 collective-permute-start.2
  29.3 1.4 collective-permute-start.3
  30.7 1.6 %collective-permute-start.1 = (f32[16,1024]{1,0:T(8,128)S(1)}, f32[16,1024]{1,0:T(8,128)S(1)}, u32[]{:S(2)}, u32[]{:S(2)}) collective-permute-start(f32[16,1024]{1,0:T(8,128)S(1)} %bitcast_add_fusion.1), channel_id=1, source_target_pairs={{0,64},{1,65},{2,66},{3,67},{4,68},{5,69},{6,70},{7,71},{8,72},{9,... | collective-permute-start | bytes 196616 | tf_op jit(solution)/shard_map/ppermute | solution.py:24
  32.3 0.0 collective-permute-done.2
  32.4 0.5 collective-permute-done.3
  32.9 2.5 %collective-permute-done.1 = f32[16,1024]{1,0:T(8,128)S(1)} collective-permute-done((f32[16,1024]{1,0:T(8,128)S(1)}, f32[16,1024]{1,0:T(8,128)S(1)}, u32[]{:S(2)}, u32[]{:S(2)}) %collective-permute-start.1) | collective-permute-done | bytes 65568 | tf_op jit(solution)/shard_map/ppermute | solution.py:24
  35.4 1.6 %collective-permute-start.5 = (f32[16,1024]{1,0:T(8,128)S(1)}, f32[16,1024]{1,0:T(8,128)S(1)}, u32[]{:S(2)}, u32[]{:S(2)}) collective-permute-start(f32[16,1024]{1,0:T(8,128)S(1)} %add_add_fusion.5), channel_id=1, source_target_pairs={{0,1},{1,2},{2,3},{3,0},{4,5},{5,6},{6,7},{7,4},{8,9},{9,10},{10,1... | collective-permute-start | bytes 196616 | tf_op jit(solution)/shard_map/ppermute | solution.py:24
  37.0 1.5 %collective-permute-start.6 = (f32[16,1024]{1,0:T(8,128)S(1)}, f32[16,1024]{1,0:T(8,128)S(1)}, u32[]{:S(2)}, u32[]{:S(2)}) collective-permute-start(f32[16,1024]{1,0:T(8,128)S(1)} %add_add_fusion.5), channel_id=1, source_target_pairs={{0,3},{1,0},{2,1},{3,2},{4,7},{5,4},{6,5},{7,6},{8,11},{9,8},{10,9... | collective-permute-start | bytes 196616 | tf_op jit(solution)/shard_map/ppermute | solution.py:24
  38.5 1.5 collective-permute-start.4
  39.9 1.6 %collective-permute-done.5 = f32[16,1024]{1,0:T(8,128)S(1)} collective-permute-done((f32[16,1024]{1,0:T(8,128)S(1)}, f32[16,1024]{1,0:T(8,128)S(1)}, u32[]{:S(2)}, u32[]{:S(2)}) %collective-permute-start.5) | collective-permute-done | bytes 65568 | tf_op jit(solution)/shard_map/ppermute | solution.py:24
  41.5 0.1 collective-permute-done.6
  41.6 3.4 %collective-permute-done.4 = f32[16,1024]{1,0:T(8,128)S(1)} collective-permute-done((f32[16,1024]{1,0:T(8,128)S(1)}, f32[16,1024]{1,0:T(8,128)S(1)}, u32[]{:S(2)}, u32[]{:S(2)}) %collective-permute-start.4) | collective-permute-done | bytes 65568 | tf_op jit(solution)/shard_map/ppermute | solution.py:24
  45.0 2.2 %collective-permute-start.8 = (f32[16,1024]{1,0:T(8,128)S(1)}, f32[16,1024]{1,0:T(8,128)S(1)}, u32[]{:S(2)}, u32[]{:S(2)}) collective-permute-start(f32[16,1024]{1,0:T(8,128)S(1)} %add_add_fusion.4), channel_id=1, source_target_pairs={{0,4},{1,5},{2,6},{3,7},{4,8},{5,9},{6,10},{7,11},{8,12},{9,13},{1... | collective-permute-start | bytes 196616 | tf_op jit(solution)/shard_map/ppermute | solution.py:24
  47.2 2.0 %collective-permute-start.9 = (f32[16,1024]{1,0:T(8,128)S(1)}, f32[16,1024]{1,0:T(8,128)S(1)}, u32[]{:S(2)}, u32[]{:S(2)}) collective-permute-start(f32[16,1024]{1,0:T(8,128)S(1)} %add_add_fusion.4), channel_id=1, source_target_pairs={{0,12},{1,13},{2,14},{3,15},{4,0},{5,1},{6,2},{7,3},{8,4},{9,5},{1... | collective-permute-start | bytes 196616 | tf_op jit(solution)/shard_map/ppermute | solution.py:24
  49.3 1.4 collective-permute-start.7
  50.7 0.9 collective-permute-done.8
  51.5 0.1 collective-permute-done.9
  51.7 3.5 %collective-permute-done.7 = f32[16,1024]{1,0:T(8,128)S(1)} collective-permute-done((f32[16,1024]{1,0:T(8,128)S(1)}, f32[16,1024]{1,0:T(8,128)S(1)}, u32[]{:S(2)}, u32[]{:S(2)}) %collective-permute-start.7) | collective-permute-done | bytes 65568 | tf_op jit(solution)/shard_map/ppermute | solution.py:24
  55.2 4.8 %collective-permute-start.10 = (f32[16,1024]{1,0:T(8,128)S(1)}, f32[16,1024]{1,0:T(8,128)S(1)}, u32[]{:S(2)}, u32[]{:S(2)}) collective-permute-start(f32[16,1024]{1,0:T(8,128)S(1)} %add_add_fusion.3), channel_id=1, source_target_pairs={{0,16},{1,17},{2,18},{3,19},{4,20},{5,21},{6,22},{7,23},{8,24},{9,... | collective-permute-start | bytes 196616 | tf_op jit(solution)/shard_map/ppermute | solution.py:24
  60.0 0.9 collective-permute-done.10
  61.0 0.7 pad_maximum_fusion.4.mat_ref
  61.6 5.0 %orthonormal.1 = (f32[32,1024]{1,0:T(8,128)}, bf16[96,1024]{1,0:T(8,128)(2,1)}) custom-call(f32[32,1024]{1,0:T(8,128)} %pad_maximum_fusion.4.mat_ref), custom_call_target="tpu_custom_call" | custom-call | tf_op jit(solution)/shard_map/orthonormal/pallas_call | solution.py:105
  66.6 5.4 %fusion = f32[96,3968]{1,0:T(8,128)S(1)} fusion(bf16[96,1024]{1,0:T(8,128)(2,1)} %get-tuple-element.6, bf16[1,1,1024,3968]{3,2,1,0:T(8,128)(2,1)} %param.3), kind=kOutput, calls=%fused_computation.1 | convolution fusion | flops 780140544 | bytes 9846784 | tf_op jit(solution)/shard_map/dot_general | solution.py:139
  72.0 1.4 convolution_add_fusion
  73.5 0.2 collective-permute-start.11
  73.7 1.4 collective-permute-done.11
  75.2 0.4 collective-permute-start.13
  75.6 2.3 %collective-permute-start.14 = (f32[16,1024]{1,0:T(8,128)S(1)}, f32[16,1024]{1,0:T(8,128)S(1)}, u32[]{:S(2)}, u32[]{:S(2)}) collective-permute-start(f32[16,1024]{1,0:T(8,128)S(1)} %get-tuple-element.19), channel_id=1, source_target_pairs={{0,96},{1,97},{2,98},{3,99},{4,100},{5,101},{6,102},{7,103},{8,104... | collective-permute-start | bytes 196616 | tf_op jit(solution)/shard_map/ppermute | solution.py:24
  77.9 0.2 collective-permute-start.12
  78.1 2.0 %collective-permute-done.13 = f32[16,1024]{1,0:T(8,128)S(1)} collective-permute-done((f32[16,1024]{1,0:T(8,128)S(1)}, f32[16,1024]{1,0:T(8,128)S(1)}, u32[]{:S(2)}, u32[]{:S(2)}) %collective-permute-start.13) | collective-permute-done | bytes 65568 | tf_op jit(solution)/shard_map/ppermute | solution.py:24
  80.1 0.0 collective-permute-done.14
  80.1 2.4 %collective-permute-done.12 = f32[16,1024]{1,0:T(8,128)S(1)} collective-permute-done((f32[16,1024]{1,0:T(8,128)S(1)}, f32[16,1024]{1,0:T(8,128)S(1)}, u32[]{:S(2)}, u32[]{:S(2)}) %collective-permute-start.12) | collective-permute-done | bytes 65568 | tf_op jit(solution)/shard_map/ppermute | solution.py:24
  82.5 1.1 collective-permute-start.16
  83.7 1.6 %collective-permute-start.17 = (f32[16,1024]{1,0:T(8,128)S(1)}, f32[16,1024]{1,0:T(8,128)S(1)}, u32[]{:S(2)}, u32[]{:S(2)}) collective-permute-start(f32[16,1024]{1,0:T(8,128)S(1)} %add_add_fusion.2), channel_id=1, source_target_pairs={{0,3},{1,0},{2,1},{3,2},{4,7},{5,4},{6,5},{7,6},{8,11},{9,8},{10,9... | collective-permute-start | bytes 196616 | tf_op jit(solution)/shard_map/ppermute | solution.py:24
  85.3 0.3 collective-permute-start.15
  85.5 3.1 %collective-permute-done.16 = f32[16,1024]{1,0:T(8,128)S(1)} collective-permute-done((f32[16,1024]{1,0:T(8,128)S(1)}, f32[16,1024]{1,0:T(8,128)S(1)}, u32[]{:S(2)}, u32[]{:S(2)}) %collective-permute-start.16) | collective-permute-done | bytes 65568 | tf_op jit(solution)/shard_map/ppermute | solution.py:24
  88.6 0.0 collective-permute-done.17
  88.6 3.3 %collective-permute-done.15 = f32[16,1024]{1,0:T(8,128)S(1)} collective-permute-done((f32[16,1024]{1,0:T(8,128)S(1)}, f32[16,1024]{1,0:T(8,128)S(1)}, u32[]{:S(2)}, u32[]{:S(2)}) %collective-permute-start.15) | collective-permute-done | bytes 65568 | tf_op jit(solution)/shard_map/ppermute | solution.py:24
  91.9 1.1 collective-permute-start.19
  93.0 1.7 %collective-permute-start.20 = (f32[16,1024]{1,0:T(8,128)S(1)}, f32[16,1024]{1,0:T(8,128)S(1)}, u32[]{:S(2)}, u32[]{:S(2)}) collective-permute-start(f32[16,1024]{1,0:T(8,128)S(1)} %add_add_fusion.1), channel_id=1, source_target_pairs={{0,12},{1,13},{2,14},{3,15},{4,0},{5,1},{6,2},{7,3},{8,4},{9,5},{1... | collective-permute-start | bytes 196616 | tf_op jit(solution)/shard_map/ppermute | solution.py:24
  94.6 0.4 collective-permute-start.18
  95.0 2.4 %collective-permute-done.19 = f32[16,1024]{1,0:T(8,128)S(1)} collective-permute-done((f32[16,1024]{1,0:T(8,128)S(1)}, f32[16,1024]{1,0:T(8,128)S(1)}, u32[]{:S(2)}, u32[]{:S(2)}) %collective-permute-start.19) | collective-permute-done | bytes 65568 | tf_op jit(solution)/shard_map/ppermute | solution.py:24
  97.5 0.3 collective-permute-done.20
  97.7 3.3 %collective-permute-done.18 = f32[16,1024]{1,0:T(8,128)S(1)} collective-permute-done((f32[16,1024]{1,0:T(8,128)S(1)}, f32[16,1024]{1,0:T(8,128)S(1)}, u32[]{:S(2)}, u32[]{:S(2)}) %collective-permute-start.18) | collective-permute-done | bytes 65568 | tf_op jit(solution)/shard_map/ppermute | solution.py:24
  101.0 0.1 collective-permute-start.23
  101.1 3.3 %collective-permute-start.22 = (f32[16,1024]{1,0:T(8,128)S(1)}, f32[16,1024]{1,0:T(8,128)S(1)}, u32[]{:S(2)}, u32[]{:S(2)}) collective-permute-start(f32[16,1024]{1,0:T(8,128)S(1)} %add_add_fusion), channel_id=1, source_target_pairs={{0,64},{1,65},{2,66},{3,67},{4,68},{5,69},{6,70},{7,71},{8,72},{9,... | collective-permute-start | bytes 196616 | tf_op jit(solution)/shard_map/ppermute | solution.py:24
  104.4 0.0 collective-permute-start.21
  104.4 0.6 fusion.27
  112.8 4.5 %collective-permute-start.24 = (f32[16,4096]{1,0:T(8,128)S(1)}, f32[16,4096]{1,0:T(8,128)S(1)}, u32[]{:S(2)}, u32[]{:S(2)}) collective-permute-start(f32[16,4096]{1,0:T(8,128)S(1)} %pad_maximum_fusion.3), channel_id=1, source_target_pairs={{0,16},{1,17},{2,18},{3,19},{4,20},{5,21},{6,22},{7,23},{8,24},{9,... | collective-permute-start | bytes 786440 | tf_op jit(solution)/shard_map/ppermute | solution.py:24
  117.4 1.2 collective-permute-done.24
  118.6 0.8 multiply_bitcast_fusion
  119.4 16.4 %reduce-scatter.2.cloned.1.call-done = f32[64,3968]{1,0:T(8,128)} async-done(((f32[1024,3968]{1,0:T(8,128)}), f32[64,3968]{1,0:T(8,128)}) %reduce-scatter.2.cloned.1.call-update) | async-done | bytes 1015824 | tf_op jit(solution)/shard_map/reduce_scatter | solution.py:124
  135.8 3.5 %fusion.10 = (f32[1,64,3968]{2,1,0:T(8,128)}, bf16[64,3968]{1,0:T(8,128)(2,1)}) fusion(f32[64,3968]{1,0:T(8,128)} %reduce-scatter.2.cloned.1.call-done, f32[1,64,3968]{2,1,0:T(8,128)S(1)} %copy-done, f32[16,4096]{1,0:T(8,128)S(1)} %get-tuple-element.10, f32[16,4096]{1,0:T(8,128)S(1)} %get-tuple-element.9, f32[32,1024]{1,0:T(8,128)} %get-tuple-element.5, ...), kind=kOutput, calls=%fused_computation.13 | convolution fusion | flops 98660352 | bytes 4096004 | tf_op jit(solution)/shard_map/dot_general | solution.py:147
  (23 shorter events, 0.4 us)
Async XLA Ops:
  7.2 128.6 %reduce-scatter.2.cloned.1.call-start = ((), (), s32[]{:S(2)}) async-start(), calls=%async_computation.1 | async-start | bytes 17268736 | tf_op jit(solution)/shard_map/reduce_scatter | solution.py:124
  17.1 1.0 copy-start.1
  17.2 7.0 %copy-start = (f32[1,64,3968]{2,1,0:T(8,128)S(1)}, f32[1,64,3968]{2,1,0:T(8,128)}, u32[]{:S(2)}) copy-start(f32[1,64,3968]{2,1,0:T(8,128)} %param.4) | copy-start | bytes 3047428
  25.6 2.4 %collective-permute-start = (f32[16,1024]{1,0:T(8,128)S(1)}, f32[16,1024]{1,0:T(8,128)S(1)}, u32[]{:S(2)}, u32[]{:S(2)}) collective-permute-start(f32[16,1024]{1,0:T(8,128)S(1)} %dynamic-slice_bitcast_fusion.4), channel_id=1, source_target_pairs={{0,16},{1,17},{2,18},{3,19},{4,20},{5,21},{6,22},{7,23},{8,24},{9,... | collective-permute-start | bytes 196616 | tf_op jit(solution)/shard_map/ppermute | solution.py:24
  28.0 4.4 %collective-permute-start.2 = (f32[16,1024]{1,0:T(8,128)S(1)}, f32[16,1024]{1,0:T(8,128)S(1)}, u32[]{:S(2)}, u32[]{:S(2)}) collective-permute-start(f32[16,1024]{1,0:T(8,128)S(1)} %bitcast_add_fusion.1), channel_id=1, source_target_pairs={{0,32},{1,33},{2,34},{3,35},{4,36},{5,37},{6,38},{7,39},{8,40},{9,... | collective-permute-start | bytes 196616 | tf_op jit(solution)/shard_map/ppermute | solution.py:24
  29.3 3.5 %collective-permute-start.3 = (f32[16,1024]{1,0:T(8,128)S(1)}, f32[16,1024]{1,0:T(8,128)S(1)}, u32[]{:S(2)}, u32[]{:S(2)}) collective-permute-start(f32[16,1024]{1,0:T(8,128)S(1)} %bitcast_add_fusion.1), channel_id=1, source_target_pairs={{0,96},{1,97},{2,98},{3,99},{4,100},{5,101},{6,102},{7,103},{8,104... | collective-permute-start | bytes 196616 | tf_op jit(solution)/shard_map/ppermute | solution.py:24
  30.7 4.7 %collective-permute-start.1 = (f32[16,1024]{1,0:T(8,128)S(1)}, f32[16,1024]{1,0:T(8,128)S(1)}, u32[]{:S(2)}, u32[]{:S(2)}) collective-permute-start(f32[16,1024]{1,0:T(8,128)S(1)} %bitcast_add_fusion.1), channel_id=1, source_target_pairs={{0,64},{1,65},{2,66},{3,67},{4,68},{5,69},{6,70},{7,71},{8,72},{9,... | collective-permute-start | bytes 196616 | tf_op jit(solution)/shard_map/ppermute | solution.py:24
  35.4 6.1 %collective-permute-start.5 = (f32[16,1024]{1,0:T(8,128)S(1)}, f32[16,1024]{1,0:T(8,128)S(1)}, u32[]{:S(2)}, u32[]{:S(2)}) collective-permute-start(f32[16,1024]{1,0:T(8,128)S(1)} %add_add_fusion.5), channel_id=1, source_target_pairs={{0,1},{1,2},{2,3},{3,0},{4,5},{5,6},{6,7},{7,4},{8,9},{9,10},{10,1... | collective-permute-start | bytes 196616 | tf_op jit(solution)/shard_map/ppermute | solution.py:24
  37.0 4.6 %collective-permute-start.6 = (f32[16,1024]{1,0:T(8,128)S(1)}, f32[16,1024]{1,0:T(8,128)S(1)}, u32[]{:S(2)}, u32[]{:S(2)}) collective-permute-start(f32[16,1024]{1,0:T(8,128)S(1)} %add_add_fusion.5), channel_id=1, source_target_pairs={{0,3},{1,0},{2,1},{3,2},{4,7},{5,4},{6,5},{7,6},{8,11},{9,8},{10,9... | collective-permute-start | bytes 196616 | tf_op jit(solution)/shard_map/ppermute | solution.py:24
  38.5 6.5 %collective-permute-start.4 = (f32[16,1024]{1,0:T(8,128)S(1)}, f32[16,1024]{1,0:T(8,128)S(1)}, u32[]{:S(2)}, u32[]{:S(2)}) collective-permute-start(f32[16,1024]{1,0:T(8,128)S(1)} %add_add_fusion.5), channel_id=1, source_target_pairs={{0,2},{1,3},{2,0},{3,1},{4,6},{5,7},{6,4},{7,5},{8,10},{9,11},{10,... | collective-permute-start | bytes 196616 | tf_op jit(solution)/shard_map/ppermute | solution.py:24
  45.0 6.5 %collective-permute-start.8 = (f32[16,1024]{1,0:T(8,128)S(1)}, f32[16,1024]{1,0:T(8,128)S(1)}, u32[]{:S(2)}, u32[]{:S(2)}) collective-permute-start(f32[16,1024]{1,0:T(8,128)S(1)} %add_add_fusion.4), channel_id=1, source_target_pairs={{0,4},{1,5},{2,6},{3,7},{4,8},{5,9},{6,10},{7,11},{8,12},{9,13},{1... | collective-permute-start | bytes 196616 | tf_op jit(solution)/shard_map/ppermute | solution.py:24
  47.2 4.4 %collective-permute-start.9 = (f32[16,1024]{1,0:T(8,128)S(1)}, f32[16,1024]{1,0:T(8,128)S(1)}, u32[]{:S(2)}, u32[]{:S(2)}) collective-permute-start(f32[16,1024]{1,0:T(8,128)S(1)} %add_add_fusion.4), channel_id=1, source_target_pairs={{0,12},{1,13},{2,14},{3,15},{4,0},{5,1},{6,2},{7,3},{8,4},{9,5},{1... | collective-permute-start | bytes 196616 | tf_op jit(solution)/shard_map/ppermute | solution.py:24
  49.3 5.9 %collective-permute-start.7 = (f32[16,1024]{1,0:T(8,128)S(1)}, f32[16,1024]{1,0:T(8,128)S(1)}, u32[]{:S(2)}, u32[]{:S(2)}) collective-permute-start(f32[16,1024]{1,0:T(8,128)S(1)} %add_add_fusion.4), channel_id=1, source_target_pairs={{0,8},{1,9},{2,10},{3,11},{4,12},{5,13},{6,14},{7,15},{8,0},{9,1},... | collective-permute-start | bytes 196616 | tf_op jit(solution)/shard_map/ppermute | solution.py:24
  55.2 5.7 %collective-permute-start.10 = (f32[16,1024]{1,0:T(8,128)S(1)}, f32[16,1024]{1,0:T(8,128)S(1)}, u32[]{:S(2)}, u32[]{:S(2)}) collective-permute-start(f32[16,1024]{1,0:T(8,128)S(1)} %add_add_fusion.3), channel_id=1, source_target_pairs={{0,16},{1,17},{2,18},{3,19},{4,20},{5,21},{6,22},{7,23},{8,24},{9,... | collective-permute-start | bytes 196616 | tf_op jit(solution)/shard_map/ppermute | solution.py:24
  73.5 1.6 %collective-permute-start.11 = (f32[16,4096]{1,0:T(8,128)S(1)}, f32[16,4096]{1,0:T(8,128)S(1)}, u32[]{:S(2)}, u32[]{:S(2)}) collective-permute-start(f32[16,4096]{1,0:T(8,128)S(1)} %pad_dynamic-slice_fusion), channel_id=1, source_target_pairs={{0,16},{1,17},{2,18},{3,19},{4,20},{5,21},{6,22},{7,23},{8,24},{9,... | collective-permute-start | bytes 786440 | tf_op jit(solution)/shard_map/ppermute | solution.py:24
  75.2 4.9 %collective-permute-start.13 = (f32[16,1024]{1,0:T(8,128)S(1)}, f32[16,1024]{1,0:T(8,128)S(1)}, u32[]{:S(2)}, u32[]{:S(2)}) collective-permute-start(f32[16,1024]{1,0:T(8,128)S(1)} %get-tuple-element.20), channel_id=1, source_target_pairs={{0,32},{1,33},{2,34},{3,35},{4,36},{5,37},{6,38},{7,39},{8,40},{9,... | collective-permute-start | bytes 196616 | tf_op jit(solution)/shard_map/ppermute | solution.py:24
  75.6 4.5 %collective-permute-start.14 = (f32[16,1024]{1,0:T(8,128)S(1)}, f32[16,1024]{1,0:T(8,128)S(1)}, u32[]{:S(2)}, u32[]{:S(2)}) collective-permute-start(f32[16,1024]{1,0:T(8,128)S(1)} %get-tuple-element.19), channel_id=1, source_target_pairs={{0,96},{1,97},{2,98},{3,99},{4,100},{5,101},{6,102},{7,103},{8,104... | collective-permute-start | bytes 196616 | tf_op jit(solution)/shard_map/ppermute | solution.py:24
  77.9 4.6 %collective-permute-start.12 = (f32[16,1024]{1,0:T(8,128)S(1)}, f32[16,1024]{1,0:T(8,128)S(1)}, u32[]{:S(2)}, u32[]{:S(2)}) collective-permute-start(f32[16,1024]{1,0:T(8,128)S(1)} %get-tuple-element.18), channel_id=1, source_target_pairs={{0,64},{1,65},{2,66},{3,67},{4,68},{5,69},{6,70},{7,71},{8,72},{9,... | collective-permute-start | bytes 196616 | tf_op jit(solution)/shard_map/ppermute | solution.py:24
  82.5 6.1 %collective-permute-start.16 = (f32[16,1024]{1,0:T(8,128)S(1)}, f32[16,1024]{1,0:T(8,128)S(1)}, u32[]{:S(2)}, u32[]{:S(2)}) collective-permute-start(f32[16,1024]{1,0:T(8,128)S(1)} %add_add_fusion.2), channel_id=1, source_target_pairs={{0,1},{1,2},{2,3},{3,0},{4,5},{5,6},{6,7},{7,4},{8,9},{9,10},{10,1... | collective-permute-start | bytes 196616 | tf_op jit(solution)/shard_map/ppermute | solution.py:24
  83.7 4.9 %collective-permute-start.17 = (f32[16,1024]{1,0:T(8,128)S(1)}, f32[16,1024]{1,0:T(8,128)S(1)}, u32[]{:S(2)}, u32[]{:S(2)}) collective-permute-start(f32[16,1024]{1,0:T(8,128)S(1)} %add_add_fusion.2), channel_id=1, source_target_pairs={{0,3},{1,0},{2,1},{3,2},{4,7},{5,4},{6,5},{7,6},{8,11},{9,8},{10,9... | collective-permute-start | bytes 196616 | tf_op jit(solution)/shard_map/ppermute | solution.py:24
  85.3 6.6 %collective-permute-start.15 = (f32[16,1024]{1,0:T(8,128)S(1)}, f32[16,1024]{1,0:T(8,128)S(1)}, u32[]{:S(2)}, u32[]{:S(2)}) collective-permute-start(f32[16,1024]{1,0:T(8,128)S(1)} %add_add_fusion.2), channel_id=1, source_target_pairs={{0,2},{1,3},{2,0},{3,1},{4,6},{5,7},{6,4},{7,5},{8,10},{9,11},{10,... | collective-permute-start | bytes 196616 | tf_op jit(solution)/shard_map/ppermute | solution.py:24
  91.9 5.6 %collective-permute-start.19 = (f32[16,1024]{1,0:T(8,128)S(1)}, f32[16,1024]{1,0:T(8,128)S(1)}, u32[]{:S(2)}, u32[]{:S(2)}) collective-permute-start(f32[16,1024]{1,0:T(8,128)S(1)} %add_add_fusion.1), channel_id=1, source_target_pairs={{0,4},{1,5},{2,6},{3,7},{4,8},{5,9},{6,10},{7,11},{8,12},{9,13},{1... | collective-permute-start | bytes 196616 | tf_op jit(solution)/shard_map/ppermute | solution.py:24
  93.0 4.7 %collective-permute-start.20 = (f32[16,1024]{1,0:T(8,128)S(1)}, f32[16,1024]{1,0:T(8,128)S(1)}, u32[]{:S(2)}, u32[]{:S(2)}) collective-permute-start(f32[16,1024]{1,0:T(8,128)S(1)} %add_add_fusion.1), channel_id=1, source_target_pairs={{0,12},{1,13},{2,14},{3,15},{4,0},{5,1},{6,2},{7,3},{8,4},{9,5},{1... | collective-permute-start | bytes 196616 | tf_op jit(solution)/shard_map/ppermute | solution.py:24
  94.6 6.4 %collective-permute-start.18 = (f32[16,1024]{1,0:T(8,128)S(1)}, f32[16,1024]{1,0:T(8,128)S(1)}, u32[]{:S(2)}, u32[]{:S(2)}) collective-permute-start(f32[16,1024]{1,0:T(8,128)S(1)} %add_add_fusion.1), channel_id=1, source_target_pairs={{0,8},{1,9},{2,10},{3,11},{4,12},{5,13},{6,14},{7,15},{8,0},{9,1},... | collective-permute-start | bytes 196616 | tf_op jit(solution)/shard_map/ppermute | solution.py:24
  101.0 11.7 %collective-permute-start.23 = (f32[16,1024]{1,0:T(8,128)S(1)}, f32[16,1024]{1,0:T(8,128)S(1)}, u32[]{:S(2)}, u32[]{:S(2)}) collective-permute-start(f32[16,1024]{1,0:T(8,128)S(1)} %add_add_fusion), channel_id=1, source_target_pairs={{0,32},{1,33},{2,34},{3,35},{4,36},{5,37},{6,38},{7,39},{8,40},{9,... | collective-permute-start | bytes 196616 | tf_op jit(solution)/shard_map/ppermute | solution.py:24
  101.1 11.6 %collective-permute-start.22 = (f32[16,1024]{1,0:T(8,128)S(1)}, f32[16,1024]{1,0:T(8,128)S(1)}, u32[]{:S(2)}, u32[]{:S(2)}) collective-permute-start(f32[16,1024]{1,0:T(8,128)S(1)} %add_add_fusion), channel_id=1, source_target_pairs={{0,64},{1,65},{2,66},{3,67},{4,68},{5,69},{6,70},{7,71},{8,72},{9,... | collective-permute-start | bytes 196616 | tf_op jit(solution)/shard_map/ppermute | solution.py:24
  104.4 8.3 %collective-permute-start.21 = (f32[16,1024]{1,0:T(8,128)S(1)}, f32[16,1024]{1,0:T(8,128)S(1)}, u32[]{:S(2)}, u32[]{:S(2)}) collective-permute-start(f32[16,1024]{1,0:T(8,128)S(1)} %add_add_fusion), channel_id=1, source_target_pairs={{0,96},{1,97},{2,98},{3,99},{4,100},{5,101},{6,102},{7,103},{8,104... | collective-permute-start | bytes 196616 | tf_op jit(solution)/shard_map/ppermute | solution.py:24
  112.8 5.7 %collective-permute-start.24 = (f32[16,4096]{1,0:T(8,128)S(1)}, f32[16,4096]{1,0:T(8,128)S(1)}, u32[]{:S(2)}, u32[]{:S(2)}) collective-permute-start(f32[16,4096]{1,0:T(8,128)S(1)} %pad_maximum_fusion.3), channel_id=1, source_target_pairs={{0,16},{1,17},{2,18},{3,19},{4,20},{5,21},{6,22},{7,23},{8,24},{9,... | collective-permute-start | bytes 786440 | tf_op jit(solution)/shard_map/ppermute | solution.py:24
Sparse Core Ops, SparseCore 0:
  17.3 118.4 reduce-scatter.1

commit v2 on v0

v2 whole, which is shorter than its diff:
```python
import functools

import jax
import jax.numpy as jnp
from jax import lax
from jax.experimental import pallas as pl
from jax.experimental.pallas import tpu as pltpu
from jax.sharding import PartitionSpec as P

BOTH = ("dp", "shard")
SIDE = 4
LANES = 128
HIGHEST = lax.Precision.HIGHEST
FREE = pl.CostEstimate(flops=0, bytes_accessed=0, transcendentals=0)
ANY = pl.BlockSpec(memory_space=pl.ANY)
WHOLE = pl.BlockSpec(memory_space=pltpu.VMEM)
SCALARS = pl.BlockSpec(memory_space=pltpu.SMEM)


def limit(mebibytes):
    return pltpu.CompilerParams(vmem_limit_bytes=mebibytes << 20)


def place(x, c, z, y):
    return ((x % SIDE) * 2 + c % 2) * SIDE * SIDE + (z % SIDE) * SIDE + y % SIDE


def moved(values, route):
    spots = [
        (x, c, z, y)
        for x in range(SIDE)
        for c in range(2)
        for z in range(SIDE)
        for y in range(SIDE)
    ]
    return lax.ppermute(values, BOTH, [(place(*spot), place(*route(*spot))) for spot in spots])


def other_core(values):
    return moved(values, lambda x, c, z, y: (x, 1 - c, z, y))


def along_x(values, step):
    return moved(values, lambda x, c, z, y: (x + step, c, z, y))


def along_first(values, step):
    return moved(values, lambda x, c, z, y: (x, c, z + step * (1 - c), y + step * c))


def along_second(values, step):
    return moved(values, lambda x, c, z, y: (x, c, z + step * c, y + step * (1 - c)))


def pair_second(values, mask):
    return moved(values, lambda x, c, z, y: (x, c, z ^ (mask * c), y ^ (mask * (1 - c))))


def shape(*dims, dtype=jnp.float32):
    return jax.ShapeDtypeStruct(dims, dtype)


def run(kernel, outs, scalars, operands, after, name, room=8):
    def body(scalar_ref, *refs):
        kernel(scalar_ref, *refs[: len(operands)], *refs[len(operands) + 1 :])

    return pl.pallas_call(
        body,
        in_specs=[SCALARS] + [WHOLE] * len(operands) + [ANY],
        out_specs=[WHOLE] * len(outs),
        out_shape=outs,
        cost_estimate=FREE,
        compiler_params=limit(room),
        name=name,
    )(scalars, *operands, after)


def span(index, size):
    return pl.ds(pl.multiple_of(index * size, size), size)


def combine_kernel(arity, coords_ref, *refs):
    inputs, outputs = refs[: sum(arity)], refs[sum(arity) + 1 :]
    start = 0
    for count, out_ref in zip(arity, outputs):
        own, *came = inputs[start : start + count]
        total = own[0, 0, 0].astype(jnp.float32)
        for ref in came:
            total = total + ref[0]
        out_ref[0] = total
        start += count


def combine(blocks, coords, wanted, after):
    depth, width = blocks.shape[3:]
    cuts = blocks.shape[2] // 2
    arity, operands, specs = [], [], []
    whole = pl.BlockSpec((1, depth, width), lambda k, i, s: (k, i, 0))
    for owner, half, came in wanted:

        def where(k, i, s, owner=owner, half=half):
            core = s[2 * SIDE]
            there = s[owner] * (1 - core) + k * core, s[owner] * core + k * (1 - core)
            return *there, half * cuts + i, 0, 0

        operands += [blocks, *came]
        specs += [pl.BlockSpec((1, 1, 1, depth, width), where)] + [whole] * len(came)
        arity.append(1 + len(came))
    return pl.pallas_call(
        functools.partial(combine_kernel, arity),
        grid_spec=pltpu.PrefetchScalarGridSpec(
            num_scalar_prefetch=1,
            grid=(SIDE, cuts),
            in_specs=specs + [ANY],
            out_specs=[whole] * len(wanted),
        ),
        out_shape=[shape(SIDE, cuts * depth, width)] * len(wanted),
        cost_estimate=FREE,
        compiler_params=limit(8),
        name="combine",
    )(coords, *operands, after)


def turn_kernel(coords_ref, *refs):
    step = pl.program_id(0)
    inputs, outputs = refs[:4], refs[5:]
    for half in (0, 1):
        total = inputs[2 * half][0] + inputs[2 * half + 1][0]
        for spot in range(SIDE):

            @pl.when(step == spot)
            def _(total=total, out_ref=outputs[half * SIDE + spot]):
                out_ref[...] = total


def turn(coords, pairs, after):
    depth, width = pairs[0][0].shape[1:]
    spec = pl.BlockSpec((1, depth, width), lambda k, s: (s[SIDE + k], 0, 0))
    outs = pl.pallas_call(
        turn_kernel,
        grid_spec=pltpu.PrefetchScalarGridSpec(
            num_scalar_prefetch=1,
            grid=(SIDE,),
            in_specs=[spec] * 4 + [ANY],
            out_specs=[pl.BlockSpec((depth, width), lambda k, s: (0, 0))] * (2 * SIDE),
        ),
        out_shape=[shape(depth, width)] * (2 * SIDE),
        cost_estimate=FREE,
        compiler_params=limit(16),
        name="turn",
    )(coords, *pairs[0], *pairs[1], after)
    return outs[:SIDE], outs[SIDE:]


def ring_add_kernel(scalar_ref, *refs):
    up_ref, down_ref = refs[6:]
    depth = refs[0].shape[0]
    up_ref[:depth, :] = refs[0][...] + refs[1][...]
    up_ref[depth:, :] = refs[2][...]
    down_ref[:depth, :] = refs[3][...]
    down_ref[depth:, :] = refs[4][...] + refs[5][...]


def pieces_of(values):
    high = values.astype(jnp.bfloat16)
    rest = values - high.astype(jnp.float32)
    middle = rest.astype(jnp.bfloat16)
    low = (rest - middle.astype(jnp.float32)).astype(jnp.bfloat16)
    return high, middle, low


def left_kernel(scalar_ref, partial_ref, basis_ref, error_ref, after_ref, keep_ref, send_ref, pieces, total):
    step = pl.program_id(0)
    count, own = basis_ref.shape[0], error_ref.shape[0]
    size = partial_ref.shape[0]
    half = count // 2
    across = (((1,), (1,)), ((), ()))

    @pl.when(step == 0)
    def _():
        for index, piece in enumerate(pieces_of(basis_ref[...])):
            pieces[index * count : (index + 1) * count, :] = piece

    three = lax.dot_general(pieces[...], partial_ref[...], across, preferred_element_type=jnp.float32)
    total[:, span(step, size)] = three[:count] + (three[count : 2 * count] + three[2 * count :])

    @pl.when(step == pl.num_programs(0) - 1)
    def _():
        shard, core = scalar_ref[0], scalar_ref[1]
        kept = lax.dot_general(
            basis_ref[...], error_ref[...], across, precision=HIGHEST, preferred_element_type=jnp.float32
        )
        wide = jnp.concatenate([kept] * (LANES // own), axis=1)
        lane = lax.broadcasted_iota(jnp.int32, wide.shape, 1)
        there = span(shard // (LANES // own), LANES)
        total[:, there] += jnp.where(lane // own == shard % (LANES // own), wide, 0.0)
        keep_ref[...] = total[span(core, half), :]
        send_ref[...] = total[span(1 - core, half), :]


def left_terms(scalars, partial, basis, error, after):
    rows, width = partial.shape
    count = basis.shape[0]
    size = rows // SIDE
    fixed = lambda k: (0, 0)
    return pl.pallas_call(
        left_kernel,
        grid=(SIDE,),
        in_specs=[
            SCALARS,
            pl.BlockSpec((size, width), lambda k: (k, 0)),
            pl.BlockSpec(basis.shape, fixed),
            pl.BlockSpec(error.shape, fixed),
            ANY,
        ],
        out_specs=[pl.BlockSpec((count // 2, rows), fixed)] * 2,
        out_shape=[shape(count // 2, rows)] * 2,
        scratch_shapes=[pltpu.VMEM((3 * count, width), jnp.bfloat16), pltpu.VMEM((count, rows), jnp.float32)],
        cost_estimate=FREE,
        compiler_params=limit(24),
        name="left_terms",
    )(scalars, partial, basis, error, after)


def ordered(core, mine, other):
    return jnp.where(core == 0, mine, other), jnp.where(core == 0, other, mine)


def orthonormal_kernel(scalar_ref, mine_ref, other_ref, out_ref, pieces_ref):
    mat = jnp.concatenate(ordered(1 - scalar_ref[1], mine_ref[...], other_ref[...]), axis=0)
    count = mat.shape[0]
    order = lax.broadcasted_iota(jnp.int32, (count, 1), 0)
    for index in range(count):
        column = mat[index : index + 1, :]
        products = jnp.sum(mat * column, axis=1, keepdims=True)
        own_norm = products[index : index + 1, :]
        weights = jnp.where(order > index, products / own_norm, 0.0)
        scaled = column / jnp.sqrt(own_norm)
        mat = jnp.where(order == index, scaled, mat - weights * column)
    out_ref[...] = mat
    for index, piece in enumerate(pieces_of(mat)):
        pieces_ref[index * count : (index + 1) * count, :] = piece


def own_rows(phat, shard, own):
    parts = [phat[:, start : start + own] for start in range(0, LANES, own)]
    chosen = parts[0]
    for index, part in enumerate(parts[1:], 1):
        chosen = jnp.where(shard % (LANES // own) == index, part, chosen)
    return chosen


def right_kernel(scalar_ref, pieces_ref, partial_ref, phat_ref, error_ref, after_ref, keep_ref, send_ref, total):
    step = pl.program_id(0)
    count, own = phat_ref.shape[0], error_ref.shape[0]
    width = partial_ref.shape[1]
    half = count // 2
    three = jnp.dot(pieces_ref[...], partial_ref[...], preferred_element_type=jnp.float32)
    terms = three[:count] + (three[count : 2 * count] + three[2 * count :])

    @pl.when(step == 0)
    def _():
        shard = scalar_ref[0]
        mine = own_rows(phat_ref[:, span(shard // (LANES // own), LANES)], shard, own)
        total[:, :width] = terms + jnp.dot(
            mine, error_ref[...], precision=HIGHEST, preferred_element_type=jnp.float32
        )
        total[:, width:] = jnp.zeros((count, total.shape[1] - width), jnp.float32)

    @pl.when(step > 0)
    def _():
        total[:, :width] += terms

    @pl.when(step == pl.num_programs(0) - 1)
    def _():
        core = scalar_ref[1]
        keep_ref[...] = total[span(core, half), :]
        send_ref[...] = total[span(1 - core, half), :]


def right_terms(scalars, pieces, partial, phat, error, after):
    rows, width = partial.shape
    count = phat.shape[0]
    padded = -(-width // (LANES * SIDE)) * LANES * SIDE
    size = rows // SIDE
    fixed = lambda k: (0, 0)
    return pl.pallas_call(
        right_kernel,
        grid=(SIDE,),
        in_specs=[
            SCALARS,
            pl.BlockSpec((3 * count, size), lambda k: (0, k)),
            pl.BlockSpec((size, width), lambda k: (k, 0)),
            pl.BlockSpec(phat.shape, fixed),
            pl.BlockSpec(error.shape, fixed),
            ANY,
        ],
        out_specs=[pl.BlockSpec((count // 2, padded), fixed)] * 2,
        out_shape=[shape(count // 2, padded)] * 2,
        scratch_shapes=[pltpu.VMEM((count, padded), jnp.float32)],
        cost_estimate=FREE,
        compiler_params=limit(24),
        name="right_terms",
    )(scalars, pieces, partial, phat, error, after)


def add_kernel(scalar_ref, a_ref, b_ref, out_ref):
    out_ref[...] = a_ref[...] + b_ref[...]


def add(scalars, a, b, after):
    return run(add_kernel, [shape(*a.shape)], scalars, [a, b], after, "add")[0]


def add_four_kernel(scalar_ref, a_ref, b_ref, c_ref, d_ref, out_ref):
    out_ref[...] = (a_ref[...] + b_ref[...]) + (c_ref[...] + d_ref[...])


def sum_four(scalars, values, along, after):
    came = [along(values, step) for step in (2, 1, -1)]
    return run(add_four_kernel, [shape(*values.shape)], scalars, [values, *came], after, "add_four")[0]


def add_cut_kernel(scalar_ref, a_ref, b_ref, *out_refs):
    x, size = scalar_ref[2], out_refs[0].shape[1]
    for index, out_ref in enumerate(out_refs):
        there = span(lax.rem(x + index, SIDE), size)
        out_ref[...] = a_ref[:, there] + b_ref[:, there]


def scatter_x(scalars, keep, came, after):
    outs = [shape(keep.shape[0], keep.shape[1] // SIDE)] * SIDE
    parts = run(add_cut_kernel, outs, scalars, [keep, came], after, "add_cut")
    came = [along_x(parts[2], 2), along_x(parts[1], 1), along_x(parts[3], -1)]
    return run(add_four_kernel, outs[:1], scalars, [parts[0], *came], parts[0], "add_four")[0]


def join_kernel(scalar_ref, *refs):
    x, size = scalar_ref[2], refs[0].shape[1]
    for index, ref in enumerate(refs[:-1]):
        refs[-1][:, span(lax.rem(x + index, SIDE), size)] = ref[...]


def gather_x(scalars, values, after):
    came = [along_x(values, -1), along_x(values, 2), along_x(values, 1)]
    outs = [shape(values.shape[0], SIDE * values.shape[1])]
    return run(join_kernel, outs, scalars, [values, *came], after, "join")[0]


def finish_kernel(replicas, scalar_ref, mine_ref, other_ref, phat_ref, error_ref, grad_ref, rest_ref, basis_ref):
    shard, core = scalar_ref[0], scalar_ref[1]
    own, width = error_ref.shape
    right = jnp.concatenate(ordered(core, mine_ref[:, :width], other_ref[:, :width]), axis=0)
    mine = own_rows(phat_ref[:, span(shard // (LANES // own), LANES)], shard, own)
    approx = lax.dot_general(
        mine, right, (((0,), (0,)), ((), ())), precision=HIGHEST, preferred_element_type=jnp.float32
    ) * (1.0 / replicas)
    grad_ref[...] = approx.astype(jnp.bfloat16)
    rest_ref[...] = error_ref[...] - approx
    basis_ref[...] = right * (1.0 / replicas)


def last_kernel(scalar_ref, rest_ref, high_ref, low_ref, up_ref, down_ref, out_ref):
    depth = high_ref.shape[0]
    for index, ref in enumerate((high_ref, low_ref)):
        rows = slice(index * depth, (index + 1) * depth)
        out_ref[rows, :] = rest_ref[rows, :] + (ref[...] + (up_ref[rows, :] + down_ref[rows, :]))


def shards(partials, error, basis):
    replicas = lax.axis_size("dp")
    dp, shard = lax.axis_index("dp"), lax.axis_index("shard")
    x, core = dp // 2, dp % 2
    partial, error, basis = partials[0, 0], error[0], basis.T
    rows, width = partial.shape
    own, count = error.shape[0], basis.shape[0]
    depth = own // 2
    scalars = jnp.stack([shard, core, x]).astype(jnp.int32)
    z, y = shard // SIDE, shard % SIDE
    first, second = jnp.where(core == 0, z, y), jnp.where(core == 0, y, z)
    near = jnp.arange(SIDE)
    coords = jnp.concatenate([(first + near) % SIDE, (second + near) % SIDE, core[None]])
    coords = coords.astype(jnp.int32)
    blocks = partial.reshape(SIDE, SIDE, 4, own // 4, width)

    sent1 = combine(blocks, coords, [(2, 0, []), (2, 1, [])], scalars)
    came1 = [along_first(sent1[0], 1), along_first(sent1[1], -1)]
    keep, send = left_terms(scalars, partial, basis, error, sent1[0])
    part = add(scalars, keep, other_core(send), send)
    part = sum_four(scalars, part, along_x, part)
    part = sum_four(scalars, part, along_second, part)
    sent2 = combine(blocks, coords, [(1, 1, []), (3, 0, [])], part)
    came2 = [along_first(sent2[0], 1), along_first(sent2[1], -1)]
    sent3 = combine(blocks, coords, [(1, 0, [came1[0]]), (3, 1, [came1[1]])], sent2[0])
    came3 = [along_first(sent3[0], 1), along_first(sent3[1], -1)]
    part = other_core(part)
    part = add(scalars, part, pair_second(part, 1), sent3[0])
    part = add(scalars, part, pair_second(part, 3), part)
    phat, pieces = run(
        orthonormal_kernel,
        [shape(count, rows), shape(3 * count, rows, dtype=jnp.bfloat16)],
        scalars,
        [part, other_core(part)],
        part,
        "orthonormal",
    )
    keep, send = right_terms(scalars, pieces, partial, phat, error, phat)
    held = combine(blocks, coords, [(0, 0, [came2[1]]), (0, 1, [came2[0]])], send)
    part = scatter_x(scalars, keep, other_core(send), held[0])
    part = sum_four(scalars, part, along_second, part)
    kept = turn(coords, [(held[0], came3[0]), (held[1], came3[1])], part)
    came4 = [along_second(kept[0][2], 1), along_second(kept[1][2], -1)]
    part = sum_four(scalars, part, along_first, kept[0][0])
    sent5 = run(
        ring_add_kernel,
        [shape(own, width)] * 2,
        scalars,
        [kept[0][1], came4[0], kept[1][1], kept[0][3], kept[1][3], came4[1]],
        part,
        "ring_add",
    )
    came5 = [along_second(sent5[0], 1), along_second(sent5[1], -1)]
    part = gather_x(scalars, part, sent5[0])
    grad, rest, right = run(
        functools.partial(finish_kernel, replicas),
        [shape(own, width, dtype=jnp.bfloat16), shape(own, width), shape(count, width)],
        scalars,
        [part, other_core(part), phat, error],
        part,
        "finish",
        room=24,
    )
    following = run(
        last_kernel,
        [shape(own, width)],
        scalars,
        [rest, kept[0][0], kept[1][0], *came5],
        rest,
        "last",
    )[0]
    return grad, following[None], right.T


def solution(mesh):
    return jax.shard_map(
        shards,
        mesh=mesh,
        in_specs=(P("dp", "shard", None, None), P("dp", "shard", None), P()),
        out_specs=(P("shard", None), P("dp", "shard", None), P()),
        check_vma=False,
    )
```

time: 1550 us -> 124 us (0.08)
  blocking collectives: 964 us -> 0 us
  waiting for transfers between devices: 481 us -> 33.5 us
  starting transfers between devices: 0.08 us -> 57.3 us
  other arithmetic: 35.6 us -> 0.16 us
  Pallas kernels: 0 us -> 28.3 us
  loops' own time: 22.8 us -> 0 us
  local copies, waits for them, and re-layouts: 19.7 us -> 3.32 us
    psum x33 -> x0, blocking collectives: 964 us -> none  [the longest x32 942 us: across_shard(): return lax.psum(values, 'shard')]
    psum x1 -> x0, waiting for transfers between devices: 369 us -> none  [shards(): qsum = lax.psum(q_terms, ('dp', 'shard'))]
    reduce_scatter x1 -> x0, waiting for transfers between devices: 111 us -> none  [shards(): lax.psum_scatter(partials[0, 0].astype(jnp.float32), 'shard', scatter_dim...]
    ppermute x0 -> x35, starting transfers between devices: none -> 57.3 us  [moved(): lax.ppermute(values, BOTH, [(place(*spot), place(*route(*spot))) for spot...]
    ppermute x0 -> x35, waiting for transfers between devices: none -> 33.5 us  [moved(): lax.ppermute(values, BOTH, [(place(*spot), place(*route(*spot))) for spot...]
    pallas_call x0 -> x21, Pallas kernels: none -> 28.3 us  [the longest x14 14.4 us: run(): pl.pallas_call(body, in_specs=[SCALARS] + [WHOLE] * len(operands) + [ANY]...]
    another operation x1 -> x0, loops' own time: 22.8 us -> none  [orthonormal(): return lax.fori_loop(0, count, sweep, pmat)]
    select_n x32 -> x1, other arithmetic: 20.9 us -> 0.01 us  [shards(): (second + near) % SIDE]
  transfers between devices with their start and end apart: 2 -> 35, of which waited for: 2 -> 23; matrix products, arithmetic and copies ran while one was open for 0% -> 0% of each run, Pallas kernels for 0% -> 19%
where the time goes in v2:
time: 124 us; the launch traced here: 123 us
  starting transfers between devices  57.3 us (46%)
  waiting for transfers between devices  33.5 us (27%)
  Pallas kernels  28.3 us (23%)
  local copies, waits for them, and re-layouts  3.32 us (3%)
    ppermute x35, starting transfers between devices, moved(): lax.ppermute(values, BOTH, [(place(*spot), place(*route(*spot))) for spot...  57.3 us
    ppermute x35, waiting for transfers between devices, moved(): lax.ppermute(values, BOTH, [(place(*spot), place(*route(*spot))) for spot...  33.5 us
    pallas_call x14, Pallas kernels, run(): pl.pallas_call(body, in_specs=[SCALARS] + [WHOLE] * len(operands) + [ANY]...  14.4 us
    pallas_call x1, Pallas kernels, left_terms(): pl.pallas_call(left_kernel, grid=(SIDE,), in_specs=[SCALARS, pl.BlockSpec...  4.91 us
    pallas_call x4, Pallas kernels, combine(): pl.pallas_call(functools.partial(combine_kernel, arity), grid_spec=pltpu....  4.21 us
    pallas_call x1, Pallas kernels, right_terms(): pl.pallas_call(right_kernel, grid=(SIDE,), in_specs=[SCALARS, pl.BlockSpe...  3.47 us
    unnamed x8, local copies, waits for them, and re-layouts  3.32 us
  transfers between devices with their start and end apart: 35, of which 23 were waited for; matrix products, arithmetic and copies ran while one was open for 0% of the time, Pallas kernels for 19%

profile of v2, /device:TPU:1, one launch (start us, length us, event | category | flops | bytes accessed | tf_op | source)
XLA Modules:
  0.0 123.5 jit_solution(5116659686413922790)
XLA Ops:
  0.9 3.3 %copy-done = bf16[1,1,1024,3968]{3,2,1,0:T(8,128)(2,1)S(1)} copy-done((bf16[1,1,1024,3968]{3,2,1,0:T(8,128)(2,1)S(1)}, bf16[1,1,1024,3968]{3,2,1,0:T(8,128)(2,1)}, u32[]{:S(2)}) %copy-start) | copy-done | bytes 8126488
  4.2 1.0 combine.4
  5.2 3.6 %collective-permute-start.10 = (f32[4,32,3968]{2,1,0:T(8,128)S(1)}, f32[4,32,3968]{2,1,0:T(8,128)S(1)}, u32[]{:S(2)}, u32[]{:S(2)}) collective-permute-start(f32[4,32,3968]{2,1,0:T(8,128)S(1)} %get-tuple-element.37), channel_id=1, source_target_pairs={{0,12},{1,13},{2,14},{3,15},{4,0},{5,1},{6,2},{7,3},{8,4},{9,5},{1... | collective-permute-start | bytes 6094856 | tf_op jit(solution)/shard_map/ppermute | solution.py:36
  8.8 4.9 %left_terms.1 = (f32[16,1024]{1,0:T(8,128)S(1)}, f32[16,1024]{1,0:T(8,128)S(1)}) custom-call(s32[3]{0:T(128)S(1)} %pad_add_fusion.refs_2_.scalar_ref, bf16[1024,3968]{1,0:T(8,128)(2,1)S(1)} %bitcast.11, f32[32,3968]{1,0:T(8,128)S(1)} %bitcast.22, f32[64,3968]{1,0:T(8,128)S(1)} %bitcast.19, f32[4,32,3968]{2,1,0:T(8,128)S(1)} %get-tuple-element.34.after_ref), custom_call_target="tpu_custom_call" | custom-call | tf_op jit(solution)/shard_map/left_terms/pallas_call | solution.py:206
  13.8 2.1 %collective-permute-start = (f32[16,1024]{1,0:T(8,128)S(1)}, f32[16,1024]{1,0:T(8,128)S(1)}, u32[]{:S(2)}, u32[]{:S(2)}) collective-permute-start(f32[16,1024]{1,0:T(8,128)S(1)} %get-tuple-element.36.refs_2_), channel_id=1, source_target_pairs={{0,16},{1,17},{2,18},{3,19},{4,20},{5,21},{6,22},{7,23},{8,24},{9,... | collective-permute-start | bytes 196616 | tf_op jit(solution)/shard_map/ppermute | solution.py:36
  15.8 0.9 collective-permute-done.refs_1_
  16.7 0.5 add.56.refs_0_.refs_4_
  17.3 2.8 %collective-permute-start.1 = (f32[16,1024]{1,0:T(8,128)S(1)}, f32[16,1024]{1,0:T(8,128)S(1)}, u32[]{:S(2)}, u32[]{:S(2)}) collective-permute-start(f32[16,1024]{1,0:T(8,128)S(1)} %add.56.refs_0_.refs_4_), channel_id=1, source_target_pairs={{0,64},{1,65},{2,66},{3,67},{4,68},{5,69},{6,70},{7,71},{8,72},{9,... | collective-permute-start | bytes 196616 | tf_op jit(solution)/shard_map/ppermute | solution.py:36
  20.4 2.4 %collective-permute-start.3 = (f32[16,1024]{1,0:T(8,128)S(1)}, f32[16,1024]{1,0:T(8,128)S(1)}, u32[]{:S(2)}, u32[]{:S(2)}) collective-permute-start(f32[16,1024]{1,0:T(8,128)S(1)} %add.56.refs_0_.refs_4_), channel_id=1, source_target_pairs={{0,96},{1,97},{2,98},{3,99},{4,100},{5,101},{6,102},{7,103},{8,104... | collective-permute-start | bytes 196616 | tf_op jit(solution)/shard_map/ppermute | solution.py:36
  22.8 1.9 %collective-permute-done.2.refs_2_ = f32[16,1024]{1,0:T(8,128)S(1)} collective-permute-done((f32[16,1024]{1,0:T(8,128)S(1)}, f32[16,1024]{1,0:T(8,128)S(1)}, u32[]{:S(2)}, u32[]{:S(2)}) %collective-permute-start.2) | collective-permute-done | bytes 65568 | tf_op jit(solution)/shard_map/ppermute | solution.py:36
  24.7 0.6 add_four.5.refs_0_.refs_4_
  25.3 1.9 %collective-permute-start.4 = (f32[16,1024]{1,0:T(8,128)S(1)}, f32[16,1024]{1,0:T(8,128)S(1)}, u32[]{:S(2)}, u32[]{:S(2)}) collective-permute-start(f32[16,1024]{1,0:T(8,128)S(1)} %add_four.5.refs_0_.refs_4_), channel_id=1, source_target_pairs={{0,2},{1,3},{2,0},{3,1},{4,6},{5,7},{6,4},{7,5},{8,10},{9,11},{10,... | collective-permute-start | bytes 196616 | tf_op jit(solution)/shard_map/ppermute | solution.py:36
  27.1 1.7 %collective-permute-start.5 = (f32[16,1024]{1,0:T(8,128)S(1)}, f32[16,1024]{1,0:T(8,128)S(1)}, u32[]{:S(2)}, u32[]{:S(2)}) collective-permute-start(f32[16,1024]{1,0:T(8,128)S(1)} %add_four.5.refs_0_.refs_4_), channel_id=1, source_target_pairs={{0,1},{1,2},{2,3},{3,0},{4,5},{5,6},{6,7},{7,4},{8,9},{9,10},{10,1... | collective-permute-start | bytes 196616 | tf_op jit(solution)/shard_map/ppermute | solution.py:36
  28.9 0.9 collective-permute-start.6
  29.8 0.9 collective-permute-done.4.refs_1_
  30.7 1.8 %collective-permute-done.5.refs_2_ = f32[16,1024]{1,0:T(8,128)S(1)} collective-permute-done((f32[16,1024]{1,0:T(8,128)S(1)}, f32[16,1024]{1,0:T(8,128)S(1)}, u32[]{:S(2)}, u32[]{:S(2)}) %collective-permute-start.5) | collective-permute-done | bytes 65568 | tf_op jit(solution)/shard_map/ppermute | solution.py:36
  33.0 0.6 add_four.6.refs_2_
  33.6 1.0 combine.5
  34.6 2.8 %collective-permute-start.14 = (f32[4,32,3968]{2,1,0:T(8,128)S(1)}, f32[4,32,3968]{2,1,0:T(8,128)S(1)}, u32[]{:S(2)}, u32[]{:S(2)}) collective-permute-start(f32[4,32,3968]{2,1,0:T(8,128)S(1)} %get-tuple-element.44), channel_id=1, source_target_pairs={{0,12},{1,13},{2,14},{3,15},{4,0},{5,1},{6,2},{7,3},{8,4},{9,5},{1... | collective-permute-start | bytes 6094856 | tf_op jit(solution)/shard_map/ppermute | solution.py:36
  37.4 1.1 combine.6
  38.6 2.7 %collective-permute-start.26 = (f32[4,32,3968]{2,1,0:T(8,128)S(1)}, f32[4,32,3968]{2,1,0:T(8,128)S(1)}, u32[]{:S(2)}, u32[]{:S(2)}) collective-permute-start(f32[4,32,3968]{2,1,0:T(8,128)S(1)} %get-tuple-element.51), channel_id=1, source_target_pairs={{0,12},{1,13},{2,14},{3,15},{4,0},{5,1},{6,2},{7,3},{8,4},{9,5},{1... | collective-permute-start | bytes 6094856 | tf_op jit(solution)/shard_map/ppermute | solution.py:36
  41.3 4.3 %collective-permute-start.7 = (f32[16,1024]{1,0:T(8,128)S(1)}, f32[16,1024]{1,0:T(8,128)S(1)}, u32[]{:S(2)}, u32[]{:S(2)}) collective-permute-start(f32[16,1024]{1,0:T(8,128)S(1)} %add_four.6.refs_2_), channel_id=1, source_target_pairs={{0,16},{1,17},{2,18},{3,19},{4,20},{5,21},{6,22},{7,23},{8,24},{9,... | collective-permute-start | bytes 196616 | tf_op jit(solution)/shard_map/ppermute | solution.py:36
  45.7 0.9 collective-permute-done.7.refs_0_
  46.6 4.2 %collective-permute-done.8.refs_1_ = f32[16,1024]{1,0:T(8,128)S(1)} collective-permute-done((f32[16,1024]{1,0:T(8,128)S(1)}, f32[16,1024]{1,0:T(8,128)S(1)}, u32[]{:S(2)}, u32[]{:S(2)}) %collective-permute-start.8) | collective-permute-done | bytes 65568 | tf_op jit(solution)/shard_map/ppermute | solution.py:36
  51.3 1.7 %collective-permute-start.11 = (f32[16,1024]{1,0:T(8,128)S(1)}, f32[16,1024]{1,0:T(8,128)S(1)}, u32[]{:S(2)}, u32[]{:S(2)}) collective-permute-start(f32[16,1024]{1,0:T(8,128)S(1)} %add.57.refs_0_.refs_2_), channel_id=1, source_target_pairs={{0,3},{1,2},{2,1},{3,0},{4,7},{5,6},{6,5},{7,4},{8,11},{9,10},{10,... | collective-permute-start | bytes 196616 | tf_op jit(solution)/shard_map/ppermute | solution.py:36
  53.0 3.7 %collective-permute-done.11.refs_1_ = f32[16,1024]{1,0:T(8,128)S(1)} collective-permute-done((f32[16,1024]{1,0:T(8,128)S(1)}, f32[16,1024]{1,0:T(8,128)S(1)}, u32[]{:S(2)}, u32[]{:S(2)}) %collective-permute-start.11) | collective-permute-done | bytes 65568 | tf_op jit(solution)/shard_map/ppermute | solution.py:36
  57.3 2.1 %collective-permute-start.12 = (f32[16,1024]{1,0:T(8,128)S(1)}, f32[16,1024]{1,0:T(8,128)S(1)}, u32[]{:S(2)}, u32[]{:S(2)}) collective-permute-start(f32[16,1024]{1,0:T(8,128)S(1)} %add.58.refs_0_.refs_2_), channel_id=1, source_target_pairs={{0,16},{1,17},{2,18},{3,19},{4,20},{5,21},{6,22},{7,23},{8,24},{9,... | collective-permute-start | bytes 196616 | tf_op jit(solution)/shard_map/ppermute | solution.py:36
  59.5 0.9 collective-permute-done.12.refs_1_
  60.4 3.9 %orthonormal.1 = (f32[32,1024]{1,0:T(8,128)S(1)}, bf16[96,1024]{1,0:T(8,128)(2,1)S(1)}) custom-call(s32[3]{0:T(128)S(1)} %pad_add_fusion.refs_2_.scalar_ref, f32[16,1024]{1,0:T(8,128)S(1)} %add.58.refs_0_.refs_2_, f32[16,1024]{1,0:T(8,128)S(1)} %collective-permute-done.12.refs_1_, f32[16,1024]{1,0:T(8,128)S(1)} %add.58.refs_0_.refs_2_), custom_call_target="tpu_custom_call" | custom-call | tf_op jit(solution)/shard_map/orthonormal/pallas_call | solution.py:67
  64.3 3.5 %right_terms.1 = (f32[16,4096]{1,0:T(8,128)S(1)}, f32[16,4096]{1,0:T(8,128)S(1)}) custom-call(s32[3]{0:T(128)S(1)} %pad_add_fusion.refs_2_.scalar_ref, bf16[96,1024]{1,0:T(8,128)(2,1)S(1)} %get-tuple-element.40.pieces_ref, bf16[1024,3968]{1,0:T(8,128)(2,1)S(1)} %bitcast.16, f32[32,1024]{1,0:T(8,128)S(1)} %get-tuple-element.41.phat_ref.after_ref.refs_2_, ...), custom_call_target="tpu_custom_call" | custom-call | tf_op jit(solution)/shard_map/right_terms/pallas_call | solution.py:287
  68.2 1.1 combine.7
  69.4 0.6 add_cut.1
  70.0 1.3 %collective-permute-start.16 = (f32[16,1024]{1,0:T(8,128)S(1)}, f32[16,1024]{1,0:T(8,128)S(1)}, u32[]{:S(2)}, u32[]{:S(2)}) collective-permute-start(f32[16,1024]{1,0:T(8,128)S(1)} %get-tuple-element.47), channel_id=1, source_target_pairs={{0,64},{1,65},{2,66},{3,67},{4,68},{5,69},{6,70},{7,71},{8,72},{9,... | collective-permute-start | bytes 196616 | tf_op jit(solution)/shard_map/ppermute | solution.py:36
  71.2 2.3 %collective-permute-start.17 = (f32[16,1024]{1,0:T(8,128)S(1)}, f32[16,1024]{1,0:T(8,128)S(1)}, u32[]{:S(2)}, u32[]{:S(2)}) collective-permute-start(f32[16,1024]{1,0:T(8,128)S(1)} %get-tuple-element.48), channel_id=1, source_target_pairs={{0,32},{1,33},{2,34},{3,35},{4,36},{5,37},{6,38},{7,39},{8,40},{9,... | collective-permute-start | bytes 196616 | tf_op jit(solution)/shard_map/ppermute | solution.py:36
  73.9 0.8 collective-permute-done.16.refs_1_
  74.7 2.0 %collective-permute-done.17.refs_2_ = f32[16,1024]{1,0:T(8,128)S(1)} collective-permute-done((f32[16,1024]{1,0:T(8,128)S(1)}, f32[16,1024]{1,0:T(8,128)S(1)}, u32[]{:S(2)}, u32[]{:S(2)}) %collective-permute-start.17) | collective-permute-done | bytes 65568 | tf_op jit(solution)/shard_map/ppermute | solution.py:36
  77.0 0.6 add_four.7.refs_0_.refs_4_
  77.6 1.2 collective-permute-start.19
  78.8 1.1 collective-permute-start.20
  79.9 1.5 %collective-permute-start.21 = (f32[16,1024]{1,0:T(8,128)S(1)}, f32[16,1024]{1,0:T(8,128)S(1)}, u32[]{:S(2)}, u32[]{:S(2)}) collective-permute-start(f32[16,1024]{1,0:T(8,128)S(1)} %add_four.7.refs_0_.refs_4_), channel_id=1, source_target_pairs={{0,3},{1,0},{2,1},{3,2},{4,7},{5,4},{6,5},{7,6},{8,11},{9,8},{10,9... | collective-permute-start | bytes 196616 | tf_op jit(solution)/shard_map/ppermute | solution.py:36
  81.5 1.6 %collective-permute-done.19.refs_1_ = f32[16,1024]{1,0:T(8,128)S(1)} collective-permute-done((f32[16,1024]{1,0:T(8,128)S(1)}, f32[16,1024]{1,0:T(8,128)S(1)}, u32[]{:S(2)}, u32[]{:S(2)}) %collective-permute-start.19) | collective-permute-done | bytes 65568 | tf_op jit(solution)/shard_map/ppermute | solution.py:36
  83.1 1.4 %collective-permute-done.20.refs_2_ = f32[16,1024]{1,0:T(8,128)S(1)} collective-permute-done((f32[16,1024]{1,0:T(8,128)S(1)}, f32[16,1024]{1,0:T(8,128)S(1)}, u32[]{:S(2)}, u32[]{:S(2)}) %collective-permute-start.20) | collective-permute-done | bytes 65568 | tf_op jit(solution)/shard_map/ppermute | solution.py:36
  84.5 0.6 add_four.8.refs_4_.refs_0_
  85.1 1.9 %collective-permute-done.25.refs_1_ = f32[4,32,3968]{2,1,0:T(8,128)S(1)} collective-permute-done((f32[4,32,3968]{2,1,0:T(8,128)S(1)}, f32[4,32,3968]{2,1,0:T(8,128)S(1)}, u32[]{:S(2)}, u32[]{:S(2)}) %collective-permute-start.25) | collective-permute-done | bytes 2031648 | tf_op jit(solution)/shard_map/ppermute | solution.py:36
  86.9 1.3 %turn.1 = (f32[32,3968]{1,0:T(8,128)S(1)}, f32[32,3968]{1,0:T(8,128)S(1)}, f32[32,3968]{1,0:T(8,128)S(1)}, f32[32,3968]{1,0:T(8,128)S(1)}, f32[32,3968]{1,0:T(8,...) custom-call(s32[9]{0:T(128)S(1)} %pad_add_fusion.1.coords_ref, ...), custom_call_target="tpu_custom_call" | custom-call | tf_op jit(solution)/shard_map/turn/pallas_call | solution.py:139
  88.4 2.7 %collective-permute-start.31 = (f32[32,3968]{1,0:T(8,128)S(1)}, f32[32,3968]{1,0:T(8,128)S(1)}, u32[]{:S(2)}, u32[]{:S(2)}) collective-permute-start(f32[32,3968]{1,0:T(8,128)S(1)} %get-tuple-element.58), channel_id=1, source_target_pairs={{0,3},{1,0},{2,1},{3,2},{4,7},{5,4},{6,5},{7,6},{8,11},{9,8},{10,9... | collective-permute-start | bytes 1523720 | tf_op jit(solution)/shard_map/ppermute | solution.py:36
  91.0 0.9 collective-permute-start.23
  91.9 1.8 %collective-permute-start.24 = (f32[16,1024]{1,0:T(8,128)S(1)}, f32[16,1024]{1,0:T(8,128)S(1)}, u32[]{:S(2)}, u32[]{:S(2)}) collective-permute-start(f32[16,1024]{1,0:T(8,128)S(1)} %add_four.8.refs_4_.refs_0_), channel_id=1, source_target_pairs={{0,12},{1,13},{2,14},{3,15},{4,0},{5,1},{6,2},{7,3},{8,4},{9,5},{1... | collective-permute-start | bytes 196616 | tf_op jit(solution)/shard_map/ppermute | solution.py:36
  93.7 2.0 %collective-permute-done.22.refs_1_ = f32[16,1024]{1,0:T(8,128)S(1)} collective-permute-done((f32[16,1024]{1,0:T(8,128)S(1)}, f32[16,1024]{1,0:T(8,128)S(1)}, u32[]{:S(2)}, u32[]{:S(2)}) %collective-permute-start.22) | collective-permute-done | bytes 65568 | tf_op jit(solution)/shard_map/ppermute | solution.py:36
  96.1 0.6 add_four.9.refs_6_.refs_0_
  96.6 1.1 collective-permute-done.30.refs_1_
  97.7 0.7 ring_add.1
  98.4 0.6 collective-permute-start.33
  99.0 2.2 %collective-permute-start.34 = (f32[64,3968]{1,0:T(8,128)S(1)}, f32[64,3968]{1,0:T(8,128)S(1)}, u32[]{:S(2)}, u32[]{:S(2)}) collective-permute-start(f32[64,3968]{1,0:T(8,128)S(1)} %get-tuple-element.63), channel_id=1, source_target_pairs={{0,3},{1,0},{2,1},{3,2},{4,7},{5,4},{6,5},{7,6},{8,11},{9,8},{10,9... | collective-permute-start | bytes 3047432 | tf_op jit(solution)/shard_map/ppermute | solution.py:36
  101.3 2.6 %collective-permute-start.27 = (f32[16,1024]{1,0:T(8,128)S(1)}, f32[16,1024]{1,0:T(8,128)S(1)}, u32[]{:S(2)}, u32[]{:S(2)}) collective-permute-start(f32[16,1024]{1,0:T(8,128)S(1)} %add_four.9.refs_6_.refs_0_), channel_id=1, source_target_pairs={{0,96},{1,97},{2,98},{3,99},{4,100},{5,101},{6,102},{7,103},{8,104... | collective-permute-start | bytes 196616 | tf_op jit(solution)/shard_map/ppermute | solution.py:36
  103.8 0.6 collective-permute-start.28
  104.5 1.3 %collective-permute-done.27.refs_1_ = f32[16,1024]{1,0:T(8,128)S(1)} collective-permute-done((f32[16,1024]{1,0:T(8,128)S(1)}, f32[16,1024]{1,0:T(8,128)S(1)}, u32[]{:S(2)}, u32[]{:S(2)}) %collective-permute-start.27) | collective-permute-done | bytes 65568 | tf_op jit(solution)/shard_map/ppermute | solution.py:36
  105.8 2.7 %collective-permute-done.28.refs_2_ = f32[16,1024]{1,0:T(8,128)S(1)} collective-permute-done((f32[16,1024]{1,0:T(8,128)S(1)}, f32[16,1024]{1,0:T(8,128)S(1)}, u32[]{:S(2)}, u32[]{:S(2)}) %collective-permute-start.28) | collective-permute-done | bytes 65568 | tf_op jit(solution)/shard_map/ppermute | solution.py:36
  108.5 1.0 collective-permute-done.29.refs_3_
  109.5 0.6 join.1.refs_0_.refs_4_
  110.0 8.1 %collective-permute-start.32 = (f32[16,4096]{1,0:T(8,128)S(1)}, f32[16,4096]{1,0:T(8,128)S(1)}, u32[]{:S(2)}, u32[]{:S(2)}) collective-permute-start(f32[16,4096]{1,0:T(8,128)S(1)} %join.1.refs_0_.refs_4_), channel_id=1, source_target_pairs={{0,16},{1,17},{2,18},{3,19},{4,20},{5,21},{6,22},{7,23},{8,24},{9,... | collective-permute-start | bytes 786440 | tf_op jit(solution)/shard_map/ppermute | solution.py:36
  118.1 1.2 collective-permute-done.32.refs_1_
  119.3 2.5 %finish.1 = (bf16[64,3968]{1,0:T(8,128)(2,1)}, f32[64,3968]{1,0:T(8,128)S(1)}, f32[32,3968]{1,0:T(8,128)}) custom-call(s32[3]{0:T(128)S(1)} %pad_add_fusion.refs_2_.scalar_ref, f32[16,4096]{1,0:T(8,128)S(1)} %join.1.refs_0_.refs_4_, f32[16,4096]{1,0:T(8,128)S(1)} %collective-permute-done.32.refs_1_, ...), custom_call_target="tpu_custom_call" | custom-call | tf_op jit(solution)/shard_map/finish/pallas_call | solution.py:67
  121.8 1.7 %last.1 = f32[64,3968]{1,0:T(8,128)} custom-call(s32[3]{0:T(128)S(1)} %pad_add_fusion.refs_2_.scalar_ref, f32[64,3968]{1,0:T(8,128)S(1)} %get-tuple-element.61.refs_0_.refs_5_, f32[32,3968]{1,0:T(8,128)S(1)} %get-tuple-element.52.refs_4_.refs_1_, f32[32,3968]{1,0:T(8,128)S(1)} %get-tuple-element.62.refs_2_, f32[64,3968]{1,0:T(8,128)S(1)} %collective-permute-done.33.refs_3_, ...), custom_call_target="tpu_custom_call" | custom-call | tf_op jit(solution)/shard_map/last/pallas_call | solution.py:67
  (38 shorter events, 3.8 us)
Async XLA Ops:
  0.9 3.3 %copy-start = (bf16[1,1,1024,3968]{3,2,1,0:T(8,128)(2,1)S(1)}, bf16[1,1,1024,3968]{3,2,1,0:T(8,128)(2,1)}, u32[]{:S(2)}) copy-start(bf16[1,1,1024,3968]{3,2,1,0:T(8,128)(2,1)} %param.3) | copy-start | bytes 24379396
  4.2 4.7 %copy-start.1 = (bf16[1,1,1024,3968]{3,2,1,0:T(8,128)(2,1)S(1)}, bf16[1,1,1024,3968]{3,2,1,0:T(8,128)(2,1)}, u32[]{:S(2)}) copy-start(bf16[1,1,1024,3968]{3,2,1,0:T(8,128)(2,1)} %param.3) | copy-start | bytes 24379396
  4.2 4.7 %copy-start.2 = (f32[1,64,3968]{2,1,0:T(8,128)S(1)}, f32[1,64,3968]{2,1,0:T(8,128)}, u32[]{:S(2)}) copy-start(f32[1,64,3968]{2,1,0:T(8,128)} %param.4) | copy-start | bytes 3047428
  4.2 4.7 %copy-start.3 = (f32[3968,32]{0,1:T(8,128)S(1)}, f32[3968,32]{0,1:T(8,128)}, u32[]{:S(2)}) copy-start(f32[3968,32]{0,1:T(8,128)} %param.5) | copy-start | bytes 1523716
  5.2 32.2 %collective-permute-start.10 = (f32[4,32,3968]{2,1,0:T(8,128)S(1)}, f32[4,32,3968]{2,1,0:T(8,128)S(1)}, u32[]{:S(2)}, u32[]{:S(2)}) collective-permute-start(f32[4,32,3968]{2,1,0:T(8,128)S(1)} %get-tuple-element.37), channel_id=1, source_target_pairs={{0,12},{1,13},{2,14},{3,15},{4,0},{5,1},{6,2},{7,3},{8,4},{9,5},{1... | collective-permute-start | bytes 6094856 | tf_op jit(solution)/shard_map/ppermute | solution.py:36
  8.8 28.6 %collective-permute-start.9 = (f32[4,32,3968]{2,1,0:T(8,128)S(1)}, f32[4,32,3968]{2,1,0:T(8,128)S(1)}, u32[]{:S(2)}, u32[]{:S(2)}) collective-permute-start(f32[4,32,3968]{2,1,0:T(8,128)S(1)} %get-tuple-element.34.after_ref), channel_id=1, source_target_pairs={{0,4},{1,5},{2,6},{3,7},{4,8},{5,9},{6,10},{7,11},{8,12},{9,13},{1... | collective-permute-start | bytes 6094856 | tf_op jit(solution)/shard_map/ppermute | solution.py:36
  13.8 3.0 %collective-permute-start = (f32[16,1024]{1,0:T(8,128)S(1)}, f32[16,1024]{1,0:T(8,128)S(1)}, u32[]{:S(2)}, u32[]{:S(2)}) collective-permute-start(f32[16,1024]{1,0:T(8,128)S(1)} %get-tuple-element.36.refs_2_), channel_id=1, source_target_pairs={{0,16},{1,17},{2,18},{3,19},{4,20},{5,21},{6,22},{7,23},{8,24},{9,... | collective-permute-start | bytes 196616 | tf_op jit(solution)/shard_map/ppermute | solution.py:36
  17.3 5.5 %collective-permute-start.1 = (f32[16,1024]{1,0:T(8,128)S(1)}, f32[16,1024]{1,0:T(8,128)S(1)}, u32[]{:S(2)}, u32[]{:S(2)}) collective-permute-start(f32[16,1024]{1,0:T(8,128)S(1)} %add.56.refs_0_.refs_4_), channel_id=1, source_target_pairs={{0,64},{1,65},{2,66},{3,67},{4,68},{5,69},{6,70},{7,71},{8,72},{9,... | collective-permute-start | bytes 196616 | tf_op jit(solution)/shard_map/ppermute | solution.py:36
  20.1 4.6 %collective-permute-start.2 = (f32[16,1024]{1,0:T(8,128)S(1)}, f32[16,1024]{1,0:T(8,128)S(1)}, u32[]{:S(2)}, u32[]{:S(2)}) collective-permute-start(f32[16,1024]{1,0:T(8,128)S(1)} %add.56.refs_0_.refs_4_), channel_id=1, source_target_pairs={{0,32},{1,33},{2,34},{3,35},{4,36},{5,37},{6,38},{7,39},{8,40},{9,... | collective-permute-start | bytes 196616 | tf_op jit(solution)/shard_map/ppermute | solution.py:36
  20.4 4.3 %collective-permute-start.3 = (f32[16,1024]{1,0:T(8,128)S(1)}, f32[16,1024]{1,0:T(8,128)S(1)}, u32[]{:S(2)}, u32[]{:S(2)}) collective-permute-start(f32[16,1024]{1,0:T(8,128)S(1)} %add.56.refs_0_.refs_4_), channel_id=1, source_target_pairs={{0,96},{1,97},{2,98},{3,99},{4,100},{5,101},{6,102},{7,103},{8,104... | collective-permute-start | bytes 196616 | tf_op jit(solution)/shard_map/ppermute | solution.py:36
  25.3 5.5 %collective-permute-start.4 = (f32[16,1024]{1,0:T(8,128)S(1)}, f32[16,1024]{1,0:T(8,128)S(1)}, u32[]{:S(2)}, u32[]{:S(2)}) collective-permute-start(f32[16,1024]{1,0:T(8,128)S(1)} %add_four.5.refs_0_.refs_4_), channel_id=1, source_target_pairs={{0,2},{1,3},{2,0},{3,1},{4,6},{5,7},{6,4},{7,5},{8,10},{9,11},{10,... | collective-permute-start | bytes 196616 | tf_op jit(solution)/shard_map/ppermute | solution.py:36
  27.1 5.4 %collective-permute-start.5 = (f32[16,1024]{1,0:T(8,128)S(1)}, f32[16,1024]{1,0:T(8,128)S(1)}, u32[]{:S(2)}, u32[]{:S(2)}) collective-permute-start(f32[16,1024]{1,0:T(8,128)S(1)} %add_four.5.refs_0_.refs_4_), channel_id=1, source_target_pairs={{0,1},{1,2},{2,3},{3,0},{4,5},{5,6},{6,7},{7,4},{8,9},{9,10},{10,1... | collective-permute-start | bytes 196616 | tf_op jit(solution)/shard_map/ppermute | solution.py:36
  28.9 4.1 %collective-permute-start.6 = (f32[16,1024]{1,0:T(8,128)S(1)}, f32[16,1024]{1,0:T(8,128)S(1)}, u32[]{:S(2)}, u32[]{:S(2)}) collective-permute-start(f32[16,1024]{1,0:T(8,128)S(1)} %add_four.5.refs_0_.refs_4_), channel_id=1, source_target_pairs={{0,3},{1,0},{2,1},{3,2},{4,7},{5,4},{6,5},{7,6},{8,11},{9,8},{10,9... | collective-permute-start | bytes 196616 | tf_op jit(solution)/shard_map/ppermute | solution.py:36
  34.6 33.6 %collective-permute-start.14 = (f32[4,32,3968]{2,1,0:T(8,128)S(1)}, f32[4,32,3968]{2,1,0:T(8,128)S(1)}, u32[]{:S(2)}, u32[]{:S(2)}) collective-permute-start(f32[4,32,3968]{2,1,0:T(8,128)S(1)} %get-tuple-element.44), channel_id=1, source_target_pairs={{0,12},{1,13},{2,14},{3,15},{4,0},{5,1},{6,2},{7,3},{8,4},{9,5},{1... | collective-permute-start | bytes 6094856 | tf_op jit(solution)/shard_map/ppermute | solution.py:36
  37.4 30.8 %collective-permute-start.15 = (f32[4,32,3968]{2,1,0:T(8,128)S(1)}, f32[4,32,3968]{2,1,0:T(8,128)S(1)}, u32[]{:S(2)}, u32[]{:S(2)}) collective-permute-start(f32[4,32,3968]{2,1,0:T(8,128)S(1)} %get-tuple-element.38.refs_4_), channel_id=1, source_target_pairs={{0,4},{1,5},{2,6},{3,7},{4,8},{5,9},{6,10},{7,11},{8,12},{9,13},{1... | collective-permute-start | bytes 6094856 | tf_op jit(solution)/shard_map/ppermute | solution.py:36
  38.5 48.4 %collective-permute-start.25 = (f32[4,32,3968]{2,1,0:T(8,128)S(1)}, f32[4,32,3968]{2,1,0:T(8,128)S(1)}, u32[]{:S(2)}, u32[]{:S(2)}) collective-permute-start(f32[4,32,3968]{2,1,0:T(8,128)S(1)} %get-tuple-element.39.refs_2_), channel_id=1, source_target_pairs={{0,4},{1,5},{2,6},{3,7},{4,8},{5,9},{6,10},{7,11},{8,12},{9,13},{1... | collective-permute-start | bytes 6094856 | tf_op jit(solution)/shard_map/ppermute | solution.py:36
  38.6 48.3 %collective-permute-start.26 = (f32[4,32,3968]{2,1,0:T(8,128)S(1)}, f32[4,32,3968]{2,1,0:T(8,128)S(1)}, u32[]{:S(2)}, u32[]{:S(2)}) collective-permute-start(f32[4,32,3968]{2,1,0:T(8,128)S(1)} %get-tuple-element.51), channel_id=1, source_target_pairs={{0,12},{1,13},{2,14},{3,15},{4,0},{5,1},{6,2},{7,3},{8,4},{9,5},{1... | collective-permute-start | bytes 6094856 | tf_op jit(solution)/shard_map/ppermute | solution.py:36
  41.3 5.2 %collective-permute-start.7 = (f32[16,1024]{1,0:T(8,128)S(1)}, f32[16,1024]{1,0:T(8,128)S(1)}, u32[]{:S(2)}, u32[]{:S(2)}) collective-permute-start(f32[16,1024]{1,0:T(8,128)S(1)} %add_four.6.refs_2_), channel_id=1, source_target_pairs={{0,16},{1,17},{2,18},{3,19},{4,20},{5,21},{6,22},{7,23},{8,24},{9,... | collective-permute-start | bytes 196616 | tf_op jit(solution)/shard_map/ppermute | solution.py:36
  46.6 4.2 %collective-permute-start.8 = (f32[16,1024]{1,0:T(8,128)S(1)}, f32[16,1024]{1,0:T(8,128)S(1)}, u32[]{:S(2)}, u32[]{:S(2)}) collective-permute-start(f32[16,1024]{1,0:T(8,128)S(1)} %collective-permute-done.7.refs_0_), channel_id=1, source_target_pairs={{0,1},{1,0},{2,3},{3,2},{4,5},{5,4},{6,7},{7,6},{8,9},{9,8},{10,11... | collective-permute-start | bytes 196616 | tf_op jit(solution)/shard_map/ppermute | solution.py:36
  51.3 5.5 %collective-permute-start.11 = (f32[16,1024]{1,0:T(8,128)S(1)}, f32[16,1024]{1,0:T(8,128)S(1)}, u32[]{:S(2)}, u32[]{:S(2)}) collective-permute-start(f32[16,1024]{1,0:T(8,128)S(1)} %add.57.refs_0_.refs_2_), channel_id=1, source_target_pairs={{0,3},{1,2},{2,1},{3,0},{4,7},{5,6},{6,5},{7,4},{8,11},{9,10},{10,... | collective-permute-start | bytes 196616 | tf_op jit(solution)/shard_map/ppermute | solution.py:36
  57.3 3.0 %collective-permute-start.12 = (f32[16,1024]{1,0:T(8,128)S(1)}, f32[16,1024]{1,0:T(8,128)S(1)}, u32[]{:S(2)}, u32[]{:S(2)}) collective-permute-start(f32[16,1024]{1,0:T(8,128)S(1)} %add.58.refs_0_.refs_2_), channel_id=1, source_target_pairs={{0,16},{1,17},{2,18},{3,19},{4,20},{5,21},{6,22},{7,23},{8,24},{9,... | collective-permute-start | bytes 196616 | tf_op jit(solution)/shard_map/ppermute | solution.py:36
  67.8 1.6 %collective-permute-start.13 = (f32[16,4096]{1,0:T(8,128)S(1)}, f32[16,4096]{1,0:T(8,128)S(1)}, u32[]{:S(2)}, u32[]{:S(2)}) collective-permute-start(f32[16,4096]{1,0:T(8,128)S(1)} %get-tuple-element.43.refs_4_), channel_id=1, source_target_pairs={{0,16},{1,17},{2,18},{3,19},{4,20},{5,21},{6,22},{7,23},{8,24},{9,... | collective-permute-start | bytes 786440 | tf_op jit(solution)/shard_map/ppermute | solution.py:36
  70.0 4.7 %collective-permute-start.16 = (f32[16,1024]{1,0:T(8,128)S(1)}, f32[16,1024]{1,0:T(8,128)S(1)}, u32[]{:S(2)}, u32[]{:S(2)}) collective-permute-start(f32[16,1024]{1,0:T(8,128)S(1)} %get-tuple-element.47), channel_id=1, source_target_pairs={{0,64},{1,65},{2,66},{3,67},{4,68},{5,69},{6,70},{7,71},{8,72},{9,... | collective-permute-start | bytes 196616 | tf_op jit(solution)/shard_map/ppermute | solution.py:36
  71.2 5.5 %collective-permute-start.17 = (f32[16,1024]{1,0:T(8,128)S(1)}, f32[16,1024]{1,0:T(8,128)S(1)}, u32[]{:S(2)}, u32[]{:S(2)}) collective-permute-start(f32[16,1024]{1,0:T(8,128)S(1)} %get-tuple-element.48), channel_id=1, source_target_pairs={{0,32},{1,33},{2,34},{3,35},{4,36},{5,37},{6,38},{7,39},{8,40},{9,... | collective-permute-start | bytes 196616 | tf_op jit(solution)/shard_map/ppermute | solution.py:36
  73.6 3.5 %collective-permute-start.18 = (f32[16,1024]{1,0:T(8,128)S(1)}, f32[16,1024]{1,0:T(8,128)S(1)}, u32[]{:S(2)}, u32[]{:S(2)}) collective-permute-start(f32[16,1024]{1,0:T(8,128)S(1)} %get-tuple-element.49), channel_id=1, source_target_pairs={{0,96},{1,97},{2,98},{3,99},{4,100},{5,101},{6,102},{7,103},{8,104... | collective-permute-start | bytes 196616 | tf_op jit(solution)/shard_map/ppermute | solution.py:36
  77.6 5.5 %collective-permute-start.19 = (f32[16,1024]{1,0:T(8,128)S(1)}, f32[16,1024]{1,0:T(8,128)S(1)}, u32[]{:S(2)}, u32[]{:S(2)}) collective-permute-start(f32[16,1024]{1,0:T(8,128)S(1)} %add_four.7.refs_0_.refs_4_), channel_id=1, source_target_pairs={{0,2},{1,3},{2,0},{3,1},{4,6},{5,7},{6,4},{7,5},{8,10},{9,11},{10,... | collective-permute-start | bytes 196616 | tf_op jit(solution)/shard_map/ppermute | solution.py:36
  78.8 5.7 %collective-permute-start.20 = (f32[16,1024]{1,0:T(8,128)S(1)}, f32[16,1024]{1,0:T(8,128)S(1)}, u32[]{:S(2)}, u32[]{:S(2)}) collective-permute-start(f32[16,1024]{1,0:T(8,128)S(1)} %add_four.7.refs_0_.refs_4_), channel_id=1, source_target_pairs={{0,1},{1,2},{2,3},{3,0},{4,5},{5,6},{6,7},{7,4},{8,9},{9,10},{10,1... | collective-permute-start | bytes 196616 | tf_op jit(solution)/shard_map/ppermute | solution.py:36
  79.9 4.6 %collective-permute-start.21 = (f32[16,1024]{1,0:T(8,128)S(1)}, f32[16,1024]{1,0:T(8,128)S(1)}, u32[]{:S(2)}, u32[]{:S(2)}) collective-permute-start(f32[16,1024]{1,0:T(8,128)S(1)} %add_four.7.refs_0_.refs_4_), channel_id=1, source_target_pairs={{0,3},{1,0},{2,1},{3,2},{4,7},{5,4},{6,5},{7,6},{8,11},{9,8},{10,9... | collective-permute-start | bytes 196616 | tf_op jit(solution)/shard_map/ppermute | solution.py:36
  88.3 9.4 %collective-permute-start.30 = (f32[32,3968]{1,0:T(8,128)S(1)}, f32[32,3968]{1,0:T(8,128)S(1)}, u32[]{:S(2)}, u32[]{:S(2)}) collective-permute-start(f32[32,3968]{1,0:T(8,128)S(1)} %get-tuple-element.54), channel_id=1, source_target_pairs={{0,1},{1,2},{2,3},{3,0},{4,5},{5,6},{6,7},{7,4},{8,9},{9,10},{10,1... | collective-permute-start | bytes 1523720 | tf_op jit(solution)/shard_map/ppermute | solution.py:36
  88.4 9.4 %collective-permute-start.31 = (f32[32,3968]{1,0:T(8,128)S(1)}, f32[32,3968]{1,0:T(8,128)S(1)}, u32[]{:S(2)}, u32[]{:S(2)}) collective-permute-start(f32[32,3968]{1,0:T(8,128)S(1)} %get-tuple-element.58), channel_id=1, source_target_pairs={{0,3},{1,0},{2,1},{3,2},{4,7},{5,4},{6,5},{7,6},{8,11},{9,8},{10,9... | collective-permute-start | bytes 1523720 | tf_op jit(solution)/shard_map/ppermute | solution.py:36
  91.0 4.7 %collective-permute-start.22 = (f32[16,1024]{1,0:T(8,128)S(1)}, f32[16,1024]{1,0:T(8,128)S(1)}, u32[]{:S(2)}, u32[]{:S(2)}) collective-permute-start(f32[16,1024]{1,0:T(8,128)S(1)} %add_four.8.refs_4_.refs_0_), channel_id=1, source_target_pairs={{0,8},{1,9},{2,10},{3,11},{4,12},{5,13},{6,14},{7,15},{8,0},{9,1},... | collective-permute-start | bytes 196616 | tf_op jit(solution)/shard_map/ppermute | solution.py:36
  91.0 5.0 %collective-permute-start.23 = (f32[16,1024]{1,0:T(8,128)S(1)}, f32[16,1024]{1,0:T(8,128)S(1)}, u32[]{:S(2)}, u32[]{:S(2)}) collective-permute-start(f32[16,1024]{1,0:T(8,128)S(1)} %add_four.8.refs_4_.refs_0_), channel_id=1, source_target_pairs={{0,4},{1,5},{2,6},{3,7},{4,8},{5,9},{6,10},{7,11},{8,12},{9,13},{1... | collective-permute-start | bytes 196616 | tf_op jit(solution)/shard_map/ppermute | solution.py:36
  91.9 4.1 %collective-permute-start.24 = (f32[16,1024]{1,0:T(8,128)S(1)}, f32[16,1024]{1,0:T(8,128)S(1)}, u32[]{:S(2)}, u32[]{:S(2)}) collective-permute-start(f32[16,1024]{1,0:T(8,128)S(1)} %add_four.8.refs_4_.refs_0_), channel_id=1, source_target_pairs={{0,12},{1,13},{2,14},{3,15},{4,0},{5,1},{6,2},{7,3},{8,4},{9,5},{1... | collective-permute-start | bytes 196616 | tf_op jit(solution)/shard_map/ppermute | solution.py:36
  98.4 23.3 %collective-permute-start.33 = (f32[64,3968]{1,0:T(8,128)S(1)}, f32[64,3968]{1,0:T(8,128)S(1)}, u32[]{:S(2)}, u32[]{:S(2)}) collective-permute-start(f32[64,3968]{1,0:T(8,128)S(1)} %get-tuple-element.59.refs_4_), channel_id=1, source_target_pairs={{0,1},{1,2},{2,3},{3,0},{4,5},{5,6},{6,7},{7,4},{8,9},{9,10},{10,1... | collective-permute-start | bytes 3047432 | tf_op jit(solution)/shard_map/ppermute | solution.py:36
  99.0 22.8 %collective-permute-start.34 = (f32[64,3968]{1,0:T(8,128)S(1)}, f32[64,3968]{1,0:T(8,128)S(1)}, u32[]{:S(2)}, u32[]{:S(2)}) collective-permute-start(f32[64,3968]{1,0:T(8,128)S(1)} %get-tuple-element.63), channel_id=1, source_target_pairs={{0,3},{1,0},{2,1},{3,2},{4,7},{5,4},{6,5},{7,6},{8,11},{9,8},{10,9... | collective-permute-start | bytes 3047432 | tf_op jit(solution)/shard_map/ppermute | solution.py:36
  101.3 4.5 %collective-permute-start.27 = (f32[16,1024]{1,0:T(8,128)S(1)}, f32[16,1024]{1,0:T(8,128)S(1)}, u32[]{:S(2)}, u32[]{:S(2)}) collective-permute-start(f32[16,1024]{1,0:T(8,128)S(1)} %add_four.9.refs_6_.refs_0_), channel_id=1, source_target_pairs={{0,96},{1,97},{2,98},{3,99},{4,100},{5,101},{6,102},{7,103},{8,104... | collective-permute-start | bytes 196616 | tf_op jit(solution)/shard_map/ppermute | solution.py:36
  103.8 4.7 %collective-permute-start.28 = (f32[16,1024]{1,0:T(8,128)S(1)}, f32[16,1024]{1,0:T(8,128)S(1)}, u32[]{:S(2)}, u32[]{:S(2)}) collective-permute-start(f32[16,1024]{1,0:T(8,128)S(1)} %add_four.9.refs_6_.refs_0_), channel_id=1, source_target_pairs={{0,64},{1,65},{2,66},{3,67},{4,68},{5,69},{6,70},{7,71},{8,72},{9,... | collective-permute-start | bytes 196616 | tf_op jit(solution)/shard_map/ppermute | solution.py:36
  104.5 5.0 %collective-permute-start.29 = (f32[16,1024]{1,0:T(8,128)S(1)}, f32[16,1024]{1,0:T(8,128)S(1)}, u32[]{:S(2)}, u32[]{:S(2)}) collective-permute-start(f32[16,1024]{1,0:T(8,128)S(1)} %add_four.9.refs_6_.refs_0_), channel_id=1, source_target_pairs={{0,32},{1,33},{2,34},{3,35},{4,36},{5,37},{6,38},{7,39},{8,40},{9,... | collective-permute-start | bytes 196616 | tf_op jit(solution)/shard_map/ppermute | solution.py:36
  110.0 9.3 %collective-permute-start.32 = (f32[16,4096]{1,0:T(8,128)S(1)}, f32[16,4096]{1,0:T(8,128)S(1)}, u32[]{:S(2)}, u32[]{:S(2)}) collective-permute-start(f32[16,4096]{1,0:T(8,128)S(1)} %join.1.refs_0_.refs_4_), channel_id=1, source_target_pairs={{0,16},{1,17},{2,18},{3,19},{4,20},{5,21},{6,22},{7,23},{8,24},{9,... | collective-permute-start | bytes 786440 | tf_op jit(solution)/shard_map/ppermute | solution.py:36

commit v3 on v2

--- a/solution.py
+++ b/solution.py
@@ -13,6 +13,7 @@
 HIGHEST = lax.Precision.HIGHEST
 FREE = pl.CostEstimate(flops=0, bytes_accessed=0, transcendentals=0)
 ANY = pl.BlockSpec(memory_space=pl.ANY)
+ONCE = pl.Buffered(1)
 WHOLE = pl.BlockSpec(memory_space=pltpu.VMEM)
 SCALARS = pl.BlockSpec(memory_space=pltpu.SMEM)
 
@@ -60,19 +61,25 @@
     return jax.ShapeDtypeStruct(dims, dtype)
 
 
-def run(kernel, outs, scalars, operands, after, name, room=8):
-    def body(scalar_ref, *refs):
-        kernel(scalar_ref, *refs[: len(operands)], *refs[len(operands) + 1 :])
+def run(kernel, outs, scalars, operands, after, name, room=8, scratch=()):
+    after = after if isinstance(after, list) else [after]
+
+    scalars = [] if scalars is None else [scalars]
+    count = len(scalars) + len(operands)
+
+    def body(*refs):
+        kernel(*refs[:count], *refs[count + len(after) :])
 
     return pl.pallas_call(
         body,
-        in_specs=[SCALARS] + [WHOLE] * len(operands) + [ANY],
+        in_specs=[SCALARS] * len(scalars) + [WHOLE] * len(operands) + [ANY] * len(after),
         out_specs=[WHOLE] * len(outs),
         out_shape=outs,
+        scratch_shapes=list(scratch),
         cost_estimate=FREE,
         compiler_params=limit(room),
         name=name,
-    )(scalars, *operands, after)
+    )(*scalars, *operands, *after)
 
 
 def span(index, size):
@@ -80,18 +87,19 @@
 
 
 def combine_kernel(arity, coords_ref, *refs):
-    inputs, outputs = refs[: sum(arity)], refs[sum(arity) + 1 :]
+    inputs, outputs = refs[: sum(arity)], refs[-len(arity) :]
     start = 0
     for count, out_ref in zip(arity, outputs):
-        own, *came = inputs[start : start + count]
+        own, *came = [ref[...] for ref in inputs[start : start + count]]
         total = own[0, 0, 0].astype(jnp.float32)
-        for ref in came:
-            total = total + ref[0]
+        for block in came:
+            total = total + block[0]
         out_ref[0] = total
         start += count
 
 
 def combine(blocks, coords, wanted, after):
+    after = after if isinstance(after, list) else [after]
     depth, width = blocks.shape[3:]
     cuts = blocks.shape[2] // 2
     arity, operands, specs = [], [], []
@@ -99,9 +107,8 @@
     for owner, half, came in wanted:
 
         def where(k, i, s, owner=owner, half=half):
-            core = s[2 * SIDE]
-            there = s[owner] * (1 - core) + k * core, s[owner] * core + k * (1 - core)
-            return *there, half * cuts + i, 0, 0
+            there, core = s[owner], s[2 * SIDE]
+            return there * (1 - core) + k * core, there * core + k * (1 - core), half * cuts + i, 0, 0
 
         operands += [blocks, *came]
         specs += [pl.BlockSpec((1, 1, 1, depth, width), where)] + [whole] * len(came)
@@ -111,54 +118,43 @@
         grid_spec=pltpu.PrefetchScalarGridSpec(
             num_scalar_prefetch=1,
             grid=(SIDE, cuts),
-            in_specs=specs + [ANY],
+            in_specs=specs + [ANY] * len(after),
             out_specs=[whole] * len(wanted),
         ),
         out_shape=[shape(SIDE, cuts * depth, width)] * len(wanted),
         cost_estimate=FREE,
         compiler_params=limit(8),
         name="combine",
-    )(coords, *operands, after)
-
-
-def turn_kernel(coords_ref, *refs):
-    step = pl.program_id(0)
-    inputs, outputs = refs[:4], refs[5:]
-    for half in (0, 1):
-        total = inputs[2 * half][0] + inputs[2 * half + 1][0]
-        for spot in range(SIDE):
-
-            @pl.when(step == spot)
-            def _(total=total, out_ref=outputs[half * SIDE + spot]):
-                out_ref[...] = total
+    )(coords, *operands, *after)
+
+
+def turn_kernel(coords_ref, held_up, came_up, held_down, came_down, up, down, *kept):
+    depth = held_up.shape[1]
+    there = [coords_ref[SIDE + spot] for spot in range(SIDE)]
+    high = lambda spot: held_up[there[spot]] + came_up[there[spot]]
+    low = lambda spot: held_down[there[spot]] + came_down[there[spot]]
+    up[...] = high(2)
+    down[...] = low(2)
+    kept[0][:depth, :] = high(1)
+    kept[0][depth:, :] = low(1)
+    kept[1][:depth, :] = high(3)
+    kept[1][depth:, :] = low(3)
+    kept[2][:depth, :] = high(0)
+    kept[2][depth:, :] = low(0)
 
 
 def turn(coords, pairs, after):
     depth, width = pairs[0][0].shape[1:]
-    spec = pl.BlockSpec((1, depth, width), lambda k, s: (s[SIDE + k], 0, 0))
-    outs = pl.pallas_call(
-        turn_kernel,
-        grid_spec=pltpu.PrefetchScalarGridSpec(
-            num_scalar_prefetch=1,
-            grid=(SIDE,),
-            in_specs=[spec] * 4 + [ANY],
-            out_specs=[pl.BlockSpec((depth, width), lambda k, s: (0, 0))] * (2 * SIDE),
-        ),
-        out_shape=[shape(depth, width)] * (2 * SIDE),
-        cost_estimate=FREE,
-        compiler_params=limit(16),
-        name="turn",
-    )(coords, *pairs[0], *pairs[1], after)
-    return outs[:SIDE], outs[SIDE:]
-
-
-def ring_add_kernel(scalar_ref, *refs):
-    up_ref, down_ref = refs[6:]
-    depth = refs[0].shape[0]
-    up_ref[:depth, :] = refs[0][...] + refs[1][...]
-    up_ref[depth:, :] = refs[2][...]
-    down_ref[:depth, :] = refs[3][...]
-    down_ref[depth:, :] = refs[4][...] + refs[5][...]
+    outs = [shape(depth, width)] * 2 + [shape(2 * depth, width)] * 3
+    return run(turn_kernel, outs, coords, [*pairs[0], *pairs[1]], after, "turn")
+
+
+def ring_add_kernel(mine_up, came_up, mine_down, came_down, up_ref, down_ref):
+    depth = came_up.shape[0]
+    up_ref[:depth, :] = mine_up[:depth, :] + came_up[...]
+    up_ref[depth:, :] = mine_up[depth:, :]
+    down_ref[:depth, :] = mine_down[:depth, :]
+    down_ref[depth:, :] = mine_down[depth:, :] + came_down[...]
 
 
 def pieces_of(values):
@@ -167,6 +163,14 @@
     middle = rest.astype(jnp.bfloat16)
     low = (rest - middle.astype(jnp.float32)).astype(jnp.bfloat16)
     return high, middle, low
+
+
+def stacked(values, order):
+    pieces = pieces_of(values)
+    return [pieces[index] for index in order]
+
+
+LEFT_ORDER, RIGHT_ORDER = (0, 0, 1, 1, 0, 2), (0, 1, 0, 1, 2, 0)
 
 
 def left_kernel(scalar_ref, partial_ref, basis_ref, error_ref, after_ref, keep_ref, send_ref, pieces, total):
@@ -209,15 +213,15 @@
         in_specs=[
             SCALARS,
             pl.BlockSpec((size, width), lambda k: (k, 0)),
-            pl.BlockSpec(basis.shape, fixed),
-            pl.BlockSpec(error.shape, fixed),
+            pl.BlockSpec(basis.shape, fixed, pipeline_mode=ONCE),
+            pl.BlockSpec(error.shape, fixed, pipeline_mode=ONCE),
             ANY,
         ],
         out_specs=[pl.BlockSpec((count // 2, rows), fixed)] * 2,
         out_shape=[shape(count // 2, rows)] * 2,
         scratch_shapes=[pltpu.VMEM((3 * count, width), jnp.bfloat16), pltpu.VMEM((count, rows), jnp.float32)],
         cost_estimate=FREE,
-        compiler_params=limit(24),
+        compiler_params=limit(12),
         name="left_terms",
     )(scalars, partial, basis, error, after)
 
@@ -291,34 +295,55 @@
             SCALARS,
             pl.BlockSpec((3 * count, size), lambda k: (0, k)),
             pl.BlockSpec((size, width), lambda k: (k, 0)),
-            pl.BlockSpec(phat.shape, fixed),
-            pl.BlockSpec(error.shape, fixed),
+            pl.BlockSpec(phat.shape, fixed, pipeline_mode=ONCE),
+            pl.BlockSpec(error.shape, fixed, pipeline_mode=ONCE),
             ANY,
         ],
         out_specs=[pl.BlockSpec((count // 2, padded), fixed)] * 2,
         out_shape=[shape(count // 2, padded)] * 2,
         scratch_shapes=[pltpu.VMEM((count, padded), jnp.float32)],
         cost_estimate=FREE,
-        compiler_params=limit(24),
+        compiler_params=limit(12),
         name="right_terms",
     )(scalars, pieces, partial, phat, error, after)
 
 
-def add_kernel(scalar_ref, a_ref, b_ref, out_ref):
-    out_ref[...] = a_ref[...] + b_ref[...]
-
-
-def add(scalars, a, b, after):
-    return run(add_kernel, [shape(*a.shape)], scalars, [a, b], after, "add")[0]
-
-
-def add_four_kernel(scalar_ref, a_ref, b_ref, c_ref, d_ref, out_ref):
+def gate(arrays, after):
+    return pl.pallas_call(
+        lambda *refs: None,
+        in_specs=[ANY] * (len(arrays) + len(after)),
+        out_specs=[ANY] * len(arrays),
+        out_shape=[shape(*array.shape) for array in arrays],
+        input_output_aliases={index: index for index in range(len(arrays))},
+        cost_estimate=FREE,
+        compiler_params=limit(1),
+        name="gate",
+    )(*arrays, *after)
+
+
+def add_kernel(*refs):
+    terms = [ref[...] for ref in refs[:-1]]
+    refs[-1][...] = sum(terms[1:], terms[0])
+
+
+def add(terms, after):
+    return run(add_kernel, [shape(*terms[0].shape)], None, terms, after, "add", room=1)[0]
+
+
+def add_four_kernel(a_ref, b_ref, c_ref, d_ref, out_ref):
     out_ref[...] = (a_ref[...] + b_ref[...]) + (c_ref[...] + d_ref[...])
 
 
-def sum_four(scalars, values, along, after):
+def sum_four(values, along, after):
     came = [along(values, step) for step in (2, 1, -1)]
-    return run(add_four_kernel, [shape(*values.shape)], scalars, [values, *came], after, "add_four")[0]
+    outs = [shape(*values.shape)]
+    return run(add_four_kernel, outs, None, [values, *came], after, "add_four", room=1)[0]
+
+
+def sum_pairs(values, pairs, after):
+    for mask in (1, 3):
+        values = after = add([values, pairs(values, mask)], after)
+    return values
 
 
 def add_cut_kernel(scalar_ref, a_ref, b_ref, *out_refs):
@@ -332,7 +357,7 @@
     outs = [shape(keep.shape[0], keep.shape[1] // SIDE)] * SIDE
     parts = run(add_cut_kernel, outs, scalars, [keep, came], after, "add_cut")
     came = [along_x(parts[2], 2), along_x(parts[1], 1), along_x(parts[3], -1)]
-    return run(add_four_kernel, outs[:1], scalars, [parts[0], *came], parts[0], "add_four")[0]
+    return run(add_four_kernel, outs[:1], None, [parts[0], *came], parts[0], "add_four", room=1)[0]
 
 
 def join_kernel(scalar_ref, *refs):
@@ -347,24 +372,22 @@
     return run(join_kernel, outs, scalars, [values, *came], after, "join")[0]
 
 
-def finish_kernel(replicas, scalar_ref, mine_ref, other_ref, phat_ref, error_ref, grad_ref, rest_ref, basis_ref):
+def finish_kernel(replicas, scalar_ref, mine_ref, other_ref, phat_ref, error_ref, *refs):
+    kept_ref, up_ref, down_ref, grad_ref, next_ref, basis_ref = refs
     shard, core = scalar_ref[0], scalar_ref[1]
     own, width = error_ref.shape
     right = jnp.concatenate(ordered(core, mine_ref[:, :width], other_ref[:, :width]), axis=0)
+    basis_ref[...] = right * (1.0 / replicas)
     mine = own_rows(phat_ref[:, span(shard // (LANES // own), LANES)], shard, own)
     approx = lax.dot_general(
-        mine, right, (((0,), (0,)), ((), ())), precision=HIGHEST, preferred_element_type=jnp.float32
+        jnp.concatenate(stacked(mine, LEFT_ORDER), axis=0),
+        jnp.concatenate(stacked(right, RIGHT_ORDER), axis=0),
+        (((0,), (0,)), ((), ())),
+        preferred_element_type=jnp.float32,
     ) * (1.0 / replicas)
     grad_ref[...] = approx.astype(jnp.bfloat16)
-    rest_ref[...] = error_ref[...] - approx
-    basis_ref[...] = right * (1.0 / replicas)
-
-
-def last_kernel(scalar_ref, rest_ref, high_ref, low_ref, up_ref, down_ref, out_ref):
-    depth = high_ref.shape[0]
-    for index, ref in enumerate((high_ref, low_ref)):
-        rows = slice(index * depth, (index + 1) * depth)
-        out_ref[rows, :] = rest_ref[rows, :] + (ref[...] + (up_ref[rows, :] + down_ref[rows, :]))
+    merged = error_ref[...] + (kept_ref[...] + (up_ref[...] + down_ref[...]))
+    next_ref[...] = merged - approx
 
 
 def shards(partials, error, basis):
@@ -386,58 +409,50 @@
     sent1 = combine(blocks, coords, [(2, 0, []), (2, 1, [])], scalars)
     came1 = [along_first(sent1[0], 1), along_first(sent1[1], -1)]
     keep, send = left_terms(scalars, partial, basis, error, sent1[0])
-    part = add(scalars, keep, other_core(send), send)
-    part = sum_four(scalars, part, along_x, part)
-    part = sum_four(scalars, part, along_second, part)
+    part = add([keep, other_core(send)], keep)
     sent2 = combine(blocks, coords, [(1, 1, []), (3, 0, [])], part)
+    part = sum_four(part, along_x, sent2[0])
+    sent2 = gate(sent2, [part])
     came2 = [along_first(sent2[0], 1), along_first(sent2[1], -1)]
-    sent3 = combine(blocks, coords, [(1, 0, [came1[0]]), (3, 1, [came1[1]])], sent2[0])
+    part = sum_pairs(part, pair_second, sent2[0])
+    sent3 = combine(blocks, coords, [(1, 0, [came1[0]]), (3, 1, [came1[1]])], part)
+    (part,) = gate([other_core(part)], [sent3[0]])
+    part = sum_four(part, along_second, part)
+    sent3 = gate(sent3, [part])
     came3 = [along_first(sent3[0], 1), along_first(sent3[1], -1)]
-    part = other_core(part)
-    part = add(scalars, part, pair_second(part, 1), sent3[0])
-    part = add(scalars, part, pair_second(part, 3), part)
     phat, pieces = run(
         orthonormal_kernel,
         [shape(count, rows), shape(3 * count, rows, dtype=jnp.bfloat16)],
         scalars,
         [part, other_core(part)],
-        part,
+        sent3[0],
         "orthonormal",
     )
     keep, send = right_terms(scalars, pieces, partial, phat, error, phat)
     held = combine(blocks, coords, [(0, 0, [came2[1]]), (0, 1, [came2[0]])], send)
     part = scatter_x(scalars, keep, other_core(send), held[0])
-    part = sum_four(scalars, part, along_second, part)
-    kept = turn(coords, [(held[0], came3[0]), (held[1], came3[1])], part)
-    came4 = [along_second(kept[0][2], 1), along_second(kept[1][2], -1)]
-    part = sum_four(scalars, part, along_first, kept[0][0])
+    part = sum_four(part, along_second, part)
+    up, down, *kept = turn(coords, [(held[0], came3[0]), (held[1], came3[1])], part)
+    came4 = [along_second(up, 1), along_second(down, -1)]
+    part = sum_four(part, along_first, part)
     sent5 = run(
         ring_add_kernel,
         [shape(own, width)] * 2,
-        scalars,
-        [kept[0][1], came4[0], kept[1][1], kept[0][3], kept[1][3], came4[1]],
+        None,
+        [kept[0], came4[0], kept[1], came4[1]],
         part,
         "ring_add",
     )
     came5 = [along_second(sent5[0], 1), along_second(sent5[1], -1)]
     part = gather_x(scalars, part, sent5[0])
-    grad, rest, right = run(
+    grad, following, right = run(
         functools.partial(finish_kernel, replicas),
         [shape(own, width, dtype=jnp.bfloat16), shape(own, width), shape(count, width)],
         scalars,
-        [part, other_core(part), phat, error],
+        [part, other_core(part), phat, error, kept[2], *came5],
         part,
         "finish",
-        room=24,
     )
-    following = run(
-        last_kernel,
-        [shape(own, width)],
-        scalars,
-        [rest, kept[0][0], kept[1][0], *came5],
-        rest,
-        "last",
-    )[0]
     return grad, following[None], right.T
 
 

time: 124 us -> 117 us (0.944)
  Pallas kernels: 28.3 us -> 21.4 us
  starting transfers between devices: 57.3 us -> 54 us
  waiting for transfers between devices: 33.5 us -> 36.2 us
    pallas_call x15 -> x17, Pallas kernels: 15.7 us -> 8.79 us  [the longest x14 8.78 us: run(): pl.pallas_call(body, in_specs=[SCALARS] * len(scalars) + [WHOLE] * len(op...]
    ppermute x35, starting transfers between devices: 57.3 us -> 54 us  [moved(): lax.ppermute(values, BOTH, [(place(*spot), place(*route(*spot))) for spot...]
    ppermute x35, waiting for transfers between devices: 33.5 us -> 36.2 us  [moved(): lax.ppermute(values, BOTH, [(place(*spot), place(*route(*spot))) for spot...]
  transfers between devices with their start and end apart: 35 -> 35, of which waited for: 23 -> 20; matrix products, arithmetic and copies ran while one was open for 0% -> 0% of each run, Pallas kernels for 19% -> 14%
where the time goes in v3:
time: 117 us; the launch traced here: 116 us
  starting transfers between devices  54 us (46%)
  waiting for transfers between devices  36.2 us (31%)
  Pallas kernels  21.4 us (18%)
  local copies, waits for them, and re-layouts  3.32 us (3%)
    ppermute x35, starting transfers between devices, moved(): lax.ppermute(values, BOTH, [(place(*spot), place(*route(*spot))) for spot...  54 us
    ppermute x35, waiting for transfers between devices, moved(): lax.ppermute(values, BOTH, [(place(*spot), place(*route(*spot))) for spot...  36.2 us
    pallas_call x14, Pallas kernels, run(): pl.pallas_call(body, in_specs=[SCALARS] * len(scalars) + [WHOLE] * len(op...  8.78 us
    pallas_call x1, Pallas kernels, left_terms(): pl.pallas_call(left_kernel, grid=(SIDE,), in_specs=[SCALARS, pl.BlockSpec...  4.9 us
    pallas_call x4, Pallas kernels, combine(): pl.pallas_call(functools.partial(combine_kernel, arity), grid_spec=pltpu....  4.22 us
    pallas_call x1, Pallas kernels, right_terms(): pl.pallas_call(right_kernel, grid=(SIDE,), in_specs=[SCALARS, pl.BlockSpe...  3.46 us
    unnamed x8, local copies, waits for them, and re-layouts  3.32 us
  transfers between devices with their start and end apart: 35, of which 20 were waited for; matrix products, arithmetic and copies ran while one was open for 0% of the time, Pallas kernels for 14%

profile of v3, /device:TPU:1, one launch (start us, length us, event | category | flops | bytes accessed | tf_op | source)
XLA Modules:
  0.0 116.1 jit_solution(4388747601258493364)
XLA Ops:
  0.7 0.1 pad_add_fusion.1.coords_ref.refs_0_
  0.9 3.3 %copy-done = bf16[1,1,1024,3968]{3,2,1,0:T(8,128)(2,1)S(1)} copy-done((bf16[1,1,1024,3968]{3,2,1,0:T(8,128)(2,1)S(1)}, bf16[1,1,1024,3968]{3,2,1,0:T(8,128)(2,1)}, u32[]{:S(2)}) %copy-start) | copy-done | bytes 8126488
  4.2 1.0 combine.4
  5.2 2.2 %collective-permute-start.7 = (f32[4,32,3968]{2,1,0:T(8,128)S(1)}, f32[4,32,3968]{2,1,0:T(8,128)S(1)}, u32[]{:S(2)}, u32[]{:S(2)}) collective-permute-start(f32[4,32,3968]{2,1,0:T(8,128)S(1)} %get-tuple-element.35.after_ref), channel_id=1, source_target_pairs={{0,4},{1,5},{2,6},{3,7},{4,8},{5,9},{6,10},{7,11},{8,12},{9,13},{1... | collective-permute-start | bytes 6094856 | tf_op jit(solution)/shard_map/ppermute | solution.py:37
  7.4 1.5 %collective-permute-start.8 = (f32[4,32,3968]{2,1,0:T(8,128)S(1)}, f32[4,32,3968]{2,1,0:T(8,128)S(1)}, u32[]{:S(2)}, u32[]{:S(2)}) collective-permute-start(f32[4,32,3968]{2,1,0:T(8,128)S(1)} %get-tuple-element.41), channel_id=1, source_target_pairs={{0,12},{1,13},{2,14},{3,15},{4,0},{5,1},{6,2},{7,3},{8,4},{9,5},{1... | collective-permute-start | bytes 6094856 | tf_op jit(solution)/shard_map/ppermute | solution.py:37
  8.9 4.9 %left_terms.1 = (f32[16,1024]{1,0:T(8,128)S(1)}, f32[16,1024]{1,0:T(8,128)S(1)}) custom-call(s32[3]{0:T(128)S(1)} %pad_add_fusion.refs_2_.scalar_ref.refs_0_, bf16[1024,3968]{1,0:T(8,128)(2,1)S(1)} %bitcast.11, f32[32,3968]{1,0:T(8,128)S(1)} %bitcast.22, f32[64,3968]{1,0:T(8,128)S(1)} %bitcast.19, f32[4,32,3968]{2,1,0:T(8,128)S(1)} %get-tuple-element.35.after_ref), custom_call_target="tpu_custom_call" | custom-call | tf_op jit(solution)/shard_map/left_terms/pallas_call | solution.py:210
  13.8 2.1 %collective-permute-start = (f32[16,1024]{1,0:T(8,128)S(1)}, f32[16,1024]{1,0:T(8,128)S(1)}, u32[]{:S(2)}, u32[]{:S(2)}) collective-permute-start(f32[16,1024]{1,0:T(8,128)S(1)} %get-tuple-element.37), channel_id=1, source_target_pairs={{0,16},{1,17},{2,18},{3,19},{4,20},{5,21},{6,22},{7,23},{8,24},{9,... | collective-permute-start | bytes 196616 | tf_op jit(solution)/shard_map/ppermute | solution.py:37
  15.9 0.9 collective-permute-done.refs_1_
  16.8 2.8 %collective-permute-start.1 = (f32[16,1024]{1,0:T(8,128)S(1)}, f32[16,1024]{1,0:T(8,128)S(1)}, u32[]{:S(2)}, u32[]{:S(2)}) collective-permute-start(f32[16,1024]{1,0:T(8,128)S(1)} %add.56.refs_2_.refs_0_), channel_id=1, source_target_pairs={{0,64},{1,65},{2,66},{3,67},{4,68},{5,69},{6,70},{7,71},{8,72},{9,... | collective-permute-start | bytes 196616 | tf_op jit(solution)/shard_map/ppermute | solution.py:37
  19.6 0.3 collective-permute-start.2
  19.9 2.4 %collective-permute-start.3 = (f32[16,1024]{1,0:T(8,128)S(1)}, f32[16,1024]{1,0:T(8,128)S(1)}, u32[]{:S(2)}, u32[]{:S(2)}) collective-permute-start(f32[16,1024]{1,0:T(8,128)S(1)} %add.56.refs_2_.refs_0_), channel_id=1, source_target_pairs={{0,96},{1,97},{2,98},{3,99},{4,100},{5,101},{6,102},{7,103},{8,104... | collective-permute-start | bytes 196616 | tf_op jit(solution)/shard_map/ppermute | solution.py:37
  22.3 1.0 combine.5
  23.3 0.9 collective-permute-done.2.refs_2_
  24.3 0.1 collective-permute-start.4
  24.4 4.2 %collective-permute-done.4.refs_1_ = f32[16,1024]{1,0:T(8,128)S(1)} collective-permute-done((f32[16,1024]{1,0:T(8,128)S(1)}, f32[16,1024]{1,0:T(8,128)S(1)}, u32[]{:S(2)}, u32[]{:S(2)}) %collective-permute-start.4) | collective-permute-done | bytes 65568 | tf_op jit(solution)/shard_map/ppermute | solution.py:37
  28.5 2.2 %collective-permute-start.5 = (f32[16,1024]{1,0:T(8,128)S(1)}, f32[16,1024]{1,0:T(8,128)S(1)}, u32[]{:S(2)}, u32[]{:S(2)}) collective-permute-start(f32[16,1024]{1,0:T(8,128)S(1)} %add.57.refs_0_.refs_2_), channel_id=1, source_target_pairs={{0,3},{1,2},{2,1},{3,0},{4,7},{5,6},{6,5},{7,4},{8,11},{9,10},{10,... | collective-permute-start | bytes 196616 | tf_op jit(solution)/shard_map/ppermute | solution.py:37
  30.8 2.7 %collective-permute-start.14 = (f32[4,32,3968]{2,1,0:T(8,128)S(1)}, f32[4,32,3968]{2,1,0:T(8,128)S(1)}, u32[]{:S(2)}, u32[]{:S(2)}) collective-permute-start(f32[4,32,3968]{2,1,0:T(8,128)S(1)} %get-tuple-element.49), channel_id=1, source_target_pairs={{0,12},{1,13},{2,14},{3,15},{4,0},{5,1},{6,2},{7,3},{8,4},{9,5},{1... | collective-permute-start | bytes 6094856 | tf_op jit(solution)/shard_map/ppermute | solution.py:37
  33.5 0.5 collective-permute-done.5.refs_1_
  34.0 2.5 %collective-permute-start.6 = (f32[16,1024]{1,0:T(8,128)S(1)}, f32[16,1024]{1,0:T(8,128)S(1)}, u32[]{:S(2)}, u32[]{:S(2)}) collective-permute-start(f32[16,1024]{1,0:T(8,128)S(1)} %add.58.refs_4_), channel_id=1, source_target_pairs={{0,16},{1,17},{2,18},{3,19},{4,20},{5,21},{6,22},{7,23},{8,24},{9,... | collective-permute-start | bytes 196616 | tf_op jit(solution)/shard_map/ppermute | solution.py:37
  36.5 1.1 combine.6
  37.7 0.2 collective-permute-start.10
  37.8 2.9 %collective-permute-start.11 = (f32[16,1024]{1,0:T(8,128)S(1)}, f32[16,1024]{1,0:T(8,128)S(1)}, u32[]{:S(2)}, u32[]{:S(2)}) collective-permute-start(f32[16,1024]{1,0:T(8,128)S(1)} %gate.4.refs_0_.refs_4_), channel_id=1, source_target_pairs={{0,3},{1,0},{2,1},{3,2},{4,7},{5,4},{6,5},{7,6},{8,11},{9,8},{10,9... | collective-permute-start | bytes 196616 | tf_op jit(solution)/shard_map/ppermute | solution.py:37
  40.8 1.1 collective-permute-start.9
  41.9 1.4 %collective-permute-done.10.refs_2_ = f32[16,1024]{1,0:T(8,128)S(1)} collective-permute-done((f32[16,1024]{1,0:T(8,128)S(1)}, f32[16,1024]{1,0:T(8,128)S(1)}, u32[]{:S(2)}, u32[]{:S(2)}) %collective-permute-start.10) | collective-permute-done | bytes 65568 | tf_op jit(solution)/shard_map/ppermute | solution.py:37
  43.3 3.1 %collective-permute-done.9.refs_1_ = f32[16,1024]{1,0:T(8,128)S(1)} collective-permute-done((f32[16,1024]{1,0:T(8,128)S(1)}, f32[16,1024]{1,0:T(8,128)S(1)}, u32[]{:S(2)}, u32[]{:S(2)}) %collective-permute-start.9) | collective-permute-done | bytes 65568 | tf_op jit(solution)/shard_map/ppermute | solution.py:37
  46.5 0.2 collective-permute-start.28
  46.6 2.9 %collective-permute-start.29 = (f32[4,32,3968]{2,1,0:T(8,128)S(1)}, f32[4,32,3968]{2,1,0:T(8,128)S(1)}, u32[]{:S(2)}, u32[]{:S(2)}) collective-permute-start(f32[4,32,3968]{2,1,0:T(8,128)S(1)} %get-tuple-element.56), channel_id=1, source_target_pairs={{0,12},{1,13},{2,14},{3,15},{4,0},{5,1},{6,2},{7,3},{8,4},{9,5},{1... | collective-permute-start | bytes 6094856 | tf_op jit(solution)/shard_map/ppermute | solution.py:37
  49.5 1.9 %collective-permute-start.12 = (f32[16,1024]{1,0:T(8,128)S(1)}, f32[16,1024]{1,0:T(8,128)S(1)}, u32[]{:S(2)}, u32[]{:S(2)}) collective-permute-start(f32[16,1024]{1,0:T(8,128)S(1)} %add_four.6.refs_2_.refs_1_), channel_id=1, source_target_pairs={{0,16},{1,17},{2,18},{3,19},{4,20},{5,21},{6,22},{7,23},{8,24},{9,... | collective-permute-start | bytes 196616 | tf_op jit(solution)/shard_map/ppermute | solution.py:37
  51.4 0.9 collective-permute-done.12.refs_2_
  52.3 3.9 %orthonormal.1 = (f32[32,1024]{1,0:T(8,128)S(1)}, bf16[96,1024]{1,0:T(8,128)(2,1)S(1)}) custom-call(s32[3]{0:T(128)S(1)} %pad_add_fusion.refs_2_.scalar_ref.refs_0_, f32[16,1024]{1,0:T(8,128)S(1)} %add_four.6.refs_2_.refs_1_, f32[16,1024]{1,0:T(8,128)S(1)} %collective-permute-done.12.refs_2_, f32[4,32,3968]{2,1,0:T(8,128)S(1)} %get-tuple-element.44.refs_3_), custom_call_target="tpu_custom_call" | custom-call | tf_op jit(solution)/shard_map/orthonormal/pallas_call | solution.py:73
  56.2 3.5 %right_terms.1 = (f32[16,4096]{1,0:T(8,128)S(1)}, f32[16,4096]{1,0:T(8,128)S(1)}) custom-call(s32[3]{0:T(128)S(1)} %pad_add_fusion.refs_2_.scalar_ref.refs_0_, bf16[96,1024]{1,0:T(8,128)(2,1)S(1)} %get-tuple-element.45.pieces_ref, bf16[1024,3968]{1,0:T(8,128)(2,1)S(1)} %bitcast.16, f32[32,1024]{1,0:T(8,128)S(1)} %get-tuple-element.46.phat_ref.after_ref.refs_3_, ...), custom_call_target="tpu_custom_call" | custom-call | tf_op jit(solution)/shard_map/right_terms/pallas_call | solution.py:291
  59.7 0.4 collective-permute-start.13
  60.1 0.5 collective-permute-done.15.refs_3_
  60.6 1.1 combine.7
  61.7 0.6 add_cut.1
  62.3 1.3 %collective-permute-start.16 = (f32[16,1024]{1,0:T(8,128)S(1)}, f32[16,1024]{1,0:T(8,128)S(1)}, u32[]{:S(2)}, u32[]{:S(2)}) collective-permute-start(f32[16,1024]{1,0:T(8,128)S(1)} %get-tuple-element.52), channel_id=1, source_target_pairs={{0,64},{1,65},{2,66},{3,67},{4,68},{5,69},{6,70},{7,71},{8,72},{9,... | collective-permute-start | bytes 196616 | tf_op jit(solution)/shard_map/ppermute | solution.py:37
  63.6 2.1 %collective-permute-start.17 = (f32[16,1024]{1,0:T(8,128)S(1)}, f32[16,1024]{1,0:T(8,128)S(1)}, u32[]{:S(2)}, u32[]{:S(2)}) collective-permute-start(f32[16,1024]{1,0:T(8,128)S(1)} %get-tuple-element.53), channel_id=1, source_target_pairs={{0,32},{1,33},{2,34},{3,35},{4,36},{5,37},{6,38},{7,39},{8,40},{9,... | collective-permute-start | bytes 196616 | tf_op jit(solution)/shard_map/ppermute | solution.py:37
  65.6 0.6 collective-permute-start.18
  66.2 0.8 collective-permute-done.16.refs_1_
  67.0 1.2 %collective-permute-done.17.refs_2_ = f32[16,1024]{1,0:T(8,128)S(1)} collective-permute-done((f32[16,1024]{1,0:T(8,128)S(1)}, f32[16,1024]{1,0:T(8,128)S(1)}, u32[]{:S(2)}, u32[]{:S(2)}) %collective-permute-start.17) | collective-permute-done | bytes 65568 | tf_op jit(solution)/shard_map/ppermute | solution.py:37
  68.2 0.9 collective-permute-done.18.refs_3_
  69.1 0.9 collective-permute-start.19
  69.9 0.9 collective-permute-start.20
  70.8 1.8 %collective-permute-start.21 = (f32[16,1024]{1,0:T(8,128)S(1)}, f32[16,1024]{1,0:T(8,128)S(1)}, u32[]{:S(2)}, u32[]{:S(2)}) collective-permute-start(f32[16,1024]{1,0:T(8,128)S(1)} %add_four.7.refs_0_.refs_4_), channel_id=1, source_target_pairs={{0,3},{1,0},{2,1},{3,2},{4,7},{5,4},{6,5},{7,6},{8,11},{9,8},{10,9... | collective-permute-start | bytes 196616 | tf_op jit(solution)/shard_map/ppermute | solution.py:37
  72.6 1.9 %collective-permute-done.19.refs_1_ = f32[16,1024]{1,0:T(8,128)S(1)} collective-permute-done((f32[16,1024]{1,0:T(8,128)S(1)}, f32[16,1024]{1,0:T(8,128)S(1)}, u32[]{:S(2)}, u32[]{:S(2)}) %collective-permute-start.19) | collective-permute-done | bytes 65568 | tf_op jit(solution)/shard_map/ppermute | solution.py:37
  74.5 1.3 %collective-permute-done.20.refs_2_ = f32[16,1024]{1,0:T(8,128)S(1)} collective-permute-done((f32[16,1024]{1,0:T(8,128)S(1)}, f32[16,1024]{1,0:T(8,128)S(1)}, u32[]{:S(2)}, u32[]{:S(2)}) %collective-permute-start.20) | collective-permute-done | bytes 65568 | tf_op jit(solution)/shard_map/ppermute | solution.py:37
  75.8 7.9 %collective-permute-done.28.refs_2_ = f32[4,32,3968]{2,1,0:T(8,128)S(1)} collective-permute-done((f32[4,32,3968]{2,1,0:T(8,128)S(1)}, f32[4,32,3968]{2,1,0:T(8,128)S(1)}, u32[]{:S(2)}, u32[]{:S(2)}) %collective-permute-start.28) | collective-permute-done | bytes 2031648 | tf_op jit(solution)/shard_map/ppermute | solution.py:37
  83.8 1.0 turn.1
  84.8 2.7 %collective-permute-start.31 = (f32[32,3968]{1,0:T(8,128)S(1)}, f32[32,3968]{1,0:T(8,128)S(1)}, u32[]{:S(2)}, u32[]{:S(2)}) collective-permute-start(f32[32,3968]{1,0:T(8,128)S(1)} %get-tuple-element.60), channel_id=1, source_target_pairs={{0,3},{1,0},{2,1},{3,2},{4,7},{5,4},{6,5},{7,6},{8,11},{9,8},{10,9... | collective-permute-start | bytes 1523720 | tf_op jit(solution)/shard_map/ppermute | solution.py:37
  87.5 1.3 %collective-permute-start.23 = (f32[16,1024]{1,0:T(8,128)S(1)}, f32[16,1024]{1,0:T(8,128)S(1)}, u32[]{:S(2)}, u32[]{:S(2)}) collective-permute-start(f32[16,1024]{1,0:T(8,128)S(1)} %add_four.8.refs_0_.refs_4_.refs_5_), channel_id=1, source_target_pairs={{0,4},{1,5},{2,6},{3,7},{4,8},{5,9},{6,10},{7,11},{8,12},{9,13},{1... | collective-permute-start | bytes 196616 | tf_op jit(solution)/shard_map/ppermute | solution.py:37
  88.8 1.4 %collective-permute-start.24 = (f32[16,1024]{1,0:T(8,128)S(1)}, f32[16,1024]{1,0:T(8,128)S(1)}, u32[]{:S(2)}, u32[]{:S(2)}) collective-permute-start(f32[16,1024]{1,0:T(8,128)S(1)} %add_four.8.refs_0_.refs_4_.refs_5_), channel_id=1, source_target_pairs={{0,12},{1,13},{2,14},{3,15},{4,0},{5,1},{6,2},{7,3},{8,4},{9,5},{1... | collective-permute-start | bytes 196616 | tf_op jit(solution)/shard_map/ppermute | solution.py:37
  90.2 2.6 %collective-permute-done.22.refs_1_ = f32[16,1024]{1,0:T(8,128)S(1)} collective-permute-done((f32[16,1024]{1,0:T(8,128)S(1)}, f32[16,1024]{1,0:T(8,128)S(1)}, u32[]{:S(2)}, u32[]{:S(2)}) %collective-permute-start.22) | collective-permute-done | bytes 65568 | tf_op jit(solution)/shard_map/ppermute | solution.py:37
  92.8 1.3 %collective-permute-done.30.refs_1_ = f32[32,3968]{1,0:T(8,128)S(1)} collective-permute-done((f32[32,3968]{1,0:T(8,128)S(1)}, f32[32,3968]{1,0:T(8,128)S(1)}, u32[]{:S(2)}, u32[]{:S(2)}) %collective-permute-start.30) | collective-permute-done | bytes 507936 | tf_op jit(solution)/shard_map/ppermute | solution.py:37
  94.2 0.2 ring_add.1
  94.4 3.4 %collective-permute-start.34 = (f32[64,3968]{1,0:T(8,128)S(1)}, f32[64,3968]{1,0:T(8,128)S(1)}, u32[]{:S(2)}, u32[]{:S(2)}) collective-permute-start(f32[64,3968]{1,0:T(8,128)S(1)} %get-tuple-element.63), channel_id=1, source_target_pairs={{0,3},{1,0},{2,1},{3,2},{4,7},{5,4},{6,5},{7,6},{8,11},{9,8},{10,9... | collective-permute-start | bytes 3047432 | tf_op jit(solution)/shard_map/ppermute | solution.py:37
  97.9 2.7 %collective-permute-start.25 = (f32[16,1024]{1,0:T(8,128)S(1)}, f32[16,1024]{1,0:T(8,128)S(1)}, u32[]{:S(2)}, u32[]{:S(2)}) collective-permute-start(f32[16,1024]{1,0:T(8,128)S(1)} %add_four.9.refs_4_.refs_1_), channel_id=1, source_target_pairs={{0,96},{1,97},{2,98},{3,99},{4,100},{5,101},{6,102},{7,103},{8,104... | collective-permute-start | bytes 196616 | tf_op jit(solution)/shard_map/ppermute | solution.py:37
  100.5 0.6 collective-permute-start.27
  101.1 1.3 %collective-permute-done.25.refs_2_ = f32[16,1024]{1,0:T(8,128)S(1)} collective-permute-done((f32[16,1024]{1,0:T(8,128)S(1)}, f32[16,1024]{1,0:T(8,128)S(1)}, u32[]{:S(2)}, u32[]{:S(2)}) %collective-permute-start.25) | collective-permute-done | bytes 65568 | tf_op jit(solution)/shard_map/ppermute | solution.py:37
  102.5 2.8 %collective-permute-done.26.refs_3_ = f32[16,1024]{1,0:T(8,128)S(1)} collective-permute-done((f32[16,1024]{1,0:T(8,128)S(1)}, f32[16,1024]{1,0:T(8,128)S(1)}, u32[]{:S(2)}, u32[]{:S(2)}) %collective-permute-start.26) | collective-permute-done | bytes 65568 | tf_op jit(solution)/shard_map/ppermute | solution.py:37
  105.3 0.6 collective-permute-done.27.refs_4_
  105.9 0.6 join.1.refs_1_.refs_8_
  106.4 6.0 %collective-permute-start.32 = (f32[16,4096]{1,0:T(8,128)S(1)}, f32[16,4096]{1,0:T(8,128)S(1)}, u32[]{:S(2)}, u32[]{:S(2)}) collective-permute-start(f32[16,4096]{1,0:T(8,128)S(1)} %join.1.refs_1_.refs_8_), channel_id=1, source_target_pairs={{0,16},{1,17},{2,18},{3,19},{4,20},{5,21},{6,22},{7,23},{8,24},{9,... | collective-permute-start | bytes 786440 | tf_op jit(solution)/shard_map/ppermute | solution.py:37
  112.4 1.2 %collective-permute-done.32.refs_2_ = f32[16,4096]{1,0:T(8,128)S(1)} collective-permute-done((f32[16,4096]{1,0:T(8,128)S(1)}, f32[16,4096]{1,0:T(8,128)S(1)}, u32[]{:S(2)}, u32[]{:S(2)}) %collective-permute-start.32) | collective-permute-done | bytes 262176 | tf_op jit(solution)/shard_map/ppermute | solution.py:37
  113.6 2.5 %finish.1 = (bf16[64,3968]{1,0:T(8,128)(2,1)}, f32[64,3968]{1,0:T(8,128)}, f32[32,3968]{1,0:T(8,128)}) custom-call(s32[3]{0:T(128)S(1)} %pad_add_fusion.refs_2_.scalar_ref.refs_0_, f32[16,4096]{1,0:T(8,128)S(1)} %join.1.refs_1_.refs_8_, f32[16,4096]{1,0:T(8,128)S(1)} %collective-permute-done.32.refs_2_, ...), custom_call_target="tpu_custom_call" | custom-call | tf_op jit(solution)/shard_map/finish/pallas_call | solution.py:73
  (40 shorter events, 0.4 us)
Async XLA Ops:
  0.9 3.3 %copy-start = (bf16[1,1,1024,3968]{3,2,1,0:T(8,128)(2,1)S(1)}, bf16[1,1,1024,3968]{3,2,1,0:T(8,128)(2,1)}, u32[]{:S(2)}) copy-start(bf16[1,1,1024,3968]{3,2,1,0:T(8,128)(2,1)} %param.3) | copy-start | bytes 24379396
  4.2 4.7 %copy-start.1 = (bf16[1,1,1024,3968]{3,2,1,0:T(8,128)(2,1)S(1)}, bf16[1,1,1024,3968]{3,2,1,0:T(8,128)(2,1)}, u32[]{:S(2)}) copy-start(bf16[1,1,1024,3968]{3,2,1,0:T(8,128)(2,1)} %param.3) | copy-start | bytes 24379396
  4.2 4.7 %copy-start.2 = (f32[1,64,3968]{2,1,0:T(8,128)S(1)}, f32[1,64,3968]{2,1,0:T(8,128)}, u32[]{:S(2)}) copy-start(f32[1,64,3968]{2,1,0:T(8,128)} %param.4) | copy-start | bytes 3047428
  4.2 4.7 %copy-start.3 = (f32[3968,32]{0,1:T(8,128)S(1)}, f32[3968,32]{0,1:T(8,128)}, u32[]{:S(2)}) copy-start(f32[3968,32]{0,1:T(8,128)} %param.5) | copy-start | bytes 1523716
  5.2 31.3 %collective-permute-start.7 = (f32[4,32,3968]{2,1,0:T(8,128)S(1)}, f32[4,32,3968]{2,1,0:T(8,128)S(1)}, u32[]{:S(2)}, u32[]{:S(2)}) collective-permute-start(f32[4,32,3968]{2,1,0:T(8,128)S(1)} %get-tuple-element.35.after_ref), channel_id=1, source_target_pairs={{0,4},{1,5},{2,6},{3,7},{4,8},{5,9},{6,10},{7,11},{8,12},{9,13},{1... | collective-permute-start | bytes 6094856 | tf_op jit(solution)/shard_map/ppermute | solution.py:37
  7.4 29.1 %collective-permute-start.8 = (f32[4,32,3968]{2,1,0:T(8,128)S(1)}, f32[4,32,3968]{2,1,0:T(8,128)S(1)}, u32[]{:S(2)}, u32[]{:S(2)}) collective-permute-start(f32[4,32,3968]{2,1,0:T(8,128)S(1)} %get-tuple-element.41), channel_id=1, source_target_pairs={{0,12},{1,13},{2,14},{3,15},{4,0},{5,1},{6,2},{7,3},{8,4},{9,5},{1... | collective-permute-start | bytes 6094856 | tf_op jit(solution)/shard_map/ppermute | solution.py:37
  13.8 3.0 %collective-permute-start = (f32[16,1024]{1,0:T(8,128)S(1)}, f32[16,1024]{1,0:T(8,128)S(1)}, u32[]{:S(2)}, u32[]{:S(2)}) collective-permute-start(f32[16,1024]{1,0:T(8,128)S(1)} %get-tuple-element.37), channel_id=1, source_target_pairs={{0,16},{1,17},{2,18},{3,19},{4,20},{5,21},{6,22},{7,23},{8,24},{9,... | collective-permute-start | bytes 196616 | tf_op jit(solution)/shard_map/ppermute | solution.py:37
  16.8 6.5 %collective-permute-start.1 = (f32[16,1024]{1,0:T(8,128)S(1)}, f32[16,1024]{1,0:T(8,128)S(1)}, u32[]{:S(2)}, u32[]{:S(2)}) collective-permute-start(f32[16,1024]{1,0:T(8,128)S(1)} %add.56.refs_2_.refs_0_), channel_id=1, source_target_pairs={{0,64},{1,65},{2,66},{3,67},{4,68},{5,69},{6,70},{7,71},{8,72},{9,... | collective-permute-start | bytes 196616 | tf_op jit(solution)/shard_map/ppermute | solution.py:37
  19.6 4.6 %collective-permute-start.2 = (f32[16,1024]{1,0:T(8,128)S(1)}, f32[16,1024]{1,0:T(8,128)S(1)}, u32[]{:S(2)}, u32[]{:S(2)}) collective-permute-start(f32[16,1024]{1,0:T(8,128)S(1)} %add.56.refs_2_.refs_0_), channel_id=1, source_target_pairs={{0,32},{1,33},{2,34},{3,35},{4,36},{5,37},{6,38},{7,39},{8,40},{9,... | collective-permute-start | bytes 196616 | tf_op jit(solution)/shard_map/ppermute | solution.py:37
  19.9 4.3 %collective-permute-start.3 = (f32[16,1024]{1,0:T(8,128)S(1)}, f32[16,1024]{1,0:T(8,128)S(1)}, u32[]{:S(2)}, u32[]{:S(2)}) collective-permute-start(f32[16,1024]{1,0:T(8,128)S(1)} %add.56.refs_2_.refs_0_), channel_id=1, source_target_pairs={{0,96},{1,97},{2,98},{3,99},{4,100},{5,101},{6,102},{7,103},{8,104... | collective-permute-start | bytes 196616 | tf_op jit(solution)/shard_map/ppermute | solution.py:37
  24.3 4.3 %collective-permute-start.4 = (f32[16,1024]{1,0:T(8,128)S(1)}, f32[16,1024]{1,0:T(8,128)S(1)}, u32[]{:S(2)}, u32[]{:S(2)}) collective-permute-start(f32[16,1024]{1,0:T(8,128)S(1)} %add_four.5.refs_2_.refs_0_), channel_id=1, source_target_pairs={{0,1},{1,0},{2,3},{3,2},{4,5},{5,4},{6,7},{7,6},{8,9},{9,8},{10,11... | collective-permute-start | bytes 196616 | tf_op jit(solution)/shard_map/ppermute | solution.py:37
  28.5 5.5 %collective-permute-start.5 = (f32[16,1024]{1,0:T(8,128)S(1)}, f32[16,1024]{1,0:T(8,128)S(1)}, u32[]{:S(2)}, u32[]{:S(2)}) collective-permute-start(f32[16,1024]{1,0:T(8,128)S(1)} %add.57.refs_0_.refs_2_), channel_id=1, source_target_pairs={{0,3},{1,2},{2,1},{3,0},{4,7},{5,6},{6,5},{7,4},{8,11},{9,10},{10,... | collective-permute-start | bytes 196616 | tf_op jit(solution)/shard_map/ppermute | solution.py:37
  30.8 29.3 %collective-permute-start.14 = (f32[4,32,3968]{2,1,0:T(8,128)S(1)}, f32[4,32,3968]{2,1,0:T(8,128)S(1)}, u32[]{:S(2)}, u32[]{:S(2)}) collective-permute-start(f32[4,32,3968]{2,1,0:T(8,128)S(1)} %get-tuple-element.49), channel_id=1, source_target_pairs={{0,12},{1,13},{2,14},{3,15},{4,0},{5,1},{6,2},{7,3},{8,4},{9,5},{1... | collective-permute-start | bytes 6094856 | tf_op jit(solution)/shard_map/ppermute | solution.py:37
  33.5 27.1 %collective-permute-start.15 = (f32[4,32,3968]{2,1,0:T(8,128)S(1)}, f32[4,32,3968]{2,1,0:T(8,128)S(1)}, u32[]{:S(2)}, u32[]{:S(2)}) collective-permute-start(f32[4,32,3968]{2,1,0:T(8,128)S(1)} %get-tuple-element.40.refs_2_), channel_id=1, source_target_pairs={{0,4},{1,5},{2,6},{3,7},{4,8},{5,9},{6,10},{7,11},{8,12},{9,13},{1... | collective-permute-start | bytes 6094856 | tf_op jit(solution)/shard_map/ppermute | solution.py:37
  34.0 3.6 %collective-permute-start.6 = (f32[16,1024]{1,0:T(8,128)S(1)}, f32[16,1024]{1,0:T(8,128)S(1)}, u32[]{:S(2)}, u32[]{:S(2)}) collective-permute-start(f32[16,1024]{1,0:T(8,128)S(1)} %add.58.refs_4_), channel_id=1, source_target_pairs={{0,16},{1,17},{2,18},{3,19},{4,20},{5,21},{6,22},{7,23},{8,24},{9,... | collective-permute-start | bytes 196616 | tf_op jit(solution)/shard_map/ppermute | solution.py:37
  37.7 5.7 %collective-permute-start.10 = (f32[16,1024]{1,0:T(8,128)S(1)}, f32[16,1024]{1,0:T(8,128)S(1)}, u32[]{:S(2)}, u32[]{:S(2)}) collective-permute-start(f32[16,1024]{1,0:T(8,128)S(1)} %gate.4.refs_0_.refs_4_), channel_id=1, source_target_pairs={{0,1},{1,2},{2,3},{3,0},{4,5},{5,6},{6,7},{7,4},{8,9},{9,10},{10,1... | collective-permute-start | bytes 196616 | tf_op jit(solution)/shard_map/ppermute | solution.py:37
  37.8 5.5 %collective-permute-start.11 = (f32[16,1024]{1,0:T(8,128)S(1)}, f32[16,1024]{1,0:T(8,128)S(1)}, u32[]{:S(2)}, u32[]{:S(2)}) collective-permute-start(f32[16,1024]{1,0:T(8,128)S(1)} %gate.4.refs_0_.refs_4_), channel_id=1, source_target_pairs={{0,3},{1,0},{2,1},{3,2},{4,7},{5,4},{6,5},{7,6},{8,11},{9,8},{10,9... | collective-permute-start | bytes 196616 | tf_op jit(solution)/shard_map/ppermute | solution.py:37
  40.8 5.7 %collective-permute-start.9 = (f32[16,1024]{1,0:T(8,128)S(1)}, f32[16,1024]{1,0:T(8,128)S(1)}, u32[]{:S(2)}, u32[]{:S(2)}) collective-permute-start(f32[16,1024]{1,0:T(8,128)S(1)} %gate.4.refs_0_.refs_4_), channel_id=1, source_target_pairs={{0,2},{1,3},{2,0},{3,1},{4,6},{5,7},{6,4},{7,5},{8,10},{9,11},{10,... | collective-permute-start | bytes 196616 | tf_op jit(solution)/shard_map/ppermute | solution.py:37
  46.5 37.3 %collective-permute-start.28 = (f32[4,32,3968]{2,1,0:T(8,128)S(1)}, f32[4,32,3968]{2,1,0:T(8,128)S(1)}, u32[]{:S(2)}, u32[]{:S(2)}) collective-permute-start(f32[4,32,3968]{2,1,0:T(8,128)S(1)} %get-tuple-element.44.refs_3_), channel_id=1, source_target_pairs={{0,4},{1,5},{2,6},{3,7},{4,8},{5,9},{6,10},{7,11},{8,12},{9,13},{1... | collective-permute-start | bytes 6094856 | tf_op jit(solution)/shard_map/ppermute | solution.py:37
  46.6 37.1 %collective-permute-start.29 = (f32[4,32,3968]{2,1,0:T(8,128)S(1)}, f32[4,32,3968]{2,1,0:T(8,128)S(1)}, u32[]{:S(2)}, u32[]{:S(2)}) collective-permute-start(f32[4,32,3968]{2,1,0:T(8,128)S(1)} %get-tuple-element.56), channel_id=1, source_target_pairs={{0,12},{1,13},{2,14},{3,15},{4,0},{5,1},{6,2},{7,3},{8,4},{9,5},{1... | collective-permute-start | bytes 6094856 | tf_op jit(solution)/shard_map/ppermute | solution.py:37
  49.5 2.8 %collective-permute-start.12 = (f32[16,1024]{1,0:T(8,128)S(1)}, f32[16,1024]{1,0:T(8,128)S(1)}, u32[]{:S(2)}, u32[]{:S(2)}) collective-permute-start(f32[16,1024]{1,0:T(8,128)S(1)} %add_four.6.refs_2_.refs_1_), channel_id=1, source_target_pairs={{0,16},{1,17},{2,18},{3,19},{4,20},{5,21},{6,22},{7,23},{8,24},{9,... | collective-permute-start | bytes 196616 | tf_op jit(solution)/shard_map/ppermute | solution.py:37
  59.7 2.0 %collective-permute-start.13 = (f32[16,4096]{1,0:T(8,128)S(1)}, f32[16,4096]{1,0:T(8,128)S(1)}, u32[]{:S(2)}, u32[]{:S(2)}) collective-permute-start(f32[16,4096]{1,0:T(8,128)S(1)} %get-tuple-element.48.refs_4_), channel_id=1, source_target_pairs={{0,16},{1,17},{2,18},{3,19},{4,20},{5,21},{6,22},{7,23},{8,24},{9,... | collective-permute-start | bytes 786440 | tf_op jit(solution)/shard_map/ppermute | solution.py:37
  62.3 4.7 %collective-permute-start.16 = (f32[16,1024]{1,0:T(8,128)S(1)}, f32[16,1024]{1,0:T(8,128)S(1)}, u32[]{:S(2)}, u32[]{:S(2)}) collective-permute-start(f32[16,1024]{1,0:T(8,128)S(1)} %get-tuple-element.52), channel_id=1, source_target_pairs={{0,64},{1,65},{2,66},{3,67},{4,68},{5,69},{6,70},{7,71},{8,72},{9,... | collective-permute-start | bytes 196616 | tf_op jit(solution)/shard_map/ppermute | solution.py:37
  63.6 4.6 %collective-permute-start.17 = (f32[16,1024]{1,0:T(8,128)S(1)}, f32[16,1024]{1,0:T(8,128)S(1)}, u32[]{:S(2)}, u32[]{:S(2)}) collective-permute-start(f32[16,1024]{1,0:T(8,128)S(1)} %get-tuple-element.53), channel_id=1, source_target_pairs={{0,32},{1,33},{2,34},{3,35},{4,36},{5,37},{6,38},{7,39},{8,40},{9,... | collective-permute-start | bytes 196616 | tf_op jit(solution)/shard_map/ppermute | solution.py:37
  65.6 3.4 %collective-permute-start.18 = (f32[16,1024]{1,0:T(8,128)S(1)}, f32[16,1024]{1,0:T(8,128)S(1)}, u32[]{:S(2)}, u32[]{:S(2)}) collective-permute-start(f32[16,1024]{1,0:T(8,128)S(1)} %get-tuple-element.54), channel_id=1, source_target_pairs={{0,96},{1,97},{2,98},{3,99},{4,100},{5,101},{6,102},{7,103},{8,104... | collective-permute-start | bytes 196616 | tf_op jit(solution)/shard_map/ppermute | solution.py:37
  69.1 5.5 %collective-permute-start.19 = (f32[16,1024]{1,0:T(8,128)S(1)}, f32[16,1024]{1,0:T(8,128)S(1)}, u32[]{:S(2)}, u32[]{:S(2)}) collective-permute-start(f32[16,1024]{1,0:T(8,128)S(1)} %add_four.7.refs_0_.refs_4_), channel_id=1, source_target_pairs={{0,2},{1,3},{2,0},{3,1},{4,6},{5,7},{6,4},{7,5},{8,10},{9,11},{10,... | collective-permute-start | bytes 196616 | tf_op jit(solution)/shard_map/ppermute | solution.py:37
  69.9 5.9 %collective-permute-start.20 = (f32[16,1024]{1,0:T(8,128)S(1)}, f32[16,1024]{1,0:T(8,128)S(1)}, u32[]{:S(2)}, u32[]{:S(2)}) collective-permute-start(f32[16,1024]{1,0:T(8,128)S(1)} %add_four.7.refs_0_.refs_4_), channel_id=1, source_target_pairs={{0,1},{1,2},{2,3},{3,0},{4,5},{5,6},{6,7},{7,4},{8,9},{9,10},{10,1... | collective-permute-start | bytes 196616 | tf_op jit(solution)/shard_map/ppermute | solution.py:37
  70.8 5.0 %collective-permute-start.21 = (f32[16,1024]{1,0:T(8,128)S(1)}, f32[16,1024]{1,0:T(8,128)S(1)}, u32[]{:S(2)}, u32[]{:S(2)}) collective-permute-start(f32[16,1024]{1,0:T(8,128)S(1)} %add_four.7.refs_0_.refs_4_), channel_id=1, source_target_pairs={{0,3},{1,0},{2,1},{3,2},{4,7},{5,4},{6,5},{7,6},{8,11},{9,8},{10,9... | collective-permute-start | bytes 196616 | tf_op jit(solution)/shard_map/ppermute | solution.py:37
  84.7 9.4 %collective-permute-start.30 = (f32[32,3968]{1,0:T(8,128)S(1)}, f32[32,3968]{1,0:T(8,128)S(1)}, u32[]{:S(2)}, u32[]{:S(2)}) collective-permute-start(f32[32,3968]{1,0:T(8,128)S(1)} %get-tuple-element.58), channel_id=1, source_target_pairs={{0,1},{1,2},{2,3},{3,0},{4,5},{5,6},{6,7},{7,4},{8,9},{9,10},{10,1... | collective-permute-start | bytes 1523720 | tf_op jit(solution)/shard_map/ppermute | solution.py:37
  84.8 9.4 %collective-permute-start.31 = (f32[32,3968]{1,0:T(8,128)S(1)}, f32[32,3968]{1,0:T(8,128)S(1)}, u32[]{:S(2)}, u32[]{:S(2)}) collective-permute-start(f32[32,3968]{1,0:T(8,128)S(1)} %get-tuple-element.60), channel_id=1, source_target_pairs={{0,3},{1,0},{2,1},{3,2},{4,7},{5,4},{6,5},{7,6},{8,11},{9,8},{10,9... | collective-permute-start | bytes 1523720 | tf_op jit(solution)/shard_map/ppermute | solution.py:37
  87.5 5.3 %collective-permute-start.22 = (f32[16,1024]{1,0:T(8,128)S(1)}, f32[16,1024]{1,0:T(8,128)S(1)}, u32[]{:S(2)}, u32[]{:S(2)}) collective-permute-start(f32[16,1024]{1,0:T(8,128)S(1)} %add_four.8.refs_0_.refs_4_.refs_5_), channel_id=1, source_target_pairs={{0,8},{1,9},{2,10},{3,11},{4,12},{5,13},{6,14},{7,15},{8,0},{9,1},... | collective-permute-start | bytes 196616 | tf_op jit(solution)/shard_map/ppermute | solution.py:37
  87.5 5.3 %collective-permute-start.23 = (f32[16,1024]{1,0:T(8,128)S(1)}, f32[16,1024]{1,0:T(8,128)S(1)}, u32[]{:S(2)}, u32[]{:S(2)}) collective-permute-start(f32[16,1024]{1,0:T(8,128)S(1)} %add_four.8.refs_0_.refs_4_.refs_5_), channel_id=1, source_target_pairs={{0,4},{1,5},{2,6},{3,7},{4,8},{5,9},{6,10},{7,11},{8,12},{9,13},{1... | collective-permute-start | bytes 196616 | tf_op jit(solution)/shard_map/ppermute | solution.py:37
  88.8 4.1 %collective-permute-start.24 = (f32[16,1024]{1,0:T(8,128)S(1)}, f32[16,1024]{1,0:T(8,128)S(1)}, u32[]{:S(2)}, u32[]{:S(2)}) collective-permute-start(f32[16,1024]{1,0:T(8,128)S(1)} %add_four.8.refs_0_.refs_4_.refs_5_), channel_id=1, source_target_pairs={{0,12},{1,13},{2,14},{3,15},{4,0},{5,1},{6,2},{7,3},{8,4},{9,5},{1... | collective-permute-start | bytes 196616 | tf_op jit(solution)/shard_map/ppermute | solution.py:37
  94.3 19.2 %collective-permute-start.33 = (f32[64,3968]{1,0:T(8,128)S(1)}, f32[64,3968]{1,0:T(8,128)S(1)}, u32[]{:S(2)}, u32[]{:S(2)}) collective-permute-start(f32[64,3968]{1,0:T(8,128)S(1)} %get-tuple-element.61.refs_5_), channel_id=1, source_target_pairs={{0,1},{1,2},{2,3},{3,0},{4,5},{5,6},{6,7},{7,4},{8,9},{9,10},{10,1... | collective-permute-start | bytes 3047432 | tf_op jit(solution)/shard_map/ppermute | solution.py:37
  94.4 19.1 %collective-permute-start.34 = (f32[64,3968]{1,0:T(8,128)S(1)}, f32[64,3968]{1,0:T(8,128)S(1)}, u32[]{:S(2)}, u32[]{:S(2)}) collective-permute-start(f32[64,3968]{1,0:T(8,128)S(1)} %get-tuple-element.63), channel_id=1, source_target_pairs={{0,3},{1,0},{2,1},{3,2},{4,7},{5,4},{6,5},{7,6},{8,11},{9,8},{10,9... | collective-permute-start | bytes 3047432 | tf_op jit(solution)/shard_map/ppermute | solution.py:37
  97.9 4.6 %collective-permute-start.25 = (f32[16,1024]{1,0:T(8,128)S(1)}, f32[16,1024]{1,0:T(8,128)S(1)}, u32[]{:S(2)}, u32[]{:S(2)}) collective-permute-start(f32[16,1024]{1,0:T(8,128)S(1)} %add_four.9.refs_4_.refs_1_), channel_id=1, source_target_pairs={{0,96},{1,97},{2,98},{3,99},{4,100},{5,101},{6,102},{7,103},{8,104... | collective-permute-start | bytes 196616 | tf_op jit(solution)/shard_map/ppermute | solution.py:37
  100.5 4.7 %collective-permute-start.26 = (f32[16,1024]{1,0:T(8,128)S(1)}, f32[16,1024]{1,0:T(8,128)S(1)}, u32[]{:S(2)}, u32[]{:S(2)}) collective-permute-start(f32[16,1024]{1,0:T(8,128)S(1)} %add_four.9.refs_4_.refs_1_), channel_id=1, source_target_pairs={{0,64},{1,65},{2,66},{3,67},{4,68},{5,69},{6,70},{7,71},{8,72},{9,... | collective-permute-start | bytes 196616 | tf_op jit(solution)/shard_map/ppermute | solution.py:37
  100.5 5.3 %collective-permute-start.27 = (f32[16,1024]{1,0:T(8,128)S(1)}, f32[16,1024]{1,0:T(8,128)S(1)}, u32[]{:S(2)}, u32[]{:S(2)}) collective-permute-start(f32[16,1024]{1,0:T(8,128)S(1)} %add_four.9.refs_4_.refs_1_), channel_id=1, source_target_pairs={{0,32},{1,33},{2,34},{3,35},{4,36},{5,37},{6,38},{7,39},{8,40},{9,... | collective-permute-start | bytes 196616 | tf_op jit(solution)/shard_map/ppermute | solution.py:37
  106.4 7.1 %collective-permute-start.32 = (f32[16,4096]{1,0:T(8,128)S(1)}, f32[16,4096]{1,0:T(8,128)S(1)}, u32[]{:S(2)}, u32[]{:S(2)}) collective-permute-start(f32[16,4096]{1,0:T(8,128)S(1)} %join.1.refs_1_.refs_8_), channel_id=1, source_target_pairs={{0,16},{1,17},{2,18},{3,19},{4,20},{5,21},{6,22},{7,23},{8,24},{9,... | collective-permute-start | bytes 786440 | tf_op jit(solution)/shard_map/ppermute | solution.py:37

commit v4 on v3

--- a/solution.py
+++ b/solution.py
@@ -51,6 +51,10 @@
 
 def along_second(values, step):
     return moved(values, lambda x, c, z, y: (x, c, z + step * c, y + step * (1 - c)))
+
+
+def pair_x(values, mask):
+    return moved(values, lambda x, c, z, y: (x ^ mask, c, z, y))
 
 
 def pair_second(values, mask):
@@ -80,6 +84,10 @@
         compiler_params=limit(room),
         name=name,
     )(*scalars, *operands, *after)
+
+
+def in_hbm(values):
+    return pltpu.with_memory_space_constraint(values, pltpu.HBM)
 
 
 def span(index, size):
@@ -128,33 +136,36 @@
     )(coords, *operands, *after)
 
 
-def turn_kernel(coords_ref, held_up, came_up, held_down, came_down, up, down, *kept):
+def turn_first_kernel(coords_ref, held_up, came_up, held_down, came_down, up, down):
+    there = coords_ref[SIDE + 2]
+    up[...] = held_up[there] + came_up[there]
+    down[...] = held_down[there] + came_down[there]
+
+
+def turn_rest_kernel(coords_ref, held_up, came_up, held_down, came_down, up, down, kept_up, kept_down, own):
     depth = held_up.shape[1]
     there = [coords_ref[SIDE + spot] for spot in range(SIDE)]
     high = lambda spot: held_up[there[spot]] + came_up[there[spot]]
     low = lambda spot: held_down[there[spot]] + came_down[there[spot]]
-    up[...] = high(2)
-    down[...] = low(2)
-    kept[0][:depth, :] = high(1)
-    kept[0][depth:, :] = low(1)
-    kept[1][:depth, :] = high(3)
-    kept[1][depth:, :] = low(3)
-    kept[2][:depth, :] = high(0)
-    kept[2][depth:, :] = low(0)
+    up[...] = low(1)
+    down[...] = high(3)
+    kept_up[...] = high(1)
+    kept_down[...] = low(3)
+    own[:depth, :] = high(0)
+    own[depth:, :] = low(0)
 
 
 def turn(coords, pairs, after):
     depth, width = pairs[0][0].shape[1:]
-    outs = [shape(depth, width)] * 2 + [shape(2 * depth, width)] * 3
-    return run(turn_kernel, outs, coords, [*pairs[0], *pairs[1]], after, "turn")
+    part, terms = shape(depth, width), [*pairs[0], *pairs[1]]
+    first = run(turn_first_kernel, [part] * 2, coords, terms, after, "turn_first")
+    outs = [part] * 4 + [shape(2 * depth, width)]
+    return [*first, *run(turn_rest_kernel, outs, coords, terms, first[0], "turn_rest")]
 
 
 def ring_add_kernel(mine_up, came_up, mine_down, came_down, up_ref, down_ref):
-    depth = came_up.shape[0]
-    up_ref[:depth, :] = mine_up[:depth, :] + came_up[...]
-    up_ref[depth:, :] = mine_up[depth:, :]
-    down_ref[:depth, :] = mine_down[:depth, :]
-    down_ref[depth:, :] = mine_down[depth:, :] + came_down[...]
+    up_ref[...] = mine_up[...] + came_up[...]
+    down_ref[...] = mine_down[...] + came_down[...]
 
 
 def pieces_of(values):
@@ -173,7 +184,9 @@
 LEFT_ORDER, RIGHT_ORDER = (0, 0, 1, 1, 0, 2), (0, 1, 0, 1, 2, 0)
 
 
-def left_kernel(scalar_ref, partial_ref, basis_ref, error_ref, after_ref, keep_ref, send_ref, pieces, total):
+def left_kernel(
+    scalar_ref, partial_ref, basis_ref, error_ref, after_ref, keep_ref, send_ref, copy_ref, pieces, total
+):
     step = pl.program_id(0)
     count, own = basis_ref.shape[0], error_ref.shape[0]
     size = partial_ref.shape[0]
@@ -185,6 +198,7 @@
         for index, piece in enumerate(pieces_of(basis_ref[...])):
             pieces[index * count : (index + 1) * count, :] = piece
 
+    copy_ref[...] = partial_ref[...]
     three = lax.dot_general(pieces[...], partial_ref[...], across, preferred_element_type=jnp.float32)
     total[:, span(step, size)] = three[:count] + (three[count : 2 * count] + three[2 * count :])
 
@@ -217,11 +231,12 @@
             pl.BlockSpec(error.shape, fixed, pipeline_mode=ONCE),
             ANY,
         ],
-        out_specs=[pl.BlockSpec((count // 2, rows), fixed)] * 2,
-        out_shape=[shape(count // 2, rows)] * 2,
+        out_specs=[pl.BlockSpec((count // 2, rows), fixed)] * 2
+        + [pl.BlockSpec((size, width), lambda k: (k, 0))],
+        out_shape=[shape(count // 2, rows)] * 2 + [shape(rows, width, dtype=partial.dtype)],
         scratch_shapes=[pltpu.VMEM((3 * count, width), jnp.bfloat16), pltpu.VMEM((count, rows), jnp.float32)],
         cost_estimate=FREE,
-        compiler_params=limit(12),
+        compiler_params=limit(16),
         name="left_terms",
     )(scalars, partial, basis, error, after)
 
@@ -335,7 +350,10 @@
 
 
 def sum_four(values, along, after):
-    came = [along(values, step) for step in (2, 1, -1)]
+    return sum_came(values, [along(values, step) for step in (2, 1, -1)], after)
+
+
+def sum_came(values, came, after):
     outs = [shape(*values.shape)]
     return run(add_four_kernel, outs, None, [values, *came], after, "add_four", room=1)[0]
 
@@ -360,20 +378,21 @@
     return run(add_four_kernel, outs[:1], None, [parts[0], *came], parts[0], "add_four", room=1)[0]
 
 
-def join_kernel(scalar_ref, *refs):
-    x, size = scalar_ref[2], refs[0].shape[1]
-    for index, ref in enumerate(refs[:-1]):
-        refs[-1][:, span(lax.rem(x + index, SIDE), size)] = ref[...]
-
-
-def gather_x(scalars, values, after):
-    came = [along_x(values, -1), along_x(values, 2), along_x(values, 1)]
-    outs = [shape(values.shape[0], SIDE * values.shape[1])]
-    return run(join_kernel, outs, scalars, [values, *came], after, "join")[0]
+def join_two_kernel(a_ref, b_ref, out_ref):
+    size = a_ref.shape[1]
+    out_ref[:, :size] = a_ref[...]
+    out_ref[:, size:] = b_ref[...]
+
+
+def join_four_kernel(scalar_ref, mine_ref, came_ref, out_ref):
+    x, size = scalar_ref[2], mine_ref.shape[1] // 2
+    for ref, masks in ((mine_ref, (0, 3)), (came_ref, (1, 2))):
+        for index, mask in enumerate(masks):
+            out_ref[:, span(x ^ mask, size)] = ref[:, index * size : (index + 1) * size]
 
 
 def finish_kernel(replicas, scalar_ref, mine_ref, other_ref, phat_ref, error_ref, *refs):
-    kept_ref, up_ref, down_ref, grad_ref, next_ref, basis_ref = refs
+    kept_ref, up_ref, down_ref, grad_ref, rest_ref, basis_ref = refs
     shard, core = scalar_ref[0], scalar_ref[1]
     own, width = error_ref.shape
     right = jnp.concatenate(ordered(core, mine_ref[:, :width], other_ref[:, :width]), axis=0)
@@ -386,8 +405,34 @@
         preferred_element_type=jnp.float32,
     ) * (1.0 / replicas)
     grad_ref[...] = approx.astype(jnp.bfloat16)
-    merged = error_ref[...] + (kept_ref[...] + (up_ref[...] + down_ref[...]))
-    next_ref[...] = merged - approx
+    depth = own // 2
+    for rows, came_ref in ((slice(0, depth), down_ref), (slice(depth, own), up_ref)):
+        rest_ref[rows, :] = (error_ref[rows, :] + (kept_ref[rows, :] + came_ref[...])) - approx[rows, :]
+
+
+def last_kernel(rest_ref, up_ref, down_ref, out_ref):
+    early = pl.program_id(0) == 0
+    out_ref[...] = rest_ref[...] + jnp.where(early, up_ref[...], down_ref[...])
+
+
+def last_sum(rest, up, down):
+    rows, width = rest.shape
+    depth = rows // SIDE
+    whole = pl.BlockSpec((depth, width), lambda h, i: (2 * h + i, 0))
+    return pl.pallas_call(
+        last_kernel,
+        grid=(2, 2),
+        in_specs=[
+            whole,
+            pl.BlockSpec((depth, width), lambda h, i: (jnp.where(h == 0, i, 1), 0)),
+            pl.BlockSpec((depth, width), lambda h, i: (jnp.where(h == 0, 0, i), 0)),
+        ],
+        out_specs=whole,
+        out_shape=shape(rows, width),
+        cost_estimate=FREE,
+        compiler_params=limit(4),
+        name="last_sum",
+    )(rest, up, down)
 
 
 def shards(partials, error, basis):
@@ -404,11 +449,12 @@
     near = jnp.arange(SIDE)
     coords = jnp.concatenate([(first + near) % SIDE, (second + near) % SIDE, core[None]])
     coords = coords.astype(jnp.int32)
+    large = in_hbm(partial.reshape(SIDE, SIDE, 2, own // 2, width))
+
+    sent1 = combine(large, coords, [(2, 0, []), (2, 1, [])], scalars)
+    came1 = [along_first(sent1[0], 1), along_first(sent1[1], -1)]
+    keep, send, partial = left_terms(scalars, in_hbm(partial), basis, error, sent1[0])
     blocks = partial.reshape(SIDE, SIDE, 4, own // 4, width)
-
-    sent1 = combine(blocks, coords, [(2, 0, []), (2, 1, [])], scalars)
-    came1 = [along_first(sent1[0], 1), along_first(sent1[1], -1)]
-    keep, send = left_terms(scalars, partial, basis, error, sent1[0])
     part = add([keep, other_core(send)], keep)
     sent2 = combine(blocks, coords, [(1, 1, []), (3, 0, [])], part)
     part = sum_four(part, along_x, sent2[0])
@@ -432,28 +478,34 @@
     held = combine(blocks, coords, [(0, 0, [came2[1]]), (0, 1, [came2[0]])], send)
     part = scatter_x(scalars, keep, other_core(send), held[0])
     part = sum_four(part, along_second, part)
-    up, down, *kept = turn(coords, [(held[0], came3[0]), (held[1], came3[1])], part)
+    came = [along_first(part, step) for step in (2, 1, -1)]
+    up, down, up_local, down_local, kept_up, kept_down, kept = turn(
+        coords, [(held[0], came3[0]), (held[1], came3[1])], came
+    )
     came4 = [along_second(up, 1), along_second(down, -1)]
-    part = sum_four(part, along_first, part)
-    sent5 = run(
+    came5 = [along_second(up_local, 1), along_second(down_local, -1)]
+    part = sum_came(part, came, kept)
+    pair = run(join_two_kernel, [shape(count // 2, 2 * part.shape[1])], None, [part, pair_x(part, 3)], part, "join", room=1)[0]
+    sent6 = run(
         ring_add_kernel,
-        [shape(own, width)] * 2,
+        [shape(own // 2, width)] * 2,
         None,
-        [kept[0], came4[0], kept[1], came4[1]],
-        part,
+        [kept_up, came4[0], kept_down, came4[1]],
+        pair,
         "ring_add",
     )
-    came5 = [along_second(sent5[0], 1), along_second(sent5[1], -1)]
-    part = gather_x(scalars, part, sent5[0])
-    grad, following, right = run(
+    came6 = [along_second(sent6[0], 1), along_second(sent6[1], -1)]
+    outs = [shape(count // 2, 2 * pair.shape[1])]
+    part = run(join_four_kernel, outs, scalars, [pair, pair_x(pair, 1)], sent6[0], "join")[0]
+    grad, rest, right = run(
         functools.partial(finish_kernel, replicas),
         [shape(own, width, dtype=jnp.bfloat16), shape(own, width), shape(count, width)],
         scalars,
-        [part, other_core(part), phat, error, kept[2], *came5],
+        [part, other_core(part), phat, error, kept, *came5],
         part,
         "finish",
     )
-    return grad, following[None], right.T
+    return grad, last_sum(rest, *came6)[None], right.T
 
 
 def solution(mesh):

time: 117 us -> 111 us (0.949)
  waiting for transfers between devices: 36.2 us -> 25.5 us
  Pallas kernels: 21.4 us -> 27.5 us
  local copies, waits for them, and re-layouts: 3.32 us -> 0.01 us
  starting transfers between devices: 54 us -> 57 us
    ppermute x35 -> x36, waiting for transfers between devices: 36.2 us -> 25.5 us  [moved(): lax.ppermute(values, BOTH, [(place(*spot), place(*route(*spot))) for spot...]
    unnamed x8 -> x4, local copies, waits for them, and re-layouts: 3.32 us -> 0.01 us
    ppermute x35 -> x36, starting transfers between devices: 54 us -> 57 us  [moved(): lax.ppermute(values, BOTH, [(place(*spot), place(*route(*spot))) for spot...]
    pallas_call x1, Pallas kernels: 4.9 us -> 7.26 us  [left_terms(): pl.pallas_call(left_kernel, grid=(SIDE,), in_specs=[SCALARS, pl.BlockSpec...]
    pallas_call x4, Pallas kernels: 4.22 us -> 6.41 us  [combine(): pl.pallas_call(functools.partial(combine_kernel, arity), grid_spec=pltpu....]
    pallas_call x0 -> x1, Pallas kernels: none -> 1.6 us  [last_sum(): pl.pallas_call(last_kernel, grid=(2, 2), in_specs=[whole, pl.BlockSpec((d...]
    pallas_call x14 -> x16, Pallas kernels: 8.78 us -> 8.73 us  [run(): pl.pallas_call(body, in_specs=[SCALARS] * len(scalars) + [WHOLE] * len(op...]
  transfers between devices with their start and end apart: 35 -> 36, of which waited for: 20 -> 18; matrix products, arithmetic and copies ran while one was open for 0% -> 0% of each run, Pallas kernels for 14% -> 20%
where the time goes in v4:
time: 111 us
  starting transfers between devices  57 us (51%)
  Pallas kernels  27.5 us (25%)
  waiting for transfers between devices  25.5 us (23%)
    ppermute x36, starting transfers between devices, moved(): lax.ppermute(values, BOTH, [(place(*spot), place(*route(*spot))) for spot...  57 us
    ppermute x36, waiting for transfers between devices, moved(): lax.ppermute(values, BOTH, [(place(*spot), place(*route(*spot))) for spot...  25.5 us
    pallas_call x16, Pallas kernels, run(): pl.pallas_call(body, in_specs=[SCALARS] * len(scalars) + [WHOLE] * len(op...  8.73 us
    pallas_call x1, Pallas kernels, left_terms(): pl.pallas_call(left_kernel, grid=(SIDE,), in_specs=[SCALARS, pl.BlockSpec...  7.26 us
    pallas_call x4, Pallas kernels, combine(): pl.pallas_call(functools.partial(combine_kernel, arity), grid_spec=pltpu....  6.41 us
    pallas_call x1, Pallas kernels, right_terms(): pl.pallas_call(right_kernel, grid=(SIDE,), in_specs=[SCALARS, pl.BlockSpe...  3.46 us
  transfers between devices with their start and end apart: 36, of which 18 were waited for; matrix products, arithmetic and copies ran while one was open for 0% of the time, Pallas kernels for 20%

profile of v4, /device:TPU:1, one launch (start us, length us, event | category | flops | bytes accessed | tf_op | source)
XLA Modules:
  0.0 111.1 jit_solution(8206751109498254735)
XLA Ops:
  0.7 0.1 pad_add_fusion.1.coords_ref.refs_0_
  0.9 3.2 %combine.4 = (f32[4,32,3968]{2,1,0:T(8,128)S(1)}, f32[4,32,3968]{2,1,0:T(8,128)S(1)}) custom-call(s32[9]{0:T(128)S(1)} %pad_add_fusion.1.coords_ref.refs_0_, bf16[4,4,2,32,3968]{4,3,2,1,0:T(8,128)(2,1)} %bitcast.20, bf16[4,4,2,32,3968]{4,3,2,1,0:T(8,128)(2,1)} %bitcast.21, s32[3]{0:T(128)S(1)} %pad_add_fusion.refs_2_.scalar_ref.refs_0_), custom_call_target="tpu_custom_call" | custom-call | tf_op jit(solution)/shard_map/combine/pallas_call | solution.py:124
  4.1 2.2 %collective-permute-start.7 = (f32[4,32,3968]{2,1,0:T(8,128)S(1)}, f32[4,32,3968]{2,1,0:T(8,128)S(1)}, u32[]{:S(2)}, u32[]{:S(2)}) collective-permute-start(f32[4,32,3968]{2,1,0:T(8,128)S(1)} %get-tuple-element.38.after_ref), channel_id=1, source_target_pairs={{0,4},{1,5},{2,6},{3,7},{4,8},{5,9},{6,10},{7,11},{8,12},{9,13},{1... | collective-permute-start | bytes 6094856 | tf_op jit(solution)/shard_map/ppermute | solution.py:37
  6.3 1.5 %collective-permute-start.8 = (f32[4,32,3968]{2,1,0:T(8,128)S(1)}, f32[4,32,3968]{2,1,0:T(8,128)S(1)}, u32[]{:S(2)}, u32[]{:S(2)}) collective-permute-start(f32[4,32,3968]{2,1,0:T(8,128)S(1)} %get-tuple-element.45), channel_id=1, source_target_pairs={{0,12},{1,13},{2,14},{3,15},{4,0},{5,1},{6,2},{7,3},{8,4},{9,5},{1... | collective-permute-start | bytes 6094856 | tf_op jit(solution)/shard_map/ppermute | solution.py:37
  7.8 7.3 %left_terms.1 = (f32[16,1024]{1,0:T(8,128)S(1)}, f32[16,1024]{1,0:T(8,128)S(1)}, bf16[1024,3968]{1,0:T(8,128)(2,1)S(1)}) custom-call(s32[3]{0:T(128)S(1)} %pad_add_fusion.refs_2_.scalar_ref.refs_0_, bf16[1024,3968]{1,0:T(8,128)(2,1)} %bitcast.22, f32[32,3968]{1,0:T(8,128)S(1)} %bitcast.19, f32[64,3968]{1,0:T(8,128)S(1)} %bitcast.16, ...), custom_call_target="tpu_custom_call" | custom-call | tf_op jit(solution)/shard_map/left_terms/pallas_call | solution.py:224
  15.0 2.1 %collective-permute-start = (f32[16,1024]{1,0:T(8,128)S(1)}, f32[16,1024]{1,0:T(8,128)S(1)}, u32[]{:S(2)}, u32[]{:S(2)}) collective-permute-start(f32[16,1024]{1,0:T(8,128)S(1)} %get-tuple-element.40), channel_id=1, source_target_pairs={{0,16},{1,17},{2,18},{3,19},{4,20},{5,21},{6,22},{7,23},{8,24},{9,... | collective-permute-start | bytes 196616 | tf_op jit(solution)/shard_map/ppermute | solution.py:37
  17.1 0.9 collective-permute-done.refs_1_
  18.0 2.8 %collective-permute-start.1 = (f32[16,1024]{1,0:T(8,128)S(1)}, f32[16,1024]{1,0:T(8,128)S(1)}, u32[]{:S(2)}, u32[]{:S(2)}) collective-permute-start(f32[16,1024]{1,0:T(8,128)S(1)} %add.56.refs_2_.refs_0_), channel_id=1, source_target_pairs={{0,64},{1,65},{2,66},{3,67},{4,68},{5,69},{6,70},{7,71},{8,72},{9,... | collective-permute-start | bytes 196616 | tf_op jit(solution)/shard_map/ppermute | solution.py:37
  20.8 0.3 collective-permute-start.2
  21.2 2.4 %collective-permute-start.3 = (f32[16,1024]{1,0:T(8,128)S(1)}, f32[16,1024]{1,0:T(8,128)S(1)}, u32[]{:S(2)}, u32[]{:S(2)}) collective-permute-start(f32[16,1024]{1,0:T(8,128)S(1)} %add.56.refs_2_.refs_0_), channel_id=1, source_target_pairs={{0,96},{1,97},{2,98},{3,99},{4,100},{5,101},{6,102},{7,103},{8,104... | collective-permute-start | bytes 196616 | tf_op jit(solution)/shard_map/ppermute | solution.py:37
  23.5 1.0 combine.5
  24.5 0.9 collective-permute-done.2.refs_2_
  25.5 0.1 collective-permute-start.4
  25.6 2.8 %collective-permute-start.14 = (f32[4,32,3968]{2,1,0:T(8,128)S(1)}, f32[4,32,3968]{2,1,0:T(8,128)S(1)}, u32[]{:S(2)}, u32[]{:S(2)}) collective-permute-start(f32[4,32,3968]{2,1,0:T(8,128)S(1)} %get-tuple-element.53), channel_id=1, source_target_pairs={{0,12},{1,13},{2,14},{3,15},{4,0},{5,1},{6,2},{7,3},{8,4},{9,5},{1... | collective-permute-start | bytes 6094856 | tf_op jit(solution)/shard_map/ppermute | solution.py:37
  28.4 1.3 %collective-permute-done.4.refs_1_ = f32[16,1024]{1,0:T(8,128)S(1)} collective-permute-done((f32[16,1024]{1,0:T(8,128)S(1)}, f32[16,1024]{1,0:T(8,128)S(1)}, u32[]{:S(2)}, u32[]{:S(2)}) %collective-permute-start.4) | collective-permute-done | bytes 65568 | tf_op jit(solution)/shard_map/ppermute | solution.py:37
  29.8 2.2 %collective-permute-start.5 = (f32[16,1024]{1,0:T(8,128)S(1)}, f32[16,1024]{1,0:T(8,128)S(1)}, u32[]{:S(2)}, u32[]{:S(2)}) collective-permute-start(f32[16,1024]{1,0:T(8,128)S(1)} %add.57.refs_0_.refs_2_), channel_id=1, source_target_pairs={{0,3},{1,2},{2,1},{3,0},{4,7},{5,6},{6,5},{7,4},{8,11},{9,10},{10,... | collective-permute-start | bytes 196616 | tf_op jit(solution)/shard_map/ppermute | solution.py:37
  32.0 2.2 %collective-permute-done.5.refs_1_ = f32[16,1024]{1,0:T(8,128)S(1)} collective-permute-done((f32[16,1024]{1,0:T(8,128)S(1)}, f32[16,1024]{1,0:T(8,128)S(1)}, u32[]{:S(2)}, u32[]{:S(2)}) %collective-permute-start.5) | collective-permute-done | bytes 65568 | tf_op jit(solution)/shard_map/ppermute | solution.py:37
  34.2 4.3 %collective-permute-start.6 = (f32[16,1024]{1,0:T(8,128)S(1)}, f32[16,1024]{1,0:T(8,128)S(1)}, u32[]{:S(2)}, u32[]{:S(2)}) collective-permute-start(f32[16,1024]{1,0:T(8,128)S(1)} %add.58.refs_4_), channel_id=1, source_target_pairs={{0,16},{1,17},{2,18},{3,19},{4,20},{5,21},{6,22},{7,23},{8,24},{9,... | collective-permute-start | bytes 196616 | tf_op jit(solution)/shard_map/ppermute | solution.py:37
  38.5 1.1 combine.6
  39.7 2.7 %collective-permute-start.11 = (f32[16,1024]{1,0:T(8,128)S(1)}, f32[16,1024]{1,0:T(8,128)S(1)}, u32[]{:S(2)}, u32[]{:S(2)}) collective-permute-start(f32[16,1024]{1,0:T(8,128)S(1)} %gate.4.refs_0_.refs_4_), channel_id=1, source_target_pairs={{0,3},{1,0},{2,1},{3,2},{4,7},{5,4},{6,5},{7,6},{8,11},{9,8},{10,9... | collective-permute-start | bytes 196616 | tf_op jit(solution)/shard_map/ppermute | solution.py:37
  42.4 0.6 collective-permute-start.9
  43.0 2.1 %collective-permute-done.10.refs_2_ = f32[16,1024]{1,0:T(8,128)S(1)} collective-permute-done((f32[16,1024]{1,0:T(8,128)S(1)}, f32[16,1024]{1,0:T(8,128)S(1)}, u32[]{:S(2)}, u32[]{:S(2)}) %collective-permute-start.10) | collective-permute-done | bytes 65568 | tf_op jit(solution)/shard_map/ppermute | solution.py:37
  45.1 3.0 %collective-permute-done.9.refs_1_ = f32[16,1024]{1,0:T(8,128)S(1)} collective-permute-done((f32[16,1024]{1,0:T(8,128)S(1)}, f32[16,1024]{1,0:T(8,128)S(1)}, u32[]{:S(2)}, u32[]{:S(2)}) %collective-permute-start.9) | collective-permute-done | bytes 65568 | tf_op jit(solution)/shard_map/ppermute | solution.py:37
  48.2 2.7 %collective-permute-start.26 = (f32[4,32,3968]{2,1,0:T(8,128)S(1)}, f32[4,32,3968]{2,1,0:T(8,128)S(1)}, u32[]{:S(2)}, u32[]{:S(2)}) collective-permute-start(f32[4,32,3968]{2,1,0:T(8,128)S(1)} %get-tuple-element.60), channel_id=1, source_target_pairs={{0,12},{1,13},{2,14},{3,15},{4,0},{5,1},{6,2},{7,3},{8,4},{9,5},{1... | collective-permute-start | bytes 6094856 | tf_op jit(solution)/shard_map/ppermute | solution.py:37
  50.9 2.0 %collective-permute-start.12 = (f32[16,1024]{1,0:T(8,128)S(1)}, f32[16,1024]{1,0:T(8,128)S(1)}, u32[]{:S(2)}, u32[]{:S(2)}) collective-permute-start(f32[16,1024]{1,0:T(8,128)S(1)} %add_four.6.refs_2_.refs_1_), channel_id=1, source_target_pairs={{0,16},{1,17},{2,18},{3,19},{4,20},{5,21},{6,22},{7,23},{8,24},{9,... | collective-permute-start | bytes 196616 | tf_op jit(solution)/shard_map/ppermute | solution.py:37
  52.9 0.9 collective-permute-done.12.refs_2_
  53.8 3.9 %orthonormal.1 = (f32[32,1024]{1,0:T(8,128)S(1)}, bf16[96,1024]{1,0:T(8,128)(2,1)S(1)}) custom-call(s32[3]{0:T(128)S(1)} %pad_add_fusion.refs_2_.scalar_ref.refs_0_, f32[16,1024]{1,0:T(8,128)S(1)} %add_four.6.refs_2_.refs_1_, f32[16,1024]{1,0:T(8,128)S(1)} %collective-permute-done.12.refs_2_, f32[4,32,3968]{2,1,0:T(8,128)S(1)} %get-tuple-element.48.refs_3_), custom_call_target="tpu_custom_call" | custom-call | tf_op jit(solution)/shard_map/orthonormal/pallas_call | solution.py:77
  57.7 3.5 %right_terms.1 = (f32[16,4096]{1,0:T(8,128)S(1)}, f32[16,4096]{1,0:T(8,128)S(1)}) custom-call(s32[3]{0:T(128)S(1)} %pad_add_fusion.refs_2_.scalar_ref.refs_0_, bf16[96,1024]{1,0:T(8,128)(2,1)S(1)} %get-tuple-element.49.pieces_ref, bf16[1024,3968]{1,0:T(8,128)(2,1)S(1)} %get-tuple-element.41.partial_ref, ...), custom_call_target="tpu_custom_call" | custom-call | tf_op jit(solution)/shard_map/right_terms/pallas_call | solution.py:306
  61.2 0.4 collective-permute-start.13
  61.6 1.1 combine.7
  62.8 0.6 add_cut.1
  63.4 1.3 %collective-permute-start.16 = (f32[16,1024]{1,0:T(8,128)S(1)}, f32[16,1024]{1,0:T(8,128)S(1)}, u32[]{:S(2)}, u32[]{:S(2)}) collective-permute-start(f32[16,1024]{1,0:T(8,128)S(1)} %get-tuple-element.56), channel_id=1, source_target_pairs={{0,64},{1,65},{2,66},{3,67},{4,68},{5,69},{6,70},{7,71},{8,72},{9,... | collective-permute-start | bytes 196616 | tf_op jit(solution)/shard_map/ppermute | solution.py:37
  64.7 2.3 %collective-permute-start.17 = (f32[16,1024]{1,0:T(8,128)S(1)}, f32[16,1024]{1,0:T(8,128)S(1)}, u32[]{:S(2)}, u32[]{:S(2)}) collective-permute-start(f32[16,1024]{1,0:T(8,128)S(1)} %get-tuple-element.57), channel_id=1, source_target_pairs={{0,32},{1,33},{2,34},{3,35},{4,36},{5,37},{6,38},{7,39},{8,40},{9,... | collective-permute-start | bytes 196616 | tf_op jit(solution)/shard_map/ppermute | solution.py:37
  67.0 0.3 collective-permute-start.18
  67.3 0.8 collective-permute-done.16.refs_1_
  68.1 2.0 %collective-permute-done.17.refs_2_ = f32[16,1024]{1,0:T(8,128)S(1)} collective-permute-done((f32[16,1024]{1,0:T(8,128)S(1)}, f32[16,1024]{1,0:T(8,128)S(1)}, u32[]{:S(2)}, u32[]{:S(2)}) %collective-permute-start.17) | collective-permute-done | bytes 65568 | tf_op jit(solution)/shard_map/ppermute | solution.py:37
  70.1 0.4 collective-permute-done.18.refs_3_
  70.5 0.6 collective-permute-start.19
  71.1 0.7 collective-permute-start.20
  71.9 1.9 %collective-permute-start.21 = (f32[16,1024]{1,0:T(8,128)S(1)}, f32[16,1024]{1,0:T(8,128)S(1)}, u32[]{:S(2)}, u32[]{:S(2)}) collective-permute-start(f32[16,1024]{1,0:T(8,128)S(1)} %add_four.7.refs_0_.refs_4_), channel_id=1, source_target_pairs={{0,3},{1,0},{2,1},{3,2},{4,7},{5,4},{6,5},{7,6},{8,11},{9,8},{10,9... | collective-permute-start | bytes 196616 | tf_op jit(solution)/shard_map/ppermute | solution.py:37
  73.8 2.2 %collective-permute-done.19.refs_1_ = f32[16,1024]{1,0:T(8,128)S(1)} collective-permute-done((f32[16,1024]{1,0:T(8,128)S(1)}, f32[16,1024]{1,0:T(8,128)S(1)}, u32[]{:S(2)}, u32[]{:S(2)}) %collective-permute-start.19) | collective-permute-done | bytes 65568 | tf_op jit(solution)/shard_map/ppermute | solution.py:37
  76.0 1.2 %collective-permute-done.20.refs_2_ = f32[16,1024]{1,0:T(8,128)S(1)} collective-permute-done((f32[16,1024]{1,0:T(8,128)S(1)}, f32[16,1024]{1,0:T(8,128)S(1)}, u32[]{:S(2)}, u32[]{:S(2)}) %collective-permute-start.20) | collective-permute-done | bytes 65568 | tf_op jit(solution)/shard_map/ppermute | solution.py:37
  77.1 0.9 collective-permute-start.22
  78.0 1.1 %collective-permute-start.23 = (f32[16,1024]{1,0:T(8,128)S(1)}, f32[16,1024]{1,0:T(8,128)S(1)}, u32[]{:S(2)}, u32[]{:S(2)}) collective-permute-start(f32[16,1024]{1,0:T(8,128)S(1)} %add_four.8.refs_0_), channel_id=1, source_target_pairs={{0,4},{1,5},{2,6},{3,7},{4,8},{5,9},{6,10},{7,11},{8,12},{9,13},{1... | collective-permute-start | bytes 196616 | tf_op jit(solution)/shard_map/ppermute | solution.py:37
  79.2 1.5 %collective-permute-start.24 = (f32[16,1024]{1,0:T(8,128)S(1)}, f32[16,1024]{1,0:T(8,128)S(1)}, u32[]{:S(2)}, u32[]{:S(2)}) collective-permute-start(f32[16,1024]{1,0:T(8,128)S(1)} %add_four.8.refs_0_), channel_id=1, source_target_pairs={{0,12},{1,13},{2,14},{3,15},{4,0},{5,1},{6,2},{7,3},{8,4},{9,5},{1... | collective-permute-start | bytes 196616 | tf_op jit(solution)/shard_map/ppermute | solution.py:37
  80.7 1.2 %collective-permute-done.22.refs_5_.refs_1_ = f32[16,1024]{1,0:T(8,128)S(1)} collective-permute-done((f32[16,1024]{1,0:T(8,128)S(1)}, f32[16,1024]{1,0:T(8,128)S(1)}, u32[]{:S(2)}, u32[]{:S(2)}) %collective-permute-start.22) | collective-permute-done | bytes 65568 | tf_op jit(solution)/shard_map/ppermute | solution.py:37
  81.9 0.7 collective-permute-done.23.refs_6_.refs_2_
  82.6 0.7 turn_first.1
  83.2 0.3 collective-permute-start.29
  83.5 2.4 %collective-permute-start.30 = (f32[32,3968]{1,0:T(8,128)S(1)}, f32[32,3968]{1,0:T(8,128)S(1)}, u32[]{:S(2)}, u32[]{:S(2)}) collective-permute-start(f32[32,3968]{1,0:T(8,128)S(1)} %get-tuple-element.65), channel_id=1, source_target_pairs={{0,3},{1,0},{2,1},{3,2},{4,7},{5,4},{6,5},{7,6},{8,11},{9,8},{10,9... | collective-permute-start | bytes 1523720 | tf_op jit(solution)/shard_map/ppermute | solution.py:37
  86.0 0.9 turn_rest.1
  86.8 2.4 %collective-permute-start.27 = (f32[16,1024]{1,0:T(8,128)S(1)}, f32[16,1024]{1,0:T(8,128)S(1)}, u32[]{:S(2)}, u32[]{:S(2)}) collective-permute-start(f32[16,1024]{1,0:T(8,128)S(1)} %add_four.9.refs_0_.refs_2_), channel_id=1, source_target_pairs={{0,96},{1,97},{2,98},{3,99},{4,100},{5,101},{6,102},{7,103},{8,104... | collective-permute-start | bytes 196616 | tf_op jit(solution)/shard_map/ppermute | solution.py:37
  89.3 2.7 %collective-permute-start.33 = (f32[32,3968]{1,0:T(8,128)S(1)}, f32[32,3968]{1,0:T(8,128)S(1)}, u32[]{:S(2)}, u32[]{:S(2)}) collective-permute-start(f32[32,3968]{1,0:T(8,128)S(1)} %get-tuple-element.68), channel_id=1, source_target_pairs={{0,3},{1,0},{2,1},{3,2},{4,7},{5,4},{6,5},{7,6},{8,11},{9,8},{10,9... | collective-permute-start | bytes 1523720 | tf_op jit(solution)/shard_map/ppermute | solution.py:37
  92.0 0.7 collective-permute-done.29.refs_1_
  92.6 0.1 ring_add.1
  92.8 0.3 collective-permute-start.34
  93.1 2.5 %collective-permute-start.35 = (f32[32,3968]{1,0:T(8,128)S(1)}, f32[32,3968]{1,0:T(8,128)S(1)}, u32[]{:S(2)}, u32[]{:S(2)}) collective-permute-start(f32[32,3968]{1,0:T(8,128)S(1)} %get-tuple-element.71), channel_id=1, source_target_pairs={{0,3},{1,0},{2,1},{3,2},{4,7},{5,4},{6,5},{7,6},{8,11},{9,8},{10,9... | collective-permute-start | bytes 1523720 | tf_op jit(solution)/shard_map/ppermute | solution.py:37
  95.6 0.2 collective-permute-start.28
  95.7 3.9 %collective-permute-done.28.refs_2_ = f32[16,2048]{1,0:T(8,128)S(1)} collective-permute-done((f32[16,2048]{1,0:T(8,128)S(1)}, f32[16,2048]{1,0:T(8,128)S(1)}, u32[]{:S(2)}, u32[]{:S(2)}) %collective-permute-start.28) | collective-permute-done | bytes 131104 | tf_op jit(solution)/shard_map/ppermute | solution.py:37
  99.7 0.6 join.3.refs_1_.refs_8_
  100.3 6.1 %collective-permute-start.31 = (f32[16,4096]{1,0:T(8,128)S(1)}, f32[16,4096]{1,0:T(8,128)S(1)}, u32[]{:S(2)}, u32[]{:S(2)}) collective-permute-start(f32[16,4096]{1,0:T(8,128)S(1)} %join.3.refs_1_.refs_8_), channel_id=1, source_target_pairs={{0,16},{1,17},{2,18},{3,19},{4,20},{5,21},{6,22},{7,23},{8,24},{9,... | collective-permute-start | bytes 786440 | tf_op jit(solution)/shard_map/ppermute | solution.py:37
  106.4 1.2 %collective-permute-done.31.refs_2_ = f32[16,4096]{1,0:T(8,128)S(1)} collective-permute-done((f32[16,4096]{1,0:T(8,128)S(1)}, f32[16,4096]{1,0:T(8,128)S(1)}, u32[]{:S(2)}, u32[]{:S(2)}) %collective-permute-start.31) | collective-permute-done | bytes 262176 | tf_op jit(solution)/shard_map/ppermute | solution.py:37
  107.6 1.9 %finish.1 = (bf16[64,3968]{1,0:T(8,128)(2,1)}, f32[64,3968]{1,0:T(8,128)S(1)}, f32[32,3968]{1,0:T(8,128)}) custom-call(s32[3]{0:T(128)S(1)} %pad_add_fusion.refs_2_.scalar_ref.refs_0_, f32[16,4096]{1,0:T(8,128)S(1)} %join.3.refs_1_.refs_8_, f32[16,4096]{1,0:T(8,128)S(1)} %collective-permute-done.31.refs_2_, ...), custom_call_target="tpu_custom_call" | custom-call | tf_op jit(solution)/shard_map/finish/pallas_call | solution.py:77
  109.5 1.6 %last_sum.1 = f32[64,3968]{1,0:T(8,128)} custom-call(f32[64,3968]{1,0:T(8,128)S(1)} %get-tuple-element.70.rest_ref, f32[32,3968]{1,0:T(8,128)S(1)} %collective-permute-done.34.up_ref, f32[32,3968]{1,0:T(8,128)S(1)} %collective-permute-done.35.down_ref), custom_call_target="tpu_custom_call" | custom-call | tf_op jit(solution)/shard_map/last_sum/pallas_call | solution.py:422
  (41 shorter events, 0.5 us)
Async XLA Ops:
  0.9 6.9 %copy-start = (f32[1,64,3968]{2,1,0:T(8,128)S(1)}, f32[1,64,3968]{2,1,0:T(8,128)}, u32[]{:S(2)}) copy-start(f32[1,64,3968]{2,1,0:T(8,128)} %param.4) | copy-start | bytes 3047428
  0.9 6.9 %copy-start.1 = (f32[3968,32]{0,1:T(8,128)S(1)}, f32[3968,32]{0,1:T(8,128)}, u32[]{:S(2)}) copy-start(f32[3968,32]{0,1:T(8,128)} %param.5) | copy-start | bytes 1523716
  4.1 34.5 %collective-permute-start.7 = (f32[4,32,3968]{2,1,0:T(8,128)S(1)}, f32[4,32,3968]{2,1,0:T(8,128)S(1)}, u32[]{:S(2)}, u32[]{:S(2)}) collective-permute-start(f32[4,32,3968]{2,1,0:T(8,128)S(1)} %get-tuple-element.38.after_ref), channel_id=1, source_target_pairs={{0,4},{1,5},{2,6},{3,7},{4,8},{5,9},{6,10},{7,11},{8,12},{9,13},{1... | collective-permute-start | bytes 6094856 | tf_op jit(solution)/shard_map/ppermute | solution.py:37
  6.3 32.3 %collective-permute-start.8 = (f32[4,32,3968]{2,1,0:T(8,128)S(1)}, f32[4,32,3968]{2,1,0:T(8,128)S(1)}, u32[]{:S(2)}, u32[]{:S(2)}) collective-permute-start(f32[4,32,3968]{2,1,0:T(8,128)S(1)} %get-tuple-element.45), channel_id=1, source_target_pairs={{0,12},{1,13},{2,14},{3,15},{4,0},{5,1},{6,2},{7,3},{8,4},{9,5},{1... | collective-permute-start | bytes 6094856 | tf_op jit(solution)/shard_map/ppermute | solution.py:37
  15.0 3.0 %collective-permute-start = (f32[16,1024]{1,0:T(8,128)S(1)}, f32[16,1024]{1,0:T(8,128)S(1)}, u32[]{:S(2)}, u32[]{:S(2)}) collective-permute-start(f32[16,1024]{1,0:T(8,128)S(1)} %get-tuple-element.40), channel_id=1, source_target_pairs={{0,16},{1,17},{2,18},{3,19},{4,20},{5,21},{6,22},{7,23},{8,24},{9,... | collective-permute-start | bytes 196616 | tf_op jit(solution)/shard_map/ppermute | solution.py:37
  18.0 6.5 %collective-permute-start.1 = (f32[16,1024]{1,0:T(8,128)S(1)}, f32[16,1024]{1,0:T(8,128)S(1)}, u32[]{:S(2)}, u32[]{:S(2)}) collective-permute-start(f32[16,1024]{1,0:T(8,128)S(1)} %add.56.refs_2_.refs_0_), channel_id=1, source_target_pairs={{0,64},{1,65},{2,66},{3,67},{4,68},{5,69},{6,70},{7,71},{8,72},{9,... | collective-permute-start | bytes 196616 | tf_op jit(solution)/shard_map/ppermute | solution.py:37
  20.8 4.6 %collective-permute-start.2 = (f32[16,1024]{1,0:T(8,128)S(1)}, f32[16,1024]{1,0:T(8,128)S(1)}, u32[]{:S(2)}, u32[]{:S(2)}) collective-permute-start(f32[16,1024]{1,0:T(8,128)S(1)} %add.56.refs_2_.refs_0_), channel_id=1, source_target_pairs={{0,32},{1,33},{2,34},{3,35},{4,36},{5,37},{6,38},{7,39},{8,40},{9,... | collective-permute-start | bytes 196616 | tf_op jit(solution)/shard_map/ppermute | solution.py:37
  21.2 4.3 %collective-permute-start.3 = (f32[16,1024]{1,0:T(8,128)S(1)}, f32[16,1024]{1,0:T(8,128)S(1)}, u32[]{:S(2)}, u32[]{:S(2)}) collective-permute-start(f32[16,1024]{1,0:T(8,128)S(1)} %add.56.refs_2_.refs_0_), channel_id=1, source_target_pairs={{0,96},{1,97},{2,98},{3,99},{4,100},{5,101},{6,102},{7,103},{8,104... | collective-permute-start | bytes 196616 | tf_op jit(solution)/shard_map/ppermute | solution.py:37
  25.5 4.3 %collective-permute-start.4 = (f32[16,1024]{1,0:T(8,128)S(1)}, f32[16,1024]{1,0:T(8,128)S(1)}, u32[]{:S(2)}, u32[]{:S(2)}) collective-permute-start(f32[16,1024]{1,0:T(8,128)S(1)} %add_four.5.refs_2_.refs_0_), channel_id=1, source_target_pairs={{0,1},{1,0},{2,3},{3,2},{4,5},{5,4},{6,7},{7,6},{8,9},{9,8},{10,11... | collective-permute-start | bytes 196616 | tf_op jit(solution)/shard_map/ppermute | solution.py:37
  25.6 36.0 %collective-permute-start.14 = (f32[4,32,3968]{2,1,0:T(8,128)S(1)}, f32[4,32,3968]{2,1,0:T(8,128)S(1)}, u32[]{:S(2)}, u32[]{:S(2)}) collective-permute-start(f32[4,32,3968]{2,1,0:T(8,128)S(1)} %get-tuple-element.53), channel_id=1, source_target_pairs={{0,12},{1,13},{2,14},{3,15},{4,0},{5,1},{6,2},{7,3},{8,4},{9,5},{1... | collective-permute-start | bytes 6094856 | tf_op jit(solution)/shard_map/ppermute | solution.py:37
  28.4 33.2 %collective-permute-start.15 = (f32[4,32,3968]{2,1,0:T(8,128)S(1)}, f32[4,32,3968]{2,1,0:T(8,128)S(1)}, u32[]{:S(2)}, u32[]{:S(2)}) collective-permute-start(f32[4,32,3968]{2,1,0:T(8,128)S(1)} %get-tuple-element.44.refs_2_), channel_id=1, source_target_pairs={{0,4},{1,5},{2,6},{3,7},{4,8},{5,9},{6,10},{7,11},{8,12},{9,13},{1... | collective-permute-start | bytes 6094856 | tf_op jit(solution)/shard_map/ppermute | solution.py:37
  29.8 4.4 %collective-permute-start.5 = (f32[16,1024]{1,0:T(8,128)S(1)}, f32[16,1024]{1,0:T(8,128)S(1)}, u32[]{:S(2)}, u32[]{:S(2)}) collective-permute-start(f32[16,1024]{1,0:T(8,128)S(1)} %add.57.refs_0_.refs_2_), channel_id=1, source_target_pairs={{0,3},{1,2},{2,1},{3,0},{4,7},{5,6},{6,5},{7,4},{8,11},{9,10},{10,... | collective-permute-start | bytes 196616 | tf_op jit(solution)/shard_map/ppermute | solution.py:37
  34.2 5.5 %collective-permute-start.6 = (f32[16,1024]{1,0:T(8,128)S(1)}, f32[16,1024]{1,0:T(8,128)S(1)}, u32[]{:S(2)}, u32[]{:S(2)}) collective-permute-start(f32[16,1024]{1,0:T(8,128)S(1)} %add.58.refs_4_), channel_id=1, source_target_pairs={{0,16},{1,17},{2,18},{3,19},{4,20},{5,21},{6,22},{7,23},{8,24},{9,... | collective-permute-start | bytes 196616 | tf_op jit(solution)/shard_map/ppermute | solution.py:37
  39.7 5.5 %collective-permute-start.10 = (f32[16,1024]{1,0:T(8,128)S(1)}, f32[16,1024]{1,0:T(8,128)S(1)}, u32[]{:S(2)}, u32[]{:S(2)}) collective-permute-start(f32[16,1024]{1,0:T(8,128)S(1)} %gate.4.refs_0_.refs_4_), channel_id=1, source_target_pairs={{0,1},{1,2},{2,3},{3,0},{4,5},{5,6},{6,7},{7,4},{8,9},{9,10},{10,1... | collective-permute-start | bytes 196616 | tf_op jit(solution)/shard_map/ppermute | solution.py:37
  39.7 5.4 %collective-permute-start.11 = (f32[16,1024]{1,0:T(8,128)S(1)}, f32[16,1024]{1,0:T(8,128)S(1)}, u32[]{:S(2)}, u32[]{:S(2)}) collective-permute-start(f32[16,1024]{1,0:T(8,128)S(1)} %gate.4.refs_0_.refs_4_), channel_id=1, source_target_pairs={{0,3},{1,0},{2,1},{3,2},{4,7},{5,4},{6,5},{7,6},{8,11},{9,8},{10,9... | collective-permute-start | bytes 196616 | tf_op jit(solution)/shard_map/ppermute | solution.py:37
  42.4 5.7 %collective-permute-start.9 = (f32[16,1024]{1,0:T(8,128)S(1)}, f32[16,1024]{1,0:T(8,128)S(1)}, u32[]{:S(2)}, u32[]{:S(2)}) collective-permute-start(f32[16,1024]{1,0:T(8,128)S(1)} %gate.4.refs_0_.refs_4_), channel_id=1, source_target_pairs={{0,2},{1,3},{2,0},{3,1},{4,6},{5,7},{6,4},{7,5},{8,10},{9,11},{10,... | collective-permute-start | bytes 196616 | tf_op jit(solution)/shard_map/ppermute | solution.py:37
  48.1 34.4 %collective-permute-start.25 = (f32[4,32,3968]{2,1,0:T(8,128)S(1)}, f32[4,32,3968]{2,1,0:T(8,128)S(1)}, u32[]{:S(2)}, u32[]{:S(2)}) collective-permute-start(f32[4,32,3968]{2,1,0:T(8,128)S(1)} %get-tuple-element.48.refs_3_), channel_id=1, source_target_pairs={{0,4},{1,5},{2,6},{3,7},{4,8},{5,9},{6,10},{7,11},{8,12},{9,13},{1... | collective-permute-start | bytes 6094856 | tf_op jit(solution)/shard_map/ppermute | solution.py:37
  48.2 34.3 %collective-permute-start.26 = (f32[4,32,3968]{2,1,0:T(8,128)S(1)}, f32[4,32,3968]{2,1,0:T(8,128)S(1)}, u32[]{:S(2)}, u32[]{:S(2)}) collective-permute-start(f32[4,32,3968]{2,1,0:T(8,128)S(1)} %get-tuple-element.60), channel_id=1, source_target_pairs={{0,12},{1,13},{2,14},{3,15},{4,0},{5,1},{6,2},{7,3},{8,4},{9,5},{1... | collective-permute-start | bytes 6094856 | tf_op jit(solution)/shard_map/ppermute | solution.py:37
  50.9 2.9 %collective-permute-start.12 = (f32[16,1024]{1,0:T(8,128)S(1)}, f32[16,1024]{1,0:T(8,128)S(1)}, u32[]{:S(2)}, u32[]{:S(2)}) collective-permute-start(f32[16,1024]{1,0:T(8,128)S(1)} %add_four.6.refs_2_.refs_1_), channel_id=1, source_target_pairs={{0,16},{1,17},{2,18},{3,19},{4,20},{5,21},{6,22},{7,23},{8,24},{9,... | collective-permute-start | bytes 196616 | tf_op jit(solution)/shard_map/ppermute | solution.py:37
  61.2 1.6 %collective-permute-start.13 = (f32[16,4096]{1,0:T(8,128)S(1)}, f32[16,4096]{1,0:T(8,128)S(1)}, u32[]{:S(2)}, u32[]{:S(2)}) collective-permute-start(f32[16,4096]{1,0:T(8,128)S(1)} %get-tuple-element.52.refs_4_), channel_id=1, source_target_pairs={{0,16},{1,17},{2,18},{3,19},{4,20},{5,21},{6,22},{7,23},{8,24},{9,... | collective-permute-start | bytes 786440 | tf_op jit(solution)/shard_map/ppermute | solution.py:37
  63.4 4.7 %collective-permute-start.16 = (f32[16,1024]{1,0:T(8,128)S(1)}, f32[16,1024]{1,0:T(8,128)S(1)}, u32[]{:S(2)}, u32[]{:S(2)}) collective-permute-start(f32[16,1024]{1,0:T(8,128)S(1)} %get-tuple-element.56), channel_id=1, source_target_pairs={{0,64},{1,65},{2,66},{3,67},{4,68},{5,69},{6,70},{7,71},{8,72},{9,... | collective-permute-start | bytes 196616 | tf_op jit(solution)/shard_map/ppermute | solution.py:37
  64.7 5.4 %collective-permute-start.17 = (f32[16,1024]{1,0:T(8,128)S(1)}, f32[16,1024]{1,0:T(8,128)S(1)}, u32[]{:S(2)}, u32[]{:S(2)}) collective-permute-start(f32[16,1024]{1,0:T(8,128)S(1)} %get-tuple-element.57), channel_id=1, source_target_pairs={{0,32},{1,33},{2,34},{3,35},{4,36},{5,37},{6,38},{7,39},{8,40},{9,... | collective-permute-start | bytes 196616 | tf_op jit(solution)/shard_map/ppermute | solution.py:37
  67.0 3.5 %collective-permute-start.18 = (f32[16,1024]{1,0:T(8,128)S(1)}, f32[16,1024]{1,0:T(8,128)S(1)}, u32[]{:S(2)}, u32[]{:S(2)}) collective-permute-start(f32[16,1024]{1,0:T(8,128)S(1)} %get-tuple-element.58), channel_id=1, source_target_pairs={{0,96},{1,97},{2,98},{3,99},{4,100},{5,101},{6,102},{7,103},{8,104... | collective-permute-start | bytes 196616 | tf_op jit(solution)/shard_map/ppermute | solution.py:37
  70.5 5.5 %collective-permute-start.19 = (f32[16,1024]{1,0:T(8,128)S(1)}, f32[16,1024]{1,0:T(8,128)S(1)}, u32[]{:S(2)}, u32[]{:S(2)}) collective-permute-start(f32[16,1024]{1,0:T(8,128)S(1)} %add_four.7.refs_0_.refs_4_), channel_id=1, source_target_pairs={{0,2},{1,3},{2,0},{3,1},{4,6},{5,7},{6,4},{7,5},{8,10},{9,11},{10,... | collective-permute-start | bytes 196616 | tf_op jit(solution)/shard_map/ppermute | solution.py:37
  71.1 6.0 %collective-permute-start.20 = (f32[16,1024]{1,0:T(8,128)S(1)}, f32[16,1024]{1,0:T(8,128)S(1)}, u32[]{:S(2)}, u32[]{:S(2)}) collective-permute-start(f32[16,1024]{1,0:T(8,128)S(1)} %add_four.7.refs_0_.refs_4_), channel_id=1, source_target_pairs={{0,1},{1,2},{2,3},{3,0},{4,5},{5,6},{6,7},{7,4},{8,9},{9,10},{10,1... | collective-permute-start | bytes 196616 | tf_op jit(solution)/shard_map/ppermute | solution.py:37
  71.9 5.3 %collective-permute-start.21 = (f32[16,1024]{1,0:T(8,128)S(1)}, f32[16,1024]{1,0:T(8,128)S(1)}, u32[]{:S(2)}, u32[]{:S(2)}) collective-permute-start(f32[16,1024]{1,0:T(8,128)S(1)} %add_four.7.refs_0_.refs_4_), channel_id=1, source_target_pairs={{0,3},{1,0},{2,1},{3,2},{4,7},{5,4},{6,5},{7,6},{8,11},{9,8},{10,9... | collective-permute-start | bytes 196616 | tf_op jit(solution)/shard_map/ppermute | solution.py:37
  77.1 4.7 %collective-permute-start.22 = (f32[16,1024]{1,0:T(8,128)S(1)}, f32[16,1024]{1,0:T(8,128)S(1)}, u32[]{:S(2)}, u32[]{:S(2)}) collective-permute-start(f32[16,1024]{1,0:T(8,128)S(1)} %add_four.8.refs_0_), channel_id=1, source_target_pairs={{0,8},{1,9},{2,10},{3,11},{4,12},{5,13},{6,14},{7,15},{8,0},{9,1},... | collective-permute-start | bytes 196616 | tf_op jit(solution)/shard_map/ppermute | solution.py:37
  78.0 4.5 %collective-permute-start.23 = (f32[16,1024]{1,0:T(8,128)S(1)}, f32[16,1024]{1,0:T(8,128)S(1)}, u32[]{:S(2)}, u32[]{:S(2)}) collective-permute-start(f32[16,1024]{1,0:T(8,128)S(1)} %add_four.8.refs_0_), channel_id=1, source_target_pairs={{0,4},{1,5},{2,6},{3,7},{4,8},{5,9},{6,10},{7,11},{8,12},{9,13},{1... | collective-permute-start | bytes 196616 | tf_op jit(solution)/shard_map/ppermute | solution.py:37
  79.2 3.4 %collective-permute-start.24 = (f32[16,1024]{1,0:T(8,128)S(1)}, f32[16,1024]{1,0:T(8,128)S(1)}, u32[]{:S(2)}, u32[]{:S(2)}) collective-permute-start(f32[16,1024]{1,0:T(8,128)S(1)} %add_four.8.refs_0_), channel_id=1, source_target_pairs={{0,12},{1,13},{2,14},{3,15},{4,0},{5,1},{6,2},{7,3},{8,4},{9,5},{1... | collective-permute-start | bytes 196616 | tf_op jit(solution)/shard_map/ppermute | solution.py:37
  83.2 9.4 %collective-permute-start.29 = (f32[32,3968]{1,0:T(8,128)S(1)}, f32[32,3968]{1,0:T(8,128)S(1)}, u32[]{:S(2)}, u32[]{:S(2)}) collective-permute-start(f32[32,3968]{1,0:T(8,128)S(1)} %get-tuple-element.61.refs_5_), channel_id=1, source_target_pairs={{0,1},{1,2},{2,3},{3,0},{4,5},{5,6},{6,7},{7,4},{8,9},{9,10},{10,1... | collective-permute-start | bytes 1523720 | tf_op jit(solution)/shard_map/ppermute | solution.py:37
  83.5 9.1 %collective-permute-start.30 = (f32[32,3968]{1,0:T(8,128)S(1)}, f32[32,3968]{1,0:T(8,128)S(1)}, u32[]{:S(2)}, u32[]{:S(2)}) collective-permute-start(f32[32,3968]{1,0:T(8,128)S(1)} %get-tuple-element.65), channel_id=1, source_target_pairs={{0,3},{1,0},{2,1},{3,2},{4,7},{5,4},{6,5},{7,6},{8,11},{9,8},{10,9... | collective-permute-start | bytes 1523720 | tf_op jit(solution)/shard_map/ppermute | solution.py:37
  86.8 5.1 %collective-permute-start.27 = (f32[16,1024]{1,0:T(8,128)S(1)}, f32[16,1024]{1,0:T(8,128)S(1)}, u32[]{:S(2)}, u32[]{:S(2)}) collective-permute-start(f32[16,1024]{1,0:T(8,128)S(1)} %add_four.9.refs_0_.refs_2_), channel_id=1, source_target_pairs={{0,96},{1,97},{2,98},{3,99},{4,100},{5,101},{6,102},{7,103},{8,104... | collective-permute-start | bytes 196616 | tf_op jit(solution)/shard_map/ppermute | solution.py:37
  89.3 17.1 %collective-permute-start.32 = (f32[32,3968]{1,0:T(8,128)S(1)}, f32[32,3968]{1,0:T(8,128)S(1)}, u32[]{:S(2)}, u32[]{:S(2)}) collective-permute-start(f32[32,3968]{1,0:T(8,128)S(1)} %get-tuple-element.67), channel_id=1, source_target_pairs={{0,1},{1,2},{2,3},{3,0},{4,5},{5,6},{6,7},{7,4},{8,9},{9,10},{10,1... | collective-permute-start | bytes 1523720 | tf_op jit(solution)/shard_map/ppermute | solution.py:37
  89.3 17.1 %collective-permute-start.33 = (f32[32,3968]{1,0:T(8,128)S(1)}, f32[32,3968]{1,0:T(8,128)S(1)}, u32[]{:S(2)}, u32[]{:S(2)}) collective-permute-start(f32[32,3968]{1,0:T(8,128)S(1)} %get-tuple-element.68), channel_id=1, source_target_pairs={{0,3},{1,0},{2,1},{3,2},{4,7},{5,4},{6,5},{7,6},{8,11},{9,8},{10,9... | collective-permute-start | bytes 1523720 | tf_op jit(solution)/shard_map/ppermute | solution.py:37
  92.8 16.8 %collective-permute-start.34 = (f32[32,3968]{1,0:T(8,128)S(1)}, f32[32,3968]{1,0:T(8,128)S(1)}, u32[]{:S(2)}, u32[]{:S(2)}) collective-permute-start(f32[32,3968]{1,0:T(8,128)S(1)} %get-tuple-element.66.refs_3_), channel_id=1, source_target_pairs={{0,1},{1,2},{2,3},{3,0},{4,5},{5,6},{6,7},{7,4},{8,9},{9,10},{10,1... | collective-permute-start | bytes 1523720 | tf_op jit(solution)/shard_map/ppermute | solution.py:37
  93.1 16.4 %collective-permute-start.35 = (f32[32,3968]{1,0:T(8,128)S(1)}, f32[32,3968]{1,0:T(8,128)S(1)}, u32[]{:S(2)}, u32[]{:S(2)}) collective-permute-start(f32[32,3968]{1,0:T(8,128)S(1)} %get-tuple-element.71), channel_id=1, source_target_pairs={{0,3},{1,0},{2,1},{3,2},{4,7},{5,4},{6,5},{7,6},{8,11},{9,8},{10,9... | collective-permute-start | bytes 1523720 | tf_op jit(solution)/shard_map/ppermute | solution.py:37
  95.6 4.1 %collective-permute-start.28 = (f32[16,2048]{1,0:T(8,128)S(1)}, f32[16,2048]{1,0:T(8,128)S(1)}, u32[]{:S(2)}, u32[]{:S(2)}) collective-permute-start(f32[16,2048]{1,0:T(8,128)S(1)} %join.2.refs_4_.refs_1_), channel_id=1, source_target_pairs={{0,32},{1,33},{2,34},{3,35},{4,36},{5,37},{6,38},{7,39},{8,40},{9,... | collective-permute-start | bytes 393224 | tf_op jit(solution)/shard_map/ppermute | solution.py:37
  100.3 7.3 %collective-permute-start.31 = (f32[16,4096]{1,0:T(8,128)S(1)}, f32[16,4096]{1,0:T(8,128)S(1)}, u32[]{:S(2)}, u32[]{:S(2)}) collective-permute-start(f32[16,4096]{1,0:T(8,128)S(1)} %join.3.refs_1_.refs_8_), channel_id=1, source_target_pairs={{0,16},{1,17},{2,18},{3,19},{4,20},{5,21},{6,22},{7,23},{8,24},{9,... | collective-permute-start | bytes 786440 | tf_op jit(solution)/shard_map/ppermute | solution.py:37

commit v5 on v4

--- a/solution.py
+++ b/solution.py
@@ -10,6 +10,7 @@
 BOTH = ("dp", "shard")
 SIDE = 4
 LANES = 128
+SUBLANES = 8
 HIGHEST = lax.Precision.HIGHEST
 FREE = pl.CostEstimate(flops=0, bytes_accessed=0, transcendentals=0)
 ANY = pl.BlockSpec(memory_space=pl.ANY)
@@ -136,6 +137,36 @@
     )(coords, *operands, *after)
 
 
+def first_kernel(coords_ref, up_even, up_odd, down_even, down_odd, after_ref, up_ref, down_ref):
+    for out_ref, refs in ((up_ref, (up_even, up_odd)), (down_ref, (down_even, down_odd))):
+        for index, ref in enumerate(refs):
+            out_ref[index] = ref[0, 0, 0].astype(jnp.float32)
+
+
+def first_blocks(blocks, coords, after):
+    depth, width = blocks.shape[3:]
+    specs = []
+    for half in (0, 1):
+        for odd in (0, 1):
+
+            def where(k, s, half=half, odd=odd):
+                there, core, spot = s[2], s[2 * SIDE], 2 * k + odd
+                return there * (1 - core) + spot * core, there * core + spot * (1 - core), half, 0, 0
+
+            specs.append(pl.BlockSpec((1, 1, 1, depth, width), where))
+    whole = pl.BlockSpec((2, depth, width), lambda k, s: (k, 0, 0))
+    return pl.pallas_call(
+        first_kernel,
+        grid_spec=pltpu.PrefetchScalarGridSpec(
+            num_scalar_prefetch=1, grid=(SIDE // 2,), in_specs=specs + [ANY], out_specs=[whole] * 2
+        ),
+        out_shape=[shape(SIDE, depth, width)] * 2,
+        cost_estimate=FREE,
+        compiler_params=limit(10),
+        name="first_blocks",
+    )(coords, *[blocks] * 4, after)
+
+
 def turn_first_kernel(coords_ref, held_up, came_up, held_down, came_down, up, down):
     there = coords_ref[SIDE + 2]
     up[...] = held_up[there] + came_up[there]
@@ -205,9 +236,10 @@
     @pl.when(step == pl.num_programs(0) - 1)
     def _():
         shard, core = scalar_ref[0], scalar_ref[1]
-        kept = lax.dot_general(
-            basis_ref[...], error_ref[...], across, precision=HIGHEST, preferred_element_type=jnp.float32
-        )
+        terms = jnp.concatenate(pieces_of(error_ref[...]), axis=0)
+        nine = lax.dot_general(pieces[...], terms, across, preferred_element_type=jnp.float32)
+        block = lambda i, j: nine[i * count : (i + 1) * count, j * own : (j + 1) * own]
+        kept = block(0, 0) + ((block(0, 1) + block(1, 0)) + (block(1, 1) + (block(0, 2) + block(2, 0))))
         wide = jnp.concatenate([kept] * (LANES // own), axis=1)
         lane = lax.broadcasted_iota(jnp.int32, wide.shape, 1)
         there = span(shard // (LANES // own), LANES)
@@ -248,14 +280,20 @@
 def orthonormal_kernel(scalar_ref, mine_ref, other_ref, out_ref, pieces_ref):
     mat = jnp.concatenate(ordered(1 - scalar_ref[1], mine_ref[...], other_ref[...]), axis=0)
     count = mat.shape[0]
-    order = lax.broadcasted_iota(jnp.int32, (count, 1), 0)
+    size = SUBLANES
+    groups = [mat[start : start + size, :] for start in range(0, count, size)]
+    order = lax.broadcasted_iota(jnp.int32, (size, 1), 0)
     for index in range(count):
-        column = mat[index : index + 1, :]
-        products = jnp.sum(mat * column, axis=1, keepdims=True)
-        own_norm = products[index : index + 1, :]
-        weights = jnp.where(order > index, products / own_norm, 0.0)
+        group, spot = index // size, index % size
+        column = groups[group][spot : spot + 1, :]
+        products = [jnp.sum(later * column, axis=1, keepdims=True) for later in groups[group:]]
+        own_norm = products[0][spot : spot + 1, :]
+        weights = [product / own_norm for product in products]
+        weights[0] = jnp.where(order > spot, weights[0], 0.0)
         scaled = column / jnp.sqrt(own_norm)
-        mat = jnp.where(order == index, scaled, mat - weights * column)
+        groups[group:] = [later - weight * column for later, weight in zip(groups[group:], weights)]
+        groups[group] = jnp.where(order == spot, scaled, groups[group])
+    mat = jnp.concatenate(groups, axis=0)
     out_ref[...] = mat
     for index, piece in enumerate(pieces_of(mat)):
         pieces_ref[index * count : (index + 1) * count, :] = piece
@@ -391,48 +429,45 @@
             out_ref[:, span(x ^ mask, size)] = ref[:, index * size : (index + 1) * size]
 
 
-def finish_kernel(replicas, scalar_ref, mine_ref, other_ref, phat_ref, error_ref, *refs):
-    kept_ref, up_ref, down_ref, grad_ref, rest_ref, basis_ref = refs
-    shard, core = scalar_ref[0], scalar_ref[1]
-    own, width = error_ref.shape
-    right = jnp.concatenate(ordered(core, mine_ref[:, :width], other_ref[:, :width]), axis=0)
-    basis_ref[...] = right * (1.0 / replicas)
-    mine = own_rows(phat_ref[:, span(shard // (LANES // own), LANES)], shard, own)
-    approx = lax.dot_general(
-        jnp.concatenate(stacked(mine, LEFT_ORDER), axis=0),
+def product(left, right, replicas):
+    total = lax.dot_general(
+        jnp.concatenate(stacked(left, LEFT_ORDER), axis=0),
         jnp.concatenate(stacked(right, RIGHT_ORDER), axis=0),
         (((0,), (0,)), ((), ())),
         preferred_element_type=jnp.float32,
-    ) * (1.0 / replicas)
-    grad_ref[...] = approx.astype(jnp.bfloat16)
+    )
+    return total * (1.0 / replicas)
+
+
+def half_product(replicas, scalar_ref, half, values_ref, phat_ref, own, width):
+    shard, count = scalar_ref[0], values_ref.shape[0]
+    mine = own_rows(phat_ref[span(half, count), span(shard // (LANES // own), LANES)], shard, own)
+    return product(mine, values_ref[:, :width], replicas)
+
+
+def nearly_kernel(replicas, scalar_ref, mine_ref, phat_ref, error_ref, kept_ref, up_ref, down_ref, *out_refs):
+    half_ref, rest_ref = out_refs
+    own, width = error_ref.shape
+    approx = half_product(replicas, scalar_ref, scalar_ref[1], mine_ref, phat_ref, own, width)
+    half_ref[...] = approx
     depth = own // 2
     for rows, came_ref in ((slice(0, depth), down_ref), (slice(depth, own), up_ref)):
         rest_ref[rows, :] = (error_ref[rows, :] + (kept_ref[rows, :] + came_ref[...])) - approx[rows, :]
 
 
-def last_kernel(rest_ref, up_ref, down_ref, out_ref):
-    early = pl.program_id(0) == 0
-    out_ref[...] = rest_ref[...] + jnp.where(early, up_ref[...], down_ref[...])
-
-
-def last_sum(rest, up, down):
-    rows, width = rest.shape
-    depth = rows // SIDE
-    whole = pl.BlockSpec((depth, width), lambda h, i: (2 * h + i, 0))
-    return pl.pallas_call(
-        last_kernel,
-        grid=(2, 2),
-        in_specs=[
-            whole,
-            pl.BlockSpec((depth, width), lambda h, i: (jnp.where(h == 0, i, 1), 0)),
-            pl.BlockSpec((depth, width), lambda h, i: (jnp.where(h == 0, 0, i), 0)),
-        ],
-        out_specs=whole,
-        out_shape=shape(rows, width),
-        cost_estimate=FREE,
-        compiler_params=limit(4),
-        name="last_sum",
-    )(rest, up, down)
+def finish_kernel(
+    replicas, scalar_ref, mine_ref, other_ref, phat_ref, half_ref, rest_ref, up_ref, down_ref, *out_refs
+):
+    grad_ref, next_ref, basis_ref = out_refs
+    core = scalar_ref[1]
+    own, width = rest_ref.shape
+    count, depth = mine_ref.shape[0], own // 2
+    basis_ref[span(core, count), :] = mine_ref[:, :width] * (1.0 / replicas)
+    basis_ref[span(1 - core, count), :] = other_ref[:, :width] * (1.0 / replicas)
+    approx = half_product(replicas, scalar_ref, 1 - core, other_ref, phat_ref, own, width)
+    grad_ref[...] = (half_ref[...] + approx).astype(jnp.bfloat16)
+    for rows, came_ref in ((slice(0, depth), up_ref), (slice(depth, own), down_ref)):
+        next_ref[rows, :] = (rest_ref[rows, :] + came_ref[...]) - approx[rows, :]
 
 
 def shards(partials, error, basis):
@@ -451,7 +486,7 @@
     coords = coords.astype(jnp.int32)
     large = in_hbm(partial.reshape(SIDE, SIDE, 2, own // 2, width))
 
-    sent1 = combine(large, coords, [(2, 0, []), (2, 1, [])], scalars)
+    sent1 = first_blocks(large, coords, scalars)
     came1 = [along_first(sent1[0], 1), along_first(sent1[1], -1)]
     keep, send, partial = left_terms(scalars, in_hbm(partial), basis, error, sent1[0])
     blocks = partial.reshape(SIDE, SIDE, 4, own // 4, width)
@@ -497,15 +532,23 @@
     came6 = [along_second(sent6[0], 1), along_second(sent6[1], -1)]
     outs = [shape(count // 2, 2 * pair.shape[1])]
     part = run(join_four_kernel, outs, scalars, [pair, pair_x(pair, 1)], sent6[0], "join")[0]
-    grad, rest, right = run(
+    half, rest = run(
+        functools.partial(nearly_kernel, replicas),
+        [shape(own, width)] * 2,
+        scalars,
+        [part, phat, error, kept, *came5],
+        part,
+        "nearly",
+    )
+    grad, following, right = run(
         functools.partial(finish_kernel, replicas),
         [shape(own, width, dtype=jnp.bfloat16), shape(own, width), shape(count, width)],
         scalars,
-        [part, other_core(part), phat, error, kept, *came5],
-        part,
+        [part, other_core(part), phat, half, rest, *came6],
+        rest,
         "finish",
     )
-    return grad, last_sum(rest, *came6)[None], right.T
+    return grad, following[None], right.T
 
 
 def solution(mesh):

time: 111 us -> 110 us (level)
    pallas_call x4 -> x3, Pallas kernels: 6.41 us -> 3.22 us  [combine(): pl.pallas_call(functools.partial(combine_kernel, arity), grid_spec=pltpu....]
    pallas_call x16 -> x17, Pallas kernels: 8.73 us -> 10.3 us  [run(): pl.pallas_call(body, in_specs=[SCALARS] * len(scalars) + [WHOLE] * len(op...]
  transfers between devices with their start and end apart: 36 -> 36, of which waited for: 18 -> 18; matrix products, arithmetic and copies ran while one was open for 0% -> 0% of each run, Pallas kernels for 20% -> 19%
where the time goes in v5:
time: 110 us; the launch traced here: 109 us
  starting transfers between devices  57.3 us (52%)
  Pallas kernels  26.4 us (24%)
  waiting for transfers between devices  24.5 us (22%)
    ppermute x36, starting transfers between devices, moved(): lax.ppermute(values, BOTH, [(place(*spot), place(*route(*spot))) for spot...  57.3 us
    ppermute x36, waiting for transfers between devices, moved(): lax.ppermute(values, BOTH, [(place(*spot), place(*route(*spot))) for spot...  24.5 us
    pallas_call x17, Pallas kernels, run(): pl.pallas_call(body, in_specs=[SCALARS] * len(scalars) + [WHOLE] * len(op...  10.3 us
    pallas_call x1, Pallas kernels, left_terms(): pl.pallas_call(left_kernel, grid=(SIDE,), in_specs=[SCALARS, pl.BlockSpec...  7.09 us
    pallas_call x1, Pallas kernels, right_terms(): pl.pallas_call(right_kernel, grid=(SIDE,), in_specs=[SCALARS, pl.BlockSpe...  3.46 us
    pallas_call x3, Pallas kernels, combine(): pl.pallas_call(functools.partial(combine_kernel, arity), grid_spec=pltpu....  3.22 us
    pallas_call x1, Pallas kernels, first_blocks(): pl.pallas_call(first_kernel, grid_spec=pltpu.PrefetchScalarGridSpec(num_s...  2.39 us
  transfers between devices with their start and end apart: 36, of which 18 were waited for; matrix products, arithmetic and copies ran while one was open for 0% of the time, Pallas kernels for 19%

profile of v5, /device:TPU:1, one launch (start us, length us, event | category | flops | bytes accessed | tf_op | source)
XLA Modules:
  0.0 109.3 jit_solution(4843073135593656046)
XLA Ops:
  0.7 0.1 pad_add_fusion.1.coords_ref.refs_0_
  0.9 2.4 %first_blocks.1 = (f32[4,32,3968]{2,1,0:T(8,128)S(1)}, f32[4,32,3968]{2,1,0:T(8,128)S(1)}) custom-call(s32[9]{0:T(128)S(1)} %pad_add_fusion.1.coords_ref.refs_0_, bf16[4,4,2,32,3968]{4,3,2,1,0:T(8,128)(2,1)} %bitcast.20, bf16[4,4,2,32,3968]{4,3,2,1,0:T(8,128)(2,1)} %bitcast.21, bf16[4,4,2,32,3968]{4,3,2,1,0:T(8,128)(2,1)} %bitcast.22, ...), custom_call_target="tpu_custom_call" | custom-call | tf_op jit(solution)/shard_map/first_blocks/pallas_call | solution.py:158
  3.3 2.2 %collective-permute-start.7 = (f32[4,32,3968]{2,1,0:T(8,128)S(1)}, f32[4,32,3968]{2,1,0:T(8,128)S(1)}, u32[]{:S(2)}, u32[]{:S(2)}) collective-permute-start(f32[4,32,3968]{2,1,0:T(8,128)S(1)} %get-tuple-element.40.after_ref), channel_id=1, source_target_pairs={{0,4},{1,5},{2,6},{3,7},{4,8},{5,9},{6,10},{7,11},{8,12},{9,13},{1... | collective-permute-start | bytes 6094856 | tf_op jit(solution)/shard_map/ppermute | solution.py:38
  5.5 1.5 %collective-permute-start.8 = (f32[4,32,3968]{2,1,0:T(8,128)S(1)}, f32[4,32,3968]{2,1,0:T(8,128)S(1)}, u32[]{:S(2)}, u32[]{:S(2)}) collective-permute-start(f32[4,32,3968]{2,1,0:T(8,128)S(1)} %get-tuple-element.47), channel_id=1, source_target_pairs={{0,12},{1,13},{2,14},{3,15},{4,0},{5,1},{6,2},{7,3},{8,4},{9,5},{1... | collective-permute-start | bytes 6094856 | tf_op jit(solution)/shard_map/ppermute | solution.py:38
  7.0 7.1 %left_terms.1 = (f32[16,1024]{1,0:T(8,128)S(1)}, f32[16,1024]{1,0:T(8,128)S(1)}, bf16[1024,3968]{1,0:T(8,128)(2,1)S(1)}) custom-call(s32[3]{0:T(128)S(1)} %pad_add_fusion.after_ref.scalar_ref.refs_0_, bf16[1024,3968]{1,0:T(8,128)(2,1)} %bitcast.24, f32[32,3968]{1,0:T(8,128)S(1)} %bitcast.19, f32[64,3968]{1,0:T(8,128)S(1)} %bitcast.16, ...), custom_call_target="tpu_custom_call" | custom-call | tf_op jit(solution)/shard_map/left_terms/pallas_call | solution.py:256
  14.1 2.1 %collective-permute-start = (f32[16,1024]{1,0:T(8,128)S(1)}, f32[16,1024]{1,0:T(8,128)S(1)}, u32[]{:S(2)}, u32[]{:S(2)}) collective-permute-start(f32[16,1024]{1,0:T(8,128)S(1)} %get-tuple-element.42), channel_id=1, source_target_pairs={{0,16},{1,17},{2,18},{3,19},{4,20},{5,21},{6,22},{7,23},{8,24},{9,... | collective-permute-start | bytes 196616 | tf_op jit(solution)/shard_map/ppermute | solution.py:38
  16.1 0.9 collective-permute-done.refs_1_
  17.0 2.8 %collective-permute-start.1 = (f32[16,1024]{1,0:T(8,128)S(1)}, f32[16,1024]{1,0:T(8,128)S(1)}, u32[]{:S(2)}, u32[]{:S(2)}) collective-permute-start(f32[16,1024]{1,0:T(8,128)S(1)} %add.56.refs_2_.refs_0_), channel_id=1, source_target_pairs={{0,64},{1,65},{2,66},{3,67},{4,68},{5,69},{6,70},{7,71},{8,72},{9,... | collective-permute-start | bytes 196616 | tf_op jit(solution)/shard_map/ppermute | solution.py:38
  19.9 0.3 collective-permute-start.2
  20.2 2.4 %collective-permute-start.3 = (f32[16,1024]{1,0:T(8,128)S(1)}, f32[16,1024]{1,0:T(8,128)S(1)}, u32[]{:S(2)}, u32[]{:S(2)}) collective-permute-start(f32[16,1024]{1,0:T(8,128)S(1)} %add.56.refs_2_.refs_0_), channel_id=1, source_target_pairs={{0,96},{1,97},{2,98},{3,99},{4,100},{5,101},{6,102},{7,103},{8,104... | collective-permute-start | bytes 196616 | tf_op jit(solution)/shard_map/ppermute | solution.py:38
  22.5 1.0 combine.3
  23.6 0.9 collective-permute-done.2.refs_2_
  24.5 0.1 collective-permute-start.4
  24.6 2.8 %collective-permute-start.14 = (f32[4,32,3968]{2,1,0:T(8,128)S(1)}, f32[4,32,3968]{2,1,0:T(8,128)S(1)}, u32[]{:S(2)}, u32[]{:S(2)}) collective-permute-start(f32[4,32,3968]{2,1,0:T(8,128)S(1)} %get-tuple-element.55), channel_id=1, source_target_pairs={{0,12},{1,13},{2,14},{3,15},{4,0},{5,1},{6,2},{7,3},{8,4},{9,5},{1... | collective-permute-start | bytes 6094856 | tf_op jit(solution)/shard_map/ppermute | solution.py:38
  27.4 1.3 %collective-permute-done.4.refs_1_ = f32[16,1024]{1,0:T(8,128)S(1)} collective-permute-done((f32[16,1024]{1,0:T(8,128)S(1)}, f32[16,1024]{1,0:T(8,128)S(1)}, u32[]{:S(2)}, u32[]{:S(2)}) %collective-permute-start.4) | collective-permute-done | bytes 65568 | tf_op jit(solution)/shard_map/ppermute | solution.py:38
  28.8 2.2 %collective-permute-start.5 = (f32[16,1024]{1,0:T(8,128)S(1)}, f32[16,1024]{1,0:T(8,128)S(1)}, u32[]{:S(2)}, u32[]{:S(2)}) collective-permute-start(f32[16,1024]{1,0:T(8,128)S(1)} %add.57.refs_0_.refs_2_), channel_id=1, source_target_pairs={{0,3},{1,2},{2,1},{3,0},{4,7},{5,6},{6,5},{7,4},{8,11},{9,10},{10,... | collective-permute-start | bytes 196616 | tf_op jit(solution)/shard_map/ppermute | solution.py:38
  31.0 2.2 %collective-permute-done.5.refs_1_ = f32[16,1024]{1,0:T(8,128)S(1)} collective-permute-done((f32[16,1024]{1,0:T(8,128)S(1)}, f32[16,1024]{1,0:T(8,128)S(1)}, u32[]{:S(2)}, u32[]{:S(2)}) %collective-permute-start.5) | collective-permute-done | bytes 65568 | tf_op jit(solution)/shard_map/ppermute | solution.py:38
  33.2 4.3 %collective-permute-start.6 = (f32[16,1024]{1,0:T(8,128)S(1)}, f32[16,1024]{1,0:T(8,128)S(1)}, u32[]{:S(2)}, u32[]{:S(2)}) collective-permute-start(f32[16,1024]{1,0:T(8,128)S(1)} %add.58.refs_4_), channel_id=1, source_target_pairs={{0,16},{1,17},{2,18},{3,19},{4,20},{5,21},{6,22},{7,23},{8,24},{9,... | collective-permute-start | bytes 196616 | tf_op jit(solution)/shard_map/ppermute | solution.py:38
  37.5 1.1 %combine.4 = (f32[4,32,3968]{2,1,0:T(8,128)S(1)}, f32[4,32,3968]{2,1,0:T(8,128)S(1)}) custom-call(s32[9]{0:T(128)S(1)} %pad_add_fusion.1.coords_ref.refs_0_, bf16[4,4,4,16,3968]{4,3,2,1,0:T(8,128)(2,1)S(1)} %bitcast.12, f32[4,32,3968]{2,1,0:T(8,128)S(1)} %collective-permute-done.7.refs_1_, bf16[4,4,4,16,3968]{4,3,2,1,0:T(8,128)(2,1)S(1)} %bitcast.13, ...), custom_call_target="tpu_custom_call" | custom-call | tf_op jit(solution)/shard_map/combine/pallas_call | solution.py:125
  38.8 2.7 %collective-permute-start.11 = (f32[16,1024]{1,0:T(8,128)S(1)}, f32[16,1024]{1,0:T(8,128)S(1)}, u32[]{:S(2)}, u32[]{:S(2)}) collective-permute-start(f32[16,1024]{1,0:T(8,128)S(1)} %gate.4.refs_0_.refs_4_), channel_id=1, source_target_pairs={{0,3},{1,0},{2,1},{3,2},{4,7},{5,4},{6,5},{7,6},{8,11},{9,8},{10,9... | collective-permute-start | bytes 196616 | tf_op jit(solution)/shard_map/ppermute | solution.py:38
  41.4 0.6 collective-permute-start.9
  42.0 2.1 %collective-permute-done.10.refs_2_ = f32[16,1024]{1,0:T(8,128)S(1)} collective-permute-done((f32[16,1024]{1,0:T(8,128)S(1)}, f32[16,1024]{1,0:T(8,128)S(1)}, u32[]{:S(2)}, u32[]{:S(2)}) %collective-permute-start.10) | collective-permute-done | bytes 65568 | tf_op jit(solution)/shard_map/ppermute | solution.py:38
  44.1 3.0 %collective-permute-done.9.refs_1_ = f32[16,1024]{1,0:T(8,128)S(1)} collective-permute-done((f32[16,1024]{1,0:T(8,128)S(1)}, f32[16,1024]{1,0:T(8,128)S(1)}, u32[]{:S(2)}, u32[]{:S(2)}) %collective-permute-start.9) | collective-permute-done | bytes 65568 | tf_op jit(solution)/shard_map/ppermute | solution.py:38
  47.2 2.7 %collective-permute-start.26 = (f32[4,32,3968]{2,1,0:T(8,128)S(1)}, f32[4,32,3968]{2,1,0:T(8,128)S(1)}, u32[]{:S(2)}, u32[]{:S(2)}) collective-permute-start(f32[4,32,3968]{2,1,0:T(8,128)S(1)} %get-tuple-element.62), channel_id=1, source_target_pairs={{0,12},{1,13},{2,14},{3,15},{4,0},{5,1},{6,2},{7,3},{8,4},{9,5},{1... | collective-permute-start | bytes 6094856 | tf_op jit(solution)/shard_map/ppermute | solution.py:38
  49.9 2.0 %collective-permute-start.12 = (f32[16,1024]{1,0:T(8,128)S(1)}, f32[16,1024]{1,0:T(8,128)S(1)}, u32[]{:S(2)}, u32[]{:S(2)}) collective-permute-start(f32[16,1024]{1,0:T(8,128)S(1)} %add_four.6.refs_2_.refs_1_), channel_id=1, source_target_pairs={{0,16},{1,17},{2,18},{3,19},{4,20},{5,21},{6,22},{7,23},{8,24},{9,... | collective-permute-start | bytes 196616 | tf_op jit(solution)/shard_map/ppermute | solution.py:38
  51.9 0.9 collective-permute-done.12.refs_2_
  52.8 3.9 %orthonormal.1 = (f32[32,1024]{1,0:T(8,128)S(1)}, bf16[96,1024]{1,0:T(8,128)(2,1)S(1)}) custom-call(s32[3]{0:T(128)S(1)} %pad_add_fusion.after_ref.scalar_ref.refs_0_, f32[16,1024]{1,0:T(8,128)S(1)} %add_four.6.refs_2_.refs_1_, f32[16,1024]{1,0:T(8,128)S(1)} %collective-permute-done.12.refs_2_, f32[4,32,3968]{2,1,0:T(8,128)S(1)} %get-tuple-element.50.refs_3_), custom_call_target="tpu_custom_call" | custom-call | tf_op jit(solution)/shard_map/orthonormal/pallas_call | solution.py:78
  56.7 3.5 %right_terms.1 = (f32[16,4096]{1,0:T(8,128)S(1)}, f32[16,4096]{1,0:T(8,128)S(1)}) custom-call(s32[3]{0:T(128)S(1)} %pad_add_fusion.after_ref.scalar_ref.refs_0_, bf16[96,1024]{1,0:T(8,128)(2,1)S(1)} %get-tuple-element.51.pieces_ref, bf16[1024,3968]{1,0:T(8,128)(2,1)S(1)} %get-tuple-element.43.partial_ref, ...), custom_call_target="tpu_custom_call" | custom-call | tf_op jit(solution)/shard_map/right_terms/pallas_call | solution.py:344
  60.2 0.4 collective-permute-start.13
  60.7 1.1 %combine.5 = (f32[4,32,3968]{2,1,0:T(8,128)S(1)}, f32[4,32,3968]{2,1,0:T(8,128)S(1)}) custom-call(s32[9]{0:T(128)S(1)} %pad_add_fusion.1.coords_ref.refs_0_, bf16[4,4,4,16,3968]{4,3,2,1,0:T(8,128)(2,1)S(1)} %bitcast.14, f32[4,32,3968]{2,1,0:T(8,128)S(1)} %collective-permute-done.14.refs_1_, bf16[4,4,4,16,3968]{4,3,2,1,0:T(8,128)(2,1)S(1)} %bitcast.15, ...), custom_call_target="tpu_custom_call" | custom-call | tf_op jit(solution)/shard_map/combine/pallas_call | solution.py:125
  61.8 0.6 add_cut.1
  62.4 1.3 %collective-permute-start.16 = (f32[16,1024]{1,0:T(8,128)S(1)}, f32[16,1024]{1,0:T(8,128)S(1)}, u32[]{:S(2)}, u32[]{:S(2)}) collective-permute-start(f32[16,1024]{1,0:T(8,128)S(1)} %get-tuple-element.58), channel_id=1, source_target_pairs={{0,64},{1,65},{2,66},{3,67},{4,68},{5,69},{6,70},{7,71},{8,72},{9,... | collective-permute-start | bytes 196616 | tf_op jit(solution)/shard_map/ppermute | solution.py:38
  63.7 2.3 %collective-permute-start.17 = (f32[16,1024]{1,0:T(8,128)S(1)}, f32[16,1024]{1,0:T(8,128)S(1)}, u32[]{:S(2)}, u32[]{:S(2)}) collective-permute-start(f32[16,1024]{1,0:T(8,128)S(1)} %get-tuple-element.59), channel_id=1, source_target_pairs={{0,32},{1,33},{2,34},{3,35},{4,36},{5,37},{6,38},{7,39},{8,40},{9,... | collective-permute-start | bytes 196616 | tf_op jit(solution)/shard_map/ppermute | solution.py:38
  66.0 0.3 collective-permute-start.18
  66.3 0.8 collective-permute-done.16.refs_1_
  67.1 2.0 %collective-permute-done.17.refs_2_ = f32[16,1024]{1,0:T(8,128)S(1)} collective-permute-done((f32[16,1024]{1,0:T(8,128)S(1)}, f32[16,1024]{1,0:T(8,128)S(1)}, u32[]{:S(2)}, u32[]{:S(2)}) %collective-permute-start.17) | collective-permute-done | bytes 65568 | tf_op jit(solution)/shard_map/ppermute | solution.py:38
  69.1 0.3 collective-permute-done.18.refs_3_
  69.5 0.7 collective-permute-start.19
  70.2 0.7 collective-permute-start.20
  70.9 1.9 %collective-permute-start.21 = (f32[16,1024]{1,0:T(8,128)S(1)}, f32[16,1024]{1,0:T(8,128)S(1)}, u32[]{:S(2)}, u32[]{:S(2)}) collective-permute-start(f32[16,1024]{1,0:T(8,128)S(1)} %add_four.7.refs_0_.refs_4_), channel_id=1, source_target_pairs={{0,3},{1,0},{2,1},{3,2},{4,7},{5,4},{6,5},{7,6},{8,11},{9,8},{10,9... | collective-permute-start | bytes 196616 | tf_op jit(solution)/shard_map/ppermute | solution.py:38
  72.8 2.1 %collective-permute-done.19.refs_1_ = f32[16,1024]{1,0:T(8,128)S(1)} collective-permute-done((f32[16,1024]{1,0:T(8,128)S(1)}, f32[16,1024]{1,0:T(8,128)S(1)}, u32[]{:S(2)}, u32[]{:S(2)}) %collective-permute-start.19) | collective-permute-done | bytes 65568 | tf_op jit(solution)/shard_map/ppermute | solution.py:38
  75.0 1.2 %collective-permute-done.20.refs_2_ = f32[16,1024]{1,0:T(8,128)S(1)} collective-permute-done((f32[16,1024]{1,0:T(8,128)S(1)}, f32[16,1024]{1,0:T(8,128)S(1)}, u32[]{:S(2)}, u32[]{:S(2)}) %collective-permute-start.20) | collective-permute-done | bytes 65568 | tf_op jit(solution)/shard_map/ppermute | solution.py:38
  76.2 1.1 collective-permute-start.22
  77.2 1.1 %collective-permute-start.23 = (f32[16,1024]{1,0:T(8,128)S(1)}, f32[16,1024]{1,0:T(8,128)S(1)}, u32[]{:S(2)}, u32[]{:S(2)}) collective-permute-start(f32[16,1024]{1,0:T(8,128)S(1)} %add_four.8.refs_0_), channel_id=1, source_target_pairs={{0,4},{1,5},{2,6},{3,7},{4,8},{5,9},{6,10},{7,11},{8,12},{9,13},{1... | collective-permute-start | bytes 196616 | tf_op jit(solution)/shard_map/ppermute | solution.py:38
  78.4 1.5 %collective-permute-start.24 = (f32[16,1024]{1,0:T(8,128)S(1)}, f32[16,1024]{1,0:T(8,128)S(1)}, u32[]{:S(2)}, u32[]{:S(2)}) collective-permute-start(f32[16,1024]{1,0:T(8,128)S(1)} %add_four.8.refs_0_), channel_id=1, source_target_pairs={{0,12},{1,13},{2,14},{3,15},{4,0},{5,1},{6,2},{7,3},{8,4},{9,5},{1... | collective-permute-start | bytes 196616 | tf_op jit(solution)/shard_map/ppermute | solution.py:38
  79.9 1.2 %collective-permute-done.22.refs_5_.refs_1_ = f32[16,1024]{1,0:T(8,128)S(1)} collective-permute-done((f32[16,1024]{1,0:T(8,128)S(1)}, f32[16,1024]{1,0:T(8,128)S(1)}, u32[]{:S(2)}, u32[]{:S(2)}) %collective-permute-start.22) | collective-permute-done | bytes 65568 | tf_op jit(solution)/shard_map/ppermute | solution.py:38
  81.1 0.7 collective-permute-done.23.refs_6_.refs_2_
  81.8 0.7 turn_first.1
  82.4 0.3 collective-permute-start.29
  82.7 2.4 %collective-permute-start.30 = (f32[32,3968]{1,0:T(8,128)S(1)}, f32[32,3968]{1,0:T(8,128)S(1)}, u32[]{:S(2)}, u32[]{:S(2)}) collective-permute-start(f32[32,3968]{1,0:T(8,128)S(1)} %get-tuple-element.67), channel_id=1, source_target_pairs={{0,3},{1,0},{2,1},{3,2},{4,7},{5,4},{6,5},{7,6},{8,11},{9,8},{10,9... | collective-permute-start | bytes 1523720 | tf_op jit(solution)/shard_map/ppermute | solution.py:38
  85.2 0.9 turn_rest.1
  86.0 2.4 %collective-permute-start.27 = (f32[16,1024]{1,0:T(8,128)S(1)}, f32[16,1024]{1,0:T(8,128)S(1)}, u32[]{:S(2)}, u32[]{:S(2)}) collective-permute-start(f32[16,1024]{1,0:T(8,128)S(1)} %add_four.9.refs_0_.refs_2_), channel_id=1, source_target_pairs={{0,96},{1,97},{2,98},{3,99},{4,100},{5,101},{6,102},{7,103},{8,104... | collective-permute-start | bytes 196616 | tf_op jit(solution)/shard_map/ppermute | solution.py:38
  88.5 2.7 %collective-permute-start.33 = (f32[32,3968]{1,0:T(8,128)S(1)}, f32[32,3968]{1,0:T(8,128)S(1)}, u32[]{:S(2)}, u32[]{:S(2)}) collective-permute-start(f32[32,3968]{1,0:T(8,128)S(1)} %get-tuple-element.70), channel_id=1, source_target_pairs={{0,3},{1,0},{2,1},{3,2},{4,7},{5,4},{6,5},{7,6},{8,11},{9,8},{10,9... | collective-permute-start | bytes 1523720 | tf_op jit(solution)/shard_map/ppermute | solution.py:38
  91.2 0.7 collective-permute-done.29.refs_1_
  91.8 0.1 ring_add.1
  92.0 0.3 collective-permute-start.34
  92.3 2.5 %collective-permute-start.35 = (f32[32,3968]{1,0:T(8,128)S(1)}, f32[32,3968]{1,0:T(8,128)S(1)}, u32[]{:S(2)}, u32[]{:S(2)}) collective-permute-start(f32[32,3968]{1,0:T(8,128)S(1)} %get-tuple-element.73), channel_id=1, source_target_pairs={{0,3},{1,0},{2,1},{3,2},{4,7},{5,4},{6,5},{7,6},{8,11},{9,8},{10,9... | collective-permute-start | bytes 1523720 | tf_op jit(solution)/shard_map/ppermute | solution.py:38
  94.8 0.2 collective-permute-start.28
  95.0 3.9 %collective-permute-done.28.refs_2_ = f32[16,2048]{1,0:T(8,128)S(1)} collective-permute-done((f32[16,2048]{1,0:T(8,128)S(1)}, f32[16,2048]{1,0:T(8,128)S(1)}, u32[]{:S(2)}, u32[]{:S(2)}) %collective-permute-start.28) | collective-permute-done | bytes 131104 | tf_op jit(solution)/shard_map/ppermute | solution.py:38
  98.9 0.6 join.3.refs_1_.refs_7_
  99.5 6.2 %collective-permute-start.31 = (f32[16,4096]{1,0:T(8,128)S(1)}, f32[16,4096]{1,0:T(8,128)S(1)}, u32[]{:S(2)}, u32[]{:S(2)}) collective-permute-start(f32[16,4096]{1,0:T(8,128)S(1)} %join.3.refs_1_.refs_7_), channel_id=1, source_target_pairs={{0,16},{1,17},{2,18},{3,19},{4,20},{5,21},{6,22},{7,23},{8,24},{9,... | collective-permute-start | bytes 786440 | tf_op jit(solution)/shard_map/ppermute | solution.py:38
  105.7 1.0 nearly.1
  106.8 0.1 collective-permute-done.31.refs_2_
  106.9 2.4 %finish.1 = (bf16[64,3968]{1,0:T(8,128)(2,1)}, f32[64,3968]{1,0:T(8,128)}, f32[32,3968]{1,0:T(8,128)}) custom-call(s32[3]{0:T(128)S(1)} %pad_add_fusion.after_ref.scalar_ref.refs_0_, f32[16,4096]{1,0:T(8,128)S(1)} %join.3.refs_1_.refs_7_, f32[16,4096]{1,0:T(8,128)S(1)} %collective-permute-done.31.refs_2_, ...), custom_call_target="tpu_custom_call" | custom-call | tf_op jit(solution)/shard_map/finish/pallas_call | solution.py:78
  (41 shorter events, 0.5 us)
Async XLA Ops:
  0.9 6.1 %copy-start = (f32[1,64,3968]{2,1,0:T(8,128)S(1)}, f32[1,64,3968]{2,1,0:T(8,128)}, u32[]{:S(2)}) copy-start(f32[1,64,3968]{2,1,0:T(8,128)} %param.4) | copy-start | bytes 3047428
  0.9 6.1 %copy-start.1 = (f32[3968,32]{0,1:T(8,128)S(1)}, f32[3968,32]{0,1:T(8,128)}, u32[]{:S(2)}) copy-start(f32[3968,32]{0,1:T(8,128)} %param.5) | copy-start | bytes 1523716
  3.3 34.3 %collective-permute-start.7 = (f32[4,32,3968]{2,1,0:T(8,128)S(1)}, f32[4,32,3968]{2,1,0:T(8,128)S(1)}, u32[]{:S(2)}, u32[]{:S(2)}) collective-permute-start(f32[4,32,3968]{2,1,0:T(8,128)S(1)} %get-tuple-element.40.after_ref), channel_id=1, source_target_pairs={{0,4},{1,5},{2,6},{3,7},{4,8},{5,9},{6,10},{7,11},{8,12},{9,13},{1... | collective-permute-start | bytes 6094856 | tf_op jit(solution)/shard_map/ppermute | solution.py:38
  5.5 32.1 %collective-permute-start.8 = (f32[4,32,3968]{2,1,0:T(8,128)S(1)}, f32[4,32,3968]{2,1,0:T(8,128)S(1)}, u32[]{:S(2)}, u32[]{:S(2)}) collective-permute-start(f32[4,32,3968]{2,1,0:T(8,128)S(1)} %get-tuple-element.47), channel_id=1, source_target_pairs={{0,12},{1,13},{2,14},{3,15},{4,0},{5,1},{6,2},{7,3},{8,4},{9,5},{1... | collective-permute-start | bytes 6094856 | tf_op jit(solution)/shard_map/ppermute | solution.py:38
  14.1 3.0 %collective-permute-start = (f32[16,1024]{1,0:T(8,128)S(1)}, f32[16,1024]{1,0:T(8,128)S(1)}, u32[]{:S(2)}, u32[]{:S(2)}) collective-permute-start(f32[16,1024]{1,0:T(8,128)S(1)} %get-tuple-element.42), channel_id=1, source_target_pairs={{0,16},{1,17},{2,18},{3,19},{4,20},{5,21},{6,22},{7,23},{8,24},{9,... | collective-permute-start | bytes 196616 | tf_op jit(solution)/shard_map/ppermute | solution.py:38
  17.0 6.5 %collective-permute-start.1 = (f32[16,1024]{1,0:T(8,128)S(1)}, f32[16,1024]{1,0:T(8,128)S(1)}, u32[]{:S(2)}, u32[]{:S(2)}) collective-permute-start(f32[16,1024]{1,0:T(8,128)S(1)} %add.56.refs_2_.refs_0_), channel_id=1, source_target_pairs={{0,64},{1,65},{2,66},{3,67},{4,68},{5,69},{6,70},{7,71},{8,72},{9,... | collective-permute-start | bytes 196616 | tf_op jit(solution)/shard_map/ppermute | solution.py:38
  19.9 4.6 %collective-permute-start.2 = (f32[16,1024]{1,0:T(8,128)S(1)}, f32[16,1024]{1,0:T(8,128)S(1)}, u32[]{:S(2)}, u32[]{:S(2)}) collective-permute-start(f32[16,1024]{1,0:T(8,128)S(1)} %add.56.refs_2_.refs_0_), channel_id=1, source_target_pairs={{0,32},{1,33},{2,34},{3,35},{4,36},{5,37},{6,38},{7,39},{8,40},{9,... | collective-permute-start | bytes 196616 | tf_op jit(solution)/shard_map/ppermute | solution.py:38
  20.2 4.3 %collective-permute-start.3 = (f32[16,1024]{1,0:T(8,128)S(1)}, f32[16,1024]{1,0:T(8,128)S(1)}, u32[]{:S(2)}, u32[]{:S(2)}) collective-permute-start(f32[16,1024]{1,0:T(8,128)S(1)} %add.56.refs_2_.refs_0_), channel_id=1, source_target_pairs={{0,96},{1,97},{2,98},{3,99},{4,100},{5,101},{6,102},{7,103},{8,104... | collective-permute-start | bytes 196616 | tf_op jit(solution)/shard_map/ppermute | solution.py:38
  24.5 4.3 %collective-permute-start.4 = (f32[16,1024]{1,0:T(8,128)S(1)}, f32[16,1024]{1,0:T(8,128)S(1)}, u32[]{:S(2)}, u32[]{:S(2)}) collective-permute-start(f32[16,1024]{1,0:T(8,128)S(1)} %add_four.5.refs_2_.refs_0_), channel_id=1, source_target_pairs={{0,1},{1,0},{2,3},{3,2},{4,5},{5,4},{6,7},{7,6},{8,9},{9,8},{10,11... | collective-permute-start | bytes 196616 | tf_op jit(solution)/shard_map/ppermute | solution.py:38
  24.6 36.0 %collective-permute-start.14 = (f32[4,32,3968]{2,1,0:T(8,128)S(1)}, f32[4,32,3968]{2,1,0:T(8,128)S(1)}, u32[]{:S(2)}, u32[]{:S(2)}) collective-permute-start(f32[4,32,3968]{2,1,0:T(8,128)S(1)} %get-tuple-element.55), channel_id=1, source_target_pairs={{0,12},{1,13},{2,14},{3,15},{4,0},{5,1},{6,2},{7,3},{8,4},{9,5},{1... | collective-permute-start | bytes 6094856 | tf_op jit(solution)/shard_map/ppermute | solution.py:38
  27.4 33.2 %collective-permute-start.15 = (f32[4,32,3968]{2,1,0:T(8,128)S(1)}, f32[4,32,3968]{2,1,0:T(8,128)S(1)}, u32[]{:S(2)}, u32[]{:S(2)}) collective-permute-start(f32[4,32,3968]{2,1,0:T(8,128)S(1)} %get-tuple-element.46.refs_2_), channel_id=1, source_target_pairs={{0,4},{1,5},{2,6},{3,7},{4,8},{5,9},{6,10},{7,11},{8,12},{9,13},{1... | collective-permute-start | bytes 6094856 | tf_op jit(solution)/shard_map/ppermute | solution.py:38
  28.8 4.4 %collective-permute-start.5 = (f32[16,1024]{1,0:T(8,128)S(1)}, f32[16,1024]{1,0:T(8,128)S(1)}, u32[]{:S(2)}, u32[]{:S(2)}) collective-permute-start(f32[16,1024]{1,0:T(8,128)S(1)} %add.57.refs_0_.refs_2_), channel_id=1, source_target_pairs={{0,3},{1,2},{2,1},{3,0},{4,7},{5,6},{6,5},{7,4},{8,11},{9,10},{10,... | collective-permute-start | bytes 196616 | tf_op jit(solution)/shard_map/ppermute | solution.py:38
  33.2 5.5 %collective-permute-start.6 = (f32[16,1024]{1,0:T(8,128)S(1)}, f32[16,1024]{1,0:T(8,128)S(1)}, u32[]{:S(2)}, u32[]{:S(2)}) collective-permute-start(f32[16,1024]{1,0:T(8,128)S(1)} %add.58.refs_4_), channel_id=1, source_target_pairs={{0,16},{1,17},{2,18},{3,19},{4,20},{5,21},{6,22},{7,23},{8,24},{9,... | collective-permute-start | bytes 196616 | tf_op jit(solution)/shard_map/ppermute | solution.py:38
  38.7 5.5 %collective-permute-start.10 = (f32[16,1024]{1,0:T(8,128)S(1)}, f32[16,1024]{1,0:T(8,128)S(1)}, u32[]{:S(2)}, u32[]{:S(2)}) collective-permute-start(f32[16,1024]{1,0:T(8,128)S(1)} %gate.4.refs_0_.refs_4_), channel_id=1, source_target_pairs={{0,1},{1,2},{2,3},{3,0},{4,5},{5,6},{6,7},{7,4},{8,9},{9,10},{10,1... | collective-permute-start | bytes 196616 | tf_op jit(solution)/shard_map/ppermute | solution.py:38
  38.8 5.4 %collective-permute-start.11 = (f32[16,1024]{1,0:T(8,128)S(1)}, f32[16,1024]{1,0:T(8,128)S(1)}, u32[]{:S(2)}, u32[]{:S(2)}) collective-permute-start(f32[16,1024]{1,0:T(8,128)S(1)} %gate.4.refs_0_.refs_4_), channel_id=1, source_target_pairs={{0,3},{1,0},{2,1},{3,2},{4,7},{5,4},{6,5},{7,6},{8,11},{9,8},{10,9... | collective-permute-start | bytes 196616 | tf_op jit(solution)/shard_map/ppermute | solution.py:38
  41.4 5.7 %collective-permute-start.9 = (f32[16,1024]{1,0:T(8,128)S(1)}, f32[16,1024]{1,0:T(8,128)S(1)}, u32[]{:S(2)}, u32[]{:S(2)}) collective-permute-start(f32[16,1024]{1,0:T(8,128)S(1)} %gate.4.refs_0_.refs_4_), channel_id=1, source_target_pairs={{0,2},{1,3},{2,0},{3,1},{4,6},{5,7},{6,4},{7,5},{8,10},{9,11},{10,... | collective-permute-start | bytes 196616 | tf_op jit(solution)/shard_map/ppermute | solution.py:38
  47.1 34.6 %collective-permute-start.25 = (f32[4,32,3968]{2,1,0:T(8,128)S(1)}, f32[4,32,3968]{2,1,0:T(8,128)S(1)}, u32[]{:S(2)}, u32[]{:S(2)}) collective-permute-start(f32[4,32,3968]{2,1,0:T(8,128)S(1)} %get-tuple-element.50.refs_3_), channel_id=1, source_target_pairs={{0,4},{1,5},{2,6},{3,7},{4,8},{5,9},{6,10},{7,11},{8,12},{9,13},{1... | collective-permute-start | bytes 6094856 | tf_op jit(solution)/shard_map/ppermute | solution.py:38
  47.2 34.5 %collective-permute-start.26 = (f32[4,32,3968]{2,1,0:T(8,128)S(1)}, f32[4,32,3968]{2,1,0:T(8,128)S(1)}, u32[]{:S(2)}, u32[]{:S(2)}) collective-permute-start(f32[4,32,3968]{2,1,0:T(8,128)S(1)} %get-tuple-element.62), channel_id=1, source_target_pairs={{0,12},{1,13},{2,14},{3,15},{4,0},{5,1},{6,2},{7,3},{8,4},{9,5},{1... | collective-permute-start | bytes 6094856 | tf_op jit(solution)/shard_map/ppermute | solution.py:38
  49.9 2.9 %collective-permute-start.12 = (f32[16,1024]{1,0:T(8,128)S(1)}, f32[16,1024]{1,0:T(8,128)S(1)}, u32[]{:S(2)}, u32[]{:S(2)}) collective-permute-start(f32[16,1024]{1,0:T(8,128)S(1)} %add_four.6.refs_2_.refs_1_), channel_id=1, source_target_pairs={{0,16},{1,17},{2,18},{3,19},{4,20},{5,21},{6,22},{7,23},{8,24},{9,... | collective-permute-start | bytes 196616 | tf_op jit(solution)/shard_map/ppermute | solution.py:38
  60.2 1.6 %collective-permute-start.13 = (f32[16,4096]{1,0:T(8,128)S(1)}, f32[16,4096]{1,0:T(8,128)S(1)}, u32[]{:S(2)}, u32[]{:S(2)}) collective-permute-start(f32[16,4096]{1,0:T(8,128)S(1)} %get-tuple-element.54.refs_4_), channel_id=1, source_target_pairs={{0,16},{1,17},{2,18},{3,19},{4,20},{5,21},{6,22},{7,23},{8,24},{9,... | collective-permute-start | bytes 786440 | tf_op jit(solution)/shard_map/ppermute | solution.py:38
  62.4 4.7 %collective-permute-start.16 = (f32[16,1024]{1,0:T(8,128)S(1)}, f32[16,1024]{1,0:T(8,128)S(1)}, u32[]{:S(2)}, u32[]{:S(2)}) collective-permute-start(f32[16,1024]{1,0:T(8,128)S(1)} %get-tuple-element.58), channel_id=1, source_target_pairs={{0,64},{1,65},{2,66},{3,67},{4,68},{5,69},{6,70},{7,71},{8,72},{9,... | collective-permute-start | bytes 196616 | tf_op jit(solution)/shard_map/ppermute | solution.py:38
  63.7 5.5 %collective-permute-start.17 = (f32[16,1024]{1,0:T(8,128)S(1)}, f32[16,1024]{1,0:T(8,128)S(1)}, u32[]{:S(2)}, u32[]{:S(2)}) collective-permute-start(f32[16,1024]{1,0:T(8,128)S(1)} %get-tuple-element.59), channel_id=1, source_target_pairs={{0,32},{1,33},{2,34},{3,35},{4,36},{5,37},{6,38},{7,39},{8,40},{9,... | collective-permute-start | bytes 196616 | tf_op jit(solution)/shard_map/ppermute | solution.py:38
  66.0 3.5 %collective-permute-start.18 = (f32[16,1024]{1,0:T(8,128)S(1)}, f32[16,1024]{1,0:T(8,128)S(1)}, u32[]{:S(2)}, u32[]{:S(2)}) collective-permute-start(f32[16,1024]{1,0:T(8,128)S(1)} %get-tuple-element.60), channel_id=1, source_target_pairs={{0,96},{1,97},{2,98},{3,99},{4,100},{5,101},{6,102},{7,103},{8,104... | collective-permute-start | bytes 196616 | tf_op jit(solution)/shard_map/ppermute | solution.py:38
  69.5 5.5 %collective-permute-start.19 = (f32[16,1024]{1,0:T(8,128)S(1)}, f32[16,1024]{1,0:T(8,128)S(1)}, u32[]{:S(2)}, u32[]{:S(2)}) collective-permute-start(f32[16,1024]{1,0:T(8,128)S(1)} %add_four.7.refs_0_.refs_4_), channel_id=1, source_target_pairs={{0,2},{1,3},{2,0},{3,1},{4,6},{5,7},{6,4},{7,5},{8,10},{9,11},{10,... | collective-permute-start | bytes 196616 | tf_op jit(solution)/shard_map/ppermute | solution.py:38
  70.2 6.0 %collective-permute-start.20 = (f32[16,1024]{1,0:T(8,128)S(1)}, f32[16,1024]{1,0:T(8,128)S(1)}, u32[]{:S(2)}, u32[]{:S(2)}) collective-permute-start(f32[16,1024]{1,0:T(8,128)S(1)} %add_four.7.refs_0_.refs_4_), channel_id=1, source_target_pairs={{0,1},{1,2},{2,3},{3,0},{4,5},{5,6},{6,7},{7,4},{8,9},{9,10},{10,1... | collective-permute-start | bytes 196616 | tf_op jit(solution)/shard_map/ppermute | solution.py:38
  70.9 5.2 %collective-permute-start.21 = (f32[16,1024]{1,0:T(8,128)S(1)}, f32[16,1024]{1,0:T(8,128)S(1)}, u32[]{:S(2)}, u32[]{:S(2)}) collective-permute-start(f32[16,1024]{1,0:T(8,128)S(1)} %add_four.7.refs_0_.refs_4_), channel_id=1, source_target_pairs={{0,3},{1,0},{2,1},{3,2},{4,7},{5,4},{6,5},{7,6},{8,11},{9,8},{10,9... | collective-permute-start | bytes 196616 | tf_op jit(solution)/shard_map/ppermute | solution.py:38
  76.2 4.9 %collective-permute-start.22 = (f32[16,1024]{1,0:T(8,128)S(1)}, f32[16,1024]{1,0:T(8,128)S(1)}, u32[]{:S(2)}, u32[]{:S(2)}) collective-permute-start(f32[16,1024]{1,0:T(8,128)S(1)} %add_four.8.refs_0_), channel_id=1, source_target_pairs={{0,8},{1,9},{2,10},{3,11},{4,12},{5,13},{6,14},{7,15},{8,0},{9,1},... | collective-permute-start | bytes 196616 | tf_op jit(solution)/shard_map/ppermute | solution.py:38
  77.2 4.5 %collective-permute-start.23 = (f32[16,1024]{1,0:T(8,128)S(1)}, f32[16,1024]{1,0:T(8,128)S(1)}, u32[]{:S(2)}, u32[]{:S(2)}) collective-permute-start(f32[16,1024]{1,0:T(8,128)S(1)} %add_four.8.refs_0_), channel_id=1, source_target_pairs={{0,4},{1,5},{2,6},{3,7},{4,8},{5,9},{6,10},{7,11},{8,12},{9,13},{1... | collective-permute-start | bytes 196616 | tf_op jit(solution)/shard_map/ppermute | solution.py:38
  78.4 3.4 %collective-permute-start.24 = (f32[16,1024]{1,0:T(8,128)S(1)}, f32[16,1024]{1,0:T(8,128)S(1)}, u32[]{:S(2)}, u32[]{:S(2)}) collective-permute-start(f32[16,1024]{1,0:T(8,128)S(1)} %add_four.8.refs_0_), channel_id=1, source_target_pairs={{0,12},{1,13},{2,14},{3,15},{4,0},{5,1},{6,2},{7,3},{8,4},{9,5},{1... | collective-permute-start | bytes 196616 | tf_op jit(solution)/shard_map/ppermute | solution.py:38
  82.4 9.4 %collective-permute-start.29 = (f32[32,3968]{1,0:T(8,128)S(1)}, f32[32,3968]{1,0:T(8,128)S(1)}, u32[]{:S(2)}, u32[]{:S(2)}) collective-permute-start(f32[32,3968]{1,0:T(8,128)S(1)} %get-tuple-element.63.refs_5_), channel_id=1, source_target_pairs={{0,1},{1,2},{2,3},{3,0},{4,5},{5,6},{6,7},{7,4},{8,9},{9,10},{10,1... | collective-permute-start | bytes 1523720 | tf_op jit(solution)/shard_map/ppermute | solution.py:38
  82.7 9.1 %collective-permute-start.30 = (f32[32,3968]{1,0:T(8,128)S(1)}, f32[32,3968]{1,0:T(8,128)S(1)}, u32[]{:S(2)}, u32[]{:S(2)}) collective-permute-start(f32[32,3968]{1,0:T(8,128)S(1)} %get-tuple-element.67), channel_id=1, source_target_pairs={{0,3},{1,0},{2,1},{3,2},{4,7},{5,4},{6,5},{7,6},{8,11},{9,8},{10,9... | collective-permute-start | bytes 1523720 | tf_op jit(solution)/shard_map/ppermute | solution.py:38
  86.0 5.1 %collective-permute-start.27 = (f32[16,1024]{1,0:T(8,128)S(1)}, f32[16,1024]{1,0:T(8,128)S(1)}, u32[]{:S(2)}, u32[]{:S(2)}) collective-permute-start(f32[16,1024]{1,0:T(8,128)S(1)} %add_four.9.refs_0_.refs_2_), channel_id=1, source_target_pairs={{0,96},{1,97},{2,98},{3,99},{4,100},{5,101},{6,102},{7,103},{8,104... | collective-permute-start | bytes 196616 | tf_op jit(solution)/shard_map/ppermute | solution.py:38
  88.5 17.3 %collective-permute-start.32 = (f32[32,3968]{1,0:T(8,128)S(1)}, f32[32,3968]{1,0:T(8,128)S(1)}, u32[]{:S(2)}, u32[]{:S(2)}) collective-permute-start(f32[32,3968]{1,0:T(8,128)S(1)} %get-tuple-element.69), channel_id=1, source_target_pairs={{0,1},{1,2},{2,3},{3,0},{4,5},{5,6},{6,7},{7,4},{8,9},{9,10},{10,1... | collective-permute-start | bytes 1523720 | tf_op jit(solution)/shard_map/ppermute | solution.py:38
  88.5 17.3 %collective-permute-start.33 = (f32[32,3968]{1,0:T(8,128)S(1)}, f32[32,3968]{1,0:T(8,128)S(1)}, u32[]{:S(2)}, u32[]{:S(2)}) collective-permute-start(f32[32,3968]{1,0:T(8,128)S(1)} %get-tuple-element.70), channel_id=1, source_target_pairs={{0,3},{1,0},{2,1},{3,2},{4,7},{5,4},{6,5},{7,6},{8,11},{9,8},{10,9... | collective-permute-start | bytes 1523720 | tf_op jit(solution)/shard_map/ppermute | solution.py:38
  92.0 14.9 %collective-permute-start.34 = (f32[32,3968]{1,0:T(8,128)S(1)}, f32[32,3968]{1,0:T(8,128)S(1)}, u32[]{:S(2)}, u32[]{:S(2)}) collective-permute-start(f32[32,3968]{1,0:T(8,128)S(1)} %get-tuple-element.68.refs_3_), channel_id=1, source_target_pairs={{0,1},{1,2},{2,3},{3,0},{4,5},{5,6},{6,7},{7,4},{8,9},{9,10},{10,1... | collective-permute-start | bytes 1523720 | tf_op jit(solution)/shard_map/ppermute | solution.py:38
  92.3 14.6 %collective-permute-start.35 = (f32[32,3968]{1,0:T(8,128)S(1)}, f32[32,3968]{1,0:T(8,128)S(1)}, u32[]{:S(2)}, u32[]{:S(2)}) collective-permute-start(f32[32,3968]{1,0:T(8,128)S(1)} %get-tuple-element.73), channel_id=1, source_target_pairs={{0,3},{1,0},{2,1},{3,2},{4,7},{5,4},{6,5},{7,6},{8,11},{9,8},{10,9... | collective-permute-start | bytes 1523720 | tf_op jit(solution)/shard_map/ppermute | solution.py:38
  94.8 4.1 %collective-permute-start.28 = (f32[16,2048]{1,0:T(8,128)S(1)}, f32[16,2048]{1,0:T(8,128)S(1)}, u32[]{:S(2)}, u32[]{:S(2)}) collective-permute-start(f32[16,2048]{1,0:T(8,128)S(1)} %join.2.refs_4_.refs_1_), channel_id=1, source_target_pairs={{0,32},{1,33},{2,34},{3,35},{4,36},{5,37},{6,38},{7,39},{8,40},{9,... | collective-permute-start | bytes 393224 | tf_op jit(solution)/shard_map/ppermute | solution.py:38
  99.5 7.4 %collective-permute-start.31 = (f32[16,4096]{1,0:T(8,128)S(1)}, f32[16,4096]{1,0:T(8,128)S(1)}, u32[]{:S(2)}, u32[]{:S(2)}) collective-permute-start(f32[16,4096]{1,0:T(8,128)S(1)} %join.3.refs_1_.refs_7_), channel_id=1, source_target_pairs={{0,16},{1,17},{2,18},{3,19},{4,20},{5,21},{6,22},{7,23},{8,24},{9,... | collective-permute-start | bytes 786440 | tf_op jit(solution)/shard_map/ppermute | solution.py:38

commit v6 on v5

--- a/solution.py
+++ b/solution.py
@@ -455,19 +455,41 @@
         rest_ref[rows, :] = (error_ref[rows, :] + (kept_ref[rows, :] + came_ref[...])) - approx[rows, :]
 
 
-def finish_kernel(
-    replicas, scalar_ref, mine_ref, other_ref, phat_ref, half_ref, rest_ref, up_ref, down_ref, *out_refs
-):
-    grad_ref, next_ref, basis_ref = out_refs
+def finish_kernel(replicas, scalar_ref, mine_ref, other_ref, phat_ref, half_ref, rest_ref, *refs):
+    up_ref, down_ref, grad_out, next_out, basis_out, grad_ref, next_ref, basis_ref, sent = refs
     core = scalar_ref[1]
     own, width = rest_ref.shape
     count, depth = mine_ref.shape[0], own // 2
     basis_ref[span(core, count), :] = mine_ref[:, :width] * (1.0 / replicas)
     basis_ref[span(1 - core, count), :] = other_ref[:, :width] * (1.0 / replicas)
+    copies = [pltpu.make_async_copy(basis_ref, basis_out, sent.at[0])]
+    copies[-1].start()
     approx = half_product(replicas, scalar_ref, 1 - core, other_ref, phat_ref, own, width)
+    for index, came_ref in enumerate((up_ref, down_ref)):
+        rows = slice(index * depth, (index + 1) * depth)
+        there = pl.ds(index * depth, depth)
+        next_ref[rows, :] = (rest_ref[rows, :] + came_ref[...]) - approx[rows, :]
+        copies.append(pltpu.make_async_copy(next_ref.at[there, :], next_out.at[there, :], sent.at[1 + index]))
+        copies[-1].start()
     grad_ref[...] = (half_ref[...] + approx).astype(jnp.bfloat16)
-    for rows, came_ref in ((slice(0, depth), up_ref), (slice(depth, own), down_ref)):
-        next_ref[rows, :] = (rest_ref[rows, :] + came_ref[...]) - approx[rows, :]
+    copies.append(pltpu.make_async_copy(grad_ref, grad_out, sent.at[3]))
+    copies[-1].start()
+    for copy in copies:
+        copy.wait()
+
+
+def finish(replicas, outs, scalars, operands):
+    return pl.pallas_call(
+        functools.partial(finish_kernel, replicas),
+        in_specs=[SCALARS] + [WHOLE] * len(operands),
+        out_specs=[ANY] * len(outs),
+        out_shape=outs,
+        scratch_shapes=[pltpu.VMEM(out.shape, out.dtype) for out in outs]
+        + [pltpu.SemaphoreType.DMA((4,))],
+        cost_estimate=FREE,
+        compiler_params=limit(10),
+        name="finish",
+    )(scalars, *operands)
 
 
 def shards(partials, error, basis):
@@ -519,7 +541,7 @@
     )
     came4 = [along_second(up, 1), along_second(down, -1)]
     came5 = [along_second(up_local, 1), along_second(down_local, -1)]
-    part = sum_came(part, came, kept)
+    part = sum_came(part, came, up)
     pair = run(join_two_kernel, [shape(count // 2, 2 * part.shape[1])], None, [part, pair_x(part, 3)], part, "join", room=1)[0]
     sent6 = run(
         ring_add_kernel,
@@ -540,13 +562,11 @@
         part,
         "nearly",
     )
-    grad, following, right = run(
-        functools.partial(finish_kernel, replicas),
+    grad, following, right = finish(
+        replicas,
         [shape(own, width, dtype=jnp.bfloat16), shape(own, width), shape(count, width)],
         scalars,
         [part, other_core(part), phat, half, rest, *came6],
-        rest,
-        "finish",
     )
     return grad, following[None], right.T
 

time: 110 us -> 111 us (level)
    pallas_call x0 -> x1, Pallas kernels: none -> 2.45 us  [finish(): pl.pallas_call(functools.partial(finish_kernel, replicas), in_specs=[SCAL...]
    pallas_call x17 -> x16, Pallas kernels: 10.3 us -> 7.83 us  [run(): pl.pallas_call(body, in_specs=[SCALARS] * len(scalars) + [WHOLE] * len(op...]
where the time goes in v6:
time: 111 us; the launch traced here: 110 us
  starting transfers between devices  57.4 us (52%)
  Pallas kernels  26.5 us (24%)
  waiting for transfers between devices  24.4 us (22%)
    ppermute x36, starting transfers between devices, moved(): lax.ppermute(values, BOTH, [(place(*spot), place(*route(*spot))) for spot...  57.4 us
    ppermute x36, waiting for transfers between devices, moved(): lax.ppermute(values, BOTH, [(place(*spot), place(*route(*spot))) for spot...  24.4 us
    pallas_call x16, Pallas kernels, run(): pl.pallas_call(body, in_specs=[SCALARS] * len(scalars) + [WHOLE] * len(op...  7.83 us
    pallas_call x1, Pallas kernels, left_terms(): pl.pallas_call(left_kernel, grid=(SIDE,), in_specs=[SCALARS, pl.BlockSpec...  7.09 us
    pallas_call x1, Pallas kernels, right_terms(): pl.pallas_call(right_kernel, grid=(SIDE,), in_specs=[SCALARS, pl.BlockSpe...  3.46 us
    pallas_call x3, Pallas kernels, combine(): pl.pallas_call(functools.partial(combine_kernel, arity), grid_spec=pltpu....  3.22 us
    pallas_call x1, Pallas kernels, finish(): pl.pallas_call(functools.partial(finish_kernel, replicas), in_specs=[SCAL...  2.45 us
    pallas_call x1, Pallas kernels, first_blocks(): pl.pallas_call(first_kernel, grid_spec=pltpu.PrefetchScalarGridSpec(num_s...  2.39 us
  transfers between devices with their start and end apart: 36, of which 18 were waited for; matrix products, arithmetic and copies ran while one was open for 0% of the time, Pallas kernels for 19%

profile of v6, /device:TPU:1, one launch (start us, length us, event | category | flops | bytes accessed | tf_op | source)
XLA Modules:
  0.0 109.5 jit_solution(12221876399247179331)
XLA Ops:
  0.7 0.1 pad_add_fusion.1.coords_ref.refs_0_
  0.9 2.4 %first_blocks.1 = (f32[4,32,3968]{2,1,0:T(8,128)S(1)}, f32[4,32,3968]{2,1,0:T(8,128)S(1)}) custom-call(s32[9]{0:T(128)S(1)} %pad_add_fusion.1.coords_ref.refs_0_, bf16[4,4,2,32,3968]{4,3,2,1,0:T(8,128)(2,1)} %bitcast.20, bf16[4,4,2,32,3968]{4,3,2,1,0:T(8,128)(2,1)} %bitcast.21, bf16[4,4,2,32,3968]{4,3,2,1,0:T(8,128)(2,1)} %bitcast.22, ...), custom_call_target="tpu_custom_call" | custom-call | tf_op jit(solution)/shard_map/first_blocks/pallas_call | solution.py:158
  3.3 2.2 %collective-permute-start.7 = (f32[4,32,3968]{2,1,0:T(8,128)S(1)}, f32[4,32,3968]{2,1,0:T(8,128)S(1)}, u32[]{:S(2)}, u32[]{:S(2)}) collective-permute-start(f32[4,32,3968]{2,1,0:T(8,128)S(1)} %get-tuple-element.40.after_ref), channel_id=1, source_target_pairs={{0,4},{1,5},{2,6},{3,7},{4,8},{5,9},{6,10},{7,11},{8,12},{9,13},{1... | collective-permute-start | bytes 6094856 | tf_op jit(solution)/shard_map/ppermute | solution.py:38
  5.5 1.5 %collective-permute-start.8 = (f32[4,32,3968]{2,1,0:T(8,128)S(1)}, f32[4,32,3968]{2,1,0:T(8,128)S(1)}, u32[]{:S(2)}, u32[]{:S(2)}) collective-permute-start(f32[4,32,3968]{2,1,0:T(8,128)S(1)} %get-tuple-element.47), channel_id=1, source_target_pairs={{0,12},{1,13},{2,14},{3,15},{4,0},{5,1},{6,2},{7,3},{8,4},{9,5},{1... | collective-permute-start | bytes 6094856 | tf_op jit(solution)/shard_map/ppermute | solution.py:38
  7.0 7.1 %left_terms.1 = (f32[16,1024]{1,0:T(8,128)S(1)}, f32[16,1024]{1,0:T(8,128)S(1)}, bf16[1024,3968]{1,0:T(8,128)(2,1)S(1)}) custom-call(s32[3]{0:T(128)S(1)} %pad_add_fusion.after_ref.scalar_ref.refs_0_, bf16[1024,3968]{1,0:T(8,128)(2,1)} %bitcast.24, f32[32,3968]{1,0:T(8,128)S(1)} %bitcast.19, f32[64,3968]{1,0:T(8,128)S(1)} %bitcast.16, ...), custom_call_target="tpu_custom_call" | custom-call | tf_op jit(solution)/shard_map/left_terms/pallas_call | solution.py:256
  14.1 2.1 %collective-permute-start = (f32[16,1024]{1,0:T(8,128)S(1)}, f32[16,1024]{1,0:T(8,128)S(1)}, u32[]{:S(2)}, u32[]{:S(2)}) collective-permute-start(f32[16,1024]{1,0:T(8,128)S(1)} %get-tuple-element.42), channel_id=1, source_target_pairs={{0,16},{1,17},{2,18},{3,19},{4,20},{5,21},{6,22},{7,23},{8,24},{9,... | collective-permute-start | bytes 196616 | tf_op jit(solution)/shard_map/ppermute | solution.py:38
  16.1 0.9 collective-permute-done.refs_1_
  17.0 2.8 %collective-permute-start.1 = (f32[16,1024]{1,0:T(8,128)S(1)}, f32[16,1024]{1,0:T(8,128)S(1)}, u32[]{:S(2)}, u32[]{:S(2)}) collective-permute-start(f32[16,1024]{1,0:T(8,128)S(1)} %add.56.refs_2_.refs_0_), channel_id=1, source_target_pairs={{0,64},{1,65},{2,66},{3,67},{4,68},{5,69},{6,70},{7,71},{8,72},{9,... | collective-permute-start | bytes 196616 | tf_op jit(solution)/shard_map/ppermute | solution.py:38
  19.9 0.3 collective-permute-start.2
  20.2 2.4 %collective-permute-start.3 = (f32[16,1024]{1,0:T(8,128)S(1)}, f32[16,1024]{1,0:T(8,128)S(1)}, u32[]{:S(2)}, u32[]{:S(2)}) collective-permute-start(f32[16,1024]{1,0:T(8,128)S(1)} %add.56.refs_2_.refs_0_), channel_id=1, source_target_pairs={{0,96},{1,97},{2,98},{3,99},{4,100},{5,101},{6,102},{7,103},{8,104... | collective-permute-start | bytes 196616 | tf_op jit(solution)/shard_map/ppermute | solution.py:38
  22.5 1.0 combine.3
  23.6 0.9 collective-permute-done.2.refs_2_
  24.5 0.1 collective-permute-start.4
  24.6 2.8 %collective-permute-start.14 = (f32[4,32,3968]{2,1,0:T(8,128)S(1)}, f32[4,32,3968]{2,1,0:T(8,128)S(1)}, u32[]{:S(2)}, u32[]{:S(2)}) collective-permute-start(f32[4,32,3968]{2,1,0:T(8,128)S(1)} %get-tuple-element.55), channel_id=1, source_target_pairs={{0,12},{1,13},{2,14},{3,15},{4,0},{5,1},{6,2},{7,3},{8,4},{9,5},{1... | collective-permute-start | bytes 6094856 | tf_op jit(solution)/shard_map/ppermute | solution.py:38
  27.4 1.3 %collective-permute-done.4.refs_1_ = f32[16,1024]{1,0:T(8,128)S(1)} collective-permute-done((f32[16,1024]{1,0:T(8,128)S(1)}, f32[16,1024]{1,0:T(8,128)S(1)}, u32[]{:S(2)}, u32[]{:S(2)}) %collective-permute-start.4) | collective-permute-done | bytes 65568 | tf_op jit(solution)/shard_map/ppermute | solution.py:38
  28.8 2.2 %collective-permute-start.5 = (f32[16,1024]{1,0:T(8,128)S(1)}, f32[16,1024]{1,0:T(8,128)S(1)}, u32[]{:S(2)}, u32[]{:S(2)}) collective-permute-start(f32[16,1024]{1,0:T(8,128)S(1)} %add.57.refs_0_.refs_2_), channel_id=1, source_target_pairs={{0,3},{1,2},{2,1},{3,0},{4,7},{5,6},{6,5},{7,4},{8,11},{9,10},{10,... | collective-permute-start | bytes 196616 | tf_op jit(solution)/shard_map/ppermute | solution.py:38
  31.0 2.2 %collective-permute-done.5.refs_1_ = f32[16,1024]{1,0:T(8,128)S(1)} collective-permute-done((f32[16,1024]{1,0:T(8,128)S(1)}, f32[16,1024]{1,0:T(8,128)S(1)}, u32[]{:S(2)}, u32[]{:S(2)}) %collective-permute-start.5) | collective-permute-done | bytes 65568 | tf_op jit(solution)/shard_map/ppermute | solution.py:38
  33.2 4.3 %collective-permute-start.6 = (f32[16,1024]{1,0:T(8,128)S(1)}, f32[16,1024]{1,0:T(8,128)S(1)}, u32[]{:S(2)}, u32[]{:S(2)}) collective-permute-start(f32[16,1024]{1,0:T(8,128)S(1)} %add.58.refs_4_), channel_id=1, source_target_pairs={{0,16},{1,17},{2,18},{3,19},{4,20},{5,21},{6,22},{7,23},{8,24},{9,... | collective-permute-start | bytes 196616 | tf_op jit(solution)/shard_map/ppermute | solution.py:38
  37.5 1.1 %combine.4 = (f32[4,32,3968]{2,1,0:T(8,128)S(1)}, f32[4,32,3968]{2,1,0:T(8,128)S(1)}) custom-call(s32[9]{0:T(128)S(1)} %pad_add_fusion.1.coords_ref.refs_0_, bf16[4,4,4,16,3968]{4,3,2,1,0:T(8,128)(2,1)S(1)} %bitcast.12, f32[4,32,3968]{2,1,0:T(8,128)S(1)} %collective-permute-done.7.refs_1_, bf16[4,4,4,16,3968]{4,3,2,1,0:T(8,128)(2,1)S(1)} %bitcast.13, ...), custom_call_target="tpu_custom_call" | custom-call | tf_op jit(solution)/shard_map/combine/pallas_call | solution.py:125
  38.8 2.7 %collective-permute-start.11 = (f32[16,1024]{1,0:T(8,128)S(1)}, f32[16,1024]{1,0:T(8,128)S(1)}, u32[]{:S(2)}, u32[]{:S(2)}) collective-permute-start(f32[16,1024]{1,0:T(8,128)S(1)} %gate.4.refs_0_.refs_4_), channel_id=1, source_target_pairs={{0,3},{1,0},{2,1},{3,2},{4,7},{5,4},{6,5},{7,6},{8,11},{9,8},{10,9... | collective-permute-start | bytes 196616 | tf_op jit(solution)/shard_map/ppermute | solution.py:38
  41.4 0.6 collective-permute-start.9
  42.0 2.1 %collective-permute-done.10.refs_2_ = f32[16,1024]{1,0:T(8,128)S(1)} collective-permute-done((f32[16,1024]{1,0:T(8,128)S(1)}, f32[16,1024]{1,0:T(8,128)S(1)}, u32[]{:S(2)}, u32[]{:S(2)}) %collective-permute-start.10) | collective-permute-done | bytes 65568 | tf_op jit(solution)/shard_map/ppermute | solution.py:38
  44.1 3.0 %collective-permute-done.9.refs_1_ = f32[16,1024]{1,0:T(8,128)S(1)} collective-permute-done((f32[16,1024]{1,0:T(8,128)S(1)}, f32[16,1024]{1,0:T(8,128)S(1)}, u32[]{:S(2)}, u32[]{:S(2)}) %collective-permute-start.9) | collective-permute-done | bytes 65568 | tf_op jit(solution)/shard_map/ppermute | solution.py:38
  47.2 2.7 %collective-permute-start.26 = (f32[4,32,3968]{2,1,0:T(8,128)S(1)}, f32[4,32,3968]{2,1,0:T(8,128)S(1)}, u32[]{:S(2)}, u32[]{:S(2)}) collective-permute-start(f32[4,32,3968]{2,1,0:T(8,128)S(1)} %get-tuple-element.62), channel_id=1, source_target_pairs={{0,12},{1,13},{2,14},{3,15},{4,0},{5,1},{6,2},{7,3},{8,4},{9,5},{1... | collective-permute-start | bytes 6094856 | tf_op jit(solution)/shard_map/ppermute | solution.py:38
  49.9 2.0 %collective-permute-start.12 = (f32[16,1024]{1,0:T(8,128)S(1)}, f32[16,1024]{1,0:T(8,128)S(1)}, u32[]{:S(2)}, u32[]{:S(2)}) collective-permute-start(f32[16,1024]{1,0:T(8,128)S(1)} %add_four.6.refs_2_.refs_1_), channel_id=1, source_target_pairs={{0,16},{1,17},{2,18},{3,19},{4,20},{5,21},{6,22},{7,23},{8,24},{9,... | collective-permute-start | bytes 196616 | tf_op jit(solution)/shard_map/ppermute | solution.py:38
  51.9 0.9 collective-permute-done.12.refs_2_
  52.8 3.9 %orthonormal.1 = (f32[32,1024]{1,0:T(8,128)S(1)}, bf16[96,1024]{1,0:T(8,128)(2,1)S(1)}) custom-call(s32[3]{0:T(128)S(1)} %pad_add_fusion.after_ref.scalar_ref.refs_0_, f32[16,1024]{1,0:T(8,128)S(1)} %add_four.6.refs_2_.refs_1_, f32[16,1024]{1,0:T(8,128)S(1)} %collective-permute-done.12.refs_2_, f32[4,32,3968]{2,1,0:T(8,128)S(1)} %get-tuple-element.50.refs_3_), custom_call_target="tpu_custom_call" | custom-call | tf_op jit(solution)/shard_map/orthonormal/pallas_call | solution.py:78
  56.7 3.5 %right_terms.1 = (f32[16,4096]{1,0:T(8,128)S(1)}, f32[16,4096]{1,0:T(8,128)S(1)}) custom-call(s32[3]{0:T(128)S(1)} %pad_add_fusion.after_ref.scalar_ref.refs_0_, bf16[96,1024]{1,0:T(8,128)(2,1)S(1)} %get-tuple-element.51.pieces_ref, bf16[1024,3968]{1,0:T(8,128)(2,1)S(1)} %get-tuple-element.43.partial_ref, ...), custom_call_target="tpu_custom_call" | custom-call | tf_op jit(solution)/shard_map/right_terms/pallas_call | solution.py:344
  60.2 0.4 collective-permute-start.13
  60.7 1.1 %combine.5 = (f32[4,32,3968]{2,1,0:T(8,128)S(1)}, f32[4,32,3968]{2,1,0:T(8,128)S(1)}) custom-call(s32[9]{0:T(128)S(1)} %pad_add_fusion.1.coords_ref.refs_0_, bf16[4,4,4,16,3968]{4,3,2,1,0:T(8,128)(2,1)S(1)} %bitcast.14, f32[4,32,3968]{2,1,0:T(8,128)S(1)} %collective-permute-done.14.refs_1_, bf16[4,4,4,16,3968]{4,3,2,1,0:T(8,128)(2,1)S(1)} %bitcast.15, ...), custom_call_target="tpu_custom_call" | custom-call | tf_op jit(solution)/shard_map/combine/pallas_call | solution.py:125
  61.8 0.6 add_cut.1
  62.4 1.3 %collective-permute-start.16 = (f32[16,1024]{1,0:T(8,128)S(1)}, f32[16,1024]{1,0:T(8,128)S(1)}, u32[]{:S(2)}, u32[]{:S(2)}) collective-permute-start(f32[16,1024]{1,0:T(8,128)S(1)} %get-tuple-element.58), channel_id=1, source_target_pairs={{0,64},{1,65},{2,66},{3,67},{4,68},{5,69},{6,70},{7,71},{8,72},{9,... | collective-permute-start | bytes 196616 | tf_op jit(solution)/shard_map/ppermute | solution.py:38
  63.7 2.3 %collective-permute-start.17 = (f32[16,1024]{1,0:T(8,128)S(1)}, f32[16,1024]{1,0:T(8,128)S(1)}, u32[]{:S(2)}, u32[]{:S(2)}) collective-permute-start(f32[16,1024]{1,0:T(8,128)S(1)} %get-tuple-element.59), channel_id=1, source_target_pairs={{0,32},{1,33},{2,34},{3,35},{4,36},{5,37},{6,38},{7,39},{8,40},{9,... | collective-permute-start | bytes 196616 | tf_op jit(solution)/shard_map/ppermute | solution.py:38
  66.0 0.3 collective-permute-start.18
  66.3 0.8 collective-permute-done.16.refs_1_
  67.1 2.0 %collective-permute-done.17.refs_2_ = f32[16,1024]{1,0:T(8,128)S(1)} collective-permute-done((f32[16,1024]{1,0:T(8,128)S(1)}, f32[16,1024]{1,0:T(8,128)S(1)}, u32[]{:S(2)}, u32[]{:S(2)}) %collective-permute-start.17) | collective-permute-done | bytes 65568 | tf_op jit(solution)/shard_map/ppermute | solution.py:38
  69.1 0.3 collective-permute-done.18.refs_3_
  69.5 0.7 collective-permute-start.19
  70.2 0.7 collective-permute-start.20
  70.9 1.9 %collective-permute-start.21 = (f32[16,1024]{1,0:T(8,128)S(1)}, f32[16,1024]{1,0:T(8,128)S(1)}, u32[]{:S(2)}, u32[]{:S(2)}) collective-permute-start(f32[16,1024]{1,0:T(8,128)S(1)} %add_four.7.refs_0_.refs_4_), channel_id=1, source_target_pairs={{0,3},{1,0},{2,1},{3,2},{4,7},{5,4},{6,5},{7,6},{8,11},{9,8},{10,9... | collective-permute-start | bytes 196616 | tf_op jit(solution)/shard_map/ppermute | solution.py:38
  72.8 2.1 %collective-permute-done.19.refs_1_ = f32[16,1024]{1,0:T(8,128)S(1)} collective-permute-done((f32[16,1024]{1,0:T(8,128)S(1)}, f32[16,1024]{1,0:T(8,128)S(1)}, u32[]{:S(2)}, u32[]{:S(2)}) %collective-permute-start.19) | collective-permute-done | bytes 65568 | tf_op jit(solution)/shard_map/ppermute | solution.py:38
  75.0 1.2 %collective-permute-done.20.refs_2_ = f32[16,1024]{1,0:T(8,128)S(1)} collective-permute-done((f32[16,1024]{1,0:T(8,128)S(1)}, f32[16,1024]{1,0:T(8,128)S(1)}, u32[]{:S(2)}, u32[]{:S(2)}) %collective-permute-start.20) | collective-permute-done | bytes 65568 | tf_op jit(solution)/shard_map/ppermute | solution.py:38
  76.2 1.1 collective-permute-start.22
  77.2 1.1 %collective-permute-start.23 = (f32[16,1024]{1,0:T(8,128)S(1)}, f32[16,1024]{1,0:T(8,128)S(1)}, u32[]{:S(2)}, u32[]{:S(2)}) collective-permute-start(f32[16,1024]{1,0:T(8,128)S(1)} %add_four.8.refs_0_), channel_id=1, source_target_pairs={{0,4},{1,5},{2,6},{3,7},{4,8},{5,9},{6,10},{7,11},{8,12},{9,13},{1... | collective-permute-start | bytes 196616 | tf_op jit(solution)/shard_map/ppermute | solution.py:38
  78.4 1.5 %collective-permute-start.24 = (f32[16,1024]{1,0:T(8,128)S(1)}, f32[16,1024]{1,0:T(8,128)S(1)}, u32[]{:S(2)}, u32[]{:S(2)}) collective-permute-start(f32[16,1024]{1,0:T(8,128)S(1)} %add_four.8.refs_0_), channel_id=1, source_target_pairs={{0,12},{1,13},{2,14},{3,15},{4,0},{5,1},{6,2},{7,3},{8,4},{9,5},{1... | collective-permute-start | bytes 196616 | tf_op jit(solution)/shard_map/ppermute | solution.py:38
  79.9 1.2 %collective-permute-done.22.refs_5_.refs_1_ = f32[16,1024]{1,0:T(8,128)S(1)} collective-permute-done((f32[16,1024]{1,0:T(8,128)S(1)}, f32[16,1024]{1,0:T(8,128)S(1)}, u32[]{:S(2)}, u32[]{:S(2)}) %collective-permute-start.22) | collective-permute-done | bytes 65568 | tf_op jit(solution)/shard_map/ppermute | solution.py:38
  81.1 0.7 collective-permute-done.23.refs_6_.refs_2_
  81.8 0.7 turn_first.1
  82.4 0.3 collective-permute-start.29
  82.7 2.4 %collective-permute-start.30 = (f32[32,3968]{1,0:T(8,128)S(1)}, f32[32,3968]{1,0:T(8,128)S(1)}, u32[]{:S(2)}, u32[]{:S(2)}) collective-permute-start(f32[32,3968]{1,0:T(8,128)S(1)} %get-tuple-element.66), channel_id=1, source_target_pairs={{0,3},{1,0},{2,1},{3,2},{4,7},{5,4},{6,5},{7,6},{8,11},{9,8},{10,9... | collective-permute-start | bytes 1523720 | tf_op jit(solution)/shard_map/ppermute | solution.py:38
  85.2 2.4 %collective-permute-start.27 = (f32[16,1024]{1,0:T(8,128)S(1)}, f32[16,1024]{1,0:T(8,128)S(1)}, u32[]{:S(2)}, u32[]{:S(2)}) collective-permute-start(f32[16,1024]{1,0:T(8,128)S(1)} %add_four.9.refs_0_.refs_2_), channel_id=1, source_target_pairs={{0,96},{1,97},{2,98},{3,99},{4,100},{5,101},{6,102},{7,103},{8,104... | collective-permute-start | bytes 196616 | tf_op jit(solution)/shard_map/ppermute | solution.py:38
  87.6 0.9 turn_rest.1
  88.5 2.7 %collective-permute-start.33 = (f32[32,3968]{1,0:T(8,128)S(1)}, f32[32,3968]{1,0:T(8,128)S(1)}, u32[]{:S(2)}, u32[]{:S(2)}) collective-permute-start(f32[32,3968]{1,0:T(8,128)S(1)} %get-tuple-element.70), channel_id=1, source_target_pairs={{0,3},{1,0},{2,1},{3,2},{4,7},{5,4},{6,5},{7,6},{8,11},{9,8},{10,9... | collective-permute-start | bytes 1523720 | tf_op jit(solution)/shard_map/ppermute | solution.py:38
  91.2 0.6 collective-permute-done.29.refs_1_
  91.8 0.1 ring_add.1
  92.0 0.3 collective-permute-start.34
  92.3 2.5 %collective-permute-start.35 = (f32[32,3968]{1,0:T(8,128)S(1)}, f32[32,3968]{1,0:T(8,128)S(1)}, u32[]{:S(2)}, u32[]{:S(2)}) collective-permute-start(f32[32,3968]{1,0:T(8,128)S(1)} %get-tuple-element.73), channel_id=1, source_target_pairs={{0,3},{1,0},{2,1},{3,2},{4,7},{5,4},{6,5},{7,6},{8,11},{9,8},{10,9... | collective-permute-start | bytes 1523720 | tf_op jit(solution)/shard_map/ppermute | solution.py:38
  94.8 0.2 collective-permute-start.28
  94.9 3.9 %collective-permute-done.28.refs_2_ = f32[16,2048]{1,0:T(8,128)S(1)} collective-permute-done((f32[16,2048]{1,0:T(8,128)S(1)}, f32[16,2048]{1,0:T(8,128)S(1)}, u32[]{:S(2)}, u32[]{:S(2)}) %collective-permute-start.28) | collective-permute-done | bytes 131104 | tf_op jit(solution)/shard_map/ppermute | solution.py:38
  98.9 0.6 join.3.refs_1_.refs_7_.mine_ref
  99.5 6.3 %collective-permute-start.31 = (f32[16,4096]{1,0:T(8,128)S(1)}, f32[16,4096]{1,0:T(8,128)S(1)}, u32[]{:S(2)}, u32[]{:S(2)}) collective-permute-start(f32[16,4096]{1,0:T(8,128)S(1)} %join.3.refs_1_.refs_7_.mine_ref), channel_id=1, source_target_pairs={{0,16},{1,17},{2,18},{3,19},{4,20},{5,21},{6,22},{7,23},{8,24},{9,... | collective-permute-start | bytes 786440 | tf_op jit(solution)/shard_map/ppermute | solution.py:38
  105.8 1.1 nearly.1
  106.8 0.1 collective-permute-done.31.other_ref
  106.9 2.4 %finish.1 = (bf16[64,3968]{1,0:T(8,128)(2,1)}, f32[64,3968]{1,0:T(8,128)}, f32[32,3968]{1,0:T(8,128)}) custom-call(s32[3]{0:T(128)S(1)} %pad_add_fusion.after_ref.scalar_ref.refs_0_, f32[16,4096]{1,0:T(8,128)S(1)} %join.3.refs_1_.refs_7_.mine_ref, f32[16,4096]{1,0:T(8,128)S(1)} %collective-permute-done.31.other_ref, ...), custom_call_target="tpu_custom_call" | custom-call | tf_op jit(solution)/shard_map/finish/pallas_call | solution.py:482
  (41 shorter events, 0.6 us)
Async XLA Ops:
  0.9 6.1 %copy-start = (f32[1,64,3968]{2,1,0:T(8,128)S(1)}, f32[1,64,3968]{2,1,0:T(8,128)}, u32[]{:S(2)}) copy-start(f32[1,64,3968]{2,1,0:T(8,128)} %param.4) | copy-start | bytes 3047428
  0.9 6.1 %copy-start.1 = (f32[3968,32]{0,1:T(8,128)S(1)}, f32[3968,32]{0,1:T(8,128)}, u32[]{:S(2)}) copy-start(f32[3968,32]{0,1:T(8,128)} %param.5) | copy-start | bytes 1523716
  3.3 34.3 %collective-permute-start.7 = (f32[4,32,3968]{2,1,0:T(8,128)S(1)}, f32[4,32,3968]{2,1,0:T(8,128)S(1)}, u32[]{:S(2)}, u32[]{:S(2)}) collective-permute-start(f32[4,32,3968]{2,1,0:T(8,128)S(1)} %get-tuple-element.40.after_ref), channel_id=1, source_target_pairs={{0,4},{1,5},{2,6},{3,7},{4,8},{5,9},{6,10},{7,11},{8,12},{9,13},{1... | collective-permute-start | bytes 6094856 | tf_op jit(solution)/shard_map/ppermute | solution.py:38
  5.5 32.1 %collective-permute-start.8 = (f32[4,32,3968]{2,1,0:T(8,128)S(1)}, f32[4,32,3968]{2,1,0:T(8,128)S(1)}, u32[]{:S(2)}, u32[]{:S(2)}) collective-permute-start(f32[4,32,3968]{2,1,0:T(8,128)S(1)} %get-tuple-element.47), channel_id=1, source_target_pairs={{0,12},{1,13},{2,14},{3,15},{4,0},{5,1},{6,2},{7,3},{8,4},{9,5},{1... | collective-permute-start | bytes 6094856 | tf_op jit(solution)/shard_map/ppermute | solution.py:38
  14.1 3.0 %collective-permute-start = (f32[16,1024]{1,0:T(8,128)S(1)}, f32[16,1024]{1,0:T(8,128)S(1)}, u32[]{:S(2)}, u32[]{:S(2)}) collective-permute-start(f32[16,1024]{1,0:T(8,128)S(1)} %get-tuple-element.42), channel_id=1, source_target_pairs={{0,16},{1,17},{2,18},{3,19},{4,20},{5,21},{6,22},{7,23},{8,24},{9,... | collective-permute-start | bytes 196616 | tf_op jit(solution)/shard_map/ppermute | solution.py:38
  17.0 6.5 %collective-permute-start.1 = (f32[16,1024]{1,0:T(8,128)S(1)}, f32[16,1024]{1,0:T(8,128)S(1)}, u32[]{:S(2)}, u32[]{:S(2)}) collective-permute-start(f32[16,1024]{1,0:T(8,128)S(1)} %add.56.refs_2_.refs_0_), channel_id=1, source_target_pairs={{0,64},{1,65},{2,66},{3,67},{4,68},{5,69},{6,70},{7,71},{8,72},{9,... | collective-permute-start | bytes 196616 | tf_op jit(solution)/shard_map/ppermute | solution.py:38
  19.9 4.6 %collective-permute-start.2 = (f32[16,1024]{1,0:T(8,128)S(1)}, f32[16,1024]{1,0:T(8,128)S(1)}, u32[]{:S(2)}, u32[]{:S(2)}) collective-permute-start(f32[16,1024]{1,0:T(8,128)S(1)} %add.56.refs_2_.refs_0_), channel_id=1, source_target_pairs={{0,32},{1,33},{2,34},{3,35},{4,36},{5,37},{6,38},{7,39},{8,40},{9,... | collective-permute-start | bytes 196616 | tf_op jit(solution)/shard_map/ppermute | solution.py:38
  20.2 4.3 %collective-permute-start.3 = (f32[16,1024]{1,0:T(8,128)S(1)}, f32[16,1024]{1,0:T(8,128)S(1)}, u32[]{:S(2)}, u32[]{:S(2)}) collective-permute-start(f32[16,1024]{1,0:T(8,128)S(1)} %add.56.refs_2_.refs_0_), channel_id=1, source_target_pairs={{0,96},{1,97},{2,98},{3,99},{4,100},{5,101},{6,102},{7,103},{8,104... | collective-permute-start | bytes 196616 | tf_op jit(solution)/shard_map/ppermute | solution.py:38
  24.5 4.3 %collective-permute-start.4 = (f32[16,1024]{1,0:T(8,128)S(1)}, f32[16,1024]{1,0:T(8,128)S(1)}, u32[]{:S(2)}, u32[]{:S(2)}) collective-permute-start(f32[16,1024]{1,0:T(8,128)S(1)} %add_four.5.refs_2_.refs_0_), channel_id=1, source_target_pairs={{0,1},{1,0},{2,3},{3,2},{4,5},{5,4},{6,7},{7,6},{8,9},{9,8},{10,11... | collective-permute-start | bytes 196616 | tf_op jit(solution)/shard_map/ppermute | solution.py:38
  24.6 36.0 %collective-permute-start.14 = (f32[4,32,3968]{2,1,0:T(8,128)S(1)}, f32[4,32,3968]{2,1,0:T(8,128)S(1)}, u32[]{:S(2)}, u32[]{:S(2)}) collective-permute-start(f32[4,32,3968]{2,1,0:T(8,128)S(1)} %get-tuple-element.55), channel_id=1, source_target_pairs={{0,12},{1,13},{2,14},{3,15},{4,0},{5,1},{6,2},{7,3},{8,4},{9,5},{1... | collective-permute-start | bytes 6094856 | tf_op jit(solution)/shard_map/ppermute | solution.py:38
  27.4 33.2 %collective-permute-start.15 = (f32[4,32,3968]{2,1,0:T(8,128)S(1)}, f32[4,32,3968]{2,1,0:T(8,128)S(1)}, u32[]{:S(2)}, u32[]{:S(2)}) collective-permute-start(f32[4,32,3968]{2,1,0:T(8,128)S(1)} %get-tuple-element.46.refs_2_), channel_id=1, source_target_pairs={{0,4},{1,5},{2,6},{3,7},{4,8},{5,9},{6,10},{7,11},{8,12},{9,13},{1... | collective-permute-start | bytes 6094856 | tf_op jit(solution)/shard_map/ppermute | solution.py:38
  28.8 4.4 %collective-permute-start.5 = (f32[16,1024]{1,0:T(8,128)S(1)}, f32[16,1024]{1,0:T(8,128)S(1)}, u32[]{:S(2)}, u32[]{:S(2)}) collective-permute-start(f32[16,1024]{1,0:T(8,128)S(1)} %add.57.refs_0_.refs_2_), channel_id=1, source_target_pairs={{0,3},{1,2},{2,1},{3,0},{4,7},{5,6},{6,5},{7,4},{8,11},{9,10},{10,... | collective-permute-start | bytes 196616 | tf_op jit(solution)/shard_map/ppermute | solution.py:38
  33.2 5.5 %collective-permute-start.6 = (f32[16,1024]{1,0:T(8,128)S(1)}, f32[16,1024]{1,0:T(8,128)S(1)}, u32[]{:S(2)}, u32[]{:S(2)}) collective-permute-start(f32[16,1024]{1,0:T(8,128)S(1)} %add.58.refs_4_), channel_id=1, source_target_pairs={{0,16},{1,17},{2,18},{3,19},{4,20},{5,21},{6,22},{7,23},{8,24},{9,... | collective-permute-start | bytes 196616 | tf_op jit(solution)/shard_map/ppermute | solution.py:38
  38.7 5.5 %collective-permute-start.10 = (f32[16,1024]{1,0:T(8,128)S(1)}, f32[16,1024]{1,0:T(8,128)S(1)}, u32[]{:S(2)}, u32[]{:S(2)}) collective-permute-start(f32[16,1024]{1,0:T(8,128)S(1)} %gate.4.refs_0_.refs_4_), channel_id=1, source_target_pairs={{0,1},{1,2},{2,3},{3,0},{4,5},{5,6},{6,7},{7,4},{8,9},{9,10},{10,1... | collective-permute-start | bytes 196616 | tf_op jit(solution)/shard_map/ppermute | solution.py:38
  38.8 5.4 %collective-permute-start.11 = (f32[16,1024]{1,0:T(8,128)S(1)}, f32[16,1024]{1,0:T(8,128)S(1)}, u32[]{:S(2)}, u32[]{:S(2)}) collective-permute-start(f32[16,1024]{1,0:T(8,128)S(1)} %gate.4.refs_0_.refs_4_), channel_id=1, source_target_pairs={{0,3},{1,0},{2,1},{3,2},{4,7},{5,4},{6,5},{7,6},{8,11},{9,8},{10,9... | collective-permute-start | bytes 196616 | tf_op jit(solution)/shard_map/ppermute | solution.py:38
  41.4 5.7 %collective-permute-start.9 = (f32[16,1024]{1,0:T(8,128)S(1)}, f32[16,1024]{1,0:T(8,128)S(1)}, u32[]{:S(2)}, u32[]{:S(2)}) collective-permute-start(f32[16,1024]{1,0:T(8,128)S(1)} %gate.4.refs_0_.refs_4_), channel_id=1, source_target_pairs={{0,2},{1,3},{2,0},{3,1},{4,6},{5,7},{6,4},{7,5},{8,10},{9,11},{10,... | collective-permute-start | bytes 196616 | tf_op jit(solution)/shard_map/ppermute | solution.py:38
  47.1 34.6 %collective-permute-start.25 = (f32[4,32,3968]{2,1,0:T(8,128)S(1)}, f32[4,32,3968]{2,1,0:T(8,128)S(1)}, u32[]{:S(2)}, u32[]{:S(2)}) collective-permute-start(f32[4,32,3968]{2,1,0:T(8,128)S(1)} %get-tuple-element.50.refs_3_), channel_id=1, source_target_pairs={{0,4},{1,5},{2,6},{3,7},{4,8},{5,9},{6,10},{7,11},{8,12},{9,13},{1... | collective-permute-start | bytes 6094856 | tf_op jit(solution)/shard_map/ppermute | solution.py:38
  47.2 34.5 %collective-permute-start.26 = (f32[4,32,3968]{2,1,0:T(8,128)S(1)}, f32[4,32,3968]{2,1,0:T(8,128)S(1)}, u32[]{:S(2)}, u32[]{:S(2)}) collective-permute-start(f32[4,32,3968]{2,1,0:T(8,128)S(1)} %get-tuple-element.62), channel_id=1, source_target_pairs={{0,12},{1,13},{2,14},{3,15},{4,0},{5,1},{6,2},{7,3},{8,4},{9,5},{1... | collective-permute-start | bytes 6094856 | tf_op jit(solution)/shard_map/ppermute | solution.py:38
  49.9 2.9 %collective-permute-start.12 = (f32[16,1024]{1,0:T(8,128)S(1)}, f32[16,1024]{1,0:T(8,128)S(1)}, u32[]{:S(2)}, u32[]{:S(2)}) collective-permute-start(f32[16,1024]{1,0:T(8,128)S(1)} %add_four.6.refs_2_.refs_1_), channel_id=1, source_target_pairs={{0,16},{1,17},{2,18},{3,19},{4,20},{5,21},{6,22},{7,23},{8,24},{9,... | collective-permute-start | bytes 196616 | tf_op jit(solution)/shard_map/ppermute | solution.py:38
  60.2 1.6 %collective-permute-start.13 = (f32[16,4096]{1,0:T(8,128)S(1)}, f32[16,4096]{1,0:T(8,128)S(1)}, u32[]{:S(2)}, u32[]{:S(2)}) collective-permute-start(f32[16,4096]{1,0:T(8,128)S(1)} %get-tuple-element.54.refs_4_), channel_id=1, source_target_pairs={{0,16},{1,17},{2,18},{3,19},{4,20},{5,21},{6,22},{7,23},{8,24},{9,... | collective-permute-start | bytes 786440 | tf_op jit(solution)/shard_map/ppermute | solution.py:38
  62.4 4.7 %collective-permute-start.16 = (f32[16,1024]{1,0:T(8,128)S(1)}, f32[16,1024]{1,0:T(8,128)S(1)}, u32[]{:S(2)}, u32[]{:S(2)}) collective-permute-start(f32[16,1024]{1,0:T(8,128)S(1)} %get-tuple-element.58), channel_id=1, source_target_pairs={{0,64},{1,65},{2,66},{3,67},{4,68},{5,69},{6,70},{7,71},{8,72},{9,... | collective-permute-start | bytes 196616 | tf_op jit(solution)/shard_map/ppermute | solution.py:38
  63.7 5.5 %collective-permute-start.17 = (f32[16,1024]{1,0:T(8,128)S(1)}, f32[16,1024]{1,0:T(8,128)S(1)}, u32[]{:S(2)}, u32[]{:S(2)}) collective-permute-start(f32[16,1024]{1,0:T(8,128)S(1)} %get-tuple-element.59), channel_id=1, source_target_pairs={{0,32},{1,33},{2,34},{3,35},{4,36},{5,37},{6,38},{7,39},{8,40},{9,... | collective-permute-start | bytes 196616 | tf_op jit(solution)/shard_map/ppermute | solution.py:38
  66.0 3.5 %collective-permute-start.18 = (f32[16,1024]{1,0:T(8,128)S(1)}, f32[16,1024]{1,0:T(8,128)S(1)}, u32[]{:S(2)}, u32[]{:S(2)}) collective-permute-start(f32[16,1024]{1,0:T(8,128)S(1)} %get-tuple-element.60), channel_id=1, source_target_pairs={{0,96},{1,97},{2,98},{3,99},{4,100},{5,101},{6,102},{7,103},{8,104... | collective-permute-start | bytes 196616 | tf_op jit(solution)/shard_map/ppermute | solution.py:38
  69.5 5.5 %collective-permute-start.19 = (f32[16,1024]{1,0:T(8,128)S(1)}, f32[16,1024]{1,0:T(8,128)S(1)}, u32[]{:S(2)}, u32[]{:S(2)}) collective-permute-start(f32[16,1024]{1,0:T(8,128)S(1)} %add_four.7.refs_0_.refs_4_), channel_id=1, source_target_pairs={{0,2},{1,3},{2,0},{3,1},{4,6},{5,7},{6,4},{7,5},{8,10},{9,11},{10,... | collective-permute-start | bytes 196616 | tf_op jit(solution)/shard_map/ppermute | solution.py:38
  70.2 6.0 %collective-permute-start.20 = (f32[16,1024]{1,0:T(8,128)S(1)}, f32[16,1024]{1,0:T(8,128)S(1)}, u32[]{:S(2)}, u32[]{:S(2)}) collective-permute-start(f32[16,1024]{1,0:T(8,128)S(1)} %add_four.7.refs_0_.refs_4_), channel_id=1, source_target_pairs={{0,1},{1,2},{2,3},{3,0},{4,5},{5,6},{6,7},{7,4},{8,9},{9,10},{10,1... | collective-permute-start | bytes 196616 | tf_op jit(solution)/shard_map/ppermute | solution.py:38
  70.9 5.2 %collective-permute-start.21 = (f32[16,1024]{1,0:T(8,128)S(1)}, f32[16,1024]{1,0:T(8,128)S(1)}, u32[]{:S(2)}, u32[]{:S(2)}) collective-permute-start(f32[16,1024]{1,0:T(8,128)S(1)} %add_four.7.refs_0_.refs_4_), channel_id=1, source_target_pairs={{0,3},{1,0},{2,1},{3,2},{4,7},{5,4},{6,5},{7,6},{8,11},{9,8},{10,9... | collective-permute-start | bytes 196616 | tf_op jit(solution)/shard_map/ppermute | solution.py:38
  76.2 4.9 %collective-permute-start.22 = (f32[16,1024]{1,0:T(8,128)S(1)}, f32[16,1024]{1,0:T(8,128)S(1)}, u32[]{:S(2)}, u32[]{:S(2)}) collective-permute-start(f32[16,1024]{1,0:T(8,128)S(1)} %add_four.8.refs_0_), channel_id=1, source_target_pairs={{0,8},{1,9},{2,10},{3,11},{4,12},{5,13},{6,14},{7,15},{8,0},{9,1},... | collective-permute-start | bytes 196616 | tf_op jit(solution)/shard_map/ppermute | solution.py:38
  77.2 4.5 %collective-permute-start.23 = (f32[16,1024]{1,0:T(8,128)S(1)}, f32[16,1024]{1,0:T(8,128)S(1)}, u32[]{:S(2)}, u32[]{:S(2)}) collective-permute-start(f32[16,1024]{1,0:T(8,128)S(1)} %add_four.8.refs_0_), channel_id=1, source_target_pairs={{0,4},{1,5},{2,6},{3,7},{4,8},{5,9},{6,10},{7,11},{8,12},{9,13},{1... | collective-permute-start | bytes 196616 | tf_op jit(solution)/shard_map/ppermute | solution.py:38
  78.4 3.4 %collective-permute-start.24 = (f32[16,1024]{1,0:T(8,128)S(1)}, f32[16,1024]{1,0:T(8,128)S(1)}, u32[]{:S(2)}, u32[]{:S(2)}) collective-permute-start(f32[16,1024]{1,0:T(8,128)S(1)} %add_four.8.refs_0_), channel_id=1, source_target_pairs={{0,12},{1,13},{2,14},{3,15},{4,0},{5,1},{6,2},{7,3},{8,4},{9,5},{1... | collective-permute-start | bytes 196616 | tf_op jit(solution)/shard_map/ppermute | solution.py:38
  82.4 9.4 %collective-permute-start.29 = (f32[32,3968]{1,0:T(8,128)S(1)}, f32[32,3968]{1,0:T(8,128)S(1)}, u32[]{:S(2)}, u32[]{:S(2)}) collective-permute-start(f32[32,3968]{1,0:T(8,128)S(1)} %get-tuple-element.63.refs_4_.refs_5_), channel_id=1, source_target_pairs={{0,1},{1,2},{2,3},{3,0},{4,5},{5,6},{6,7},{7,4},{8,9},{9,10},{10,1... | collective-permute-start | bytes 1523720 | tf_op jit(solution)/shard_map/ppermute | solution.py:38
  82.7 9.1 %collective-permute-start.30 = (f32[32,3968]{1,0:T(8,128)S(1)}, f32[32,3968]{1,0:T(8,128)S(1)}, u32[]{:S(2)}, u32[]{:S(2)}) collective-permute-start(f32[32,3968]{1,0:T(8,128)S(1)} %get-tuple-element.66), channel_id=1, source_target_pairs={{0,3},{1,0},{2,1},{3,2},{4,7},{5,4},{6,5},{7,6},{8,11},{9,8},{10,9... | collective-permute-start | bytes 1523720 | tf_op jit(solution)/shard_map/ppermute | solution.py:38
  85.2 6.0 %collective-permute-start.27 = (f32[16,1024]{1,0:T(8,128)S(1)}, f32[16,1024]{1,0:T(8,128)S(1)}, u32[]{:S(2)}, u32[]{:S(2)}) collective-permute-start(f32[16,1024]{1,0:T(8,128)S(1)} %add_four.9.refs_0_.refs_2_), channel_id=1, source_target_pairs={{0,96},{1,97},{2,98},{3,99},{4,100},{5,101},{6,102},{7,103},{8,104... | collective-permute-start | bytes 196616 | tf_op jit(solution)/shard_map/ppermute | solution.py:38
  88.5 17.3 %collective-permute-start.32 = (f32[32,3968]{1,0:T(8,128)S(1)}, f32[32,3968]{1,0:T(8,128)S(1)}, u32[]{:S(2)}, u32[]{:S(2)}) collective-permute-start(f32[32,3968]{1,0:T(8,128)S(1)} %get-tuple-element.69), channel_id=1, source_target_pairs={{0,1},{1,2},{2,3},{3,0},{4,5},{5,6},{6,7},{7,4},{8,9},{9,10},{10,1... | collective-permute-start | bytes 1523720 | tf_op jit(solution)/shard_map/ppermute | solution.py:38
  88.5 17.2 %collective-permute-start.33 = (f32[32,3968]{1,0:T(8,128)S(1)}, f32[32,3968]{1,0:T(8,128)S(1)}, u32[]{:S(2)}, u32[]{:S(2)}) collective-permute-start(f32[32,3968]{1,0:T(8,128)S(1)} %get-tuple-element.70), channel_id=1, source_target_pairs={{0,3},{1,0},{2,1},{3,2},{4,7},{5,4},{6,5},{7,6},{8,11},{9,8},{10,9... | collective-permute-start | bytes 1523720 | tf_op jit(solution)/shard_map/ppermute | solution.py:38
  92.0 15.0 %collective-permute-start.34 = (f32[32,3968]{1,0:T(8,128)S(1)}, f32[32,3968]{1,0:T(8,128)S(1)}, u32[]{:S(2)}, u32[]{:S(2)}) collective-permute-start(f32[32,3968]{1,0:T(8,128)S(1)} %get-tuple-element.67.refs_3_), channel_id=1, source_target_pairs={{0,1},{1,2},{2,3},{3,0},{4,5},{5,6},{6,7},{7,4},{8,9},{9,10},{10,1... | collective-permute-start | bytes 1523720 | tf_op jit(solution)/shard_map/ppermute | solution.py:38
  92.3 14.6 %collective-permute-start.35 = (f32[32,3968]{1,0:T(8,128)S(1)}, f32[32,3968]{1,0:T(8,128)S(1)}, u32[]{:S(2)}, u32[]{:S(2)}) collective-permute-start(f32[32,3968]{1,0:T(8,128)S(1)} %get-tuple-element.73), channel_id=1, source_target_pairs={{0,3},{1,0},{2,1},{3,2},{4,7},{5,4},{6,5},{7,6},{8,11},{9,8},{10,9... | collective-permute-start | bytes 1523720 | tf_op jit(solution)/shard_map/ppermute | solution.py:38
  94.8 4.1 %collective-permute-start.28 = (f32[16,2048]{1,0:T(8,128)S(1)}, f32[16,2048]{1,0:T(8,128)S(1)}, u32[]{:S(2)}, u32[]{:S(2)}) collective-permute-start(f32[16,2048]{1,0:T(8,128)S(1)} %join.2.refs_4_.refs_1_), channel_id=1, source_target_pairs={{0,32},{1,33},{2,34},{3,35},{4,36},{5,37},{6,38},{7,39},{8,40},{9,... | collective-permute-start | bytes 393224 | tf_op jit(solution)/shard_map/ppermute | solution.py:38
  99.5 7.5 %collective-permute-start.31 = (f32[16,4096]{1,0:T(8,128)S(1)}, f32[16,4096]{1,0:T(8,128)S(1)}, u32[]{:S(2)}, u32[]{:S(2)}) collective-permute-start(f32[16,4096]{1,0:T(8,128)S(1)} %join.3.refs_1_.refs_7_.mine_ref), channel_id=1, source_target_pairs={{0,16},{1,17},{2,18},{3,19},{4,20},{5,21},{6,22},{7,23},{8,24},{9,... | collective-permute-start | bytes 786440 | tf_op jit(solution)/shard_map/ppermute | solution.py:38

commit v7 on v6

--- a/solution.py
+++ b/solution.py
@@ -537,7 +537,7 @@
     part = sum_four(part, along_second, part)
     came = [along_first(part, step) for step in (2, 1, -1)]
     up, down, up_local, down_local, kept_up, kept_down, kept = turn(
-        coords, [(held[0], came3[0]), (held[1], came3[1])], came
+        coords, [(held[0], came3[0]), (held[1], came3[1])], came[:2]
     )
     came4 = [along_second(up, 1), along_second(down, -1)]
     came5 = [along_second(up_local, 1), along_second(down_local, -1)]

time: 111 us -> 116 us (1.045)
  waiting for transfers between devices: 24.4 us -> 27.6 us
  starting transfers between devices: 57.4 us -> 59.8 us
    ppermute x36, waiting for transfers between devices: 24.4 us -> 27.6 us  [moved(): lax.ppermute(values, BOTH, [(place(*spot), place(*route(*spot))) for spot...]
    ppermute x36, starting transfers between devices: 57.4 us -> 59.8 us  [moved(): lax.ppermute(values, BOTH, [(place(*spot), place(*route(*spot))) for spot...]
  transfers between devices with their start and end apart: 36 -> 36, of which waited for: 18 -> 18; matrix products, arithmetic and copies ran while one was open for 0% -> 0% of each run, Pallas kernels for 19% -> 18%
where the time goes in v7:
time: 116 us; the launch traced here: 115 us
  starting transfers between devices  59.8 us (52%)
  waiting for transfers between devices  27.6 us (24%)
  Pallas kernels  26.5 us (23%)
    ppermute x36, starting transfers between devices, moved(): lax.ppermute(values, BOTH, [(place(*spot), place(*route(*spot))) for spot...  59.8 us
    ppermute x36, waiting for transfers between devices, moved(): lax.ppermute(values, BOTH, [(place(*spot), place(*route(*spot))) for spot...  27.6 us
    pallas_call x16, Pallas kernels, run(): pl.pallas_call(body, in_specs=[SCALARS] * len(scalars) + [WHOLE] * len(op...  7.84 us
    pallas_call x1, Pallas kernels, left_terms(): pl.pallas_call(left_kernel, grid=(SIDE,), in_specs=[SCALARS, pl.BlockSpec...  7.09 us
    pallas_call x1, Pallas kernels, right_terms(): pl.pallas_call(right_kernel, grid=(SIDE,), in_specs=[SCALARS, pl.BlockSpe...  3.46 us
    pallas_call x3, Pallas kernels, combine(): pl.pallas_call(functools.partial(combine_kernel, arity), grid_spec=pltpu....  3.22 us
    pallas_call x1, Pallas kernels, finish(): pl.pallas_call(functools.partial(finish_kernel, replicas), in_specs=[SCAL...  2.45 us
    pallas_call x1, Pallas kernels, first_blocks(): pl.pallas_call(first_kernel, grid_spec=pltpu.PrefetchScalarGridSpec(num_s...  2.39 us
  transfers between devices with their start and end apart: 36, of which 18 were waited for; matrix products, arithmetic and copies ran while one was open for 0% of the time, Pallas kernels for 18%

profile of v7, /device:TPU:1, one launch (start us, length us, event | category | flops | bytes accessed | tf_op | source)
XLA Modules:
  0.0 115.2 jit_solution(18399115300373767477)
XLA Ops:
  0.7 0.1 pad_add_fusion.1.coords_ref.refs_0_
  0.8 0.1 pad_add_fusion.after_ref.scalar_ref.refs_0_
  0.9 2.4 %first_blocks.1 = (f32[4,32,3968]{2,1,0:T(8,128)S(1)}, f32[4,32,3968]{2,1,0:T(8,128)S(1)}) custom-call(s32[9]{0:T(128)S(1)} %pad_add_fusion.1.coords_ref.refs_0_, bf16[4,4,2,32,3968]{4,3,2,1,0:T(8,128)(2,1)} %bitcast.20, bf16[4,4,2,32,3968]{4,3,2,1,0:T(8,128)(2,1)} %bitcast.21, bf16[4,4,2,32,3968]{4,3,2,1,0:T(8,128)(2,1)} %bitcast.22, ...), custom_call_target="tpu_custom_call" | custom-call | tf_op jit(solution)/shard_map/first_blocks/pallas_call | solution.py:158
  3.3 2.2 %collective-permute-start.7 = (f32[4,32,3968]{2,1,0:T(8,128)S(1)}, f32[4,32,3968]{2,1,0:T(8,128)S(1)}, u32[]{:S(2)}, u32[]{:S(2)}) collective-permute-start(f32[4,32,3968]{2,1,0:T(8,128)S(1)} %get-tuple-element.40.after_ref), channel_id=1, source_target_pairs={{0,4},{1,5},{2,6},{3,7},{4,8},{5,9},{6,10},{7,11},{8,12},{9,13},{1... | collective-permute-start | bytes 6094856 | tf_op jit(solution)/shard_map/ppermute | solution.py:38
  5.5 1.5 %collective-permute-start.8 = (f32[4,32,3968]{2,1,0:T(8,128)S(1)}, f32[4,32,3968]{2,1,0:T(8,128)S(1)}, u32[]{:S(2)}, u32[]{:S(2)}) collective-permute-start(f32[4,32,3968]{2,1,0:T(8,128)S(1)} %get-tuple-element.47), channel_id=1, source_target_pairs={{0,12},{1,13},{2,14},{3,15},{4,0},{5,1},{6,2},{7,3},{8,4},{9,5},{1... | collective-permute-start | bytes 6094856 | tf_op jit(solution)/shard_map/ppermute | solution.py:38
  7.0 7.1 %left_terms.1 = (f32[16,1024]{1,0:T(8,128)S(1)}, f32[16,1024]{1,0:T(8,128)S(1)}, bf16[1024,3968]{1,0:T(8,128)(2,1)S(1)}) custom-call(s32[3]{0:T(128)S(1)} %pad_add_fusion.after_ref.scalar_ref.refs_0_, bf16[1024,3968]{1,0:T(8,128)(2,1)} %bitcast.24, f32[32,3968]{1,0:T(8,128)S(1)} %bitcast.19, f32[64,3968]{1,0:T(8,128)S(1)} %bitcast.16, ...), custom_call_target="tpu_custom_call" | custom-call | tf_op jit(solution)/shard_map/left_terms/pallas_call | solution.py:256
  14.1 2.1 %collective-permute-start = (f32[16,1024]{1,0:T(8,128)S(1)}, f32[16,1024]{1,0:T(8,128)S(1)}, u32[]{:S(2)}, u32[]{:S(2)}) collective-permute-start(f32[16,1024]{1,0:T(8,128)S(1)} %get-tuple-element.42), channel_id=1, source_target_pairs={{0,16},{1,17},{2,18},{3,19},{4,20},{5,21},{6,22},{7,23},{8,24},{9,... | collective-permute-start | bytes 196616 | tf_op jit(solution)/shard_map/ppermute | solution.py:38
  16.1 0.9 collective-permute-done.refs_1_
  17.0 2.8 %collective-permute-start.1 = (f32[16,1024]{1,0:T(8,128)S(1)}, f32[16,1024]{1,0:T(8,128)S(1)}, u32[]{:S(2)}, u32[]{:S(2)}) collective-permute-start(f32[16,1024]{1,0:T(8,128)S(1)} %add.56.refs_2_.refs_0_), channel_id=1, source_target_pairs={{0,64},{1,65},{2,66},{3,67},{4,68},{5,69},{6,70},{7,71},{8,72},{9,... | collective-permute-start | bytes 196616 | tf_op jit(solution)/shard_map/ppermute | solution.py:38
  19.9 0.3 collective-permute-start.2
  20.2 2.4 %collective-permute-start.3 = (f32[16,1024]{1,0:T(8,128)S(1)}, f32[16,1024]{1,0:T(8,128)S(1)}, u32[]{:S(2)}, u32[]{:S(2)}) collective-permute-start(f32[16,1024]{1,0:T(8,128)S(1)} %add.56.refs_2_.refs_0_), channel_id=1, source_target_pairs={{0,96},{1,97},{2,98},{3,99},{4,100},{5,101},{6,102},{7,103},{8,104... | collective-permute-start | bytes 196616 | tf_op jit(solution)/shard_map/ppermute | solution.py:38
  22.5 1.0 combine.3
  23.6 0.9 collective-permute-done.2.refs_2_
  24.5 0.1 collective-permute-start.4
  24.6 2.8 %collective-permute-start.14 = (f32[4,32,3968]{2,1,0:T(8,128)S(1)}, f32[4,32,3968]{2,1,0:T(8,128)S(1)}, u32[]{:S(2)}, u32[]{:S(2)}) collective-permute-start(f32[4,32,3968]{2,1,0:T(8,128)S(1)} %get-tuple-element.55), channel_id=1, source_target_pairs={{0,12},{1,13},{2,14},{3,15},{4,0},{5,1},{6,2},{7,3},{8,4},{9,5},{1... | collective-permute-start | bytes 6094856 | tf_op jit(solution)/shard_map/ppermute | solution.py:38
  27.4 1.3 %collective-permute-done.4.refs_1_ = f32[16,1024]{1,0:T(8,128)S(1)} collective-permute-done((f32[16,1024]{1,0:T(8,128)S(1)}, f32[16,1024]{1,0:T(8,128)S(1)}, u32[]{:S(2)}, u32[]{:S(2)}) %collective-permute-start.4) | collective-permute-done | bytes 65568 | tf_op jit(solution)/shard_map/ppermute | solution.py:38
  28.8 2.2 %collective-permute-start.5 = (f32[16,1024]{1,0:T(8,128)S(1)}, f32[16,1024]{1,0:T(8,128)S(1)}, u32[]{:S(2)}, u32[]{:S(2)}) collective-permute-start(f32[16,1024]{1,0:T(8,128)S(1)} %add.57.refs_0_.refs_2_), channel_id=1, source_target_pairs={{0,3},{1,2},{2,1},{3,0},{4,7},{5,6},{6,5},{7,4},{8,11},{9,10},{10,... | collective-permute-start | bytes 196616 | tf_op jit(solution)/shard_map/ppermute | solution.py:38
  31.0 2.2 %collective-permute-done.5.refs_1_ = f32[16,1024]{1,0:T(8,128)S(1)} collective-permute-done((f32[16,1024]{1,0:T(8,128)S(1)}, f32[16,1024]{1,0:T(8,128)S(1)}, u32[]{:S(2)}, u32[]{:S(2)}) %collective-permute-start.5) | collective-permute-done | bytes 65568 | tf_op jit(solution)/shard_map/ppermute | solution.py:38
  33.2 4.3 %collective-permute-start.6 = (f32[16,1024]{1,0:T(8,128)S(1)}, f32[16,1024]{1,0:T(8,128)S(1)}, u32[]{:S(2)}, u32[]{:S(2)}) collective-permute-start(f32[16,1024]{1,0:T(8,128)S(1)} %add.58.refs_4_), channel_id=1, source_target_pairs={{0,16},{1,17},{2,18},{3,19},{4,20},{5,21},{6,22},{7,23},{8,24},{9,... | collective-permute-start | bytes 196616 | tf_op jit(solution)/shard_map/ppermute | solution.py:38
  37.5 1.1 combine.4
  38.8 2.7 %collective-permute-start.11 = (f32[16,1024]{1,0:T(8,128)S(1)}, f32[16,1024]{1,0:T(8,128)S(1)}, u32[]{:S(2)}, u32[]{:S(2)}) collective-permute-start(f32[16,1024]{1,0:T(8,128)S(1)} %gate.4.refs_0_.refs_4_), channel_id=1, source_target_pairs={{0,3},{1,0},{2,1},{3,2},{4,7},{5,4},{6,5},{7,6},{8,11},{9,8},{10,9... | collective-permute-start | bytes 196616 | tf_op jit(solution)/shard_map/ppermute | solution.py:38
  41.4 0.6 collective-permute-start.9
  42.0 2.1 %collective-permute-done.10.refs_2_ = f32[16,1024]{1,0:T(8,128)S(1)} collective-permute-done((f32[16,1024]{1,0:T(8,128)S(1)}, f32[16,1024]{1,0:T(8,128)S(1)}, u32[]{:S(2)}, u32[]{:S(2)}) %collective-permute-start.10) | collective-permute-done | bytes 65568 | tf_op jit(solution)/shard_map/ppermute | solution.py:38
  44.1 3.0 %collective-permute-done.9.refs_1_ = f32[16,1024]{1,0:T(8,128)S(1)} collective-permute-done((f32[16,1024]{1,0:T(8,128)S(1)}, f32[16,1024]{1,0:T(8,128)S(1)}, u32[]{:S(2)}, u32[]{:S(2)}) %collective-permute-start.9) | collective-permute-done | bytes 65568 | tf_op jit(solution)/shard_map/ppermute | solution.py:38
  47.1 0.1 collective-permute-start.25
  47.2 2.7 %collective-permute-start.26 = (f32[4,32,3968]{2,1,0:T(8,128)S(1)}, f32[4,32,3968]{2,1,0:T(8,128)S(1)}, u32[]{:S(2)}, u32[]{:S(2)}) collective-permute-start(f32[4,32,3968]{2,1,0:T(8,128)S(1)} %get-tuple-element.62), channel_id=1, source_target_pairs={{0,12},{1,13},{2,14},{3,15},{4,0},{5,1},{6,2},{7,3},{8,4},{9,5},{1... | collective-permute-start | bytes 6094856 | tf_op jit(solution)/shard_map/ppermute | solution.py:38
  49.9 2.0 %collective-permute-start.12 = (f32[16,1024]{1,0:T(8,128)S(1)}, f32[16,1024]{1,0:T(8,128)S(1)}, u32[]{:S(2)}, u32[]{:S(2)}) collective-permute-start(f32[16,1024]{1,0:T(8,128)S(1)} %add_four.6.refs_2_.refs_1_), channel_id=1, source_target_pairs={{0,16},{1,17},{2,18},{3,19},{4,20},{5,21},{6,22},{7,23},{8,24},{9,... | collective-permute-start | bytes 196616 | tf_op jit(solution)/shard_map/ppermute | solution.py:38
  51.9 0.9 collective-permute-done.12.refs_2_
  52.8 3.9 %orthonormal.1 = (f32[32,1024]{1,0:T(8,128)S(1)}, bf16[96,1024]{1,0:T(8,128)(2,1)S(1)}) custom-call(s32[3]{0:T(128)S(1)} %pad_add_fusion.after_ref.scalar_ref.refs_0_, f32[16,1024]{1,0:T(8,128)S(1)} %add_four.6.refs_2_.refs_1_, f32[16,1024]{1,0:T(8,128)S(1)} %collective-permute-done.12.refs_2_, f32[4,32,3968]{2,1,0:T(8,128)S(1)} %get-tuple-element.50.refs_3_), custom_call_target="tpu_custom_call" | custom-call | tf_op jit(solution)/shard_map/orthonormal/pallas_call | solution.py:78
  56.7 3.5 %right_terms.1 = (f32[16,4096]{1,0:T(8,128)S(1)}, f32[16,4096]{1,0:T(8,128)S(1)}) custom-call(s32[3]{0:T(128)S(1)} %pad_add_fusion.after_ref.scalar_ref.refs_0_, bf16[96,1024]{1,0:T(8,128)(2,1)S(1)} %get-tuple-element.51.pieces_ref, bf16[1024,3968]{1,0:T(8,128)(2,1)S(1)} %get-tuple-element.43.partial_ref, ...), custom_call_target="tpu_custom_call" | custom-call | tf_op jit(solution)/shard_map/right_terms/pallas_call | solution.py:344
  60.2 0.4 collective-permute-start.13
  60.7 1.1 combine.5
  61.8 0.6 add_cut.1
  62.4 1.3 %collective-permute-start.16 = (f32[16,1024]{1,0:T(8,128)S(1)}, f32[16,1024]{1,0:T(8,128)S(1)}, u32[]{:S(2)}, u32[]{:S(2)}) collective-permute-start(f32[16,1024]{1,0:T(8,128)S(1)} %get-tuple-element.58), channel_id=1, source_target_pairs={{0,64},{1,65},{2,66},{3,67},{4,68},{5,69},{6,70},{7,71},{8,72},{9,... | collective-permute-start | bytes 196616 | tf_op jit(solution)/shard_map/ppermute | solution.py:38
  63.7 2.3 %collective-permute-start.17 = (f32[16,1024]{1,0:T(8,128)S(1)}, f32[16,1024]{1,0:T(8,128)S(1)}, u32[]{:S(2)}, u32[]{:S(2)}) collective-permute-start(f32[16,1024]{1,0:T(8,128)S(1)} %get-tuple-element.59), channel_id=1, source_target_pairs={{0,32},{1,33},{2,34},{3,35},{4,36},{5,37},{6,38},{7,39},{8,40},{9,... | collective-permute-start | bytes 196616 | tf_op jit(solution)/shard_map/ppermute | solution.py:38
  66.0 0.3 collective-permute-start.18
  66.3 0.8 collective-permute-done.16.refs_1_
  67.1 2.0 %collective-permute-done.17.refs_2_ = f32[16,1024]{1,0:T(8,128)S(1)} collective-permute-done((f32[16,1024]{1,0:T(8,128)S(1)}, f32[16,1024]{1,0:T(8,128)S(1)}, u32[]{:S(2)}, u32[]{:S(2)}) %collective-permute-start.17) | collective-permute-done | bytes 65568 | tf_op jit(solution)/shard_map/ppermute | solution.py:38
  69.1 0.3 collective-permute-done.18.refs_3_
  69.5 0.7 collective-permute-start.19
  70.2 0.7 collective-permute-start.20
  70.9 1.9 %collective-permute-start.21 = (f32[16,1024]{1,0:T(8,128)S(1)}, f32[16,1024]{1,0:T(8,128)S(1)}, u32[]{:S(2)}, u32[]{:S(2)}) collective-permute-start(f32[16,1024]{1,0:T(8,128)S(1)} %add_four.7.refs_0_.refs_4_), channel_id=1, source_target_pairs={{0,3},{1,0},{2,1},{3,2},{4,7},{5,4},{6,5},{7,6},{8,11},{9,8},{10,9... | collective-permute-start | bytes 196616 | tf_op jit(solution)/shard_map/ppermute | solution.py:38
  72.8 2.1 %collective-permute-done.19.refs_1_ = f32[16,1024]{1,0:T(8,128)S(1)} collective-permute-done((f32[16,1024]{1,0:T(8,128)S(1)}, f32[16,1024]{1,0:T(8,128)S(1)}, u32[]{:S(2)}, u32[]{:S(2)}) %collective-permute-start.19) | collective-permute-done | bytes 65568 | tf_op jit(solution)/shard_map/ppermute | solution.py:38
  75.0 1.2 %collective-permute-done.20.refs_2_ = f32[16,1024]{1,0:T(8,128)S(1)} collective-permute-done((f32[16,1024]{1,0:T(8,128)S(1)}, f32[16,1024]{1,0:T(8,128)S(1)}, u32[]{:S(2)}, u32[]{:S(2)}) %collective-permute-start.20) | collective-permute-done | bytes 65568 | tf_op jit(solution)/shard_map/ppermute | solution.py:38
  76.2 1.1 collective-permute-start.22
  77.2 1.1 collective-permute-start.23
  78.4 2.7 %collective-permute-done.22.refs_5_.refs_1_ = f32[16,1024]{1,0:T(8,128)S(1)} collective-permute-done((f32[16,1024]{1,0:T(8,128)S(1)}, f32[16,1024]{1,0:T(8,128)S(1)}, u32[]{:S(2)}, u32[]{:S(2)}) %collective-permute-start.22) | collective-permute-done | bytes 65568 | tf_op jit(solution)/shard_map/ppermute | solution.py:38
  81.1 0.7 collective-permute-done.23.refs_6_.refs_2_
  81.7 0.7 turn_first.1
  82.4 0.3 collective-permute-start.29
  82.7 2.4 %collective-permute-start.30 = (f32[32,3968]{1,0:T(8,128)S(1)}, f32[32,3968]{1,0:T(8,128)S(1)}, u32[]{:S(2)}, u32[]{:S(2)}) collective-permute-start(f32[32,3968]{1,0:T(8,128)S(1)} %get-tuple-element.66), channel_id=1, source_target_pairs={{0,3},{1,0},{2,1},{3,2},{4,7},{5,4},{6,5},{7,6},{8,11},{9,8},{10,9... | collective-permute-start | bytes 1523720 | tf_op jit(solution)/shard_map/ppermute | solution.py:38
  85.2 0.7 collective-permute-start.24
  85.8 2.4 %collective-permute-done.24.refs_3_ = f32[16,1024]{1,0:T(8,128)S(1)} collective-permute-done((f32[16,1024]{1,0:T(8,128)S(1)}, f32[16,1024]{1,0:T(8,128)S(1)}, u32[]{:S(2)}, u32[]{:S(2)}) %collective-permute-start.24) | collective-permute-done | bytes 65568 | tf_op jit(solution)/shard_map/ppermute | solution.py:38
  88.3 2.4 %collective-permute-start.27 = (f32[16,1024]{1,0:T(8,128)S(1)}, f32[16,1024]{1,0:T(8,128)S(1)}, u32[]{:S(2)}, u32[]{:S(2)}) collective-permute-start(f32[16,1024]{1,0:T(8,128)S(1)} %add_four.9.refs_0_.refs_2_), channel_id=1, source_target_pairs={{0,96},{1,97},{2,98},{3,99},{4,100},{5,101},{6,102},{7,103},{8,104... | collective-permute-start | bytes 196616 | tf_op jit(solution)/shard_map/ppermute | solution.py:38
  90.7 0.9 turn_rest.1
  91.7 2.7 %collective-permute-start.33 = (f32[32,3968]{1,0:T(8,128)S(1)}, f32[32,3968]{1,0:T(8,128)S(1)}, u32[]{:S(2)}, u32[]{:S(2)}) collective-permute-start(f32[32,3968]{1,0:T(8,128)S(1)} %get-tuple-element.70), channel_id=1, source_target_pairs={{0,3},{1,0},{2,1},{3,2},{4,7},{5,4},{6,5},{7,6},{8,11},{9,8},{10,9... | collective-permute-start | bytes 1523720 | tf_op jit(solution)/shard_map/ppermute | solution.py:38
  94.4 0.1 ring_add.1
  94.5 2.7 %collective-permute-start.35 = (f32[32,3968]{1,0:T(8,128)S(1)}, f32[32,3968]{1,0:T(8,128)S(1)}, u32[]{:S(2)}, u32[]{:S(2)}) collective-permute-start(f32[32,3968]{1,0:T(8,128)S(1)} %get-tuple-element.73), channel_id=1, source_target_pairs={{0,3},{1,0},{2,1},{3,2},{4,7},{5,4},{6,5},{7,6},{8,11},{9,8},{10,9... | collective-permute-start | bytes 1523720 | tf_op jit(solution)/shard_map/ppermute | solution.py:38
  97.2 3.8 %collective-permute-done.28.refs_2_ = f32[16,2048]{1,0:T(8,128)S(1)} collective-permute-done((f32[16,2048]{1,0:T(8,128)S(1)}, f32[16,2048]{1,0:T(8,128)S(1)}, u32[]{:S(2)}, u32[]{:S(2)}) %collective-permute-start.28) | collective-permute-done | bytes 131104 | tf_op jit(solution)/shard_map/ppermute | solution.py:38
  101.0 0.6 join.3.refs_1_.refs_7_.mine_ref
  101.6 9.8 %collective-permute-start.31 = (f32[16,4096]{1,0:T(8,128)S(1)}, f32[16,4096]{1,0:T(8,128)S(1)}, u32[]{:S(2)}, u32[]{:S(2)}) collective-permute-start(f32[16,4096]{1,0:T(8,128)S(1)} %join.3.refs_1_.refs_7_.mine_ref), channel_id=1, source_target_pairs={{0,16},{1,17},{2,18},{3,19},{4,20},{5,21},{6,22},{7,23},{8,24},{9,... | collective-permute-start | bytes 786440 | tf_op jit(solution)/shard_map/ppermute | solution.py:38
  111.4 1.1 nearly.1
  112.5 0.1 collective-permute-done.31.other_ref
  112.6 2.5 %finish.1 = (bf16[64,3968]{1,0:T(8,128)(2,1)}, f32[64,3968]{1,0:T(8,128)}, f32[32,3968]{1,0:T(8,128)}) custom-call(s32[3]{0:T(128)S(1)} %pad_add_fusion.after_ref.scalar_ref.refs_0_, f32[16,4096]{1,0:T(8,128)S(1)} %join.3.refs_1_.refs_7_.mine_ref, f32[16,4096]{1,0:T(8,128)S(1)} %collective-permute-done.31.other_ref, ...), custom_call_target="tpu_custom_call" | custom-call | tf_op jit(solution)/shard_map/finish/pallas_call | solution.py:482
  (41 shorter events, 0.5 us)
Async XLA Ops:
  0.9 6.1 %copy-start = (f32[1,64,3968]{2,1,0:T(8,128)S(1)}, f32[1,64,3968]{2,1,0:T(8,128)}, u32[]{:S(2)}) copy-start(f32[1,64,3968]{2,1,0:T(8,128)} %param.4) | copy-start | bytes 3047428
  0.9 6.1 %copy-start.1 = (f32[3968,32]{0,1:T(8,128)S(1)}, f32[3968,32]{0,1:T(8,128)}, u32[]{:S(2)}) copy-start(f32[3968,32]{0,1:T(8,128)} %param.5) | copy-start | bytes 1523716
  3.3 34.3 %collective-permute-start.7 = (f32[4,32,3968]{2,1,0:T(8,128)S(1)}, f32[4,32,3968]{2,1,0:T(8,128)S(1)}, u32[]{:S(2)}, u32[]{:S(2)}) collective-permute-start(f32[4,32,3968]{2,1,0:T(8,128)S(1)} %get-tuple-element.40.after_ref), channel_id=1, source_target_pairs={{0,4},{1,5},{2,6},{3,7},{4,8},{5,9},{6,10},{7,11},{8,12},{9,13},{1... | collective-permute-start | bytes 6094856 | tf_op jit(solution)/shard_map/ppermute | solution.py:38
  5.5 32.1 %collective-permute-start.8 = (f32[4,32,3968]{2,1,0:T(8,128)S(1)}, f32[4,32,3968]{2,1,0:T(8,128)S(1)}, u32[]{:S(2)}, u32[]{:S(2)}) collective-permute-start(f32[4,32,3968]{2,1,0:T(8,128)S(1)} %get-tuple-element.47), channel_id=1, source_target_pairs={{0,12},{1,13},{2,14},{3,15},{4,0},{5,1},{6,2},{7,3},{8,4},{9,5},{1... | collective-permute-start | bytes 6094856 | tf_op jit(solution)/shard_map/ppermute | solution.py:38
  14.1 3.0 %collective-permute-start = (f32[16,1024]{1,0:T(8,128)S(1)}, f32[16,1024]{1,0:T(8,128)S(1)}, u32[]{:S(2)}, u32[]{:S(2)}) collective-permute-start(f32[16,1024]{1,0:T(8,128)S(1)} %get-tuple-element.42), channel_id=1, source_target_pairs={{0,16},{1,17},{2,18},{3,19},{4,20},{5,21},{6,22},{7,23},{8,24},{9,... | collective-permute-start | bytes 196616 | tf_op jit(solution)/shard_map/ppermute | solution.py:38
  17.0 6.5 %collective-permute-start.1 = (f32[16,1024]{1,0:T(8,128)S(1)}, f32[16,1024]{1,0:T(8,128)S(1)}, u32[]{:S(2)}, u32[]{:S(2)}) collective-permute-start(f32[16,1024]{1,0:T(8,128)S(1)} %add.56.refs_2_.refs_0_), channel_id=1, source_target_pairs={{0,64},{1,65},{2,66},{3,67},{4,68},{5,69},{6,70},{7,71},{8,72},{9,... | collective-permute-start | bytes 196616 | tf_op jit(solution)/shard_map/ppermute | solution.py:38
  19.9 4.6 %collective-permute-start.2 = (f32[16,1024]{1,0:T(8,128)S(1)}, f32[16,1024]{1,0:T(8,128)S(1)}, u32[]{:S(2)}, u32[]{:S(2)}) collective-permute-start(f32[16,1024]{1,0:T(8,128)S(1)} %add.56.refs_2_.refs_0_), channel_id=1, source_target_pairs={{0,32},{1,33},{2,34},{3,35},{4,36},{5,37},{6,38},{7,39},{8,40},{9,... | collective-permute-start | bytes 196616 | tf_op jit(solution)/shard_map/ppermute | solution.py:38
  20.2 4.3 %collective-permute-start.3 = (f32[16,1024]{1,0:T(8,128)S(1)}, f32[16,1024]{1,0:T(8,128)S(1)}, u32[]{:S(2)}, u32[]{:S(2)}) collective-permute-start(f32[16,1024]{1,0:T(8,128)S(1)} %add.56.refs_2_.refs_0_), channel_id=1, source_target_pairs={{0,96},{1,97},{2,98},{3,99},{4,100},{5,101},{6,102},{7,103},{8,104... | collective-permute-start | bytes 196616 | tf_op jit(solution)/shard_map/ppermute | solution.py:38
  24.5 4.3 %collective-permute-start.4 = (f32[16,1024]{1,0:T(8,128)S(1)}, f32[16,1024]{1,0:T(8,128)S(1)}, u32[]{:S(2)}, u32[]{:S(2)}) collective-permute-start(f32[16,1024]{1,0:T(8,128)S(1)} %add_four.5.refs_2_.refs_0_), channel_id=1, source_target_pairs={{0,1},{1,0},{2,3},{3,2},{4,5},{5,4},{6,7},{7,6},{8,9},{9,8},{10,11... | collective-permute-start | bytes 196616 | tf_op jit(solution)/shard_map/ppermute | solution.py:38
  24.6 36.0 %collective-permute-start.14 = (f32[4,32,3968]{2,1,0:T(8,128)S(1)}, f32[4,32,3968]{2,1,0:T(8,128)S(1)}, u32[]{:S(2)}, u32[]{:S(2)}) collective-permute-start(f32[4,32,3968]{2,1,0:T(8,128)S(1)} %get-tuple-element.55), channel_id=1, source_target_pairs={{0,12},{1,13},{2,14},{3,15},{4,0},{5,1},{6,2},{7,3},{8,4},{9,5},{1... | collective-permute-start | bytes 6094856 | tf_op jit(solution)/shard_map/ppermute | solution.py:38
  27.4 33.2 %collective-permute-start.15 = (f32[4,32,3968]{2,1,0:T(8,128)S(1)}, f32[4,32,3968]{2,1,0:T(8,128)S(1)}, u32[]{:S(2)}, u32[]{:S(2)}) collective-permute-start(f32[4,32,3968]{2,1,0:T(8,128)S(1)} %get-tuple-element.46.refs_2_), channel_id=1, source_target_pairs={{0,4},{1,5},{2,6},{3,7},{4,8},{5,9},{6,10},{7,11},{8,12},{9,13},{1... | collective-permute-start | bytes 6094856 | tf_op jit(solution)/shard_map/ppermute | solution.py:38
  28.8 4.4 %collective-permute-start.5 = (f32[16,1024]{1,0:T(8,128)S(1)}, f32[16,1024]{1,0:T(8,128)S(1)}, u32[]{:S(2)}, u32[]{:S(2)}) collective-permute-start(f32[16,1024]{1,0:T(8,128)S(1)} %add.57.refs_0_.refs_2_), channel_id=1, source_target_pairs={{0,3},{1,2},{2,1},{3,0},{4,7},{5,6},{6,5},{7,4},{8,11},{9,10},{10,... | collective-permute-start | bytes 196616 | tf_op jit(solution)/shard_map/ppermute | solution.py:38
  33.2 5.5 %collective-permute-start.6 = (f32[16,1024]{1,0:T(8,128)S(1)}, f32[16,1024]{1,0:T(8,128)S(1)}, u32[]{:S(2)}, u32[]{:S(2)}) collective-permute-start(f32[16,1024]{1,0:T(8,128)S(1)} %add.58.refs_4_), channel_id=1, source_target_pairs={{0,16},{1,17},{2,18},{3,19},{4,20},{5,21},{6,22},{7,23},{8,24},{9,... | collective-permute-start | bytes 196616 | tf_op jit(solution)/shard_map/ppermute | solution.py:38
  38.7 5.5 %collective-permute-start.10 = (f32[16,1024]{1,0:T(8,128)S(1)}, f32[16,1024]{1,0:T(8,128)S(1)}, u32[]{:S(2)}, u32[]{:S(2)}) collective-permute-start(f32[16,1024]{1,0:T(8,128)S(1)} %gate.4.refs_0_.refs_4_), channel_id=1, source_target_pairs={{0,1},{1,2},{2,3},{3,0},{4,5},{5,6},{6,7},{7,4},{8,9},{9,10},{10,1... | collective-permute-start | bytes 196616 | tf_op jit(solution)/shard_map/ppermute | solution.py:38
  38.8 5.4 %collective-permute-start.11 = (f32[16,1024]{1,0:T(8,128)S(1)}, f32[16,1024]{1,0:T(8,128)S(1)}, u32[]{:S(2)}, u32[]{:S(2)}) collective-permute-start(f32[16,1024]{1,0:T(8,128)S(1)} %gate.4.refs_0_.refs_4_), channel_id=1, source_target_pairs={{0,3},{1,0},{2,1},{3,2},{4,7},{5,4},{6,5},{7,6},{8,11},{9,8},{10,9... | collective-permute-start | bytes 196616 | tf_op jit(solution)/shard_map/ppermute | solution.py:38
  41.4 5.7 %collective-permute-start.9 = (f32[16,1024]{1,0:T(8,128)S(1)}, f32[16,1024]{1,0:T(8,128)S(1)}, u32[]{:S(2)}, u32[]{:S(2)}) collective-permute-start(f32[16,1024]{1,0:T(8,128)S(1)} %gate.4.refs_0_.refs_4_), channel_id=1, source_target_pairs={{0,2},{1,3},{2,0},{3,1},{4,6},{5,7},{6,4},{7,5},{8,10},{9,11},{10,... | collective-permute-start | bytes 196616 | tf_op jit(solution)/shard_map/ppermute | solution.py:38
  47.1 34.6 %collective-permute-start.25 = (f32[4,32,3968]{2,1,0:T(8,128)S(1)}, f32[4,32,3968]{2,1,0:T(8,128)S(1)}, u32[]{:S(2)}, u32[]{:S(2)}) collective-permute-start(f32[4,32,3968]{2,1,0:T(8,128)S(1)} %get-tuple-element.50.refs_3_), channel_id=1, source_target_pairs={{0,4},{1,5},{2,6},{3,7},{4,8},{5,9},{6,10},{7,11},{8,12},{9,13},{1... | collective-permute-start | bytes 6094856 | tf_op jit(solution)/shard_map/ppermute | solution.py:38
  47.2 34.5 %collective-permute-start.26 = (f32[4,32,3968]{2,1,0:T(8,128)S(1)}, f32[4,32,3968]{2,1,0:T(8,128)S(1)}, u32[]{:S(2)}, u32[]{:S(2)}) collective-permute-start(f32[4,32,3968]{2,1,0:T(8,128)S(1)} %get-tuple-element.62), channel_id=1, source_target_pairs={{0,12},{1,13},{2,14},{3,15},{4,0},{5,1},{6,2},{7,3},{8,4},{9,5},{1... | collective-permute-start | bytes 6094856 | tf_op jit(solution)/shard_map/ppermute | solution.py:38
  49.9 2.9 %collective-permute-start.12 = (f32[16,1024]{1,0:T(8,128)S(1)}, f32[16,1024]{1,0:T(8,128)S(1)}, u32[]{:S(2)}, u32[]{:S(2)}) collective-permute-start(f32[16,1024]{1,0:T(8,128)S(1)} %add_four.6.refs_2_.refs_1_), channel_id=1, source_target_pairs={{0,16},{1,17},{2,18},{3,19},{4,20},{5,21},{6,22},{7,23},{8,24},{9,... | collective-permute-start | bytes 196616 | tf_op jit(solution)/shard_map/ppermute | solution.py:38
  60.2 1.6 %collective-permute-start.13 = (f32[16,4096]{1,0:T(8,128)S(1)}, f32[16,4096]{1,0:T(8,128)S(1)}, u32[]{:S(2)}, u32[]{:S(2)}) collective-permute-start(f32[16,4096]{1,0:T(8,128)S(1)} %get-tuple-element.54.refs_4_), channel_id=1, source_target_pairs={{0,16},{1,17},{2,18},{3,19},{4,20},{5,21},{6,22},{7,23},{8,24},{9,... | collective-permute-start | bytes 786440 | tf_op jit(solution)/shard_map/ppermute | solution.py:38
  62.4 4.7 %collective-permute-start.16 = (f32[16,1024]{1,0:T(8,128)S(1)}, f32[16,1024]{1,0:T(8,128)S(1)}, u32[]{:S(2)}, u32[]{:S(2)}) collective-permute-start(f32[16,1024]{1,0:T(8,128)S(1)} %get-tuple-element.58), channel_id=1, source_target_pairs={{0,64},{1,65},{2,66},{3,67},{4,68},{5,69},{6,70},{7,71},{8,72},{9,... | collective-permute-start | bytes 196616 | tf_op jit(solution)/shard_map/ppermute | solution.py:38
  63.7 5.5 %collective-permute-start.17 = (f32[16,1024]{1,0:T(8,128)S(1)}, f32[16,1024]{1,0:T(8,128)S(1)}, u32[]{:S(2)}, u32[]{:S(2)}) collective-permute-start(f32[16,1024]{1,0:T(8,128)S(1)} %get-tuple-element.59), channel_id=1, source_target_pairs={{0,32},{1,33},{2,34},{3,35},{4,36},{5,37},{6,38},{7,39},{8,40},{9,... | collective-permute-start | bytes 196616 | tf_op jit(solution)/shard_map/ppermute | solution.py:38
  66.0 3.5 %collective-permute-start.18 = (f32[16,1024]{1,0:T(8,128)S(1)}, f32[16,1024]{1,0:T(8,128)S(1)}, u32[]{:S(2)}, u32[]{:S(2)}) collective-permute-start(f32[16,1024]{1,0:T(8,128)S(1)} %get-tuple-element.60), channel_id=1, source_target_pairs={{0,96},{1,97},{2,98},{3,99},{4,100},{5,101},{6,102},{7,103},{8,104... | collective-permute-start | bytes 196616 | tf_op jit(solution)/shard_map/ppermute | solution.py:38
  69.5 5.5 %collective-permute-start.19 = (f32[16,1024]{1,0:T(8,128)S(1)}, f32[16,1024]{1,0:T(8,128)S(1)}, u32[]{:S(2)}, u32[]{:S(2)}) collective-permute-start(f32[16,1024]{1,0:T(8,128)S(1)} %add_four.7.refs_0_.refs_4_), channel_id=1, source_target_pairs={{0,2},{1,3},{2,0},{3,1},{4,6},{5,7},{6,4},{7,5},{8,10},{9,11},{10,... | collective-permute-start | bytes 196616 | tf_op jit(solution)/shard_map/ppermute | solution.py:38
  70.2 6.0 %collective-permute-start.20 = (f32[16,1024]{1,0:T(8,128)S(1)}, f32[16,1024]{1,0:T(8,128)S(1)}, u32[]{:S(2)}, u32[]{:S(2)}) collective-permute-start(f32[16,1024]{1,0:T(8,128)S(1)} %add_four.7.refs_0_.refs_4_), channel_id=1, source_target_pairs={{0,1},{1,2},{2,3},{3,0},{4,5},{5,6},{6,7},{7,4},{8,9},{9,10},{10,1... | collective-permute-start | bytes 196616 | tf_op jit(solution)/shard_map/ppermute | solution.py:38
  70.9 5.2 %collective-permute-start.21 = (f32[16,1024]{1,0:T(8,128)S(1)}, f32[16,1024]{1,0:T(8,128)S(1)}, u32[]{:S(2)}, u32[]{:S(2)}) collective-permute-start(f32[16,1024]{1,0:T(8,128)S(1)} %add_four.7.refs_0_.refs_4_), channel_id=1, source_target_pairs={{0,3},{1,0},{2,1},{3,2},{4,7},{5,4},{6,5},{7,6},{8,11},{9,8},{10,9... | collective-permute-start | bytes 196616 | tf_op jit(solution)/shard_map/ppermute | solution.py:38
  76.2 4.9 %collective-permute-start.22 = (f32[16,1024]{1,0:T(8,128)S(1)}, f32[16,1024]{1,0:T(8,128)S(1)}, u32[]{:S(2)}, u32[]{:S(2)}) collective-permute-start(f32[16,1024]{1,0:T(8,128)S(1)} %add_four.8.refs_0_), channel_id=1, source_target_pairs={{0,8},{1,9},{2,10},{3,11},{4,12},{5,13},{6,14},{7,15},{8,0},{9,1},... | collective-permute-start | bytes 196616 | tf_op jit(solution)/shard_map/ppermute | solution.py:38
  77.2 4.5 %collective-permute-start.23 = (f32[16,1024]{1,0:T(8,128)S(1)}, f32[16,1024]{1,0:T(8,128)S(1)}, u32[]{:S(2)}, u32[]{:S(2)}) collective-permute-start(f32[16,1024]{1,0:T(8,128)S(1)} %add_four.8.refs_0_), channel_id=1, source_target_pairs={{0,4},{1,5},{2,6},{3,7},{4,8},{5,9},{6,10},{7,11},{8,12},{9,13},{1... | collective-permute-start | bytes 196616 | tf_op jit(solution)/shard_map/ppermute | solution.py:38
  82.4 11.9 %collective-permute-start.29 = (f32[32,3968]{1,0:T(8,128)S(1)}, f32[32,3968]{1,0:T(8,128)S(1)}, u32[]{:S(2)}, u32[]{:S(2)}) collective-permute-start(f32[32,3968]{1,0:T(8,128)S(1)} %get-tuple-element.63.refs_4_.refs_5_), channel_id=1, source_target_pairs={{0,1},{1,2},{2,3},{3,0},{4,5},{5,6},{6,7},{7,4},{8,9},{9,10},{10,1... | collective-permute-start | bytes 1523720 | tf_op jit(solution)/shard_map/ppermute | solution.py:38
  82.7 11.6 %collective-permute-start.30 = (f32[32,3968]{1,0:T(8,128)S(1)}, f32[32,3968]{1,0:T(8,128)S(1)}, u32[]{:S(2)}, u32[]{:S(2)}) collective-permute-start(f32[32,3968]{1,0:T(8,128)S(1)} %get-tuple-element.66), channel_id=1, source_target_pairs={{0,3},{1,0},{2,1},{3,2},{4,7},{5,4},{6,5},{7,6},{8,11},{9,8},{10,9... | collective-permute-start | bytes 1523720 | tf_op jit(solution)/shard_map/ppermute | solution.py:38
  85.2 3.1 %collective-permute-start.24 = (f32[16,1024]{1,0:T(8,128)S(1)}, f32[16,1024]{1,0:T(8,128)S(1)}, u32[]{:S(2)}, u32[]{:S(2)}) collective-permute-start(f32[16,1024]{1,0:T(8,128)S(1)} %add_four.8.refs_0_), channel_id=1, source_target_pairs={{0,12},{1,13},{2,14},{3,15},{4,0},{5,1},{6,2},{7,3},{8,4},{9,5},{1... | collective-permute-start | bytes 196616 | tf_op jit(solution)/shard_map/ppermute | solution.py:38
  88.3 6.0 %collective-permute-start.27 = (f32[16,1024]{1,0:T(8,128)S(1)}, f32[16,1024]{1,0:T(8,128)S(1)}, u32[]{:S(2)}, u32[]{:S(2)}) collective-permute-start(f32[16,1024]{1,0:T(8,128)S(1)} %add_four.9.refs_0_.refs_2_), channel_id=1, source_target_pairs={{0,96},{1,97},{2,98},{3,99},{4,100},{5,101},{6,102},{7,103},{8,104... | collective-permute-start | bytes 196616 | tf_op jit(solution)/shard_map/ppermute | solution.py:38
  91.6 19.8 %collective-permute-start.32 = (f32[32,3968]{1,0:T(8,128)S(1)}, f32[32,3968]{1,0:T(8,128)S(1)}, u32[]{:S(2)}, u32[]{:S(2)}) collective-permute-start(f32[32,3968]{1,0:T(8,128)S(1)} %get-tuple-element.69), channel_id=1, source_target_pairs={{0,1},{1,2},{2,3},{3,0},{4,5},{5,6},{6,7},{7,4},{8,9},{9,10},{10,1... | collective-permute-start | bytes 1523720 | tf_op jit(solution)/shard_map/ppermute | solution.py:38
  91.7 19.7 %collective-permute-start.33 = (f32[32,3968]{1,0:T(8,128)S(1)}, f32[32,3968]{1,0:T(8,128)S(1)}, u32[]{:S(2)}, u32[]{:S(2)}) collective-permute-start(f32[32,3968]{1,0:T(8,128)S(1)} %get-tuple-element.70), channel_id=1, source_target_pairs={{0,3},{1,0},{2,1},{3,2},{4,7},{5,4},{6,5},{7,6},{8,11},{9,8},{10,9... | collective-permute-start | bytes 1523720 | tf_op jit(solution)/shard_map/ppermute | solution.py:38
  94.5 18.1 %collective-permute-start.34 = (f32[32,3968]{1,0:T(8,128)S(1)}, f32[32,3968]{1,0:T(8,128)S(1)}, u32[]{:S(2)}, u32[]{:S(2)}) collective-permute-start(f32[32,3968]{1,0:T(8,128)S(1)} %get-tuple-element.67.refs_3_), channel_id=1, source_target_pairs={{0,1},{1,2},{2,3},{3,0},{4,5},{5,6},{6,7},{7,4},{8,9},{9,10},{10,1... | collective-permute-start | bytes 1523720 | tf_op jit(solution)/shard_map/ppermute | solution.py:38
  94.5 18.0 %collective-permute-start.35 = (f32[32,3968]{1,0:T(8,128)S(1)}, f32[32,3968]{1,0:T(8,128)S(1)}, u32[]{:S(2)}, u32[]{:S(2)}) collective-permute-start(f32[32,3968]{1,0:T(8,128)S(1)} %get-tuple-element.73), channel_id=1, source_target_pairs={{0,3},{1,0},{2,1},{3,2},{4,7},{5,4},{6,5},{7,6},{8,11},{9,8},{10,9... | collective-permute-start | bytes 1523720 | tf_op jit(solution)/shard_map/ppermute | solution.py:38
  97.2 3.8 %collective-permute-start.28 = (f32[16,2048]{1,0:T(8,128)S(1)}, f32[16,2048]{1,0:T(8,128)S(1)}, u32[]{:S(2)}, u32[]{:S(2)}) collective-permute-start(f32[16,2048]{1,0:T(8,128)S(1)} %join.2.refs_4_.refs_1_), channel_id=1, source_target_pairs={{0,32},{1,33},{2,34},{3,35},{4,36},{5,37},{6,38},{7,39},{8,40},{9,... | collective-permute-start | bytes 393224 | tf_op jit(solution)/shard_map/ppermute | solution.py:38
  101.6 10.9 %collective-permute-start.31 = (f32[16,4096]{1,0:T(8,128)S(1)}, f32[16,4096]{1,0:T(8,128)S(1)}, u32[]{:S(2)}, u32[]{:S(2)}) collective-permute-start(f32[16,4096]{1,0:T(8,128)S(1)} %join.3.refs_1_.refs_7_.mine_ref), channel_id=1, source_target_pairs={{0,16},{1,17},{2,18},{3,19},{4,20},{5,21},{6,22},{7,23},{8,24},{9,... | collective-permute-start | bytes 786440 | tf_op jit(solution)/shard_map/ppermute | solution.py:38
